TPU v7x, 32 devices: a whole 2x2x4 slice. The times are simulated.
32 devices in a mesh: dp: 4 (over y, x), pipe: 4 (over z), tensor: 2 (over core).
Axes of the slice: x: 2, y: 2, z: 4, core: 2. Of those that a mesh axis runs over, the one named last changes fastest.
Arguments:
- enc_out: bfloat16 [512, 4096], P('dp', 'tensor'), may hold values from -1.25 to 1.25
- mlp_input: bfloat16 [512, 4096], P('dp', 'tensor'), may hold values from -170 to 170
- grad_kv: bfloat16 [512, 2, 4, 512], P('dp', None, 'pipe', 'tensor'), may hold values from -1.5 to 1.5
- kv_weight: bfloat16 [4096, 2, 4, 512], P('dp', None, 'pipe', 'tensor'), may hold values from -0.09375 to 0.09375
- gate_weight: bfloat16 [4096, 1024], P('dp', ('pipe', 'tensor')), may hold values from -0.09375 to 0.09375
- up_weight: bfloat16 [4096, 1024], P('dp', ('pipe', 'tensor')), may hold values from -0.09375 to 0.09375
- down_weight: bfloat16 [1024, 4096], P(('pipe', 'tensor'), 'dp'), may hold values from -0.1875 to 0.1875
- norm_gain: bfloat16 [4096], replicated, may hold values from 0.099609375 to 1.8984375
Outputs:
- input_grad: bfloat16 [512, 4096], P('dp')
- kv_grad: bfloat16 [4096, 2, 4, 512], P('dp', None, 'pipe', 'tensor')
All inputs are finite; a program needn't handle non-finite values.
Results may differ from a plain program's by a relative error of at most 0.009.
Values may be sent and summed in bfloat16 or wider, within the bound.
No kernel may reach another device: no remote copies, remote signals or barrier semaphores. Data moves between devices by JAX's collectives and lax.ppermute only.
A program may use at most 64 MiB of HBM per device.

v0:
```python
import math

import jax
import jax.numpy as jnp
from jax import lax
from jax.sharding import PartitionSpec as P


def gelu_parts(preact):
    factor = math.sqrt(2.0 / math.pi)
    tangent = jnp.tanh(factor * (preact + 0.044715 * preact * preact * preact))
    gelu_value = 0.5 * preact * (1.0 + tangent)
    gelu_slope = 0.5 * (1.0 + tangent) + 0.5 * preact * (1.0 - tangent * tangent) * factor * (
        1.0 + 3.0 * 0.044715 * preact * preact
    )
    return (gelu_value, gelu_slope)


def fold_blocks(received, groups):
    tok_rows = received.shape[0] // groups
    return jnp.sum(received.reshape(groups, tok_rows, received.shape[1]), axis=0)


def on_device(
    enc_out, mlp_input, grad_kv, kv_weight, gate_weight, up_weight, down_weight, norm_gain
):
    encoded, resid_full = (
        lax.all_gather(enc_out, "tensor", axis=1, tiled=True),
        lax.all_gather(mlp_input, "tensor", axis=1, tiled=True),
    )
    partial_value = jnp.einsum(
        "tslc,dslc->td",
        grad_kv,
        lax.all_gather(kv_weight, "dp", axis=0, tiled=True),
        preferred_element_type=jnp.float32,
    )
    gate_full, up_full, down_full = (
        lax.all_gather(gate_weight, "dp", axis=0, tiled=True),
        lax.all_gather(up_weight, "dp", axis=0, tiled=True),
        lax.all_gather(down_weight, "dp", axis=1, tiled=True),
    )
    values_in = resid_full.astype(jnp.float32)
    width = values_in.shape[1]
    row_scale = lax.rsqrt(jnp.mean(values_in * values_in, axis=1, keepdims=True) + 1e-06)
    gain_row = norm_gain.astype(jnp.float32)
    normed = (values_in * row_scale * gain_row).astype(jnp.bfloat16)
    gate_pre = jnp.dot(normed, gate_full, preferred_element_type=jnp.float32)
    up_pre = jnp.dot(normed, up_full, preferred_element_type=jnp.float32)
    groups = lax.axis_size(("pipe", "tensor"))
    share_cols = width // groups
    col_start = lax.axis_index(("pipe", "tensor")) * share_cols
    upstream_share = fold_blocks(
        lax.all_to_all(
            partial_value.astype(jnp.bfloat16),
            ("pipe", "tensor"),
            split_axis=1,
            concat_axis=0,
            tiled=True,
        ).astype(partial_value.dtype),
        groups,
    )
    upstream_half = lax.all_gather(
        upstream_share.astype(jnp.bfloat16), ("pipe", "tensor"), axis=1, tiled=True
    )
    contract = (((1,), (1,)), ((), ()))
    hidden_grad = lax.dot_general(
        upstream_half, down_full, contract, preferred_element_type=jnp.float32
    )
    gelu_value, gelu_slope = gelu_parts(gate_pre)
    gate_grad = (hidden_grad * up_pre * gelu_slope).astype(jnp.bfloat16)
    up_grad = (hidden_grad * gelu_value).astype(jnp.bfloat16)
    normed_part = lax.dot_general(
        gate_grad, gate_full, contract, preferred_element_type=jnp.float32
    ) + lax.dot_general(up_grad, up_full, contract, preferred_element_type=jnp.float32)
    normed_share = fold_blocks(
        lax.all_to_all(
            normed_part.astype(jnp.bfloat16),
            ("pipe", "tensor"),
            split_axis=1,
            concat_axis=0,
            tiled=True,
        ).astype(normed_part.dtype),
        groups,
    )
    values_share = lax.dynamic_slice_in_dim(values_in, col_start, share_cols, 1)
    gain_share = lax.dynamic_slice_in_dim(gain_row, col_start, share_cols, 0)
    scaled_share = gain_share * normed_share
    row_total = lax.psum(
        jnp.sum(values_share * scaled_share, axis=1, keepdims=True), ("pipe", "tensor")
    )
    row_average = row_total / width
    input_share = (
        upstream_share
        + row_scale * scaled_share
        - values_share * (row_scale * row_scale * row_scale) * row_average
    )
    input_grad = lax.all_gather(
        input_share.astype(jnp.bfloat16), ("pipe", "tensor"), axis=1, tiled=True
    )
    kv_grad = lax.psum_scatter(
        jnp.einsum("td,tslc->dslc", encoded, grad_kv, preferred_element_type=jnp.float32).astype(
            jnp.bfloat16
        ),
        "dp",
        scatter_dimension=0,
        tiled=True,
    )
    return (input_grad, kv_grad)


def solution(mesh):
    placed = (
        P("dp", "tensor"),
        P("dp", "tensor"),
        P("dp", None, "pipe", "tensor"),
        P("dp", None, "pipe", "tensor"),
        P("dp", ("pipe", "tensor")),
        P("dp", ("pipe", "tensor")),
        P(("pipe", "tensor"), "dp"),
        P(),
    )
    return jax.shard_map(
        on_device,
        mesh=mesh,
        in_specs=placed,
        out_specs=(P("dp", None), P("dp", None, "pipe", "tensor")),
        check_vma=False,
    )
```

profile of v0, /device:TPU:9, one launch (start us, length us, event | category | flops | bytes accessed | tf_op | source)
XLA Modules:
  0.0 287.1 jit_solution(15799203669953135067)
XLA Ops:
  7.2 2.4 copy.15
  9.7 1.0 copy.19
  10.8 0.7 all-gather.11.cloned.1.call-update
  12.0 52.3 %all-gather.9.cloned.1.call-done = bf16[4096,2,1,256]{3,0,1,2:T(8,128)(2,1)} async-done(((bf16[1024,2,1,256]{3,0,1,2:T(8,128)(2,1)}), bf16[4096,2,1,256]{3,0,1,2:T(8,128)(2,1)}) %all-gather.9.cloned.1.call-update) | async-done | bytes 4194320 | tf_op jit(solution)/shard_map/all_gather | solution.py:34
  64.3 3.7 %fusion.1 = bf16[128,4096]{1,0:T(8,128)(2,1)S(1)} fusion(bf16[4096,2,1,256]{3,0,1,2:T(8,128)(2,1)} %all-gather.9.cloned.1.call-done, bf16[128,2,256]{2,1,0:T(2,128)(2,1)S(1)} %bitcast.32), kind=kOutput, calls=%fused_computation.4 | convolution fusion | flops 537395200 | bytes 5373952 | tf_op jit(solution)/shard_map/tslc,dslc->td/dot_general | solution.py:31
  68.0 1.1 copy.31
  69.1 5.5 %all-to-all-start = ((bf16[128,8,512]{2,0,1:T(8,128)(2,1)}), bf16[128,8,512]{2,0,1:T(8,128)(2,1)S(1)}, u32[]{:S(2)}, u32[]{:S(2)}) async-start(bf16[128,8,512]{2,0,1:T(8,128)(2,1)} %bitcast.29), calls=%async_computation | async-start | bytes 2097152 | tf_op jit(solution)/shard_map/all_to_all | solution.py:53
  75.1 22.4 %all-to-all-done = bf16[128,8,512]{2,0,1:T(8,128)(2,1)S(1)} async-done(((bf16[128,8,512]{2,0,1:T(8,128)(2,1)}), bf16[128,8,512]{2,0,1:T(8,128)(2,1)S(1)}, u32[]{:S(2)}, u32[]{:S(2)}) %all-to-all-start) | async-done | bytes 1048608 | tf_op jit(solution)/shard_map/all_to_all | solution.py:53
  97.7 0.7 convert_element_type.47
  98.5 0.7 all-gather.17.cloned.1.call-update
  99.2 4.4 %fusion = bf16[4096,2,1,256]{3,0,1,2:T(8,128)(2,1)} fusion(bf16[128,4096]{0,1:T(8,128)(2,1)} %all-gather.23.cloned.1.call-done, bf16[128,2,256]{2,1,0:T(2,128)(2,1)S(1)} %bitcast.33), kind=kOutput, calls=%fused_computation.1 | convolution fusion | flops 538968064 | bytes 5373952 | tf_op jit(solution)/shard_map/td,tslc->dslc/dot_general | solution.py:101
  104.3 1.5 multiply_reduce_fusion
  106.4 10.4 %all-gather.19.cloned.1.call-done = bf16[4096,128]{1,0:T(8,128)(2,1)} async-done(((bf16[1024,128]{1,0:T(8,128)(2,1)}), bf16[4096,128]{1,0:T(8,128)(2,1)}) %all-gather.19.cloned.1.call-update) | async-done | bytes 1048592 | tf_op jit(solution)/shard_map/all_gather | solution.py:38
  116.8 2.1 fusion.8
  119.0 26.2 %all-gather.15.cloned.1.call-done = bf16[128,4096]{1,0:T(8,128)(2,1)} async-done(((bf16[128,1024]{1,0:T(8,128)(2,1)}), bf16[128,4096]{1,0:T(8,128)(2,1)}) %all-gather.15.cloned.1.call-update) | async-done | bytes 1048592 | tf_op jit(solution)/shard_map/all_gather | solution.py:40
  145.2 24.8 %all-gather.13.cloned.1.call-done = bf16[128,4096]{1,0:T(8,128)(2,1)} async-done(((bf16[128,512]{1,0:T(8,128)(2,1)}), bf16[128,4096]{1,0:T(8,128)(2,1)}) %all-gather.13.cloned.1.call-update) | async-done | bytes 1048592 | tf_op jit(solution)/shard_map/all_gather | solution.py:62
  170.0 2.0 fusion.43
  172.0 25.5 %all-gather.17.cloned.1.call-done = bf16[4096,128]{1,0:T(8,128)(2,1)} async-done(((bf16[1024,128]{1,0:T(8,128)(2,1)}), bf16[4096,128]{1,0:T(8,128)(2,1)}) %all-gather.17.cloned.1.call-update) | async-done | bytes 1048592 | tf_op jit(solution)/shard_map/all_gather | solution.py:39
  197.5 2.4 fusion.6
  199.9 1.7 fusion.2
  201.6 1.1 copy.30
  202.6 5.5 %all-to-all-start.1 = ((bf16[128,8,512]{2,0,1:T(8,128)(2,1)}), bf16[128,8,512]{2,0,1:T(8,128)(2,1)S(1)}, u32[]{:S(2)}, u32[]{:S(2)}) async-start(bf16[128,8,512]{2,0,1:T(8,128)(2,1)} %bitcast.28), calls=%async_computation.1 | async-start | bytes 2097152 | tf_op jit(solution)/shard_map/all_to_all | solution.py:76
  208.1 0.8 dynamic_slice.6
  208.8 1.6 convert_element_type.45
  210.4 20.7 %all-to-all-done.1 = bf16[128,8,512]{2,0,1:T(8,128)(2,1)S(1)} async-done(((bf16[128,8,512]{2,0,1:T(8,128)(2,1)}), bf16[128,8,512]{2,0,1:T(8,128)(2,1)S(1)}, u32[]{:S(2)}, u32[]{:S(2)}) %all-to-all-start.1) | async-done | bytes 1048608 | tf_op jit(solution)/shard_map/all_to_all | solution.py:76
  231.3 1.1 multiply_reduce_fusion.1
  232.3 12.8 %psum.7 = f32[128,1]{0,1:T(1,128)S(1)} all-reduce(f32[128,1]{0,1:T(1,128)S(1)} %bitcast.34), channel_id=1, replica_groups=mesh['dp'=4,'pipe'=4,'tensor'=2] {'pipe','tensor'}, use_global_device_ids=true, to_apply=%region_4.0 | all-reduce | flops 128 | bytes 1024 | tf_op jit(solution)/shard_map/psum | solution.py:88
  245.2 1.7 subtract_convert_fusion
  246.9 6.2 %reduce-scatter.2.cloned.1.call-done = bf16[1024,2,1,256]{3,0,1,2:T(8,128)(2,1)} async-done(((bf16[4096,2,1,256]{3,0,1,2:T(8,128)(2,1)}), bf16[1024,2,1,256]{3,0,1,2:T(8,128)(2,1)}) %reduce-scatter.2.cloned.1.call-update) | async-done | bytes 1048592 | tf_op jit(solution)/shard_map/reduce_scatter | solution.py:100
  253.1 3.3 %copy.21 = bf16[1024,2,1,256]{3,1,2,0:T(2,128)(2,1)} copy(bf16[1024,2,1,256]{3,0,1,2:T(8,128)(2,1)} %reduce-scatter.2.cloned.1.call-done) | data formatting | bytes 2097152
  256.4 21.8 %all-gather.21.cloned.1.call-done = bf16[128,4096]{1,0:T(8,128)(2,1)} async-done(((bf16[128,512]{1,0:T(8,128)(2,1)}), bf16[128,4096]{1,0:T(8,128)(2,1)}) %all-gather.21.cloned.1.call-update) | async-done | bytes 1048592 | tf_op jit(solution)/shard_map/all_gather | solution.py:97
  278.3 2.3 copy.33
  (37 shorter events, 3.0 us)
Async XLA Ops:
  7.2 2.5 copy-start.1
  7.2 57.2 %all-gather.9.cloned.1.call-start = ((), (), s32[]{:S(2)}) async-start(), calls=%async_computation.3 | async-start | bytes 5242880 | tf_op jit(solution)/shard_map/all_gather | solution.py:34
  9.6 54.7 %copy-start.2 = (bf16[128,2,1,256]{3,1,2,0:T(2,128)(2,1)S(1)}, bf16[128,2,1,256]{3,1,2,0:T(2,128)(2,1)}, u32[]{:S(2)}) copy-start(bf16[128,2,1,256]{3,1,2,0:T(2,128)(2,1)} %param.10) | copy-start | bytes 393220
  9.6 89.6 %all-gather.23.cloned.1.call-start = ((), (), s32[]{:S(2)}) async-start(), calls=%async_computation.10 | async-start | bytes 1572864 | tf_op jit(solution)/shard_map/all_gather | solution.py:28
  10.7 93.6 %all-gather.11.cloned.1.call-start = ((), (), s32[]{:S(2)}) async-start(), calls=%async_computation.4 | async-start | bytes 1572864 | tf_op jit(solution)/shard_map/all_gather | solution.py:29
  11.4 105.4 %all-gather.19.cloned.1.call-start = ((), (), s32[]{:S(2)}) async-start(), calls=%async_computation.8 | async-start | bytes 1310720 | tf_op jit(solution)/shard_map/all_gather | solution.py:38
  69.1 28.5 %all-to-all-start = ((bf16[128,8,512]{2,0,1:T(8,128)(2,1)}), bf16[128,8,512]{2,0,1:T(8,128)(2,1)S(1)}, u32[]{:S(2)}, u32[]{:S(2)}) async-start(bf16[128,8,512]{2,0,1:T(8,128)(2,1)} %bitcast.29), calls=%async_computation | async-start | bytes 2097152 | tf_op jit(solution)/shard_map/all_to_all | solution.py:53
  74.5 70.6 %all-gather.15.cloned.1.call-start = ((), (), s32[]{:S(2)}) async-start(), calls=%async_computation.6 | async-start | bytes 1310720 | tf_op jit(solution)/shard_map/all_gather | solution.py:40
  75.1 94.9 %all-gather.13.cloned.1.call-start = ((), (), s32[]{:S(2)}) async-start(), calls=%async_computation.5 | async-start | bytes 1179648 | tf_op jit(solution)/shard_map/all_gather | solution.py:62
  98.4 99.1 %all-gather.17.cloned.1.call-start = ((), (), s32[]{:S(2)}) async-start(), calls=%async_computation.7 | async-start | bytes 1310720 | tf_op jit(solution)/shard_map/all_gather | solution.py:39
  99.2 154.0 %reduce-scatter.2.cloned.1.call-start = ((), (), s32[]{:S(2)}) async-start(), calls=%async_computation.11 | async-start | bytes 5242880 | tf_op jit(solution)/shard_map/reduce_scatter | solution.py:100
  103.6 0.7 copy-start.3
  106.4 38.8 %copy-start.4 = (f32[128]{0:T(128)}, f32[128]{0:T(128)S(1)}, u32[]{:S(2)}) copy-start(f32[128]{0:T(128)S(1)} %get-tuple-element.7) | copy-start | bytes 1540
  116.8 80.6 %copy-start = (bf16[128,4096]{1,0:T(8,128)(2,1)S(1)}, bf16[128,4096]{1,0:T(8,128)(2,1)}, u32[]{:S(2)}) copy-start(bf16[128,4096]{1,0:T(8,128)(2,1)} %all-gather.11.cloned.1.call-done) | copy-start | bytes 3145732
  202.6 28.5 %all-to-all-start.1 = ((bf16[128,8,512]{2,0,1:T(8,128)(2,1)}), bf16[128,8,512]{2,0,1:T(8,128)(2,1)S(1)}, u32[]{:S(2)}, u32[]{:S(2)}) async-start(bf16[128,8,512]{2,0,1:T(8,128)(2,1)} %bitcast.28), calls=%async_computation.1 | async-start | bytes 2097152 | tf_op jit(solution)/shard_map/all_to_all | solution.py:76
  208.1 70.2 %all-gather.21.cloned.1.call-start = ((), (), s32[]{:S(2)}) async-start(), calls=%async_computation.9 | async-start | bytes 1179648 | tf_op jit(solution)/shard_map/all_gather | solution.py:97
  208.8 36.3 %copy-start.5 = (f32[128]{0:T(128)S(1)}, f32[128]{0:T(128)}, u32[]{:S(2)}) copy-start(f32[128]{0:T(128)} %copy-done.4) | copy-start | bytes 1540
  208.8 36.3 %copy-start.6 = (f32[128]{0:T(128)S(1)}, f32[128]{0:T(128)}, u32[]{:S(2)}) copy-start(f32[128]{0:T(128)} %get-tuple-element.6) | copy-start | bytes 1540
Sparse Core Ops, SparseCore 0:
  10.4 53.8 all-gather.8
  66.4 9.9 all-gather.22
  78.0 10.0 all-gather.10
  89.7 27.0 all-gather.18
  118.5 26.6 all-gather.14
  147.2 22.7 all-gather.12
  171.8 25.5 all-gather.16
  200.4 52.6 reduce-scatter.1
  255.4 22.7 all-gather.20
where the time goes:
time: 289 us; the launch traced here: 287 us
  waiting for transfers between devices  213 us (74%)
  matrix products  16.2 us (6%)
  between operations  13.9 us (5%)
  blocking collectives  12.8 us (4%)
  local copies, waits for them, and re-layouts  12.5 us (4%)
  starting transfers between devices  11.2 us (4%)
  other arithmetic  7.38 us (3%)
    all_gather x1, waiting for transfers between devices, on_device(): lax.all_gather(kv_weight, 'dp', axis=0, tiled=True)  52.3 us
    all_gather x1, waiting for transfers between devices, on_device(): lax.all_gather(down_weight, 'dp', axis=1, tiled=True)  26.2 us
    all_gather x1, waiting for transfers between devices, on_device(): lax.all_gather(up_weight, 'dp', axis=0, tiled=True)  25.5 us
    all_gather x1, waiting for transfers between devices, on_device(): lax.all_gather(upstream_share.astype(jnp.bfloat16), ('pipe', 'tensor'), a...  24.8 us
    all_to_all x1, waiting for transfers between devices, on_device(): lax.all_to_all(partial_value.astype(jnp.bfloat16), ('pipe', 'tensor'), sp...  22.4 us
    all_gather x1, waiting for transfers between devices, on_device(): lax.all_gather(input_share.astype(jnp.bfloat16), ('pipe', 'tensor'), axis...  21.8 us
    all_to_all x1, waiting for transfers between devices, on_device(): lax.all_to_all(normed_part.astype(jnp.bfloat16), ('pipe', 'tensor'), spli...  20.7 us
    psum x1, blocking collectives, on_device(): lax.psum(jnp.sum(values_share * scaled_share, axis=1, keepdims=True), ('p...  12.8 us
  transfers between devices with their start and end apart: 11, of which 9 were waited for; matrix products, arithmetic and copies ran while one was open for 11% of the time, Pallas kernels for 0%

commit v1 on v0

v1 whole, which is shorter than its diff:
```python
import math

import jax
import jax.numpy as jnp
from jax import lax
from jax.sharding import PartitionSpec as P

DP, PIPE, TENSOR = "dp", "pipe", "tensor"
BF16, F32 = jnp.bfloat16, jnp.float32


def gelu_parts(preact):
    factor = math.sqrt(2.0 / math.pi)
    tangent = jnp.tanh(factor * (preact + 0.044715 * preact * preact * preact))
    gelu_value = 0.5 * preact * (1.0 + tangent)
    gelu_slope = 0.5 * (1.0 + tangent) + 0.5 * preact * (1.0 - tangent * tangent) * factor * (
        1.0 + 3.0 * 0.044715 * preact * preact
    )
    return (gelu_value, gelu_slope)


def send(value, axis, step):
    if step == 0:
        return value
    size = lax.axis_size(axis)
    return lax.ppermute(value, axis, [(src, src ^ step) for src in range(size)])


def gather(value, axis):
    return [send(value, axis, step) for step in range(lax.axis_size(axis))]


def natural(parts, axis, dim):
    mine = lax.axis_index(axis)
    width = parts[0].shape[dim]
    shape = list(parts[0].shape)
    shape[dim] = width * len(parts)
    out = jnp.zeros(shape, parts[0].dtype)
    for step, part in enumerate(parts):
        out = lax.dynamic_update_slice_in_dim(out, part, (mine ^ step) * width, dim)
    return out


def block(value, axis, step, dim):
    width = value.shape[dim] // lax.axis_size(axis)
    start = (lax.axis_index(axis) ^ step) * width
    return lax.dynamic_slice_in_dim(value, start, width, dim)


def total(blocks, axis):
    out = blocks[0].astype(F32)
    for step in range(1, len(blocks)):
        out = out + send(blocks[step].astype(BF16), axis, step).astype(F32)
    return out


def dot_nt(left, right):
    return lax.dot_general(left, right, (((1,), (1,)), ((), ())), preferred_element_type=F32)


def on_device(
    enc_out, mlp_input, grad_kv, kv_weight, gate_weight, up_weight, down_weight, norm_gain
):
    n_dp, n_pipe, n_ten = (lax.axis_size(a) for a in (DP, PIPE, TENSOR))
    tok = grad_kv.shape[0]
    width = norm_gain.shape[0]
    cols = kv_weight.shape[0]
    units = gate_weight.shape[1]
    share = cols // (n_pipe * n_ten)

    grads = jnp.concatenate(gather(grad_kv.reshape(tok, -1), DP), axis=0)

    section = kv_weight.reshape(cols, -1)
    partial = dot_nt(grads, section)
    partial = total([block(partial, TENSOR, k, 1) for k in range(n_ten)], TENSOR)
    partial = total([block(partial, PIPE, k, 1) for k in range(n_pipe)], PIPE)
    partial = partial.astype(BF16).reshape(n_dp, tok, share)
    upstream = jnp.concatenate([send(partial[k], DP, k) for k in range(n_dp)], axis=1)

    down = jnp.concatenate([send(block(down_weight, TENSOR, k, 1), TENSOR, k) for k in range(n_ten)], axis=0)
    down = jnp.concatenate([send(block(down, PIPE, k, 1), PIPE, k) for k in range(n_pipe)], axis=0)
    down = jnp.concatenate(gather(down, DP), axis=1)
    hidden = dot_nt(upstream, down).reshape(tok, n_pipe, n_ten, units)
    hidden = total([hidden[:, :, k] for k in range(n_ten)], TENSOR)
    hidden_grad = total([hidden[:, k] for k in range(n_pipe)], PIPE)

    both = jnp.concatenate([gate_weight, up_weight], axis=1)
    both = jnp.concatenate(gather(both, DP), axis=0)
    resid = natural(gather(mlp_input, TENSOR), TENSOR, 1)
    resid = jnp.concatenate([block(resid, DP, k, 1) for k in range(n_dp)], axis=1)
    gain_row = jnp.concatenate([block(norm_gain, DP, k, 0) for k in range(n_dp)], axis=0).astype(F32)
    values_in = resid.astype(F32)
    row_scale = lax.rsqrt(jnp.mean(values_in * values_in, axis=1, keepdims=True) + 1e-06)
    normed = (values_in * row_scale * gain_row).astype(BF16)
    pre = jnp.dot(normed, both, preferred_element_type=F32)
    gate_pre, up_pre = pre[:, :units], pre[:, units:]

    gelu_value, gelu_slope = gelu_parts(gate_pre)
    gate_grad = hidden_grad * up_pre * gelu_slope
    up_grad = hidden_grad * gelu_value
    dotted = jnp.sum(gate_grad * gate_pre + up_grad * up_pre, axis=1, keepdims=True)
    grads_both = jnp.concatenate([gate_grad, up_grad], axis=1).astype(BF16)
    normed_part = dot_nt(grads_both, both)
    part = row_scale * gain_row * normed_part - values_in * (row_scale * row_scale * (dotted / width))

    part = part.reshape(tok, n_dp, cols)
    part = total([block(part, TENSOR, k, 2) for k in range(n_ten)], TENSOR)
    part = total([block(part, PIPE, k, 2) for k in range(n_pipe)], PIPE)
    part = (part + upstream.reshape(tok, n_dp, share).astype(F32)).astype(BF16)
    whole = natural(gather(part, PIPE), PIPE, 2)
    whole = natural(gather(whole, TENSOR), TENSOR, 2)
    input_grad = natural([whole[:, k] for k in range(n_dp)], DP, 1)

    encoded = natural(gather(enc_out, TENSOR), TENSOR, 1)
    mine = [send(block(block(encoded, DP, k, 1), TENSOR, 0, 1), DP, k) for k in range(n_dp)]
    mine = jnp.concatenate(mine, axis=0)
    mine = natural(gather(mine, TENSOR), TENSOR, 1)
    kv_grad = lax.dot_general(
        mine, grads, (((0,), (0,)), ((), ())), preferred_element_type=F32
    ).astype(BF16)
    return (input_grad, kv_grad.reshape(kv_weight.shape))


def solution(mesh):
    placed = (
        P(DP, TENSOR),
        P(DP, TENSOR),
        P(DP, None, PIPE, TENSOR),
        P(DP, None, PIPE, TENSOR),
        P(DP, (PIPE, TENSOR)),
        P(DP, (PIPE, TENSOR)),
        P((PIPE, TENSOR), DP),
        P(),
    )
    return jax.shard_map(
        on_device,
        mesh=mesh,
        in_specs=placed,
        out_specs=(P(DP, None), P(DP, None, PIPE, TENSOR)),
        check_vma=False,
    )
```

time: 289 us -> 123 us (0.43)
  waiting for transfers between devices: 213 us -> 41.1 us
  starting transfers between devices: 11.2 us -> 43.8 us
  blocking collectives: 12.8 us -> 0 us
  between operations: 13.9 us -> 1.36 us
  local copies, waits for them, and re-layouts: 12.5 us -> 24.3 us
  matrix products: 16.2 us -> 8.42 us
  other arithmetic: 7.38 us -> 3.24 us
    all_gather x8 -> x0, waiting for transfers between devices: 161 us -> none  [the longest x1 52.3 us: on_device(): lax.all_gather(kv_weight, 'dp', axis=0, tiled=True)]
    ppermute x0 -> x38, starting transfers between devices: none -> 43.8 us  [send(): return lax.ppermute(value, axis, [(src, src ^ step) for src in range(size)])]
    all_to_all x2 -> x0, waiting for transfers between devices: 43.1 us -> none  [the longest x1 22.4 us: on_device(): lax.all_to_all(partial_value.astype(jnp.bfloat16), ('pipe', 'tensor'), sp...]
    ppermute x0 -> x38, waiting for transfers between devices: none -> 41.1 us  [send(): return lax.ppermute(value, axis, [(src, src ^ step) for src in range(size)])]
    psum x1 -> x0, blocking collectives: 12.8 us -> none  [on_device(): lax.psum(jnp.sum(values_share * scaled_share, axis=1, keepdims=True), ('p...]
    all_to_all x2 -> x0, starting transfers between devices: 10.9 us -> none  [the longest x1 5.46 us: on_device(): lax.all_to_all(normed_part.astype(jnp.bfloat16), ('pipe', 'tensor'), spli...]
    dot_general x6 -> x5, matrix products: 16.2 us -> 8.42 us  [the longest x3 5.82 us: dot_nt(): lax.dot_general(left, right, (((1,), (1,)), ((), ())), preferred_element_...]
    reduce_scatter x1 -> x0, waiting for transfers between devices: 6.22 us -> none  [on_device(): lax.psum_scatter(jnp.einsum('td,tslc->dslc', encoded, grad_kv, preferred_...]
  transfers between devices with their start and end apart: 11 -> 38, of which waited for: 9 -> 15; matrix products, arithmetic and copies ran while one was open for 11% -> 21% of each run, Pallas kernels for 0% -> 0%
where the time goes in v1:
time: 123 us; the launch traced here: 122 us
  starting transfers between devices  43.8 us (36%)
  waiting for transfers between devices  41.1 us (33%)
  local copies, waits for them, and re-layouts  24.3 us (20%)
  matrix products  8.42 us (7%)
  other arithmetic  3.24 us (3%)
  between operations  1.36 us (1%)
    ppermute x38, starting transfers between devices, send(): return lax.ppermute(value, axis, [(src, src ^ step) for src in range(size)])  43.8 us
    ppermute x38, waiting for transfers between devices, send(): return lax.ppermute(value, axis, [(src, src ^ step) for src in range(size)])  41.1 us
    unnamed x46, local copies, waits for them, and re-layouts  8.31 us
    dot_general x3, matrix products, dot_nt(): lax.dot_general(left, right, (((1,), (1,)), ((), ())), preferred_element_...  5.82 us
    dynamic_update_slice x13, local copies, waits for them, and re-layouts, natural(): out = lax.dynamic_update_slice_in_dim(out, part, (mine ^ step) * width, dim)  5.42 us
    dynamic_slice x6, local copies, waits for them, and re-layouts, block(): return lax.dynamic_slice_in_dim(value, start, width, dim)  4.28 us
  transfers between devices with their start and end apart: 38, of which 15 were waited for; matrix products, arithmetic and copies ran while one was open for 21% of the time, Pallas kernels for 0%

profile of v1, /device:TPU:9, one launch (start us, length us, event | category | flops | bytes accessed | tf_op | source)
XLA Modules:
  0.0 122.3 jit_solution(6537596215548163085)
XLA Ops:
  1.6 1.3 %collective-permute-start.1 = (bf16[128,512]{1,0:T(8,128)(2,1)S(1)}, bf16[128,512]{1,0:T(8,128)(2,1)}, u32[]{:S(2)}, u32[]{:S(2)}) collective-permute-start(bf16[128,512]{1,0:T(8,128)(2,1)S(1)} %bitcast.68), channel_id=1, source_target_pairs={{0,8},{8,0},{16,24},{24,16},{1,9},{9,1},{17,25},{25,17},{2,10},{10... | collective-permute-start | bytes 393224 | tf_op jit(solution)/shard_map/ppermute | solution.py:26
  2.9 1.2 %collective-permute-start.2 = (bf16[128,512]{1,0:T(8,128)(2,1)S(1)}, bf16[128,512]{1,0:T(8,128)(2,1)S(1)}, u32[]{:S(2)}, u32[]{:S(2)}) collective-permute-start(bf16[128,512]{1,0:T(8,128)(2,1)S(1)} %bitcast.69), channel_id=1, source_target_pairs={{0,16},{8,24},{16,0},{24,8},{1,17},{9,25},{17,1},{25,9},{2,18},{10... | collective-permute-start | bytes 393224 | tf_op jit(solution)/shard_map/ppermute | solution.py:26
  4.3 1.5 %collective-permute-start = (bf16[128,2048]{1,0:T(8,128)(2,1)}, bf16[128,2048]{1,0:T(8,128)(2,1)}, u32[]{:S(2)}, u32[]{:S(2)}) collective-permute-start(bf16[128,2048]{1,0:T(8,128)(2,1)} %param.9), channel_id=1, source_target_pairs={{0,1},{1,0},{2,3},{3,2},{4,5},{5,4},{6,7},{7,6},{8,9},{9,8},{10,11... | collective-permute-start | bytes 1572872 | tf_op jit(solution)/shard_map/ppermute | solution.py:26
  6.9 1.9 %constant_dynamic-update-slice_fusion.17 = bf16[128,4096]{1,0:T(8,128)(2,1)} fusion(bf16[128,4096]{1,0:T(8,128)(2,1)} %broadcast.38.clone.1, bf16[128,2048]{1,0:T(8,128)(2,1)} %param.9, s32[]{:T(128)S(6)} %select_n.34), kind=kLoop, calls=%fused_computation.121 | loop fusion | bytes 1048580 | tf_op jit(solution)/shard_map/dynamic_update_slice | solution.py:40
  15.1 1.8 %fusion.61 = f32[512,1024]{1,0:T(8,128)S(1)} fusion(bf16[512,512]{1,0:T(8,128)(2,1)} %copy-done.2, bf16[1024,512]{1,0:T(8,128)(2,1)S(1)} %bitcast.65), kind=kOutput, calls=%fused_computation.134 | convolution fusion | flops 536870912 | bytes 3670016 | tf_op jit(solution)/shard_map/dot_general | solution.py:58
  17.2 2.5 %collective-permute-start.13 = (bf16[256,128]{1,0:T(8,128)(2,1)S(1)}, bf16[256,128]{1,0:T(8,128)(2,1)S(1)}, u32[]{:S(2)}, u32[]{:S(2)}) collective-permute-start(bf16[256,128]{1,0:T(8,128)(2,1)S(1)} %get-tuple-element.34), channel_id=1, source_target_pairs={{0,4},{2,6},{4,0},{6,2},{1,5},{3,7},{5,1},{7,3},{8,12},{10,14},{12... | collective-permute-start | bytes 196616 | tf_op jit(solution)/shard_map/ppermute | solution.py:26
  20.3 1.3 %collective-permute-start.14 = (bf16[256,128]{1,0:T(8,128)(2,1)S(1)}, bf16[256,128]{1,0:T(8,128)(2,1)S(1)}, u32[]{:S(2)}, u32[]{:S(2)}) collective-permute-start(bf16[256,128]{1,0:T(8,128)(2,1)S(1)} %get-tuple-element.35), channel_id=1, source_target_pairs={{0,6},{2,4},{4,2},{6,0},{1,7},{3,5},{5,3},{7,1},{8,14},{10,12},{12... | collective-permute-start | bytes 196616 | tf_op jit(solution)/shard_map/ppermute | solution.py:26
  22.5 3.0 %collective-permute-done.14 = bf16[256,128]{1,0:T(8,128)(2,1)S(1)} collective-permute-done((bf16[256,128]{1,0:T(8,128)(2,1)S(1)}, bf16[256,128]{1,0:T(8,128)(2,1)S(1)}, u32[]{:S(2)}, u32[]{:S(2)}) %collective-permute-start.14) | collective-permute-done | bytes 65568 | tf_op jit(solution)/shard_map/ppermute | solution.py:26
  25.5 1.3 %collective-permute-start.15 = (bf16[1024,128]{1,0:T(8,128)(2,1)S(1)}, bf16[1024,128]{1,0:T(8,128)(2,1)S(1)}, u32[]{:S(2)}, u32[]{:S(2)}) collective-permute-start(bf16[1024,128]{1,0:T(8,128)(2,1)S(1)} %pad_maximum_fusion.5), channel_id=1, source_target_pairs={{0,8},{8,0},{16,24},{24,16},{1,9},{9,1},{17,25},{25,17},{2,10},{10... | collective-permute-start | bytes 786440 | tf_op jit(solution)/shard_map/ppermute | solution.py:26
  28.1 2.3 %constant_dynamic-update-slice_fusion.8 = (bf16[128,4096]{1,0:T(8,128)(2,1)}, bf16[128,4096]{1,0:T(8,128)(2,1)}) fusion(bf16[128,4096]{1,0:T(8,128)(2,1)} %constant_dynamic-update-slice_fusion.9, bf16[128,2048]{1,0:T(8,128)(2,1)} %collective-permute-done.33, s32[]{:T(128)S(6)} %select_n.35, bf16[128,4096]{1,0:T(8,128)(2,1)} %constant_dynamic-update-slice_fusion.17, ...), kind=kLoop, calls=%fused_computation.104 | loop fusion | bytes 2097156 | tf_op jit(solution)/shard_map/dynamic_update_slice | solution.py:40
  31.2 1.6 %collective-permute-start.6 = (bf16[512,128]{1,0:T(8,128)(2,1)S(1)}, bf16[512,128]{1,0:T(8,128)(2,1)S(1)}, u32[]{:S(2)}, u32[]{:S(2)}) collective-permute-start(bf16[512,128]{1,0:T(8,128)(2,1)S(1)} %get-tuple-element.27), channel_id=1, source_target_pairs={{0,4},{2,6},{4,0},{6,2},{1,5},{3,7},{5,1},{7,3},{8,12},{10,14},{12... | collective-permute-start | bytes 393224 | tf_op jit(solution)/shard_map/ppermute | solution.py:26
  33.4 1.3 %constant_dynamic-slice_fusion.11 = (bf16[128,1024]{1,0:T(8,128)(2,1)S(1)}, bf16[128,1024]{1,0:T(8,128)(2,1)S(1)}, bf16[128,1024]{1,0:T(8,128)(2,1)S(1)}, bf16[128,1024]{1,0:T(8,128)(2,1)S(1)}) fusion(bf16[128,4096]{1,0:T(8,128)(2,1)} %get-tuple-element.51, s32[]{:T(128)S(6)} %select_n.36, s32[]{:T(128)S(6)} %select_n.39, s32[]{:T(128)S(6)} %select_n.38, ...), kind=kLoop, calls=%fused_computation.119 | loop fusion | bytes 2097168 | tf_op jit(solution)/shard_map/dynamic_slice | solution.py:47
  35.0 1.6 %collective-permute-done.6 = bf16[512,128]{1,0:T(8,128)(2,1)S(1)} collective-permute-done((bf16[512,128]{1,0:T(8,128)(2,1)S(1)}, bf16[512,128]{1,0:T(8,128)(2,1)S(1)}, u32[]{:S(2)}, u32[]{:S(2)}) %collective-permute-start.6) | collective-permute-done | bytes 131104 | tf_op jit(solution)/shard_map/ppermute | solution.py:26
  36.6 5.7 %collective-permute-done.7 = bf16[512,128]{1,0:T(8,128)(2,1)S(1)} collective-permute-done((bf16[512,128]{1,0:T(8,128)(2,1)S(1)}, bf16[512,128]{1,0:T(8,128)(2,1)S(1)}, u32[]{:S(2)}, u32[]{:S(2)}) %collective-permute-start.7) | collective-permute-done | bytes 131104 | tf_op jit(solution)/shard_map/ppermute | solution.py:26
  46.6 2.0 %collective-permute-start.24 = (bf16[1024,256]{1,0:T(8,128)(2,1)S(1)}, bf16[1024,256]{1,0:T(8,128)(2,1)}, u32[]{:S(2)}, u32[]{:S(2)}) collective-permute-start(bf16[1024,256]{1,0:T(8,128)(2,1)S(1)} %copy-done.9), channel_id=1, source_target_pairs={{0,24},{8,16},{16,8},{24,0},{1,25},{9,17},{17,9},{25,1},{2,26},{10... | collective-permute-start | bytes 1572872 | tf_op jit(solution)/shard_map/ppermute | solution.py:26
  50.1 5.7 %collective-permute-start.18 = (bf16[128,4,128]{2,0,1:T(8,128)(2,1)S(1)}, bf16[128,4,128]{2,0,1:T(8,128)(2,1)S(1)}, u32[]{:S(2)}, u32[]{:S(2)}) collective-permute-start(bf16[128,4,128]{2,0,1:T(8,128)(2,1)S(1)} %bitcast.72), channel_id=1, source_target_pairs={{0,1},{1,0},{2,3},{3,2},{4,5},{5,4},{6,7},{7,6},{8,9},{9,8},{10,11... | collective-permute-start | bytes 393224 | tf_op jit(solution)/shard_map/ppermute | solution.py:26
  56.9 2.1 %collective-permute-start.20 = (bf16[128,128]{1,0:T(8,128)(2,1)S(1)}, bf16[128,128]{1,0:T(8,128)(2,1)S(1)}, u32[]{:S(2)}, u32[]{:S(2)}) collective-permute-start(bf16[128,128]{1,0:T(8,128)(2,1)S(1)} %get-tuple-element.40), channel_id=1, source_target_pairs={{0,4},{2,6},{4,0},{6,2},{1,5},{3,7},{5,1},{7,3},{8,12},{10,14},{12... | collective-permute-start | bytes 98312 | tf_op jit(solution)/shard_map/ppermute | solution.py:26
  59.6 7.8 %collective-permute-done.24 = bf16[1024,256]{1,0:T(8,128)(2,1)} collective-permute-done((bf16[1024,256]{1,0:T(8,128)(2,1)S(1)}, bf16[1024,256]{1,0:T(8,128)(2,1)}, u32[]{:S(2)}, u32[]{:S(2)}) %collective-permute-start.24) | collective-permute-done | bytes 524320 | tf_op jit(solution)/shard_map/ppermute | solution.py:26
  67.4 1.8 %fusion.4 = f32[128,256]{1,0:T(8,128)S(1)} fusion(f32[4096]{0:T(1024)S(1)} %maximum_convert_fusion, f32[128]{0:T(128)S(1)} %add_rsqrt_fusion, bf16[1024,256]{1,0:T(8,128)(2,1)} %collective-permute-done.24, bf16[1024,256]{1,0:T(8,128)(2,1)} %collective-permute-done.23, bf16[1024,256]{1,0:T(8,128)(2,1)} %collective-permute-done.22, ...), kind=kOutput, calls=%fused_computation.10 | convolution fusion | flops 282591232 | bytes 3293696 | tf_op jit(solution)/shard_map/dot_general | solution.py:95
  69.5 3.6 %fusion = f32[128,4096]{1,0:T(8,128)} fusion(f32[128]{0:T(128)S(1)} %multiply_multiply_fusion.2, f32[4096]{0:T(1024)S(1)} %maximum_convert_fusion, f32[128]{0:T(128)S(1)} %add_rsqrt_fusion, bf16[1024,256]{1,0:T(8,128)(2,1)} %collective-permute-done.24, bf16[1024,256]{1,0:T(8,128)(2,1)} %collective-permute-done.23, ...), kind=kOutput, calls=%fused_computation.1 | convolution fusion | flops 283246592 | bytes 5325824 | tf_op jit(solution)/shard_map/dot_general | solution.py:58
  73.0 1.9 %copy.15 = f32[128,4096]{0,1:T(8,128)S(1)} copy(f32[128,4096]{1,0:T(8,128)} %fusion) | data formatting | bytes 4194304 | tf_op jit(solution)/shard_map/sub | solution.py:104
  76.0 5.3 %collective-permute-start.25 = (bf16[128,4,512]{2,0,1:T(8,128)(2,1)}, bf16[128,4,512]{2,0,1:T(8,128)(2,1)}, u32[]{:S(2)}, u32[]{:S(2)}) collective-permute-start(bf16[128,4,512]{2,0,1:T(8,128)(2,1)} %copy.20), channel_id=1, source_target_pairs={{0,1},{1,0},{2,3},{3,2},{4,5},{5,4},{6,7},{7,6},{8,9},{9,8},{10,11... | collective-permute-start | bytes 1572872 | tf_op jit(solution)/shard_map/ppermute | solution.py:26
  81.3 2.1 %constant_dynamic-slice_fusion.3 = (bf16[128,512]{1,0:T(8,128)(2,1)S(1)}, bf16[128,512]{1,0:T(8,128)(2,1)}, bf16[128,512]{1,0:T(8,128)(2,1)}, bf16[128,512]{1,0:T(8,128)(2,1)}) fusion(bf16[128,4096]{1,0:T(8,128)(2,1)} %get-tuple-element.50, s32[]{:T(128)S(6)} %dynamic_slice.132, s32[]{:T(128)S(6)} %dynamic_slice.138, s32[]{:T(128)S(6)} %dynamic_slice.136, ...), kind=kLoop, calls=%fused_computation.103 | loop fusion | bytes 1048592 | tf_op jit(solution)/shard_map/dynamic_slice | solution.py:47
  88.0 1.6 %collective-permute-start.27 = (bf16[128,4,128]{2,0,1:T(8,128)(2,1)S(1)}, bf16[128,4,128]{2,0,1:T(8,128)(2,1)S(1)}, u32[]{:S(2)}, u32[]{:S(2)}) collective-permute-start(bf16[128,4,128]{2,0,1:T(8,128)(2,1)S(1)} %get-tuple-element.20), channel_id=1, source_target_pairs={{0,4},{2,6},{4,0},{6,2},{1,5},{3,7},{5,1},{7,3},{8,12},{10,14},{12... | collective-permute-start | bytes 393224 | tf_op jit(solution)/shard_map/ppermute | solution.py:26
  90.6 1.8 %collective-permute-done.36 = bf16[128,512]{1,0:T(8,128)(2,1)} collective-permute-done((bf16[128,512]{1,0:T(8,128)(2,1)}, bf16[128,512]{1,0:T(8,128)(2,1)}, u32[]{:S(2)}, u32[]{:S(2)}) %collective-permute-start.36) | collective-permute-done | bytes 131104 | tf_op jit(solution)/shard_map/ppermute | solution.py:26
  93.5 1.3 %collective-permute-start.37 = (bf16[512,512]{1,0:T(8,128)(2,1)S(1)}, bf16[512,512]{1,0:T(8,128)(2,1)S(1)}, u32[]{:S(2)}, u32[]{:S(2)}) collective-permute-start(bf16[512,512]{1,0:T(8,128)(2,1)S(1)} %get-tuple-element.28), channel_id=1, source_target_pairs={{0,1},{1,0},{2,3},{3,2},{4,5},{5,4},{6,7},{7,6},{8,9},{9,8},{10,11... | collective-permute-start | bytes 1572872 | tf_op jit(solution)/shard_map/ppermute | solution.py:26
  95.2 6.8 %collective-permute-done.28 = bf16[128,4,128]{2,0,1:T(8,128)(2,1)S(1)} collective-permute-done((bf16[128,4,128]{2,0,1:T(8,128)(2,1)S(1)}, bf16[128,4,128]{2,0,1:T(8,128)(2,1)S(1)}, u32[]{:S(2)}, u32[]{:S(2)}) %collective-permute-start.28) | collective-permute-done | bytes 131104 | tf_op jit(solution)/shard_map/ppermute | solution.py:26
  102.3 1.5 %collective-permute-start.30 = (bf16[128,4,128]{2,0,1:T(8,128)(2,1)S(1)}, bf16[128,4,128]{2,0,1:T(8,128)(2,1)S(1)}, u32[]{:S(2)}, u32[]{:S(2)}) collective-permute-start(bf16[128,4,128]{2,0,1:T(8,128)(2,1)S(1)} %get-tuple-element.7), channel_id=1, source_target_pairs={{0,4},{2,6},{4,0},{6,2},{1,5},{3,7},{5,1},{7,3},{8,12},{10,14},{12... | collective-permute-start | bytes 393224 | tf_op jit(solution)/shard_map/ppermute | solution.py:26
  106.1 2.1 %collective-permute-done.30 = bf16[128,4,128]{2,0,1:T(8,128)(2,1)S(1)} collective-permute-done((bf16[128,4,128]{2,0,1:T(8,128)(2,1)S(1)}, bf16[128,4,128]{2,0,1:T(8,128)(2,1)S(1)}, u32[]{:S(2)}, u32[]{:S(2)}) %collective-permute-start.30) | collective-permute-done | bytes 131104 | tf_op jit(solution)/shard_map/ppermute | solution.py:26
  108.2 8.2 %collective-permute-done.31 = bf16[128,4,128]{2,0,1:T(8,128)(2,1)S(1)} collective-permute-done((bf16[128,4,128]{2,0,1:T(8,128)(2,1)S(1)}, bf16[128,4,128]{2,0,1:T(8,128)(2,1)S(1)}, u32[]{:S(2)}, u32[]{:S(2)}) %collective-permute-start.31) | collective-permute-done | bytes 131104 | tf_op jit(solution)/shard_map/ppermute | solution.py:26
  116.5 1.4 %collective-permute-start.32 = (bf16[128,4,512]{2,0,1:T(8,128)(2,1)S(1)}, bf16[128,4,512]{2,0,1:T(8,128)(2,1)S(1)}, u32[]{:S(2)}, u32[]{:S(2)}) collective-permute-start(bf16[128,4,512]{2,0,1:T(8,128)(2,1)S(1)} %constant_dynamic-update-slice_fusion.12), channel_id=1, source_target_pairs={{0,1},{1,0},{2,3},{3,2},{4,5},{5,4},{6,7},{7,6},{8,9},{9,8},{10,11... | collective-permute-start | bytes 1572872 | tf_op jit(solution)/shard_map/ppermute | solution.py:26
  118.7 2.0 %copy.18 = bf16[1024,2,1,256]{3,1,2,0:T(2,128)(2,1)} copy(bf16[1024,2,1,256]{0,3,1,2:T(8,128)(2,1)S(1)} %bitcast.67) | data formatting | bytes 2097152
  (145 shorter events, 33.5 us)
Async XLA Ops:
  1.6 11.1 %collective-permute-start.1 = (bf16[128,512]{1,0:T(8,128)(2,1)S(1)}, bf16[128,512]{1,0:T(8,128)(2,1)}, u32[]{:S(2)}, u32[]{:S(2)}) collective-permute-start(bf16[128,512]{1,0:T(8,128)(2,1)S(1)} %bitcast.68), channel_id=1, source_target_pairs={{0,8},{8,0},{16,24},{24,16},{1,9},{9,1},{17,25},{25,17},{2,10},{10... | collective-permute-start | bytes 393224 | tf_op jit(solution)/shard_map/ppermute | solution.py:26
  2.9 11.3 %collective-permute-start.2 = (bf16[128,512]{1,0:T(8,128)(2,1)S(1)}, bf16[128,512]{1,0:T(8,128)(2,1)S(1)}, u32[]{:S(2)}, u32[]{:S(2)}) collective-permute-start(bf16[128,512]{1,0:T(8,128)(2,1)S(1)} %bitcast.69), channel_id=1, source_target_pairs={{0,16},{8,24},{16,0},{24,8},{1,17},{9,25},{17,1},{25,9},{2,18},{10... | collective-permute-start | bytes 393224 | tf_op jit(solution)/shard_map/ppermute | solution.py:26
  4.1 10.1 %collective-permute-start.3 = (bf16[128,512]{1,0:T(8,128)(2,1)S(1)}, bf16[128,512]{1,0:T(8,128)(2,1)S(1)}, u32[]{:S(2)}, u32[]{:S(2)}) collective-permute-start(bf16[128,512]{1,0:T(8,128)(2,1)S(1)} %bitcast.70), channel_id=1, source_target_pairs={{0,24},{8,16},{16,8},{24,0},{1,25},{9,17},{17,9},{25,1},{2,26},{10... | collective-permute-start | bytes 393224 | tf_op jit(solution)/shard_map/ppermute | solution.py:26
  4.3 23.7 %collective-permute-start = (bf16[128,2048]{1,0:T(8,128)(2,1)}, bf16[128,2048]{1,0:T(8,128)(2,1)}, u32[]{:S(2)}, u32[]{:S(2)}) collective-permute-start(bf16[128,2048]{1,0:T(8,128)(2,1)} %param.9), channel_id=1, source_target_pairs={{0,1},{1,0},{2,3},{3,2},{4,5},{5,4},{6,7},{7,6},{8,9},{9,8},{10,11... | collective-permute-start | bytes 1572872 | tf_op jit(solution)/shard_map/ppermute | solution.py:26
  5.9 22.2 %collective-permute-start.33 = (bf16[128,2048]{1,0:T(8,128)(2,1)}, bf16[128,2048]{1,0:T(8,128)(2,1)}, u32[]{:S(2)}, u32[]{:S(2)}) collective-permute-start(bf16[128,2048]{1,0:T(8,128)(2,1)} %param.8), channel_id=1, source_target_pairs={{0,1},{1,0},{2,3},{3,2},{4,5},{5,4},{6,7},{7,6},{8,9},{9,8},{10,11... | collective-permute-start | bytes 1572872 | tf_op jit(solution)/shard_map/ppermute | solution.py:26
  17.0 13.4 %collective-permute-start.4 = (bf16[512,512]{1,0:T(8,128)(2,1)S(1)}, bf16[512,512]{1,0:T(8,128)(2,1)S(1)}, u32[]{:S(2)}, u32[]{:S(2)}) collective-permute-start(bf16[512,512]{1,0:T(8,128)(2,1)S(1)} %dynamic-slice_convert_fusion), channel_id=1, source_target_pairs={{0,1},{1,0},{2,3},{3,2},{4,5},{5,4},{6,7},{7,6},{8,9},{9,8},{10,11... | collective-permute-start | bytes 1572872 | tf_op jit(solution)/shard_map/ppermute | solution.py:26
  17.2 5.3 %collective-permute-start.13 = (bf16[256,128]{1,0:T(8,128)(2,1)S(1)}, bf16[256,128]{1,0:T(8,128)(2,1)S(1)}, u32[]{:S(2)}, u32[]{:S(2)}) collective-permute-start(bf16[256,128]{1,0:T(8,128)(2,1)S(1)} %get-tuple-element.34), channel_id=1, source_target_pairs={{0,4},{2,6},{4,0},{6,2},{1,5},{3,7},{5,1},{7,3},{8,12},{10,14},{12... | collective-permute-start | bytes 196616 | tf_op jit(solution)/shard_map/ppermute | solution.py:26
  20.3 5.2 %collective-permute-start.14 = (bf16[256,128]{1,0:T(8,128)(2,1)S(1)}, bf16[256,128]{1,0:T(8,128)(2,1)S(1)}, u32[]{:S(2)}, u32[]{:S(2)}) collective-permute-start(bf16[256,128]{1,0:T(8,128)(2,1)S(1)} %get-tuple-element.35), channel_id=1, source_target_pairs={{0,6},{2,4},{4,2},{6,0},{1,7},{3,5},{5,3},{7,1},{8,14},{10,12},{12... | collective-permute-start | bytes 196616 | tf_op jit(solution)/shard_map/ppermute | solution.py:26
  25.5 18.9 %collective-permute-start.15 = (bf16[1024,128]{1,0:T(8,128)(2,1)S(1)}, bf16[1024,128]{1,0:T(8,128)(2,1)S(1)}, u32[]{:S(2)}, u32[]{:S(2)}) collective-permute-start(bf16[1024,128]{1,0:T(8,128)(2,1)S(1)} %pad_maximum_fusion.5), channel_id=1, source_target_pairs={{0,8},{8,0},{16,24},{24,16},{1,9},{9,1},{17,25},{25,17},{2,10},{10... | collective-permute-start | bytes 786440 | tf_op jit(solution)/shard_map/ppermute | solution.py:26
  26.8 19.1 %collective-permute-start.16 = (bf16[1024,128]{1,0:T(8,128)(2,1)S(1)}, bf16[1024,128]{1,0:T(8,128)(2,1)S(1)}, u32[]{:S(2)}, u32[]{:S(2)}) collective-permute-start(bf16[1024,128]{1,0:T(8,128)(2,1)S(1)} %pad_maximum_fusion.5), channel_id=1, source_target_pairs={{0,16},{8,24},{16,0},{24,8},{1,17},{9,25},{17,1},{25,9},{2,18},{10... | collective-permute-start | bytes 786440 | tf_op jit(solution)/shard_map/ppermute | solution.py:26
  31.2 5.4 %collective-permute-start.6 = (bf16[512,128]{1,0:T(8,128)(2,1)S(1)}, bf16[512,128]{1,0:T(8,128)(2,1)S(1)}, u32[]{:S(2)}, u32[]{:S(2)}) collective-permute-start(bf16[512,128]{1,0:T(8,128)(2,1)S(1)} %get-tuple-element.27), channel_id=1, source_target_pairs={{0,4},{2,6},{4,0},{6,2},{1,5},{3,7},{5,1},{7,3},{8,12},{10,14},{12... | collective-permute-start | bytes 393224 | tf_op jit(solution)/shard_map/ppermute | solution.py:26
  32.8 9.5 %collective-permute-start.7 = (bf16[512,128]{1,0:T(8,128)(2,1)S(1)}, bf16[512,128]{1,0:T(8,128)(2,1)S(1)}, u32[]{:S(2)}, u32[]{:S(2)}) collective-permute-start(bf16[512,128]{1,0:T(8,128)(2,1)S(1)} %get-tuple-element.26), channel_id=1, source_target_pairs={{0,6},{2,4},{4,2},{6,0},{1,7},{3,5},{5,3},{7,1},{8,14},{10,12},{12... | collective-permute-start | bytes 393224 | tf_op jit(solution)/shard_map/ppermute | solution.py:26
  34.8 11.4 %collective-permute-start.17 = (bf16[1024,128]{1,0:T(8,128)(2,1)S(1)}, bf16[1024,128]{1,0:T(8,128)(2,1)S(1)}, u32[]{:S(2)}, u32[]{:S(2)}) collective-permute-start(bf16[1024,128]{1,0:T(8,128)(2,1)S(1)} %pad_maximum_fusion.5), channel_id=1, source_target_pairs={{0,24},{8,16},{16,8},{24,0},{1,25},{9,17},{17,9},{25,1},{2,26},{10... | collective-permute-start | bytes 786440 | tf_op jit(solution)/shard_map/ppermute | solution.py:26
  43.2 5.5 %collective-permute-start.8 = (bf16[128,128]{1,0:T(8,128)(2,1)S(1)}, bf16[128,128]{1,0:T(8,128)(2,1)S(1)}, u32[]{:S(2)}, u32[]{:S(2)}) collective-permute-start(bf16[128,128]{1,0:T(8,128)(2,1)S(1)} %get-tuple-element.45), channel_id=1, source_target_pairs={{0,8},{8,0},{16,24},{24,16},{1,9},{9,1},{17,25},{25,17},{2,10},{10... | collective-permute-start | bytes 98312 | tf_op jit(solution)/shard_map/ppermute | solution.py:26
  46.0 13.1 %collective-permute-start.22 = (bf16[1024,256]{1,0:T(8,128)(2,1)S(1)}, bf16[1024,256]{1,0:T(8,128)(2,1)}, u32[]{:S(2)}, u32[]{:S(2)}) collective-permute-start(bf16[1024,256]{1,0:T(8,128)(2,1)S(1)} %copy-done.9), channel_id=1, source_target_pairs={{0,8},{8,0},{16,24},{24,16},{1,9},{9,1},{17,25},{25,17},{2,10},{10... | collective-permute-start | bytes 1572872 | tf_op jit(solution)/shard_map/ppermute | solution.py:26
  46.3 13.3 %collective-permute-start.23 = (bf16[1024,256]{1,0:T(8,128)(2,1)S(1)}, bf16[1024,256]{1,0:T(8,128)(2,1)}, u32[]{:S(2)}, u32[]{:S(2)}) collective-permute-start(bf16[1024,256]{1,0:T(8,128)(2,1)S(1)} %copy-done.9), channel_id=1, source_target_pairs={{0,16},{8,24},{16,0},{24,8},{1,17},{9,25},{17,1},{25,9},{2,18},{10... | collective-permute-start | bytes 1572872 | tf_op jit(solution)/shard_map/ppermute | solution.py:26
  46.6 20.7 %collective-permute-start.24 = (bf16[1024,256]{1,0:T(8,128)(2,1)S(1)}, bf16[1024,256]{1,0:T(8,128)(2,1)}, u32[]{:S(2)}, u32[]{:S(2)}) collective-permute-start(bf16[1024,256]{1,0:T(8,128)(2,1)S(1)} %copy-done.9), channel_id=1, source_target_pairs={{0,24},{8,16},{16,8},{24,0},{1,25},{9,17},{17,9},{25,1},{2,26},{10... | collective-permute-start | bytes 1572872 | tf_op jit(solution)/shard_map/ppermute | solution.py:26
  50.1 6.7 %collective-permute-start.18 = (bf16[128,4,128]{2,0,1:T(8,128)(2,1)S(1)}, bf16[128,4,128]{2,0,1:T(8,128)(2,1)S(1)}, u32[]{:S(2)}, u32[]{:S(2)}) collective-permute-start(bf16[128,4,128]{2,0,1:T(8,128)(2,1)S(1)} %bitcast.72), channel_id=1, source_target_pairs={{0,1},{1,0},{2,3},{3,2},{4,5},{5,4},{6,7},{7,6},{8,9},{9,8},{10,11... | collective-permute-start | bytes 393224 | tf_op jit(solution)/shard_map/ppermute | solution.py:26
  56.8 12.4 %collective-permute-start.19 = (bf16[128,128]{1,0:T(8,128)(2,1)S(1)}, bf16[128,128]{1,0:T(8,128)(2,1)S(1)}, u32[]{:S(2)}, u32[]{:S(2)}) collective-permute-start(bf16[128,128]{1,0:T(8,128)(2,1)S(1)} %get-tuple-element.38), channel_id=1, source_target_pairs={{0,2},{2,0},{4,6},{6,4},{1,3},{3,1},{5,7},{7,5},{8,10},{10,8},{12,... | collective-permute-start | bytes 98312 | tf_op jit(solution)/shard_map/ppermute | solution.py:26
  56.9 12.3 %collective-permute-start.20 = (bf16[128,128]{1,0:T(8,128)(2,1)S(1)}, bf16[128,128]{1,0:T(8,128)(2,1)S(1)}, u32[]{:S(2)}, u32[]{:S(2)}) collective-permute-start(bf16[128,128]{1,0:T(8,128)(2,1)S(1)} %get-tuple-element.40), channel_id=1, source_target_pairs={{0,4},{2,6},{4,0},{6,2},{1,5},{3,7},{5,1},{7,3},{8,12},{10,14},{12... | collective-permute-start | bytes 98312 | tf_op jit(solution)/shard_map/ppermute | solution.py:26
  59.0 10.2 %collective-permute-start.21 = (bf16[128,128]{1,0:T(8,128)(2,1)S(1)}, bf16[128,128]{1,0:T(8,128)(2,1)S(1)}, u32[]{:S(2)}, u32[]{:S(2)}) collective-permute-start(bf16[128,128]{1,0:T(8,128)(2,1)S(1)} %get-tuple-element.39), channel_id=1, source_target_pairs={{0,6},{2,4},{4,2},{6,0},{1,7},{3,5},{5,3},{7,1},{8,14},{10,12},{12... | collective-permute-start | bytes 98312 | tf_op jit(solution)/shard_map/ppermute | solution.py:26
  76.0 10.5 %collective-permute-start.25 = (bf16[128,4,512]{2,0,1:T(8,128)(2,1)}, bf16[128,4,512]{2,0,1:T(8,128)(2,1)}, u32[]{:S(2)}, u32[]{:S(2)}) collective-permute-start(bf16[128,4,512]{2,0,1:T(8,128)(2,1)} %copy.20), channel_id=1, source_target_pairs={{0,1},{1,0},{2,3},{3,2},{4,5},{5,4},{6,7},{7,6},{8,9},{9,8},{10,11... | collective-permute-start | bytes 1572872 | tf_op jit(solution)/shard_map/ppermute | solution.py:26
  83.5 6.2 %collective-permute-start.34 = (bf16[128,512]{1,0:T(8,128)(2,1)}, bf16[128,512]{1,0:T(8,128)(2,1)S(1)}, u32[]{:S(2)}, u32[]{:S(2)}) collective-permute-start(bf16[128,512]{1,0:T(8,128)(2,1)} %get-tuple-element.17), channel_id=1, source_target_pairs={{0,8},{8,0},{16,24},{24,16},{1,9},{9,1},{17,25},{25,17},{2,10},{10... | collective-permute-start | bytes 393224 | tf_op jit(solution)/shard_map/ppermute | solution.py:26
  84.7 6.0 %collective-permute-start.35 = (bf16[128,512]{1,0:T(8,128)(2,1)}, bf16[128,512]{1,0:T(8,128)(2,1)S(1)}, u32[]{:S(2)}, u32[]{:S(2)}) collective-permute-start(bf16[128,512]{1,0:T(8,128)(2,1)} %get-tuple-element.16), channel_id=1, source_target_pairs={{0,16},{8,24},{16,0},{24,8},{1,17},{9,25},{17,1},{25,9},{2,18},{10... | collective-permute-start | bytes 393224 | tf_op jit(solution)/shard_map/ppermute | solution.py:26
  84.9 7.5 %collective-permute-start.36 = (bf16[128,512]{1,0:T(8,128)(2,1)}, bf16[128,512]{1,0:T(8,128)(2,1)}, u32[]{:S(2)}, u32[]{:S(2)}) collective-permute-start(bf16[128,512]{1,0:T(8,128)(2,1)} %get-tuple-element.15), channel_id=1, source_target_pairs={{0,24},{8,16},{16,8},{24,0},{1,25},{9,17},{17,9},{25,1},{2,26},{10... | collective-permute-start | bytes 393224 | tf_op jit(solution)/shard_map/ppermute | solution.py:26
  87.9 6.9 %collective-permute-start.26 = (bf16[128,4,128]{2,0,1:T(8,128)(2,1)S(1)}, bf16[128,4,128]{2,0,1:T(8,128)(2,1)S(1)}, u32[]{:S(2)}, u32[]{:S(2)}) collective-permute-start(bf16[128,4,128]{2,0,1:T(8,128)(2,1)S(1)} %get-tuple-element.18), channel_id=1, source_target_pairs={{0,2},{2,0},{4,6},{6,4},{1,3},{3,1},{5,7},{7,5},{8,10},{10,8},{12,... | collective-permute-start | bytes 393224 | tf_op jit(solution)/shard_map/ppermute | solution.py:26
  88.0 7.2 %collective-permute-start.27 = (bf16[128,4,128]{2,0,1:T(8,128)(2,1)S(1)}, bf16[128,4,128]{2,0,1:T(8,128)(2,1)S(1)}, u32[]{:S(2)}, u32[]{:S(2)}) collective-permute-start(bf16[128,4,128]{2,0,1:T(8,128)(2,1)S(1)} %get-tuple-element.20), channel_id=1, source_target_pairs={{0,4},{2,6},{4,0},{6,2},{1,5},{3,7},{5,1},{7,3},{8,12},{10,14},{12... | collective-permute-start | bytes 393224 | tf_op jit(solution)/shard_map/ppermute | solution.py:26
  89.6 12.4 %collective-permute-start.28 = (bf16[128,4,128]{2,0,1:T(8,128)(2,1)S(1)}, bf16[128,4,128]{2,0,1:T(8,128)(2,1)S(1)}, u32[]{:S(2)}, u32[]{:S(2)}) collective-permute-start(bf16[128,4,128]{2,0,1:T(8,128)(2,1)S(1)} %get-tuple-element.19), channel_id=1, source_target_pairs={{0,6},{2,4},{4,2},{6,0},{1,7},{3,5},{5,3},{7,1},{8,14},{10,12},{12... | collective-permute-start | bytes 393224 | tf_op jit(solution)/shard_map/ppermute | solution.py:26
  93.5 24.4 %collective-permute-start.37 = (bf16[512,512]{1,0:T(8,128)(2,1)S(1)}, bf16[512,512]{1,0:T(8,128)(2,1)S(1)}, u32[]{:S(2)}, u32[]{:S(2)}) collective-permute-start(bf16[512,512]{1,0:T(8,128)(2,1)S(1)} %get-tuple-element.28), channel_id=1, source_target_pairs={{0,1},{1,0},{2,3},{3,2},{4,5},{5,4},{6,7},{7,6},{8,9},{9,8},{10,11... | collective-permute-start | bytes 1572872 | tf_op jit(solution)/shard_map/ppermute | solution.py:26
  102.3 5.9 %collective-permute-start.30 = (bf16[128,4,128]{2,0,1:T(8,128)(2,1)S(1)}, bf16[128,4,128]{2,0,1:T(8,128)(2,1)S(1)}, u32[]{:S(2)}, u32[]{:S(2)}) collective-permute-start(bf16[128,4,128]{2,0,1:T(8,128)(2,1)S(1)} %get-tuple-element.7), channel_id=1, source_target_pairs={{0,4},{2,6},{4,0},{6,2},{1,5},{3,7},{5,1},{7,3},{8,12},{10,14},{12... | collective-permute-start | bytes 393224 | tf_op jit(solution)/shard_map/ppermute | solution.py:26
  103.8 12.7 %collective-permute-start.31 = (bf16[128,4,128]{2,0,1:T(8,128)(2,1)S(1)}, bf16[128,4,128]{2,0,1:T(8,128)(2,1)S(1)}, u32[]{:S(2)}, u32[]{:S(2)}) collective-permute-start(bf16[128,4,128]{2,0,1:T(8,128)(2,1)S(1)} %get-tuple-element.7), channel_id=1, source_target_pairs={{0,6},{2,4},{4,2},{6,0},{1,7},{3,5},{5,3},{7,1},{8,14},{10,12},{12... | collective-permute-start | bytes 393224 | tf_op jit(solution)/shard_map/ppermute | solution.py:26
  116.5 4.5 %collective-permute-start.32 = (bf16[128,4,512]{2,0,1:T(8,128)(2,1)S(1)}, bf16[128,4,512]{2,0,1:T(8,128)(2,1)S(1)}, u32[]{:S(2)}, u32[]{:S(2)}) collective-permute-start(bf16[128,4,512]{2,0,1:T(8,128)(2,1)S(1)} %constant_dynamic-update-slice_fusion.12), channel_id=1, source_target_pairs={{0,1},{1,0},{2,3},{3,2},{4,5},{5,4},{6,7},{7,6},{8,9},{9,8},{10,11... | collective-permute-start | bytes 1572872 | tf_op jit(solution)/shard_map/ppermute | solution.py:26
  (24 other events, 152.7 us)

commit v2 on v1

--- a/solution.py
+++ b/solution.py
@@ -3,6 +3,8 @@
 import jax
 import jax.numpy as jnp
 from jax import lax
+from jax.experimental import pallas as pl
+from jax.experimental.pallas import tpu as pltpu
 from jax.sharding import PartitionSpec as P
 
 DP, PIPE, TENSOR = "dp", "pipe", "tensor"
@@ -28,6 +30,11 @@
 
 def gather(value, axis):
     return [send(value, axis, step) for step in range(lax.axis_size(axis))]
+
+
+def relayed(value, axis):
+    far, near = send(value, axis, 2), send(value, axis, 1)
+    return [value, near, far, send(far, axis, 1)]
 
 
 def natural(parts, axis, dim):
@@ -58,7 +65,7 @@
     return lax.dot_general(left, right, (((1,), (1,)), ((), ())), preferred_element_type=F32)
 
 
-def on_device(
+def on_device_any(
     enc_out, mlp_input, grad_kv, kv_weight, gate_weight, up_weight, down_weight, norm_gain
 ):
     n_dp, n_pipe, n_ten = (lax.axis_size(a) for a in (DP, PIPE, TENSOR))
@@ -121,6 +128,270 @@
     return (input_grad, kv_grad.reshape(kv_weight.shape))
 
 
+def aligned(start, lanes):
+    return pl.ds(pl.multiple_of(start, lanes), lanes)
+
+
+def call(body, name, out, operands, scratch=(), flops=0):
+    specs = [pl.BlockSpec(memory_space=pltpu.SMEM)]
+    specs += [pl.BlockSpec(memory_space=pltpu.VMEM)] * (len(operands) - 1)
+    moved = sum(a.size * a.dtype.itemsize for a in (*operands, *out))
+    return pl.pallas_call(
+        body,
+        name=name,
+        out_shape=out,
+        in_specs=specs,
+        out_specs=[pl.BlockSpec(memory_space=pltpu.VMEM)] * len(out),
+        scratch_shapes=list(scratch),
+        compiler_params=pltpu.CompilerParams(vmem_limit_bytes=40 * 1024 * 1024),
+        cost_estimate=pl.CostEstimate(flops=flops, bytes_accessed=moved, transcendentals=0),
+    )(*operands)
+
+
+def shaped(shape, dtype):
+    return jax.ShapeDtypeStruct(shape, dtype)
+
+
+def pack_kernel(where, gate, up, out):
+    cols = gate.shape[0]
+    out[:cols, :] = gate[...]
+    out[cols:, :] = up[...]
+
+
+def upstream_kernel(n_dp, where, *refs):
+    pieces, (section, out, grads) = refs[:n_dp], refs[n_dp:]
+    tok = pieces[0].shape[0]
+    for k, piece in enumerate(pieces):
+        grads[k * tok : (k + 1) * tok, :] = piece[...]
+    out[...] = dot_nt(grads[...], section[...]).astype(out.dtype)
+
+
+def hidden_kernel(n_dp, n_pipe, n_ten, where, mine, other, *refs):
+    downs, (own_hidden, own_upstream), outs = refs[:n_pipe], refs[n_pipe : n_pipe + 2], refs[n_pipe + 2 : -2]
+    upstream, down = refs[-2:]
+    upstream[...] = (mine[...].astype(F32) + other[...].astype(F32)).astype(BF16)
+    units = downs[0].shape[0]
+    for k, part in enumerate(downs):
+        down[k * units : (k + 1) * units, :] = part[...]
+    result = dot_nt(upstream[...], down[...])
+    tok, width = own_hidden.shape
+    half = upstream.shape[1] // n_ten
+    spot = aligned(where[2] * half, half)
+    own_hidden[...] = result[:tok, :]
+    own_upstream[...] = upstream[:tok, spot]
+    for k, out in enumerate(outs, 1):
+        out[:, :width] = result[k * tok : (k + 1) * tok, :].astype(BF16)
+        out[:, width:] = upstream[k * tok : (k + 1) * tok, spot]
+
+
+def forward_kernel(n_dp, where, *refs):
+    packs, (x_mine, x_other, gain, resid, scale, pre, normed) = refs[:n_dp], refs[n_dp:]
+    ten = where[2]
+    half = x_mine.shape[1]
+    resid[:, aligned(ten * half, half)] = x_mine[...]
+    resid[:, aligned((ten ^ 1) * half, half)] = x_other[...]
+    values_in = resid[...].astype(F32)
+    row_scale = lax.rsqrt(jnp.mean(values_in * values_in, axis=1, keepdims=True) + 1e-06)
+    scale[...] = jnp.broadcast_to(row_scale, scale.shape)
+    normed[...] = (values_in * row_scale * gain[...].astype(F32)).astype(BF16)
+    cols = resid.shape[1] // n_dp
+    result = jnp.zeros(pre.shape, F32)
+    for k, pack in enumerate(packs):
+        left = normed[:, aligned((where[0] ^ k) * cols, cols)]
+        right = jnp.concatenate([pack[:cols, :], pack[cols:, :]], axis=1)
+        result += jnp.dot(left, right, preferred_element_type=F32)
+    pre[...] = result
+
+
+def backward_kernel(n_dp, n_pipe, n_ten, where, *refs):
+    terms, ups, packs = refs[:n_pipe], refs[n_pipe : n_pipe + n_dp], refs[n_pipe + n_dp : n_pipe + 2 * n_dp]
+    pre, scale, resid, gain, other, mine = refs[n_pipe + 2 * n_dp :]
+    pipe, ten = where[1], where[2]
+    hidden_grad = terms[0][...]
+    for term in terms[1:]:
+        hidden_grad = hidden_grad + term[...].astype(F32)
+    units = hidden_grad.shape[1]
+    gate_pre, up_pre = pre[:, :units], pre[:, units:]
+    gelu_value, gelu_slope = gelu_parts(gate_pre)
+    gate_grad = hidden_grad * up_pre * gelu_slope
+    up_grad = hidden_grad * gelu_value
+    dotted = jnp.sum(gate_grad * gate_pre + up_grad * up_pre, axis=1, keepdims=True)
+    grads = jnp.concatenate([gate_grad, up_grad], axis=1).astype(BF16)
+    row_scale = scale[:, :1]
+    width = resid.shape[1]
+    pull = row_scale * row_scale * (dotted / width)
+    cols = width // n_dp
+    half = cols // n_ten
+    share = half // n_pipe
+    for step, out in ((1, other), (0, mine)):
+        start = (ten ^ step) * half
+        for k, pack in enumerate(packs):
+            i = where[0] ^ k
+            spot = aligned(i * cols + start, half)
+            rows = [pack[aligned(start, half), :], pack[aligned(cols + start, half), :]]
+            part = dot_nt(grads, jnp.concatenate(rows, axis=1))
+            part = row_scale * (gain[:, spot].astype(F32) * part) - resid[:, spot].astype(F32) * pull
+            if step == 0:
+                part = part + ups[k][:, ups[k].shape[1] - half :].astype(F32)
+            part = part.astype(out.dtype)
+            for j in range(n_pipe):
+                out[pipe ^ j, :, aligned(i * share, share)] = part[:, j * share : (j + 1) * share]
+
+
+def assemble_kernel(n_dp, n_pipe, n_ten, where, *refs):
+    parts, out = refs[:-1], refs[-1]
+    pipe, ten = where[1], where[2]
+    share = parts[0].shape[1] // n_dp
+    for core in range(n_ten):
+        for k in range(n_pipe):
+            part = parts[core * n_pipe + k]
+            for i in range(n_dp):
+                start = ((i * n_ten + (ten ^ core)) * n_pipe + (pipe ^ k)) * share
+                out[:, aligned(start, share)] = part[:, i * share : (i + 1) * share]
+
+
+def encoded_kernel(n_dp, n_ten, where, mine, other, own, near, far):
+    dp, ten = where[0], where[2]
+    tok, half = own.shape
+    held = n_dp // n_ten
+    for k, out in ((0, own), (1, near.at[:tok]), (3, near.at[tok:]), (2, far)):
+        i = dp ^ k
+        spot = aligned((lax.rem(i, held) * n_ten + ten) * half, half)
+        here = i // held == ten
+
+        @pl.when(here)
+        def _(out=out, spot=spot):
+            out[...] = mine[:, spot]
+
+        @pl.when(jnp.logical_not(here))
+        def _(out=out, spot=spot):
+            out[...] = other[:, spot]
+
+
+def kv_kernel(n_dp, where, *refs):
+    pieces, (enc_mine, enc_other, out, grads) = refs[:n_dp], refs[n_dp:]
+    tok = pieces[0].shape[0]
+    half = enc_mine.shape[1]
+    for k, piece in enumerate(pieces):
+        grads[k * tok : (k + 1) * tok, :] = piece[...]
+    for step, enc in ((0, enc_mine), (1, enc_other)):
+        out[aligned((where[2] ^ step) * half, half), :] = lax.dot_general(
+            enc[...], grads[...], (((0,), (0,)), ((), ())), preferred_element_type=F32
+        ).astype(out.dtype)
+
+
+def on_device(
+    enc_out, mlp_input, grad_kv, kv_weight, gate_weight, up_weight, down_weight, norm_gain
+):
+    n_dp, n_pipe, n_ten = (lax.axis_size(a) for a in (DP, PIPE, TENSOR))
+    tok = grad_kv.shape[0]
+    width = norm_gain.shape[0]
+    cols = kv_weight.shape[0]
+    units = gate_weight.shape[1]
+    share = cols // (n_pipe * n_ten)
+    if (n_dp, n_pipe, n_ten) != (4, 4, 2) or share % 128 or tok % 128 or units % 128:
+        return on_device_any(
+            enc_out, mlp_input, grad_kv, kv_weight, gate_weight, up_weight, down_weight, norm_gain
+        )
+    where = jnp.stack([lax.axis_index(a) for a in (DP, PIPE, TENSOR)]).astype(jnp.int32)
+
+    far, near = send(down_weight, PIPE, 2), send(down_weight, PIPE, 1)
+    grads = gather(grad_kv.reshape(tok, -1), DP)
+    x_other = send(mlp_input, TENSOR, 1)
+    (both,) = call(
+        pack_kernel, "gate_and_up", [shaped((2 * cols, units), BF16)], [where, gate_weight, up_weight]
+    )
+    grads, both = lax.optimization_barrier((grads, both))
+    packs = gather(both, DP)
+    grads, far, near = lax.optimization_barrier((grads, far, near))
+    downs = [down_weight, near, far, send(far, PIPE, 1)]
+
+    section = kv_weight.reshape(cols, -1)
+    half = cols // n_ten
+    (mine,) = call(
+        lambda *refs: upstream_kernel(n_dp, *refs),
+        "upstream_terms",
+        [shaped((n_dp * tok, cols), BF16)],
+        [where, *grads, section],
+        [pltpu.VMEM((n_dp * tok, section.shape[1]), BF16)],
+        flops=2 * n_dp * tok * section.size,
+    )
+    other = send(mine, TENSOR, 1)
+    other, packs[1], packs[2] = lax.optimization_barrier((other, packs[1], packs[2]))
+    group = n_pipe * units
+    hidden, upstream, *outs = call(
+        lambda *refs: hidden_kernel(n_dp, n_pipe, n_ten, *refs),
+        "hidden_terms",
+        [shaped((tok, group), F32), shaped((tok, half), BF16)]
+        + [shaped((tok, group + half), BF16)] * (n_dp - 1),
+        [where, mine, other, *downs],
+        [pltpu.VMEM((n_dp * tok, cols), BF16), pltpu.VMEM((group, cols), BF16)],
+        flops=2 * n_dp * tok * cols * group,
+    )
+    ups = [send(out, DP, k) for k, out in enumerate(outs, 1)]
+    encoded = [enc_out, send(enc_out, TENSOR, 1)]
+    encoded = call(
+        lambda *refs: encoded_kernel(n_dp, n_ten, *refs),
+        "encoded_blocks",
+        [shaped((tok, half), BF16), shaped((2 * tok, half), BF16), shaped((tok, half), BF16)],
+        [where, *encoded],
+    )
+    ups, encoded = lax.optimization_barrier((ups, encoded))
+    for part in ups:
+        hidden = hidden + part[:, :group].astype(F32)
+    terms = [hidden[:, :units]]
+    terms += [send(hidden[:, k * units : (k + 1) * units].astype(BF16), PIPE, k) for k in range(1, n_pipe)]
+
+    gain_row = norm_gain.reshape(1, width)
+    resid, scale, pre = call(
+        lambda *refs: forward_kernel(n_dp, *refs),
+        "mlp_forward",
+        [shaped((tok, width), BF16), shaped((tok, 128), F32), shaped((tok, 2 * units), F32)],
+        [where, *packs, mlp_input, x_other, gain_row],
+        [pltpu.VMEM((tok, width), BF16)],
+        flops=4 * tok * width * units,
+    )
+    other, mine = call(
+        lambda *refs: backward_kernel(n_dp, n_pipe, n_ten, *refs),
+        "mlp_backward",
+        [shaped((n_pipe, tok, n_dp * share), BF16), shaped((n_pipe, tok, n_dp * share), F32)],
+        [where, *terms, upstream, *ups, *packs, pre, scale, resid, gain_row],
+        flops=4 * tok * width * units,
+    )
+    mine = mine + send(other, TENSOR, 1).astype(F32)
+    first = send(encoded[1], DP, 1)
+    second = jnp.concatenate([encoded[2], first[tok:]], axis=0)
+    mine, second = lax.optimization_barrier((mine, second))
+    terms = [send(mine[k].astype(BF16), PIPE, k) for k in range(1, n_pipe)]
+    second = send(second, DP, 2)
+    part = mine[0]
+    for term in terms:
+        part = part + term.astype(F32)
+    part = part.astype(BF16)
+    part, second = lax.optimization_barrier((part, second))
+    parts = gather(part, PIPE)
+
+    mine_enc = jnp.concatenate([encoded[0], first[:tok], second], axis=0)
+    (kv_grad,) = call(
+        lambda *refs: kv_kernel(n_dp, *refs),
+        "kv_grad",
+        [shaped((cols, section.shape[1]), BF16)],
+        [where, *grads, mine_enc, send(mine_enc, TENSOR, 1)],
+        [pltpu.VMEM((n_dp * tok, section.shape[1]), BF16)],
+        flops=2 * n_dp * tok * section.size,
+    )
+    kv_grad = kv_grad.reshape(kv_weight.shape)
+    parts, kv_grad = lax.optimization_barrier((parts, kv_grad))
+    parts = parts + [send(part, TENSOR, 1) for part in parts]
+    (input_grad,) = call(
+        lambda *refs: assemble_kernel(n_dp, n_pipe, n_ten, *refs),
+        "input_grad",
+        [shaped((tok, width), BF16)],
+        [where, *parts],
+    )
+    return (input_grad, kv_grad)
+
+
 def solution(mesh):
     placed = (
         P(DP, TENSOR),

time: 123 us -> 105 us (0.85)
  local copies, waits for them, and re-layouts: 24.3 us -> 3.65 us
  Pallas kernels: 0 us -> 10.1 us
  matrix products: 8.42 us -> 0 us
  waiting for transfers between devices: 41.1 us -> 49 us
  starting transfers between devices: 43.8 us -> 39.7 us
  other arithmetic: 3.24 us -> 0.53 us
    pallas_call x0 -> x8, Pallas kernels: none -> 10.1 us  [call(): pl.pallas_call(body, name=name, out_shape=out, in_specs=specs, out_specs=...]
    dot_general x5 -> x0, matrix products: 8.42 us -> none  [the longest x3 5.82 us: dot_nt(): lax.dot_general(left, right, (((1,), (1,)), ((), ())), preferred_element_...]
    ppermute x38 -> x32, waiting for transfers between devices: 41.1 us -> 49 us  [send(): return lax.ppermute(value, axis, [(src, src ^ step) for src in range(size)])]
    unnamed x46 -> x14, local copies, waits for them, and re-layouts: 8.31 us -> 2.45 us
    dynamic_update_slice x13 -> x0, local copies, waits for them, and re-layouts: 5.42 us -> none  [natural(): out = lax.dynamic_update_slice_in_dim(out, part, (mine ^ step) * width, dim)]
    dynamic_slice x6 -> x0, local copies, waits for them, and re-layouts: 4.28 us -> none  [block(): return lax.dynamic_slice_in_dim(value, start, width, dim)]
    ppermute x38 -> x32, starting transfers between devices: 43.8 us -> 39.7 us  [send(): return lax.ppermute(value, axis, [(src, src ^ step) for src in range(size)])]
    another operation x3 -> x0, local copies, waits for them, and re-layouts: 2.25 us -> none
  transfers between devices with their start and end apart: 38 -> 32, of which waited for: 15 -> 20; matrix products, arithmetic and copies ran while one was open for 21% -> 4% of each run, Pallas kernels for 0% -> 7%
where the time goes in v2:
time: 105 us; the launch traced here: 104 us
  waiting for transfers between devices  49 us (47%)
  starting transfers between devices  39.7 us (38%)
  Pallas kernels  10.1 us (10%)
  local copies, waits for them, and re-layouts  3.65 us (3%)
    ppermute x32, waiting for transfers between devices, send(): return lax.ppermute(value, axis, [(src, src ^ step) for src in range(size)])  49 us
    ppermute x32, starting transfers between devices, send(): return lax.ppermute(value, axis, [(src, src ^ step) for src in range(size)])  39.7 us
    pallas_call x8, Pallas kernels, call(): pl.pallas_call(body, name=name, out_shape=out, in_specs=specs, out_specs=...  10.1 us
    unnamed x14, local copies, waits for them, and re-layouts  2.45 us
  transfers between devices with their start and end apart: 32, of which 20 were waited for; matrix products, arithmetic and copies ran while one was open for 4% of the time, Pallas kernels for 7%

profile of v2, /device:TPU:9, one launch (start us, length us, event | category | flops | bytes accessed | tf_op | source)
XLA Modules:
  0.0 103.8 jit_solution(8148169292878627083)
XLA Ops:
  0.6 2.4 %collective-permute-start.3 = (bf16[128,1024]{1,0:T(8,128)(2,1)}, bf16[128,1024]{1,0:T(8,128)(2,1)S(1)}, u32[]{:S(2)}, u32[]{:S(2)}) collective-permute-start(bf16[128,1024]{1,0:T(8,128)(2,1)} %refs_3_.1), channel_id=1, source_target_pairs={{0,4},{2,6},{4,0},{6,2},{1,5},{3,7},{5,1},{7,3},{8,12},{10,14},{12... | collective-permute-start | bytes 786440 | tf_op jit(solution)/shard_map/ppermute | solution.py:28
  4.1 1.3 %collective-permute-start = (bf16[128,512]{1,0:T(8,128)(2,1)S(1)}, bf16[128,512]{1,0:T(8,128)(2,1)S(1)}, u32[]{:S(2)}, u32[]{:S(2)}) collective-permute-start(bf16[128,512]{1,0:T(8,128)(2,1)S(1)} %bitcast.27), channel_id=1, source_target_pairs={{0,8},{8,0},{16,24},{24,16},{1,9},{9,1},{17,25},{25,17},{2,10},{10... | collective-permute-start | bytes 393224 | tf_op jit(solution)/shard_map/ppermute | solution.py:28
  5.4 1.2 %collective-permute-start.1 = (bf16[128,512]{1,0:T(8,128)(2,1)S(1)}, bf16[128,512]{1,0:T(8,128)(2,1)S(1)}, u32[]{:S(2)}, u32[]{:S(2)}) collective-permute-start(bf16[128,512]{1,0:T(8,128)(2,1)S(1)} %bitcast.28), channel_id=1, source_target_pairs={{0,16},{8,24},{16,0},{24,8},{1,17},{9,25},{17,1},{25,9},{2,18},{10... | collective-permute-start | bytes 393224 | tf_op jit(solution)/shard_map/ppermute | solution.py:28
  6.8 1.5 %copy.12 = bf16[128,8,2,256]{3,1,2,0:T(8,128)(2,1)S(1)} copy(bf16[128,8,2,256]{3,2,1,0:T(2,128)(2,1)} %bitcast.32) | data formatting | bytes 2097152
  9.5 2.6 %collective-permute-done.2.refs_4_ = bf16[128,512]{1,0:T(8,128)(2,1)S(1)} collective-permute-done((bf16[128,512]{1,0:T(8,128)(2,1)S(1)}, bf16[128,512]{1,0:T(8,128)(2,1)S(1)}, u32[]{:S(2)}, u32[]{:S(2)}) %collective-permute-start.2) | collective-permute-done | bytes 131104 | tf_op jit(solution)/shard_map/ppermute | solution.py:28
  12.1 2.8 %collective-permute-done.3.refs_5_ = bf16[128,1024]{1,0:T(8,128)(2,1)S(1)} collective-permute-done((bf16[128,1024]{1,0:T(8,128)(2,1)}, bf16[128,1024]{1,0:T(8,128)(2,1)S(1)}, u32[]{:S(2)}, u32[]{:S(2)}) %collective-permute-start.3) | collective-permute-done | bytes 262176 | tf_op jit(solution)/shard_map/ppermute | solution.py:28
  14.9 1.3 %upstream_terms.1.refs_1_ = bf16[512,1024]{1,0:T(8,128)(2,1)S(1)} custom-call(s32[3]{0:T(128)S(1)} %pad_add_fusion.where.refs_0_, bf16[128,512]{1,0:T(8,128)(2,1)S(1)} %bitcast.30, bf16[128,512]{1,0:T(8,128)(2,1)S(1)} %collective-permute-done.refs_2_, bf16[128,512]{1,0:T(8,128)(2,1)S(1)} %collective-permute-done.1.refs_3_, ...), custom_call_target="tpu_custom_call" | custom-call | flops 536870912 | bytes 2621452 | tf_op jit(solution)/shard_map/upstream_terms/pallas_call | solution.py:139
  16.2 1.5 %collective-permute-start.5 = (bf16[512,1024]{1,0:T(8,128)(2,1)S(1)}, bf16[512,1024]{1,0:T(8,128)(2,1)S(1)}, u32[]{:S(2)}, u32[]{:S(2)}) collective-permute-start(bf16[512,1024]{1,0:T(8,128)(2,1)S(1)} %upstream_terms.1.refs_1_), channel_id=1, source_target_pairs={{0,1},{1,0},{2,3},{3,2},{4,5},{5,4},{6,7},{7,6},{8,9},{9,8},{10,11... | collective-permute-start | bytes 3145736 | tf_op jit(solution)/shard_map/ppermute | solution.py:28
  17.7 1.2 %collective-permute-start.6 = (bf16[2048,128]{1,0:T(8,128)(2,1)S(1)}, bf16[2048,128]{1,0:T(8,128)(2,1)S(1)}, u32[]{:S(2)}, u32[]{:S(2)}) collective-permute-start(bf16[2048,128]{1,0:T(8,128)(2,1)S(1)} %gate_and_up.1.refs_1_.refs_9_), channel_id=1, source_target_pairs={{0,8},{8,0},{16,24},{24,16},{1,9},{9,1},{17,25},{25,17},{2,10},{10... | collective-permute-start | bytes 1572872 | tf_op jit(solution)/shard_map/ppermute | solution.py:28
  18.9 1.2 %collective-permute-start.7 = (bf16[2048,128]{1,0:T(8,128)(2,1)S(1)}, bf16[2048,128]{1,0:T(8,128)(2,1)S(1)}, u32[]{:S(2)}, u32[]{:S(2)}) collective-permute-start(bf16[2048,128]{1,0:T(8,128)(2,1)S(1)} %gate_and_up.1.refs_1_.refs_9_), channel_id=1, source_target_pairs={{0,16},{8,24},{16,0},{24,8},{1,17},{9,25},{17,1},{25,9},{2,18},{10... | collective-permute-start | bytes 1572872 | tf_op jit(solution)/shard_map/ppermute | solution.py:28
  21.4 9.8 %collective-permute-done.6.refs_2_.refs_10_ = bf16[2048,128]{1,0:T(8,128)(2,1)S(1)} collective-permute-done((bf16[2048,128]{1,0:T(8,128)(2,1)S(1)}, bf16[2048,128]{1,0:T(8,128)(2,1)S(1)}, u32[]{:S(2)}, u32[]{:S(2)}) %collective-permute-start.6) | collective-permute-done | bytes 524320 | tf_op jit(solution)/shard_map/ppermute | solution.py:28
  32.1 1.3 %hidden_terms.1 = (f32[128,512]{1,0:T(8,128)S(1)}, bf16[128,512]{1,0:T(8,128)(2,1)S(1)}, bf16[128,1024]{1,0:T(8,128)(2,1)S(1)}, bf16[128,1024]{1,0:T(8,128)(2,1)S(1)}, bf16[128,1024]{1,0:T(8,128)(2,1)S(1)}) custom-call(s32[3]{0:T(128)S(1)} %pad_add_fusion.where.refs_0_, bf16[512,1024]{1,0:T(8,128)(2,1)S(1)} %upstream_terms.1.refs_1_, ...), custom_call_target="tpu_custom_call" | custom-call | flops 536870912 | bytes 4325388 | tf_op jit(solution)/shard_map/hidden_terms/pallas_call | solution.py:139
  33.8 1.2 %collective-permute-start.10 = (bf16[128,1024]{1,0:T(8,128)(2,1)S(1)}, bf16[128,1024]{1,0:T(8,128)(2,1)S(1)}, u32[]{:S(2)}, u32[]{:S(2)}) collective-permute-start(bf16[128,1024]{1,0:T(8,128)(2,1)S(1)} %get-tuple-element.58), channel_id=1, source_target_pairs={{0,16},{8,24},{16,0},{24,8},{1,17},{9,25},{17,1},{25,9},{2,18},{10... | collective-permute-start | bytes 786440 | tf_op jit(solution)/shard_map/ppermute | solution.py:28
  36.1 2.0 %collective-permute-start.17 = (bf16[128,2048]{1,0:T(8,128)(2,1)S(1)}, bf16[128,2048]{1,0:T(8,128)(2,1)S(1)}, u32[]{:S(2)}, u32[]{:S(2)}) collective-permute-start(bf16[128,2048]{1,0:T(8,128)(2,1)S(1)} %copy-done.1), channel_id=1, source_target_pairs={{0,1},{1,0},{2,3},{3,2},{4,5},{5,4},{6,7},{7,6},{8,9},{9,8},{10,11... | collective-permute-start | bytes 1572872 | tf_op jit(solution)/shard_map/ppermute | solution.py:28
  40.2 6.4 %collective-permute-done.11.refs_8_ = bf16[128,1024]{1,0:T(8,128)(2,1)S(1)} collective-permute-done((bf16[128,1024]{1,0:T(8,128)(2,1)S(1)}, bf16[128,1024]{1,0:T(8,128)(2,1)S(1)}, u32[]{:S(2)}, u32[]{:S(2)}) %collective-permute-start.11) | collective-permute-done | bytes 262176 | tf_op jit(solution)/shard_map/ppermute | solution.py:28
  47.6 1.8 %collective-permute-start.14 = (bf16[128,128]{1,0:T(8,128)(2,1)S(1)}, bf16[128,128]{1,0:T(8,128)(2,1)S(1)}, u32[]{:S(2)}, u32[]{:S(2)}) collective-permute-start(bf16[128,128]{1,0:T(8,128)(2,1)S(1)} %get-tuple-element.96), channel_id=1, source_target_pairs={{0,4},{2,6},{4,0},{6,2},{1,5},{3,7},{5,1},{7,3},{8,12},{10,14},{12... | collective-permute-start | bytes 98312 | tf_op jit(solution)/shard_map/ppermute | solution.py:28
  50.0 7.9 %collective-permute-done.16.refs_4_.refs_12_ = bf16[2048,128]{1,0:T(8,128)(2,1)S(1)} collective-permute-done((bf16[2048,128]{1,0:T(8,128)(2,1)S(1)}, bf16[2048,128]{1,0:T(8,128)(2,1)S(1)}, u32[]{:S(2)}, u32[]{:S(2)}) %collective-permute-start.16) | collective-permute-done | bytes 524320 | tf_op jit(solution)/shard_map/ppermute | solution.py:28
  57.9 1.6 %mlp_forward.1 = (bf16[128,4096]{1,0:T(8,128)(2,1)S(1)}, f32[128,128]{1,0:T(8,128)S(1)}, f32[128,256]{1,0:T(8,128)S(1)}) custom-call(s32[3]{0:T(128)S(1)} %pad_add_fusion.where.refs_0_, bf16[2048,128]{1,0:T(8,128)(2,1)S(1)} %gate_and_up.1.refs_1_.refs_9_, bf16[2048,128]{1,0:T(8,128)(2,1)S(1)} %collective-permute-done.6.refs_2_.refs_10_, ...), custom_call_target="tpu_custom_call" | custom-call | flops 268435456 | bytes 4399116 | tf_op jit(solution)/shard_map/mlp_forward/pallas_call | solution.py:139
  59.5 1.5 %mlp_backward.1 = (bf16[4,128,512]{2,1,0:T(8,128)(2,1)S(1)}, f32[4,128,512]{2,1,0:T(8,128)S(1)}) custom-call(s32[3]{0:T(128)S(1)} %pad_add_fusion.where.refs_0_, f32[128,128]{1,0:T(8,128)S(1)} %slice.58.refs_1_, bf16[128,128]{1,0:T(8,128)(2,1)S(1)} %collective-permute-done.13.refs_2_, bf16[128,128]{1,0:T(8,128)(2,1)S(1)} %collective-permute-done.14.refs_3_, ...), custom_call_target="tpu_custom_call" | custom-call | flops 268435456 | bytes 6004748 | tf_op jit(solution)/shard_map/mlp_backward/pallas_call | solution.py:139
  61.1 6.3 %collective-permute-start.18 = (bf16[4,128,512]{2,1,0:T(8,128)(2,1)S(1)}, bf16[4,128,512]{2,1,0:T(8,128)(2,1)S(1)}, u32[]{:S(2)}, u32[]{:S(2)}) collective-permute-start(bf16[4,128,512]{2,1,0:T(8,128)(2,1)S(1)} %get-tuple-element.73), channel_id=1, source_target_pairs={{0,1},{1,0},{2,3},{3,2},{4,5},{5,4},{6,7},{7,6},{8,9},{9,8},{10,11... | collective-permute-start | bytes 1572872 | tf_op jit(solution)/shard_map/ppermute | solution.py:28
  67.5 1.5 %collective-permute-done.18 = bf16[4,128,512]{2,1,0:T(8,128)(2,1)S(1)} collective-permute-done((bf16[4,128,512]{2,1,0:T(8,128)(2,1)S(1)}, bf16[4,128,512]{2,1,0:T(8,128)(2,1)S(1)}, u32[]{:S(2)}, u32[]{:S(2)}) %collective-permute-start.18) | collective-permute-done | bytes 524320 | tf_op jit(solution)/shard_map/ppermute | solution.py:28
  69.3 1.2 %collective-permute-start.22 = (bf16[128,512]{1,0:T(8,128)(2,1)S(1)}, bf16[128,512]{1,0:T(8,128)(2,1)S(1)}, u32[]{:S(2)}, u32[]{:S(2)}) collective-permute-start(bf16[128,512]{1,0:T(8,128)(2,1)S(1)} %get-tuple-element.91), channel_id=1, source_target_pairs={{0,6},{2,4},{4,2},{6,0},{1,7},{3,5},{5,3},{7,1},{8,14},{10,12},{12... | collective-permute-start | bytes 393224 | tf_op jit(solution)/shard_map/ppermute | solution.py:28
  70.5 4.4 %collective-permute-start.21 = (bf16[128,512]{1,0:T(8,128)(2,1)S(1)}, bf16[128,512]{1,0:T(8,128)(2,1)S(1)}, u32[]{:S(2)}, u32[]{:S(2)}) collective-permute-start(bf16[128,512]{1,0:T(8,128)(2,1)S(1)} %get-tuple-element.92), channel_id=1, source_target_pairs={{0,4},{2,6},{4,0},{6,2},{1,5},{3,7},{5,1},{7,3},{8,12},{10,14},{12... | collective-permute-start | bytes 393224 | tf_op jit(solution)/shard_map/ppermute | solution.py:28
  74.9 2.2 %collective-permute-start.23 = (bf16[256,512]{1,0:T(8,128)(2,1)S(1)}, bf16[256,512]{1,0:T(8,128)(2,1)S(1)}, u32[]{:S(2)}, u32[]{:S(2)}) collective-permute-start(bf16[256,512]{1,0:T(8,128)(2,1)S(1)} %pad_maximum_fusion.1), channel_id=1, source_target_pairs={{0,16},{8,24},{16,0},{24,8},{1,17},{9,25},{17,1},{25,9},{2,18},{10... | collective-permute-start | bytes 786440 | tf_op jit(solution)/shard_map/ppermute | solution.py:28
  77.1 4.8 %collective-permute-done.21 = bf16[128,512]{1,0:T(8,128)(2,1)S(1)} collective-permute-done((bf16[128,512]{1,0:T(8,128)(2,1)S(1)}, bf16[128,512]{1,0:T(8,128)(2,1)S(1)}, u32[]{:S(2)}, u32[]{:S(2)}) %collective-permute-start.21) | collective-permute-done | bytes 131104 | tf_op jit(solution)/shard_map/ppermute | solution.py:28
  82.9 1.6 %collective-permute-start.27 = (bf16[512,512]{1,0:T(8,128)(2,1)S(1)}, bf16[512,512]{1,0:T(8,128)(2,1)S(1)}, u32[]{:S(2)}, u32[]{:S(2)}) collective-permute-start(bf16[512,512]{1,0:T(8,128)(2,1)S(1)} %pad_maximum_fusion.refs_5_), channel_id=1, source_target_pairs={{0,1},{1,0},{2,3},{3,2},{4,5},{5,4},{6,7},{7,6},{8,9},{9,8},{10,11... | collective-permute-start | bytes 1572872 | tf_op jit(solution)/shard_map/ppermute | solution.py:28
  84.5 1.5 %collective-permute-start.24 = (bf16[128,512]{1,0:T(8,128)(2,1)S(1)}, bf16[128,512]{1,0:T(8,128)(2,1)S(1)}, u32[]{:S(2)}, u32[]{:S(2)}) collective-permute-start(bf16[128,512]{1,0:T(8,128)(2,1)S(1)} %fusion.2.refs_1_), channel_id=1, source_target_pairs={{0,2},{2,0},{4,6},{6,4},{1,3},{3,1},{5,7},{7,5},{8,10},{10,8},{12,... | collective-permute-start | bytes 393224 | tf_op jit(solution)/shard_map/ppermute | solution.py:28
  87.1 1.3 %kv_grad.1 = bf16[1024,512]{1,0:T(8,128)(2,1)S(1)} custom-call(s32[3]{0:T(128)S(1)} %pad_add_fusion.where.refs_0_, bf16[128,512]{1,0:T(8,128)(2,1)S(1)} %bitcast.31, bf16[128,512]{1,0:T(8,128)(2,1)S(1)} %collective-permute-done.refs_2_, bf16[128,512]{1,0:T(8,128)(2,1)S(1)} %collective-permute-done.1.refs_3_, ...), custom_call_target="tpu_custom_call" | custom-call | flops 536870912 | bytes 2621452 | tf_op jit(solution)/shard_map/kv_grad/pallas_call | solution.py:139
  89.6 1.3 %collective-permute-done.24.refs_2_ = bf16[128,512]{1,0:T(8,128)(2,1)S(1)} collective-permute-done((bf16[128,512]{1,0:T(8,128)(2,1)S(1)}, bf16[128,512]{1,0:T(8,128)(2,1)S(1)}, u32[]{:S(2)}, u32[]{:S(2)}) %collective-permute-start.24) | collective-permute-done | bytes 131104 | tf_op jit(solution)/shard_map/ppermute | solution.py:28
  90.9 2.2 %collective-permute-done.25.refs_3_ = bf16[128,512]{1,0:T(8,128)(2,1)S(1)} collective-permute-done((bf16[128,512]{1,0:T(8,128)(2,1)S(1)}, bf16[128,512]{1,0:T(8,128)(2,1)S(1)}, u32[]{:S(2)}, u32[]{:S(2)}) %collective-permute-start.25) | collective-permute-done | bytes 131104 | tf_op jit(solution)/shard_map/ppermute | solution.py:28
  93.1 5.7 %collective-permute-done.26.refs_4_ = bf16[128,512]{1,0:T(8,128)(2,1)S(1)} collective-permute-done((bf16[128,512]{1,0:T(8,128)(2,1)S(1)}, bf16[128,512]{1,0:T(8,128)(2,1)S(1)}, u32[]{:S(2)}, u32[]{:S(2)}) %collective-permute-start.26) | collective-permute-done | bytes 131104 | tf_op jit(solution)/shard_map/ppermute | solution.py:28
  101.9 1.8 %input_grad.1 = bf16[128,4096]{1,0:T(8,128)(2,1)} custom-call(s32[3]{0:T(128)S(1)} %pad_add_fusion.where.refs_0_, bf16[128,512]{1,0:T(8,128)(2,1)S(1)} %fusion.2.refs_1_, bf16[128,512]{1,0:T(8,128)(2,1)S(1)} %collective-permute-done.24.refs_2_, bf16[128,512]{1,0:T(8,128)(2,1)S(1)} %collective-permute-done.25.refs_3_, ...), custom_call_target="tpu_custom_call" | custom-call | bytes 2097164 | tf_op jit(solution)/shard_map/input_grad/pallas_call | solution.py:139
  (67 shorter events, 16.2 us)
Async XLA Ops:
  0.6 14.2 %collective-permute-start.3 = (bf16[128,1024]{1,0:T(8,128)(2,1)}, bf16[128,1024]{1,0:T(8,128)(2,1)S(1)}, u32[]{:S(2)}, u32[]{:S(2)}) collective-permute-start(bf16[128,1024]{1,0:T(8,128)(2,1)} %refs_3_.1), channel_id=1, source_target_pairs={{0,4},{2,6},{4,0},{6,2},{1,5},{3,7},{5,1},{7,3},{8,12},{10,14},{12... | collective-permute-start | bytes 786440 | tf_op jit(solution)/shard_map/ppermute | solution.py:28
  3.0 11.8 %collective-permute-start.4 = (bf16[128,1024]{1,0:T(8,128)(2,1)}, bf16[128,1024]{1,0:T(8,128)(2,1)S(1)}, u32[]{:S(2)}, u32[]{:S(2)}) collective-permute-start(bf16[128,1024]{1,0:T(8,128)(2,1)} %refs_3_.1), channel_id=1, source_target_pairs={{0,2},{2,0},{4,6},{6,4},{1,3},{3,1},{5,7},{7,5},{8,10},{10,8},{12,... | collective-permute-start | bytes 786440 | tf_op jit(solution)/shard_map/ppermute | solution.py:28
  4.1 4.9 %collective-permute-start = (bf16[128,512]{1,0:T(8,128)(2,1)S(1)}, bf16[128,512]{1,0:T(8,128)(2,1)S(1)}, u32[]{:S(2)}, u32[]{:S(2)}) collective-permute-start(bf16[128,512]{1,0:T(8,128)(2,1)S(1)} %bitcast.27), channel_id=1, source_target_pairs={{0,8},{8,0},{16,24},{24,16},{1,9},{9,1},{17,25},{25,17},{2,10},{10... | collective-permute-start | bytes 393224 | tf_op jit(solution)/shard_map/ppermute | solution.py:28
  5.4 4.1 %collective-permute-start.1 = (bf16[128,512]{1,0:T(8,128)(2,1)S(1)}, bf16[128,512]{1,0:T(8,128)(2,1)S(1)}, u32[]{:S(2)}, u32[]{:S(2)}) collective-permute-start(bf16[128,512]{1,0:T(8,128)(2,1)S(1)} %bitcast.28), channel_id=1, source_target_pairs={{0,16},{8,24},{16,0},{24,8},{1,17},{9,25},{17,1},{25,9},{2,18},{10... | collective-permute-start | bytes 393224 | tf_op jit(solution)/shard_map/ppermute | solution.py:28
  6.6 5.5 %collective-permute-start.2 = (bf16[128,512]{1,0:T(8,128)(2,1)S(1)}, bf16[128,512]{1,0:T(8,128)(2,1)S(1)}, u32[]{:S(2)}, u32[]{:S(2)}) collective-permute-start(bf16[128,512]{1,0:T(8,128)(2,1)S(1)} %bitcast.29), channel_id=1, source_target_pairs={{0,24},{8,16},{16,8},{24,0},{1,25},{9,17},{17,9},{25,1},{2,26},{10... | collective-permute-start | bytes 393224 | tf_op jit(solution)/shard_map/ppermute | solution.py:28
  16.2 15.9 %collective-permute-start.5 = (bf16[512,1024]{1,0:T(8,128)(2,1)S(1)}, bf16[512,1024]{1,0:T(8,128)(2,1)S(1)}, u32[]{:S(2)}, u32[]{:S(2)}) collective-permute-start(bf16[512,1024]{1,0:T(8,128)(2,1)S(1)} %upstream_terms.1.refs_1_), channel_id=1, source_target_pairs={{0,1},{1,0},{2,3},{3,2},{4,5},{5,4},{6,7},{7,6},{8,9},{9,8},{10,11... | collective-permute-start | bytes 3145736 | tf_op jit(solution)/shard_map/ppermute | solution.py:28
  17.7 13.5 %collective-permute-start.6 = (bf16[2048,128]{1,0:T(8,128)(2,1)S(1)}, bf16[2048,128]{1,0:T(8,128)(2,1)S(1)}, u32[]{:S(2)}, u32[]{:S(2)}) collective-permute-start(bf16[2048,128]{1,0:T(8,128)(2,1)S(1)} %gate_and_up.1.refs_1_.refs_9_), channel_id=1, source_target_pairs={{0,8},{8,0},{16,24},{24,16},{1,9},{9,1},{17,25},{25,17},{2,10},{10... | collective-permute-start | bytes 1572872 | tf_op jit(solution)/shard_map/ppermute | solution.py:28
  18.9 13.2 %collective-permute-start.7 = (bf16[2048,128]{1,0:T(8,128)(2,1)S(1)}, bf16[2048,128]{1,0:T(8,128)(2,1)S(1)}, u32[]{:S(2)}, u32[]{:S(2)}) collective-permute-start(bf16[2048,128]{1,0:T(8,128)(2,1)S(1)} %gate_and_up.1.refs_1_.refs_9_), channel_id=1, source_target_pairs={{0,16},{8,24},{16,0},{24,8},{1,17},{9,25},{17,1},{25,9},{2,18},{10... | collective-permute-start | bytes 1572872 | tf_op jit(solution)/shard_map/ppermute | solution.py:28
  20.1 11.9 %collective-permute-start.8 = (bf16[128,1024]{1,0:T(8,128)(2,1)S(1)}, bf16[128,1024]{1,0:T(8,128)(2,1)S(1)}, u32[]{:S(2)}, u32[]{:S(2)}) collective-permute-start(bf16[128,1024]{1,0:T(8,128)(2,1)S(1)} %collective-permute-done.3.refs_5_), channel_id=1, source_target_pairs={{0,2},{2,0},{4,6},{6,4},{1,3},{3,1},{5,7},{7,5},{8,10},{10,8},{12,... | collective-permute-start | bytes 786440 | tf_op jit(solution)/shard_map/ppermute | solution.py:28
  20.5 17.7 %collective-permute-start.12 = (bf16[128,2048]{1,0:T(8,128)(2,1)S(1)}, bf16[128,2048]{1,0:T(8,128)(2,1)S(1)}, u32[]{:S(2)}, u32[]{:S(2)}) collective-permute-start(bf16[128,2048]{1,0:T(8,128)(2,1)S(1)} %copy-done), channel_id=1, source_target_pairs={{0,1},{1,0},{2,3},{3,2},{4,5},{5,4},{6,7},{7,6},{8,9},{9,8},{10,11... | collective-permute-start | bytes 1572872 | tf_op jit(solution)/shard_map/ppermute | solution.py:28
  33.4 6.7 %collective-permute-start.9 = (bf16[128,1024]{1,0:T(8,128)(2,1)S(1)}, bf16[128,1024]{1,0:T(8,128)(2,1)S(1)}, u32[]{:S(2)}, u32[]{:S(2)}) collective-permute-start(bf16[128,1024]{1,0:T(8,128)(2,1)S(1)} %get-tuple-element.57), channel_id=1, source_target_pairs={{0,8},{8,0},{16,24},{24,16},{1,9},{9,1},{17,25},{25,17},{2,10},{10... | collective-permute-start | bytes 786440 | tf_op jit(solution)/shard_map/ppermute | solution.py:28
  33.8 6.4 %collective-permute-start.10 = (bf16[128,1024]{1,0:T(8,128)(2,1)S(1)}, bf16[128,1024]{1,0:T(8,128)(2,1)S(1)}, u32[]{:S(2)}, u32[]{:S(2)}) collective-permute-start(bf16[128,1024]{1,0:T(8,128)(2,1)S(1)} %get-tuple-element.58), channel_id=1, source_target_pairs={{0,16},{8,24},{16,0},{24,8},{1,17},{9,25},{17,1},{25,9},{2,18},{10... | collective-permute-start | bytes 786440 | tf_op jit(solution)/shard_map/ppermute | solution.py:28
  35.0 11.6 %collective-permute-start.11 = (bf16[128,1024]{1,0:T(8,128)(2,1)S(1)}, bf16[128,1024]{1,0:T(8,128)(2,1)S(1)}, u32[]{:S(2)}, u32[]{:S(2)}) collective-permute-start(bf16[128,1024]{1,0:T(8,128)(2,1)S(1)} %get-tuple-element.59), channel_id=1, source_target_pairs={{0,24},{8,16},{16,8},{24,0},{1,25},{9,17},{17,9},{25,1},{2,26},{10... | collective-permute-start | bytes 786440 | tf_op jit(solution)/shard_map/ppermute | solution.py:28
  36.1 13.3 %collective-permute-start.17 = (bf16[128,2048]{1,0:T(8,128)(2,1)S(1)}, bf16[128,2048]{1,0:T(8,128)(2,1)S(1)}, u32[]{:S(2)}, u32[]{:S(2)}) collective-permute-start(bf16[128,2048]{1,0:T(8,128)(2,1)S(1)} %copy-done.1), channel_id=1, source_target_pairs={{0,1},{1,0},{2,3},{3,2},{4,5},{5,4},{6,7},{7,6},{8,9},{9,8},{10,11... | collective-permute-start | bytes 1572872 | tf_op jit(solution)/shard_map/ppermute | solution.py:28
  38.1 19.8 %collective-permute-start.16 = (bf16[2048,128]{1,0:T(8,128)(2,1)S(1)}, bf16[2048,128]{1,0:T(8,128)(2,1)S(1)}, u32[]{:S(2)}, u32[]{:S(2)}) collective-permute-start(bf16[2048,128]{1,0:T(8,128)(2,1)S(1)} %gate_and_up.1.refs_1_.refs_9_), channel_id=1, source_target_pairs={{0,24},{8,16},{16,8},{24,0},{1,25},{9,17},{17,9},{25,1},{2,26},{10... | collective-permute-start | bytes 1572872 | tf_op jit(solution)/shard_map/ppermute | solution.py:28
  46.7 20.7 %collective-permute-start.19 = (bf16[256,512]{1,0:T(8,128)(2,1)S(1)}, bf16[256,512]{1,0:T(8,128)(2,1)S(1)}, u32[]{:S(2)}, u32[]{:S(2)}) collective-permute-start(bf16[256,512]{1,0:T(8,128)(2,1)S(1)} %get-tuple-element.75), channel_id=1, source_target_pairs={{0,8},{8,0},{16,24},{24,16},{1,9},{9,1},{17,25},{25,17},{2,10},{10... | collective-permute-start | bytes 786440 | tf_op jit(solution)/shard_map/ppermute | solution.py:28
  47.2 12.3 %collective-permute-start.13 = (bf16[128,128]{1,0:T(8,128)(2,1)S(1)}, bf16[128,128]{1,0:T(8,128)(2,1)S(1)}, u32[]{:S(2)}, u32[]{:S(2)}) collective-permute-start(bf16[128,128]{1,0:T(8,128)(2,1)S(1)} %get-tuple-element.97), channel_id=1, source_target_pairs={{0,2},{2,0},{4,6},{6,4},{1,3},{3,1},{5,7},{7,5},{8,10},{10,8},{12,... | collective-permute-start | bytes 98312 | tf_op jit(solution)/shard_map/ppermute | solution.py:28
  47.6 11.9 %collective-permute-start.14 = (bf16[128,128]{1,0:T(8,128)(2,1)S(1)}, bf16[128,128]{1,0:T(8,128)(2,1)S(1)}, u32[]{:S(2)}, u32[]{:S(2)}) collective-permute-start(bf16[128,128]{1,0:T(8,128)(2,1)S(1)} %get-tuple-element.96), channel_id=1, source_target_pairs={{0,4},{2,6},{4,0},{6,2},{1,5},{3,7},{5,1},{7,3},{8,12},{10,14},{12... | collective-permute-start | bytes 98312 | tf_op jit(solution)/shard_map/ppermute | solution.py:28
  49.4 10.1 %collective-permute-start.15 = (bf16[128,128]{1,0:T(8,128)(2,1)S(1)}, bf16[128,128]{1,0:T(8,128)(2,1)S(1)}, u32[]{:S(2)}, u32[]{:S(2)}) collective-permute-start(bf16[128,128]{1,0:T(8,128)(2,1)S(1)} %get-tuple-element.95), channel_id=1, source_target_pairs={{0,6},{2,4},{4,2},{6,0},{1,7},{3,5},{5,3},{7,1},{8,14},{10,12},{12... | collective-permute-start | bytes 98312 | tf_op jit(solution)/shard_map/ppermute | solution.py:28
  61.1 7.9 %collective-permute-start.18 = (bf16[4,128,512]{2,1,0:T(8,128)(2,1)S(1)}, bf16[4,128,512]{2,1,0:T(8,128)(2,1)S(1)}, u32[]{:S(2)}, u32[]{:S(2)}) collective-permute-start(bf16[4,128,512]{2,1,0:T(8,128)(2,1)S(1)} %get-tuple-element.73), channel_id=1, source_target_pairs={{0,1},{1,0},{2,3},{3,2},{4,5},{5,4},{6,7},{7,6},{8,9},{9,8},{10,11... | collective-permute-start | bytes 1572872 | tf_op jit(solution)/shard_map/ppermute | solution.py:28
  69.3 7.9 %collective-permute-start.22 = (bf16[128,512]{1,0:T(8,128)(2,1)S(1)}, bf16[128,512]{1,0:T(8,128)(2,1)S(1)}, u32[]{:S(2)}, u32[]{:S(2)}) collective-permute-start(bf16[128,512]{1,0:T(8,128)(2,1)S(1)} %get-tuple-element.91), channel_id=1, source_target_pairs={{0,6},{2,4},{4,2},{6,0},{1,7},{3,5},{5,3},{7,1},{8,14},{10,12},{12... | collective-permute-start | bytes 393224 | tf_op jit(solution)/shard_map/ppermute | solution.py:28
  70.5 11.5 %collective-permute-start.21 = (bf16[128,512]{1,0:T(8,128)(2,1)S(1)}, bf16[128,512]{1,0:T(8,128)(2,1)S(1)}, u32[]{:S(2)}, u32[]{:S(2)}) collective-permute-start(bf16[128,512]{1,0:T(8,128)(2,1)S(1)} %get-tuple-element.92), channel_id=1, source_target_pairs={{0,4},{2,6},{4,0},{6,2},{1,5},{3,7},{5,1},{7,3},{8,12},{10,14},{12... | collective-permute-start | bytes 393224 | tf_op jit(solution)/shard_map/ppermute | solution.py:28
  74.9 7.2 %collective-permute-start.20 = (bf16[128,512]{1,0:T(8,128)(2,1)S(1)}, bf16[128,512]{1,0:T(8,128)(2,1)S(1)}, u32[]{:S(2)}, u32[]{:S(2)}) collective-permute-start(bf16[128,512]{1,0:T(8,128)(2,1)S(1)} %get-tuple-element.90), channel_id=1, source_target_pairs={{0,2},{2,0},{4,6},{6,4},{1,3},{3,1},{5,7},{7,5},{8,10},{10,8},{12,... | collective-permute-start | bytes 393224 | tf_op jit(solution)/shard_map/ppermute | solution.py:28
  74.9 8.0 %collective-permute-start.23 = (bf16[256,512]{1,0:T(8,128)(2,1)S(1)}, bf16[256,512]{1,0:T(8,128)(2,1)S(1)}, u32[]{:S(2)}, u32[]{:S(2)}) collective-permute-start(bf16[256,512]{1,0:T(8,128)(2,1)S(1)} %pad_maximum_fusion.1), channel_id=1, source_target_pairs={{0,16},{8,24},{16,0},{24,8},{1,17},{9,25},{17,1},{25,9},{2,18},{10... | collective-permute-start | bytes 786440 | tf_op jit(solution)/shard_map/ppermute | solution.py:28
  82.9 4.3 %collective-permute-start.27 = (bf16[512,512]{1,0:T(8,128)(2,1)S(1)}, bf16[512,512]{1,0:T(8,128)(2,1)S(1)}, u32[]{:S(2)}, u32[]{:S(2)}) collective-permute-start(bf16[512,512]{1,0:T(8,128)(2,1)S(1)} %pad_maximum_fusion.refs_5_), channel_id=1, source_target_pairs={{0,1},{1,0},{2,3},{3,2},{4,5},{5,4},{6,7},{7,6},{8,9},{9,8},{10,11... | collective-permute-start | bytes 1572872 | tf_op jit(solution)/shard_map/ppermute | solution.py:28
  84.5 6.4 %collective-permute-start.24 = (bf16[128,512]{1,0:T(8,128)(2,1)S(1)}, bf16[128,512]{1,0:T(8,128)(2,1)S(1)}, u32[]{:S(2)}, u32[]{:S(2)}) collective-permute-start(bf16[128,512]{1,0:T(8,128)(2,1)S(1)} %fusion.2.refs_1_), channel_id=1, source_target_pairs={{0,2},{2,0},{4,6},{6,4},{1,3},{3,1},{5,7},{7,5},{8,10},{10,8},{12,... | collective-permute-start | bytes 393224 | tf_op jit(solution)/shard_map/ppermute | solution.py:28
  86.0 7.2 %collective-permute-start.25 = (bf16[128,512]{1,0:T(8,128)(2,1)S(1)}, bf16[128,512]{1,0:T(8,128)(2,1)S(1)}, u32[]{:S(2)}, u32[]{:S(2)}) collective-permute-start(bf16[128,512]{1,0:T(8,128)(2,1)S(1)} %fusion.2.refs_1_), channel_id=1, source_target_pairs={{0,4},{2,6},{4,0},{6,2},{1,5},{3,7},{5,1},{7,3},{8,12},{10,14},{12... | collective-permute-start | bytes 393224 | tf_op jit(solution)/shard_map/ppermute | solution.py:28
  86.7 12.2 %collective-permute-start.26 = (bf16[128,512]{1,0:T(8,128)(2,1)S(1)}, bf16[128,512]{1,0:T(8,128)(2,1)S(1)}, u32[]{:S(2)}, u32[]{:S(2)}) collective-permute-start(bf16[128,512]{1,0:T(8,128)(2,1)S(1)} %fusion.2.refs_1_), channel_id=1, source_target_pairs={{0,6},{2,4},{4,2},{6,0},{1,7},{3,5},{5,3},{7,1},{8,14},{10,12},{12... | collective-permute-start | bytes 393224 | tf_op jit(solution)/shard_map/ppermute | solution.py:28
  98.9 2.2 %collective-permute-start.28 = (bf16[128,512]{1,0:T(8,128)(2,1)S(1)}, bf16[128,512]{1,0:T(8,128)(2,1)S(1)}, u32[]{:S(2)}, u32[]{:S(2)}) collective-permute-start(bf16[128,512]{1,0:T(8,128)(2,1)S(1)} %fusion.2.refs_1_), channel_id=1, source_target_pairs={{0,1},{1,0},{2,3},{3,2},{4,5},{5,4},{6,7},{7,6},{8,9},{9,8},{10,11... | collective-permute-start | bytes 393224 | tf_op jit(solution)/shard_map/ppermute | solution.py:28
  100.1 1.3 %collective-permute-start.29 = (bf16[128,512]{1,0:T(8,128)(2,1)S(1)}, bf16[128,512]{1,0:T(8,128)(2,1)S(1)}, u32[]{:S(2)}, u32[]{:S(2)}) collective-permute-start(bf16[128,512]{1,0:T(8,128)(2,1)S(1)} %collective-permute-done.24.refs_2_), channel_id=1, source_target_pairs={{0,1},{1,0},{2,3},{3,2},{4,5},{5,4},{6,7},{7,6},{8,9},{9,8},{10,11... | collective-permute-start | bytes 393224 | tf_op jit(solution)/shard_map/ppermute | solution.py:28
  100.1 1.5 %collective-permute-start.30 = (bf16[128,512]{1,0:T(8,128)(2,1)S(1)}, bf16[128,512]{1,0:T(8,128)(2,1)S(1)}, u32[]{:S(2)}, u32[]{:S(2)}) collective-permute-start(bf16[128,512]{1,0:T(8,128)(2,1)S(1)} %collective-permute-done.25.refs_3_), channel_id=1, source_target_pairs={{0,1},{1,0},{2,3},{3,2},{4,5},{5,4},{6,7},{7,6},{8,9},{9,8},{10,11... | collective-permute-start | bytes 393224 | tf_op jit(solution)/shard_map/ppermute | solution.py:28
  100.6 1.3 %collective-permute-start.31 = (bf16[128,512]{1,0:T(8,128)(2,1)S(1)}, bf16[128,512]{1,0:T(8,128)(2,1)S(1)}, u32[]{:S(2)}, u32[]{:S(2)}) collective-permute-start(bf16[128,512]{1,0:T(8,128)(2,1)S(1)} %collective-permute-done.26.refs_4_), channel_id=1, source_target_pairs={{0,1},{1,0},{2,3},{3,2},{4,5},{5,4},{6,7},{7,6},{8,9},{9,8},{10,11... | collective-permute-start | bytes 393224 | tf_op jit(solution)/shard_map/ppermute | solution.py:28
  (6 other events, 48.8 us)

commit v3 on v2

--- a/solution.py
+++ b/solution.py
@@ -167,25 +167,44 @@
 
 
 def hidden_kernel(n_dp, n_pipe, n_ten, where, mine, other, *refs):
-    downs, (own_hidden, own_upstream), outs = refs[:n_pipe], refs[n_pipe : n_pipe + 2], refs[n_pipe + 2 : -2]
+    downs, hidden, outs = refs[:n_pipe], refs[n_pipe : 2 * n_pipe], refs[2 * n_pipe : 2 * n_pipe + n_dp]
     upstream, down = refs[-2:]
     upstream[...] = (mine[...].astype(F32) + other[...].astype(F32)).astype(BF16)
     units = downs[0].shape[0]
     for k, part in enumerate(downs):
         down[k * units : (k + 1) * units, :] = part[...]
     result = dot_nt(upstream[...], down[...])
-    tok, width = own_hidden.shape
-    half = upstream.shape[1] // n_ten
-    spot = aligned(where[2] * half, half)
-    own_hidden[...] = result[:tok, :]
-    own_upstream[...] = upstream[:tok, spot]
-    for k, out in enumerate(outs, 1):
-        out[:, :width] = result[k * tok : (k + 1) * tok, :].astype(BF16)
-        out[:, width:] = upstream[k * tok : (k + 1) * tok, spot]
+    for k, out in enumerate(hidden):
+        out[...] = result[:, k * units : (k + 1) * units].astype(out.dtype)
+    tok, half = outs[0].shape
+    for k, out in enumerate(outs):
+        out[...] = upstream[k * tok : (k + 1) * tok, aligned(where[2] * half, half)]
+
+
+def owner_kernel(n_dp, n_pipe, where, *refs):
+    terms, ups, own, outs = refs[:n_pipe], refs[n_pipe : n_pipe + n_dp - 1], refs[-n_dp], refs[1 - n_dp :]
+    tok, units = own.shape
+    for k in range(n_dp):
+        total_here = terms[0][k * tok : (k + 1) * tok, :]
+        for term in terms[1:]:
+            total_here = total_here + term[k * tok : (k + 1) * tok, :].astype(F32)
+        if k == 0:
+            own[...] = total_here
+        else:
+            outs[k - 1][:, :units] = total_here.astype(BF16)
+            outs[k - 1][:, units:] = ups[k - 1][...]
+
+
+def gate_and_up(packs, k, cols, start, rows):
+    if k < len(packs) - 2:
+        pieces = [packs[k][aligned(s * cols + start, rows), :] for s in (0, 1)]
+    else:
+        pieces = [pack[aligned(start, rows), :] for pack in packs[-2:]]
+    return jnp.concatenate(pieces, axis=1)
 
 
 def forward_kernel(n_dp, where, *refs):
-    packs, (x_mine, x_other, gain, resid, scale, pre, normed) = refs[:n_dp], refs[n_dp:]
+    packs, (x_mine, x_other, gain, resid, scale, pre, normed) = refs[: n_dp + 1], refs[n_dp + 1 :]
     ten = where[2]
     half = x_mine.shape[1]
     resid[:, aligned(ten * half, half)] = x_mine[...]
@@ -196,21 +215,21 @@
     normed[...] = (values_in * row_scale * gain[...].astype(F32)).astype(BF16)
     cols = resid.shape[1] // n_dp
     result = jnp.zeros(pre.shape, F32)
-    for k, pack in enumerate(packs):
+    for k in range(n_dp):
         left = normed[:, aligned((where[0] ^ k) * cols, cols)]
-        right = jnp.concatenate([pack[:cols, :], pack[cols:, :]], axis=1)
-        result += jnp.dot(left, right, preferred_element_type=F32)
+        result += jnp.dot(left, gate_and_up(packs, k, cols, 0, cols), preferred_element_type=F32)
     pre[...] = result
 
 
 def backward_kernel(n_dp, n_pipe, n_ten, where, *refs):
-    terms, ups, packs = refs[:n_pipe], refs[n_pipe : n_pipe + n_dp], refs[n_pipe + n_dp : n_pipe + 2 * n_dp]
-    pre, scale, resid, gain, other, mine = refs[n_pipe + 2 * n_dp :]
+    terms, upstream, rest = refs[:n_dp], refs[n_dp], refs[n_dp + 1 :]
+    units = terms[0].shape[1]
+    ups = [upstream] + [term.at[:, units:] for term in terms[1:]]
+    packs, (pre, scale, resid, gain, other, mine) = rest[: n_dp + 1], rest[n_dp + 1 :]
     pipe, ten = where[1], where[2]
     hidden_grad = terms[0][...]
     for term in terms[1:]:
-        hidden_grad = hidden_grad + term[...].astype(F32)
-    units = hidden_grad.shape[1]
+        hidden_grad = hidden_grad + term[:, :units].astype(F32)
     gate_pre, up_pre = pre[:, :units], pre[:, units:]
     gelu_value, gelu_slope = gelu_parts(gate_pre)
     gate_grad = hidden_grad * up_pre * gelu_slope
@@ -225,14 +244,13 @@
     share = half // n_pipe
     for step, out in ((1, other), (0, mine)):
         start = (ten ^ step) * half
-        for k, pack in enumerate(packs):
+        for k in range(n_dp):
             i = where[0] ^ k
             spot = aligned(i * cols + start, half)
-            rows = [pack[aligned(start, half), :], pack[aligned(cols + start, half), :]]
-            part = dot_nt(grads, jnp.concatenate(rows, axis=1))
+            part = dot_nt(grads, gate_and_up(packs, k, cols, start, half))
             part = row_scale * (gain[:, spot].astype(F32) * part) - resid[:, spot].astype(F32) * pull
             if step == 0:
-                part = part + ups[k][:, ups[k].shape[1] - half :].astype(F32)
+                part = part + ups[k][...].astype(F32)
             part = part.astype(out.dtype)
             for j in range(n_pipe):
                 out[pipe ^ j, :, aligned(i * share, share)] = part[:, j * share : (j + 1) * share]
@@ -295,14 +313,14 @@
         )
     where = jnp.stack([lax.axis_index(a) for a in (DP, PIPE, TENSOR)]).astype(jnp.int32)
 
-    far, near = send(down_weight, PIPE, 2), send(down_weight, PIPE, 1)
     grads = gather(grad_kv.reshape(tok, -1), DP)
     x_other = send(mlp_input, TENSOR, 1)
+    far, near = send(down_weight, PIPE, 2), send(down_weight, PIPE, 1)
     (both,) = call(
         pack_kernel, "gate_and_up", [shaped((2 * cols, units), BF16)], [where, gate_weight, up_weight]
     )
     grads, both = lax.optimization_barrier((grads, both))
-    packs = gather(both, DP)
+    packs = [both, send(both, DP, 1), send(both, DP, 2)]
     grads, far, near = lax.optimization_barrier((grads, far, near))
     downs = [down_weight, near, far, send(far, PIPE, 1)]
 
@@ -317,30 +335,37 @@
         flops=2 * n_dp * tok * section.size,
     )
     other = send(mine, TENSOR, 1)
-    other, packs[1], packs[2] = lax.optimization_barrier((other, packs[1], packs[2]))
+    enc_other = send(enc_out, TENSOR, 1)
+    other, x_other, enc_other = lax.optimization_barrier((other, x_other, enc_other))
     group = n_pipe * units
-    hidden, upstream, *outs = call(
+    outs = call(
         lambda *refs: hidden_kernel(n_dp, n_pipe, n_ten, *refs),
         "hidden_terms",
-        [shaped((tok, group), F32), shaped((tok, half), BF16)]
-        + [shaped((tok, group + half), BF16)] * (n_dp - 1),
+        [shaped((n_dp * tok, units), F32)]
+        + [shaped((n_dp * tok, units), BF16)] * (n_pipe - 1)
+        + [shaped((tok, half), BF16)] * n_dp,
         [where, mine, other, *downs],
         [pltpu.VMEM((n_dp * tok, cols), BF16), pltpu.VMEM((group, cols), BF16)],
         flops=2 * n_dp * tok * cols * group,
     )
-    ups = [send(out, DP, k) for k, out in enumerate(outs, 1)]
-    encoded = [enc_out, send(enc_out, TENSOR, 1)]
+    terms = [send(out, PIPE, k) for k, out in enumerate(outs[:n_pipe])]
+    packs = lax.optimization_barrier((terms[1], packs))[1]
+    packs += [send(packs[1][:cols], DP, 2), send(packs[2][cols:], DP, 1)]
+    hidden, *ups = call(
+        lambda *refs: owner_kernel(n_dp, n_pipe, *refs),
+        "hidden_sums",
+        [shaped((tok, units), F32)] + [shaped((tok, units + half), BF16)] * (n_dp - 1),
+        [where, *terms, *outs[n_pipe + 1 :]],
+    )
+    terms = [hidden] + [send(up, DP, k) for k, up in enumerate(ups, 1)]
+    encoded = [enc_out, enc_other]
     encoded = call(
         lambda *refs: encoded_kernel(n_dp, n_ten, *refs),
         "encoded_blocks",
         [shaped((tok, half), BF16), shaped((2 * tok, half), BF16), shaped((tok, half), BF16)],
         [where, *encoded],
     )
-    ups, encoded = lax.optimization_barrier((ups, encoded))
-    for part in ups:
-        hidden = hidden + part[:, :group].astype(F32)
-    terms = [hidden[:, :units]]
-    terms += [send(hidden[:, k * units : (k + 1) * units].astype(BF16), PIPE, k) for k in range(1, n_pipe)]
+    terms, encoded = lax.optimization_barrier((terms, encoded))
 
     gain_row = norm_gain.reshape(1, width)
     resid, scale, pre = call(
@@ -355,7 +380,7 @@
         lambda *refs: backward_kernel(n_dp, n_pipe, n_ten, *refs),
         "mlp_backward",
         [shaped((n_pipe, tok, n_dp * share), BF16), shaped((n_pipe, tok, n_dp * share), F32)],
-        [where, *terms, upstream, *ups, *packs, pre, scale, resid, gain_row],
+        [where, *terms, outs[n_pipe], *packs, pre, scale, resid, gain_row],
         flops=4 * tok * width * units,
     )
     mine = mine + send(other, TENSOR, 1).astype(F32)

time: 105 us -> 95.3 us (0.908); the launches traced: 104 us -> 95.2 us
  starting transfers between devices: 39.7 us -> 31.4 us
    ppermute x32 -> x33, starting transfers between devices: 39.7 us -> 31.4 us  [send(): return lax.ppermute(value, axis, [(src, src ^ step) for src in range(size)])]
    ppermute x32 -> x33, waiting for transfers between devices: 49 us -> 48.2 us  [send(): return lax.ppermute(value, axis, [(src, src ^ step) for src in range(size)])]
    pallas_call x8 -> x9, Pallas kernels: 10.1 us -> 10.7 us  [call(): pl.pallas_call(body, name=name, out_shape=out, in_specs=specs, out_specs=...]
  transfers between devices with their start and end apart: 32 -> 33, of which waited for: 20 -> 23; matrix products, arithmetic and copies ran while one was open for 4% -> 4% of each run, Pallas kernels for 7% -> 8%
where the time goes in v3:
time: 95.3 us; the launch traced here: 95.2 us
  waiting for transfers between devices  48.2 us (51%)
  starting transfers between devices  31.4 us (33%)
  Pallas kernels  10.7 us (11%)
  local copies, waits for them, and re-layouts  3.65 us (4%)
    ppermute x33, waiting for transfers between devices, send(): return lax.ppermute(value, axis, [(src, src ^ step) for src in range(size)])  48.2 us
    ppermute x33, starting transfers between devices, send(): return lax.ppermute(value, axis, [(src, src ^ step) for src in range(size)])  31.4 us
    pallas_call x9, Pallas kernels, call(): pl.pallas_call(body, name=name, out_shape=out, in_specs=specs, out_specs=...  10.7 us
    unnamed x14, local copies, waits for them, and re-layouts  2.45 us
  transfers between devices with their start and end apart: 33, of which 23 were waited for; matrix products, arithmetic and copies ran while one was open for 4% of the time, Pallas kernels for 8%

profile of v3, /device:TPU:9, one launch (start us, length us, event | category | flops | bytes accessed | tf_op | source)
XLA Modules:
  0.0 95.2 jit_solution(6509036341105543625)
XLA Ops:
  0.6 2.4 %collective-permute-start.3 = (bf16[128,1024]{1,0:T(8,128)(2,1)}, bf16[128,1024]{1,0:T(8,128)(2,1)S(1)}, u32[]{:S(2)}, u32[]{:S(2)}) collective-permute-start(bf16[128,1024]{1,0:T(8,128)(2,1)} %refs_3_.1), channel_id=1, source_target_pairs={{0,4},{2,6},{4,0},{6,2},{1,5},{3,7},{5,1},{7,3},{8,12},{10,14},{12... | collective-permute-start | bytes 786440 | tf_op jit(solution)/shard_map/ppermute | solution.py:28
  4.1 1.3 %collective-permute-start = (bf16[128,512]{1,0:T(8,128)(2,1)S(1)}, bf16[128,512]{1,0:T(8,128)(2,1)S(1)}, u32[]{:S(2)}, u32[]{:S(2)}) collective-permute-start(bf16[128,512]{1,0:T(8,128)(2,1)S(1)} %bitcast.27), channel_id=1, source_target_pairs={{0,8},{8,0},{16,24},{24,16},{1,9},{9,1},{17,25},{25,17},{2,10},{10... | collective-permute-start | bytes 393224 | tf_op jit(solution)/shard_map/ppermute | solution.py:28
  5.4 1.2 %collective-permute-start.1 = (bf16[128,512]{1,0:T(8,128)(2,1)S(1)}, bf16[128,512]{1,0:T(8,128)(2,1)S(1)}, u32[]{:S(2)}, u32[]{:S(2)}) collective-permute-start(bf16[128,512]{1,0:T(8,128)(2,1)S(1)} %bitcast.28), channel_id=1, source_target_pairs={{0,16},{8,24},{16,0},{24,8},{1,17},{9,25},{17,1},{25,9},{2,18},{10... | collective-permute-start | bytes 393224 | tf_op jit(solution)/shard_map/ppermute | solution.py:28
  6.8 1.5 %copy.12 = bf16[128,8,2,256]{3,1,2,0:T(8,128)(2,1)S(1)} copy(bf16[128,8,2,256]{3,2,1,0:T(2,128)(2,1)} %bitcast.32) | data formatting | bytes 2097152
  9.5 2.6 %collective-permute-done.2.refs_4_ = bf16[128,512]{1,0:T(8,128)(2,1)S(1)} collective-permute-done((bf16[128,512]{1,0:T(8,128)(2,1)S(1)}, bf16[128,512]{1,0:T(8,128)(2,1)S(1)}, u32[]{:S(2)}, u32[]{:S(2)}) %collective-permute-start.2) | collective-permute-done | bytes 131104 | tf_op jit(solution)/shard_map/ppermute | solution.py:28
  12.1 2.8 %collective-permute-done.3.refs_5_ = bf16[128,1024]{1,0:T(8,128)(2,1)S(1)} collective-permute-done((bf16[128,1024]{1,0:T(8,128)(2,1)}, bf16[128,1024]{1,0:T(8,128)(2,1)S(1)}, u32[]{:S(2)}, u32[]{:S(2)}) %collective-permute-start.3) | collective-permute-done | bytes 262176 | tf_op jit(solution)/shard_map/ppermute | solution.py:28
  14.9 1.3 %upstream_terms.1.refs_1_ = bf16[512,1024]{1,0:T(8,128)(2,1)S(1)} custom-call(s32[3]{0:T(128)S(1)} %pad_add_fusion.where.refs_0_, bf16[128,512]{1,0:T(8,128)(2,1)S(1)} %bitcast.30, bf16[128,512]{1,0:T(8,128)(2,1)S(1)} %collective-permute-done.refs_2_, bf16[128,512]{1,0:T(8,128)(2,1)S(1)} %collective-permute-done.1.refs_3_, ...), custom_call_target="tpu_custom_call" | custom-call | flops 536870912 | bytes 2621452 | tf_op jit(solution)/shard_map/upstream_terms/pallas_call | solution.py:139
  16.2 1.5 %collective-permute-start.5 = (bf16[512,1024]{1,0:T(8,128)(2,1)S(1)}, bf16[512,1024]{1,0:T(8,128)(2,1)S(1)}, u32[]{:S(2)}, u32[]{:S(2)}) collective-permute-start(bf16[512,1024]{1,0:T(8,128)(2,1)S(1)} %upstream_terms.1.refs_1_), channel_id=1, source_target_pairs={{0,1},{1,0},{2,3},{3,2},{4,5},{5,4},{6,7},{7,6},{8,9},{9,8},{10,11... | collective-permute-start | bytes 3145736 | tf_op jit(solution)/shard_map/ppermute | solution.py:28
  18.2 1.2 %collective-permute-start.15 = (bf16[2048,128]{1,0:T(8,128)(2,1)S(1)}, bf16[2048,128]{1,0:T(8,128)(2,1)S(1)}, u32[]{:S(2)}, u32[]{:S(2)}) collective-permute-start(bf16[2048,128]{1,0:T(8,128)(2,1)S(1)} %gate_and_up.1.refs_1_.refs_6_), channel_id=1, source_target_pairs={{0,8},{8,0},{16,24},{24,16},{1,9},{9,1},{17,25},{25,17},{2,10},{10... | collective-permute-start | bytes 1572872 | tf_op jit(solution)/shard_map/ppermute | solution.py:28
  19.4 1.2 %collective-permute-start.16 = (bf16[2048,128]{1,0:T(8,128)(2,1)S(1)}, bf16[2048,128]{1,0:T(8,128)(2,1)S(1)}, u32[]{:S(2)}, u32[]{:S(2)}) collective-permute-start(bf16[2048,128]{1,0:T(8,128)(2,1)S(1)} %gate_and_up.1.refs_1_.refs_6_), channel_id=1, source_target_pairs={{0,16},{8,24},{16,0},{24,8},{1,17},{9,25},{17,1},{25,9},{2,18},{10... | collective-permute-start | bytes 1572872 | tf_op jit(solution)/shard_map/ppermute | solution.py:28
  21.5 6.5 %collective-permute-done.8.refs_6_ = bf16[128,1024]{1,0:T(8,128)(2,1)S(1)} collective-permute-done((bf16[128,1024]{1,0:T(8,128)(2,1)S(1)}, bf16[128,1024]{1,0:T(8,128)(2,1)S(1)}, u32[]{:S(2)}, u32[]{:S(2)}) %collective-permute-start.8) | collective-permute-done | bytes 262176 | tf_op jit(solution)/shard_map/ppermute | solution.py:28
  28.0 1.3 %hidden_terms.1 = (f32[512,128]{1,0:T(8,128)S(1)}, bf16[512,128]{1,0:T(8,128)(2,1)S(1)}, bf16[512,128]{1,0:T(8,128)(2,1)S(1)}, bf16[512,128]{1,0:T(8,128)(2,1)S(...) custom-call(s32[3]{0:T(128)S(1)} %pad_add_fusion.where.refs_0_, ...), custom_call_target="tpu_custom_call" | custom-call | flops 536870912 | bytes 4325388 | tf_op jit(solution)/shard_map/hidden_terms/pallas_call | solution.py:139
  29.6 2.2 %collective-permute-start.10 = (bf16[512,128]{1,0:T(8,128)(2,1)S(1)}, bf16[512,128]{1,0:T(8,128)(2,1)S(1)}, u32[]{:S(2)}, u32[]{:S(2)}) collective-permute-start(bf16[512,128]{1,0:T(8,128)(2,1)S(1)} %get-tuple-element.68), channel_id=1, source_target_pairs={{0,4},{2,6},{4,0},{6,2},{1,5},{3,7},{5,1},{7,3},{8,12},{10,14},{12... | collective-permute-start | bytes 393224 | tf_op jit(solution)/shard_map/ppermute | solution.py:28
  33.4 1.4 %collective-permute-start.17 = (bf16[1024,128]{1,0:T(8,128)(2,1)S(1)}, bf16[1024,128]{1,0:T(8,128)(2,1)S(1)}, u32[]{:S(2)}, u32[]{:S(2)}) collective-permute-start(bf16[1024,128]{1,0:T(8,128)(2,1)S(1)} %slice.27), channel_id=1, source_target_pairs={{0,16},{8,24},{16,0},{24,8},{1,17},{9,25},{17,1},{25,9},{2,18},{10... | collective-permute-start | bytes 786440 | tf_op jit(solution)/shard_map/ppermute | solution.py:28
  34.8 1.3 %collective-permute-start.18 = (bf16[1024,128]{1,0:T(8,128)(2,1)S(1)}, bf16[1024,128]{1,0:T(8,128)(2,1)S(1)}, u32[]{:S(2)}, u32[]{:S(2)}) collective-permute-start(bf16[1024,128]{1,0:T(8,128)(2,1)S(1)} %slice.28), channel_id=1, source_target_pairs={{0,8},{8,0},{16,24},{24,16},{1,9},{9,1},{17,25},{25,17},{2,10},{10... | collective-permute-start | bytes 786440 | tf_op jit(solution)/shard_map/ppermute | solution.py:28
  36.7 6.3 %collective-permute-done.11.refs_4_ = bf16[512,128]{1,0:T(8,128)(2,1)S(1)} collective-permute-done((bf16[512,128]{1,0:T(8,128)(2,1)S(1)}, bf16[512,128]{1,0:T(8,128)(2,1)S(1)}, u32[]{:S(2)}, u32[]{:S(2)}) %collective-permute-start.11) | collective-permute-done | bytes 131104 | tf_op jit(solution)/shard_map/ppermute | solution.py:28
  43.6 1.5 %collective-permute-start.12 = (bf16[128,640]{1,0:T(8,128)(2,1)S(1)}, bf16[128,640]{1,0:T(8,128)(2,1)S(1)}, u32[]{:S(2)}, u32[]{:S(2)}) collective-permute-start(bf16[128,640]{1,0:T(8,128)(2,1)S(1)} %get-tuple-element.74), channel_id=1, source_target_pairs={{0,8},{8,0},{16,24},{24,16},{1,9},{9,1},{17,25},{25,17},{2,10},{10... | collective-permute-start | bytes 491528 | tf_op jit(solution)/shard_map/ppermute | solution.py:28
  45.1 1.2 %collective-permute-start.13 = (bf16[128,640]{1,0:T(8,128)(2,1)S(1)}, bf16[128,640]{1,0:T(8,128)(2,1)S(1)}, u32[]{:S(2)}, u32[]{:S(2)}) collective-permute-start(bf16[128,640]{1,0:T(8,128)(2,1)S(1)} %get-tuple-element.75), channel_id=1, source_target_pairs={{0,16},{8,24},{16,0},{24,8},{1,17},{9,25},{17,1},{25,9},{2,18},{10... | collective-permute-start | bytes 491528 | tf_op jit(solution)/shard_map/ppermute | solution.py:28
  47.8 1.7 %collective-permute-done.13.refs_3_ = bf16[128,640]{1,0:T(8,128)(2,1)S(1)} collective-permute-done((bf16[128,640]{1,0:T(8,128)(2,1)S(1)}, bf16[128,640]{1,0:T(8,128)(2,1)S(1)}, u32[]{:S(2)}, u32[]{:S(2)}) %collective-permute-start.13) | collective-permute-done | bytes 163872 | tf_op jit(solution)/shard_map/ppermute | solution.py:28
  49.6 3.6 %collective-permute-done.14.refs_4_ = bf16[128,640]{1,0:T(8,128)(2,1)S(1)} collective-permute-done((bf16[128,640]{1,0:T(8,128)(2,1)S(1)}, bf16[128,640]{1,0:T(8,128)(2,1)S(1)}, u32[]{:S(2)}, u32[]{:S(2)}) %collective-permute-start.14) | collective-permute-done | bytes 163872 | tf_op jit(solution)/shard_map/ppermute | solution.py:28
  53.2 1.6 %mlp_forward.1 = (bf16[128,4096]{1,0:T(8,128)(2,1)S(1)}, f32[128,128]{1,0:T(8,128)S(1)}, f32[128,256]{1,0:T(8,128)S(1)}) custom-call(s32[3]{0:T(128)S(1)} %pad_add_fusion.where.refs_0_, bf16[2048,128]{1,0:T(8,128)(2,1)S(1)} %gate_and_up.1.refs_1_.refs_6_, bf16[2048,128]{1,0:T(8,128)(2,1)S(1)} %collective-permute-done.15.refs_2_.refs_7_, ...), custom_call_target="tpu_custom_call" | custom-call | flops 268435456 | bytes 4399116 | tf_op jit(solution)/shard_map/mlp_forward/pallas_call | solution.py:139
  54.8 1.6 %mlp_backward.1 = (bf16[4,128,512]{2,1,0:T(8,128)(2,1)S(1)}, f32[4,128,512]{2,1,0:T(8,128)S(1)}) custom-call(s32[3]{0:T(128)S(1)} %pad_add_fusion.where.refs_0_, f32[128,128]{1,0:T(8,128)S(1)} %get-tuple-element.81.refs_1_, bf16[128,640]{1,0:T(8,128)(2,1)S(1)} %collective-permute-done.12.refs_2_, bf16[128,640]{1,0:T(8,128)(2,1)S(1)} %collective-permute-done.13.refs_3_, ...), custom_call_target="tpu_custom_call" | custom-call | flops 268435456 | bytes 5611532 | tf_op jit(solution)/shard_map/mlp_backward/pallas_call | solution.py:139
  56.4 3.4 %collective-permute-start.19 = (bf16[4,128,512]{2,1,0:T(8,128)(2,1)S(1)}, bf16[4,128,512]{2,1,0:T(8,128)(2,1)S(1)}, u32[]{:S(2)}, u32[]{:S(2)}) collective-permute-start(bf16[4,128,512]{2,1,0:T(8,128)(2,1)S(1)} %get-tuple-element.95), channel_id=1, source_target_pairs={{0,1},{1,0},{2,3},{3,2},{4,5},{5,4},{6,7},{7,6},{8,9},{9,8},{10,11... | collective-permute-start | bytes 1572872 | tf_op jit(solution)/shard_map/ppermute | solution.py:28
  59.8 1.5 %collective-permute-done.19 = bf16[4,128,512]{2,1,0:T(8,128)(2,1)S(1)} collective-permute-done((bf16[4,128,512]{2,1,0:T(8,128)(2,1)S(1)}, bf16[4,128,512]{2,1,0:T(8,128)(2,1)S(1)}, u32[]{:S(2)}, u32[]{:S(2)}) %collective-permute-start.19) | collective-permute-done | bytes 524320 | tf_op jit(solution)/shard_map/ppermute | solution.py:28
  61.6 1.5 %collective-permute-start.23 = (bf16[128,512]{1,0:T(8,128)(2,1)S(1)}, bf16[128,512]{1,0:T(8,128)(2,1)S(1)}, u32[]{:S(2)}, u32[]{:S(2)}) collective-permute-start(bf16[128,512]{1,0:T(8,128)(2,1)S(1)} %get-tuple-element.111), channel_id=1, source_target_pairs={{0,6},{2,4},{4,2},{6,0},{1,7},{3,5},{5,3},{7,1},{8,14},{10,12},{12... | collective-permute-start | bytes 393224 | tf_op jit(solution)/shard_map/ppermute | solution.py:28
  64.9 6.0 %collective-permute-done.23 = bf16[128,512]{1,0:T(8,128)(2,1)S(1)} collective-permute-done((bf16[128,512]{1,0:T(8,128)(2,1)S(1)}, bf16[128,512]{1,0:T(8,128)(2,1)S(1)}, u32[]{:S(2)}, u32[]{:S(2)}) %collective-permute-start.23) | collective-permute-done | bytes 131104 | tf_op jit(solution)/shard_map/ppermute | solution.py:28
  70.9 2.4 %collective-permute-done.22 = bf16[128,512]{1,0:T(8,128)(2,1)S(1)} collective-permute-done((bf16[128,512]{1,0:T(8,128)(2,1)S(1)}, bf16[128,512]{1,0:T(8,128)(2,1)S(1)}, u32[]{:S(2)}, u32[]{:S(2)}) %collective-permute-start.22) | collective-permute-done | bytes 131104 | tf_op jit(solution)/shard_map/ppermute | solution.py:28
  74.5 2.9 %collective-permute-start.25 = (bf16[128,512]{1,0:T(8,128)(2,1)S(1)}, bf16[128,512]{1,0:T(8,128)(2,1)S(1)}, u32[]{:S(2)}, u32[]{:S(2)}) collective-permute-start(bf16[128,512]{1,0:T(8,128)(2,1)S(1)} %fusion.2.refs_1_), channel_id=1, source_target_pairs={{0,2},{2,0},{4,6},{6,4},{1,3},{3,1},{5,7},{7,5},{8,10},{10,8},{12,... | collective-permute-start | bytes 393224 | tf_op jit(solution)/shard_map/ppermute | solution.py:28
  78.5 1.3 %kv_grad.1 = bf16[1024,512]{1,0:T(8,128)(2,1)S(1)} custom-call(s32[3]{0:T(128)S(1)} %pad_add_fusion.where.refs_0_, bf16[128,512]{1,0:T(8,128)(2,1)S(1)} %bitcast.31, bf16[128,512]{1,0:T(8,128)(2,1)S(1)} %collective-permute-done.refs_2_, bf16[128,512]{1,0:T(8,128)(2,1)S(1)} %collective-permute-done.1.refs_3_, ...), custom_call_target="tpu_custom_call" | custom-call | flops 536870912 | bytes 2621452 | tf_op jit(solution)/shard_map/kv_grad/pallas_call | solution.py:139
  82.2 2.1 %collective-permute-done.26.refs_3_ = bf16[128,512]{1,0:T(8,128)(2,1)S(1)} collective-permute-done((bf16[128,512]{1,0:T(8,128)(2,1)S(1)}, bf16[128,512]{1,0:T(8,128)(2,1)S(1)}, u32[]{:S(2)}, u32[]{:S(2)}) %collective-permute-start.26) | collective-permute-done | bytes 131104 | tf_op jit(solution)/shard_map/ppermute | solution.py:28
  84.3 6.3 %collective-permute-done.27.refs_4_ = bf16[128,512]{1,0:T(8,128)(2,1)S(1)} collective-permute-done((bf16[128,512]{1,0:T(8,128)(2,1)S(1)}, bf16[128,512]{1,0:T(8,128)(2,1)S(1)}, u32[]{:S(2)}, u32[]{:S(2)}) %collective-permute-start.27) | collective-permute-done | bytes 131104 | tf_op jit(solution)/shard_map/ppermute | solution.py:28
  93.3 1.8 %input_grad.1 = bf16[128,4096]{1,0:T(8,128)(2,1)} custom-call(s32[3]{0:T(128)S(1)} %pad_add_fusion.where.refs_0_, bf16[128,512]{1,0:T(8,128)(2,1)S(1)} %fusion.2.refs_1_, bf16[128,512]{1,0:T(8,128)(2,1)S(1)} %collective-permute-done.25.refs_2_, bf16[128,512]{1,0:T(8,128)(2,1)S(1)} %collective-permute-done.26.refs_3_, ...), custom_call_target="tpu_custom_call" | custom-call | bytes 2097164 | tf_op jit(solution)/shard_map/input_grad/pallas_call | solution.py:139
  (69 shorter events, 17.9 us)
Async XLA Ops:
  0.6 14.2 %collective-permute-start.3 = (bf16[128,1024]{1,0:T(8,128)(2,1)}, bf16[128,1024]{1,0:T(8,128)(2,1)S(1)}, u32[]{:S(2)}, u32[]{:S(2)}) collective-permute-start(bf16[128,1024]{1,0:T(8,128)(2,1)} %refs_3_.1), channel_id=1, source_target_pairs={{0,4},{2,6},{4,0},{6,2},{1,5},{3,7},{5,1},{7,3},{8,12},{10,14},{12... | collective-permute-start | bytes 786440 | tf_op jit(solution)/shard_map/ppermute | solution.py:28
  3.0 11.8 %collective-permute-start.4 = (bf16[128,1024]{1,0:T(8,128)(2,1)}, bf16[128,1024]{1,0:T(8,128)(2,1)S(1)}, u32[]{:S(2)}, u32[]{:S(2)}) collective-permute-start(bf16[128,1024]{1,0:T(8,128)(2,1)} %refs_3_.1), channel_id=1, source_target_pairs={{0,2},{2,0},{4,6},{6,4},{1,3},{3,1},{5,7},{7,5},{8,10},{10,8},{12,... | collective-permute-start | bytes 786440 | tf_op jit(solution)/shard_map/ppermute | solution.py:28
  4.1 4.9 %collective-permute-start = (bf16[128,512]{1,0:T(8,128)(2,1)S(1)}, bf16[128,512]{1,0:T(8,128)(2,1)S(1)}, u32[]{:S(2)}, u32[]{:S(2)}) collective-permute-start(bf16[128,512]{1,0:T(8,128)(2,1)S(1)} %bitcast.27), channel_id=1, source_target_pairs={{0,8},{8,0},{16,24},{24,16},{1,9},{9,1},{17,25},{25,17},{2,10},{10... | collective-permute-start | bytes 393224 | tf_op jit(solution)/shard_map/ppermute | solution.py:28
  5.4 4.1 %collective-permute-start.1 = (bf16[128,512]{1,0:T(8,128)(2,1)S(1)}, bf16[128,512]{1,0:T(8,128)(2,1)S(1)}, u32[]{:S(2)}, u32[]{:S(2)}) collective-permute-start(bf16[128,512]{1,0:T(8,128)(2,1)S(1)} %bitcast.28), channel_id=1, source_target_pairs={{0,16},{8,24},{16,0},{24,8},{1,17},{9,25},{17,1},{25,9},{2,18},{10... | collective-permute-start | bytes 393224 | tf_op jit(solution)/shard_map/ppermute | solution.py:28
  6.6 5.5 %collective-permute-start.2 = (bf16[128,512]{1,0:T(8,128)(2,1)S(1)}, bf16[128,512]{1,0:T(8,128)(2,1)S(1)}, u32[]{:S(2)}, u32[]{:S(2)}) collective-permute-start(bf16[128,512]{1,0:T(8,128)(2,1)S(1)} %bitcast.29), channel_id=1, source_target_pairs={{0,24},{8,16},{16,8},{24,0},{1,25},{9,17},{17,9},{25,1},{2,26},{10... | collective-permute-start | bytes 393224 | tf_op jit(solution)/shard_map/ppermute | solution.py:28
  16.2 5.3 %collective-permute-start.5 = (bf16[512,1024]{1,0:T(8,128)(2,1)S(1)}, bf16[512,1024]{1,0:T(8,128)(2,1)S(1)}, u32[]{:S(2)}, u32[]{:S(2)}) collective-permute-start(bf16[512,1024]{1,0:T(8,128)(2,1)S(1)} %upstream_terms.1.refs_1_), channel_id=1, source_target_pairs={{0,1},{1,0},{2,3},{3,2},{4,5},{5,4},{6,7},{7,6},{8,9},{9,8},{10,11... | collective-permute-start | bytes 3145736 | tf_op jit(solution)/shard_map/ppermute | solution.py:28
  17.7 3.0 %collective-permute-start.6 = (bf16[128,2048]{1,0:T(8,128)(2,1)S(1)}, bf16[128,2048]{1,0:T(8,128)(2,1)S(1)}, u32[]{:S(2)}, u32[]{:S(2)}) collective-permute-start(bf16[128,2048]{1,0:T(8,128)(2,1)S(1)} %copy-done.1), channel_id=1, source_target_pairs={{0,1},{1,0},{2,3},{3,2},{4,5},{5,4},{6,7},{7,6},{8,9},{9,8},{10,11... | collective-permute-start | bytes 1572872 | tf_op jit(solution)/shard_map/ppermute | solution.py:28
  17.8 3.7 %collective-permute-start.7 = (bf16[128,2048]{1,0:T(8,128)(2,1)S(1)}, bf16[128,2048]{1,0:T(8,128)(2,1)S(1)}, u32[]{:S(2)}, u32[]{:S(2)}) collective-permute-start(bf16[128,2048]{1,0:T(8,128)(2,1)S(1)} %copy-done), channel_id=1, source_target_pairs={{0,1},{1,0},{2,3},{3,2},{4,5},{5,4},{6,7},{7,6},{8,9},{9,8},{10,11... | collective-permute-start | bytes 1572872 | tf_op jit(solution)/shard_map/ppermute | solution.py:28
  18.2 13.8 %collective-permute-start.15 = (bf16[2048,128]{1,0:T(8,128)(2,1)S(1)}, bf16[2048,128]{1,0:T(8,128)(2,1)S(1)}, u32[]{:S(2)}, u32[]{:S(2)}) collective-permute-start(bf16[2048,128]{1,0:T(8,128)(2,1)S(1)} %gate_and_up.1.refs_1_.refs_6_), channel_id=1, source_target_pairs={{0,8},{8,0},{16,24},{24,16},{1,9},{9,1},{17,25},{25,17},{2,10},{10... | collective-permute-start | bytes 1572872 | tf_op jit(solution)/shard_map/ppermute | solution.py:28
  19.4 13.2 %collective-permute-start.16 = (bf16[2048,128]{1,0:T(8,128)(2,1)S(1)}, bf16[2048,128]{1,0:T(8,128)(2,1)S(1)}, u32[]{:S(2)}, u32[]{:S(2)}) collective-permute-start(bf16[2048,128]{1,0:T(8,128)(2,1)S(1)} %gate_and_up.1.refs_1_.refs_6_), channel_id=1, source_target_pairs={{0,16},{8,24},{16,0},{24,8},{1,17},{9,25},{17,1},{25,9},{2,18},{10... | collective-permute-start | bytes 1572872 | tf_op jit(solution)/shard_map/ppermute | solution.py:28
  20.7 7.3 %collective-permute-start.8 = (bf16[128,1024]{1,0:T(8,128)(2,1)S(1)}, bf16[128,1024]{1,0:T(8,128)(2,1)S(1)}, u32[]{:S(2)}, u32[]{:S(2)}) collective-permute-start(bf16[128,1024]{1,0:T(8,128)(2,1)S(1)} %collective-permute-done.3.refs_5_), channel_id=1, source_target_pairs={{0,2},{2,0},{4,6},{6,4},{1,3},{3,1},{5,7},{7,5},{8,10},{10,8},{12,... | collective-permute-start | bytes 786440 | tf_op jit(solution)/shard_map/ppermute | solution.py:28
  29.3 4.0 %collective-permute-start.9 = (bf16[512,128]{1,0:T(8,128)(2,1)S(1)}, bf16[512,128]{1,0:T(8,128)(2,1)S(1)}, u32[]{:S(2)}, u32[]{:S(2)}) collective-permute-start(bf16[512,128]{1,0:T(8,128)(2,1)S(1)} %get-tuple-element.67), channel_id=1, source_target_pairs={{0,2},{2,0},{4,6},{6,4},{1,3},{3,1},{5,7},{7,5},{8,10},{10,8},{12,... | collective-permute-start | bytes 393224 | tf_op jit(solution)/shard_map/ppermute | solution.py:28
  29.6 7.1 %collective-permute-start.10 = (bf16[512,128]{1,0:T(8,128)(2,1)S(1)}, bf16[512,128]{1,0:T(8,128)(2,1)S(1)}, u32[]{:S(2)}, u32[]{:S(2)}) collective-permute-start(bf16[512,128]{1,0:T(8,128)(2,1)S(1)} %get-tuple-element.68), channel_id=1, source_target_pairs={{0,4},{2,6},{4,0},{6,2},{1,5},{3,7},{5,1},{7,3},{8,12},{10,14},{12... | collective-permute-start | bytes 393224 | tf_op jit(solution)/shard_map/ppermute | solution.py:28
  31.8 11.2 %collective-permute-start.11 = (bf16[512,128]{1,0:T(8,128)(2,1)S(1)}, bf16[512,128]{1,0:T(8,128)(2,1)S(1)}, u32[]{:S(2)}, u32[]{:S(2)}) collective-permute-start(bf16[512,128]{1,0:T(8,128)(2,1)S(1)} %get-tuple-element.69), channel_id=1, source_target_pairs={{0,6},{2,4},{4,2},{6,0},{1,7},{3,5},{5,3},{7,1},{8,14},{10,12},{12... | collective-permute-start | bytes 393224 | tf_op jit(solution)/shard_map/ppermute | solution.py:28
  33.4 19.8 %collective-permute-start.17 = (bf16[1024,128]{1,0:T(8,128)(2,1)S(1)}, bf16[1024,128]{1,0:T(8,128)(2,1)S(1)}, u32[]{:S(2)}, u32[]{:S(2)}) collective-permute-start(bf16[1024,128]{1,0:T(8,128)(2,1)S(1)} %slice.27), channel_id=1, source_target_pairs={{0,16},{8,24},{16,0},{24,8},{1,17},{9,25},{17,1},{25,9},{2,18},{10... | collective-permute-start | bytes 786440 | tf_op jit(solution)/shard_map/ppermute | solution.py:28
  34.8 18.4 %collective-permute-start.18 = (bf16[1024,128]{1,0:T(8,128)(2,1)S(1)}, bf16[1024,128]{1,0:T(8,128)(2,1)S(1)}, u32[]{:S(2)}, u32[]{:S(2)}) collective-permute-start(bf16[1024,128]{1,0:T(8,128)(2,1)S(1)} %slice.28), channel_id=1, source_target_pairs={{0,8},{8,0},{16,24},{24,16},{1,9},{9,1},{17,25},{25,17},{2,10},{10... | collective-permute-start | bytes 786440 | tf_op jit(solution)/shard_map/ppermute | solution.py:28
  43.6 4.2 %collective-permute-start.12 = (bf16[128,640]{1,0:T(8,128)(2,1)S(1)}, bf16[128,640]{1,0:T(8,128)(2,1)S(1)}, u32[]{:S(2)}, u32[]{:S(2)}) collective-permute-start(bf16[128,640]{1,0:T(8,128)(2,1)S(1)} %get-tuple-element.74), channel_id=1, source_target_pairs={{0,8},{8,0},{16,24},{24,16},{1,9},{9,1},{17,25},{25,17},{2,10},{10... | collective-permute-start | bytes 491528 | tf_op jit(solution)/shard_map/ppermute | solution.py:28
  45.1 4.5 %collective-permute-start.13 = (bf16[128,640]{1,0:T(8,128)(2,1)S(1)}, bf16[128,640]{1,0:T(8,128)(2,1)S(1)}, u32[]{:S(2)}, u32[]{:S(2)}) collective-permute-start(bf16[128,640]{1,0:T(8,128)(2,1)S(1)} %get-tuple-element.75), channel_id=1, source_target_pairs={{0,16},{8,24},{16,0},{24,8},{1,17},{9,25},{17,1},{25,9},{2,18},{10... | collective-permute-start | bytes 491528 | tf_op jit(solution)/shard_map/ppermute | solution.py:28
  46.4 6.8 %collective-permute-start.14 = (bf16[128,640]{1,0:T(8,128)(2,1)S(1)}, bf16[128,640]{1,0:T(8,128)(2,1)S(1)}, u32[]{:S(2)}, u32[]{:S(2)}) collective-permute-start(bf16[128,640]{1,0:T(8,128)(2,1)S(1)} %get-tuple-element.76), channel_id=1, source_target_pairs={{0,24},{8,16},{16,8},{24,0},{1,25},{9,17},{17,9},{25,1},{2,26},{10... | collective-permute-start | bytes 491528 | tf_op jit(solution)/shard_map/ppermute | solution.py:28
  53.2 6.6 %collective-permute-start.20 = (bf16[256,512]{1,0:T(8,128)(2,1)S(1)}, bf16[256,512]{1,0:T(8,128)(2,1)S(1)}, u32[]{:S(2)}, u32[]{:S(2)}) collective-permute-start(bf16[256,512]{1,0:T(8,128)(2,1)S(1)} %get-tuple-element.97), channel_id=1, source_target_pairs={{0,8},{8,0},{16,24},{24,16},{1,9},{9,1},{17,25},{25,17},{2,10},{10... | collective-permute-start | bytes 786440 | tf_op jit(solution)/shard_map/ppermute | solution.py:28
  56.4 4.9 %collective-permute-start.19 = (bf16[4,128,512]{2,1,0:T(8,128)(2,1)S(1)}, bf16[4,128,512]{2,1,0:T(8,128)(2,1)S(1)}, u32[]{:S(2)}, u32[]{:S(2)}) collective-permute-start(bf16[4,128,512]{2,1,0:T(8,128)(2,1)S(1)} %get-tuple-element.95), channel_id=1, source_target_pairs={{0,1},{1,0},{2,3},{3,2},{4,5},{5,4},{6,7},{7,6},{8,9},{9,8},{10,11... | collective-permute-start | bytes 1572872 | tf_op jit(solution)/shard_map/ppermute | solution.py:28
  61.6 9.3 %collective-permute-start.23 = (bf16[128,512]{1,0:T(8,128)(2,1)S(1)}, bf16[128,512]{1,0:T(8,128)(2,1)S(1)}, u32[]{:S(2)}, u32[]{:S(2)}) collective-permute-start(bf16[128,512]{1,0:T(8,128)(2,1)S(1)} %get-tuple-element.111), channel_id=1, source_target_pairs={{0,6},{2,4},{4,2},{6,0},{1,7},{3,5},{5,3},{7,1},{8,14},{10,12},{12... | collective-permute-start | bytes 393224 | tf_op jit(solution)/shard_map/ppermute | solution.py:28
  63.1 10.3 %collective-permute-start.22 = (bf16[128,512]{1,0:T(8,128)(2,1)S(1)}, bf16[128,512]{1,0:T(8,128)(2,1)S(1)}, u32[]{:S(2)}, u32[]{:S(2)}) collective-permute-start(bf16[128,512]{1,0:T(8,128)(2,1)S(1)} %get-tuple-element.112), channel_id=1, source_target_pairs={{0,4},{2,6},{4,0},{6,2},{1,5},{3,7},{5,1},{7,3},{8,12},{10,14},{12... | collective-permute-start | bytes 393224 | tf_op jit(solution)/shard_map/ppermute | solution.py:28
  64.1 9.3 %collective-permute-start.21 = (bf16[128,512]{1,0:T(8,128)(2,1)S(1)}, bf16[128,512]{1,0:T(8,128)(2,1)S(1)}, u32[]{:S(2)}, u32[]{:S(2)}) collective-permute-start(bf16[128,512]{1,0:T(8,128)(2,1)S(1)} %get-tuple-element.110), channel_id=1, source_target_pairs={{0,2},{2,0},{4,6},{6,4},{1,3},{3,1},{5,7},{7,5},{8,10},{10,8},{12,... | collective-permute-start | bytes 393224 | tf_op jit(solution)/shard_map/ppermute | solution.py:28
  64.3 9.1 %collective-permute-start.24 = (bf16[256,512]{1,0:T(8,128)(2,1)S(1)}, bf16[256,512]{1,0:T(8,128)(2,1)S(1)}, u32[]{:S(2)}, u32[]{:S(2)}) collective-permute-start(bf16[256,512]{1,0:T(8,128)(2,1)S(1)} %pad_maximum_fusion.1), channel_id=1, source_target_pairs={{0,16},{8,24},{16,0},{24,8},{1,17},{9,25},{17,1},{25,9},{2,18},{10... | collective-permute-start | bytes 786440 | tf_op jit(solution)/shard_map/ppermute | solution.py:28
  73.5 5.1 %collective-permute-start.28 = (bf16[512,512]{1,0:T(8,128)(2,1)S(1)}, bf16[512,512]{1,0:T(8,128)(2,1)S(1)}, u32[]{:S(2)}, u32[]{:S(2)}) collective-permute-start(bf16[512,512]{1,0:T(8,128)(2,1)S(1)} %pad_maximum_fusion.refs_5_), channel_id=1, source_target_pairs={{0,1},{1,0},{2,3},{3,2},{4,5},{5,4},{6,7},{7,6},{8,9},{9,8},{10,11... | collective-permute-start | bytes 1572872 | tf_op jit(solution)/shard_map/ppermute | solution.py:28
  74.5 7.7 %collective-permute-start.25 = (bf16[128,512]{1,0:T(8,128)(2,1)S(1)}, bf16[128,512]{1,0:T(8,128)(2,1)S(1)}, u32[]{:S(2)}, u32[]{:S(2)}) collective-permute-start(bf16[128,512]{1,0:T(8,128)(2,1)S(1)} %fusion.2.refs_1_), channel_id=1, source_target_pairs={{0,2},{2,0},{4,6},{6,4},{1,3},{3,1},{5,7},{7,5},{8,10},{10,8},{12,... | collective-permute-start | bytes 393224 | tf_op jit(solution)/shard_map/ppermute | solution.py:28
  77.4 6.9 %collective-permute-start.26 = (bf16[128,512]{1,0:T(8,128)(2,1)S(1)}, bf16[128,512]{1,0:T(8,128)(2,1)S(1)}, u32[]{:S(2)}, u32[]{:S(2)}) collective-permute-start(bf16[128,512]{1,0:T(8,128)(2,1)S(1)} %fusion.2.refs_1_), channel_id=1, source_target_pairs={{0,4},{2,6},{4,0},{6,2},{1,5},{3,7},{5,1},{7,3},{8,12},{10,14},{12... | collective-permute-start | bytes 393224 | tf_op jit(solution)/shard_map/ppermute | solution.py:28
  77.6 12.9 %collective-permute-start.27 = (bf16[128,512]{1,0:T(8,128)(2,1)S(1)}, bf16[128,512]{1,0:T(8,128)(2,1)S(1)}, u32[]{:S(2)}, u32[]{:S(2)}) collective-permute-start(bf16[128,512]{1,0:T(8,128)(2,1)S(1)} %fusion.2.refs_1_), channel_id=1, source_target_pairs={{0,6},{2,4},{4,2},{6,0},{1,7},{3,5},{5,3},{7,1},{8,14},{10,12},{12... | collective-permute-start | bytes 393224 | tf_op jit(solution)/shard_map/ppermute | solution.py:28
  90.5 1.9 %collective-permute-start.29 = (bf16[128,512]{1,0:T(8,128)(2,1)S(1)}, bf16[128,512]{1,0:T(8,128)(2,1)S(1)}, u32[]{:S(2)}, u32[]{:S(2)}) collective-permute-start(bf16[128,512]{1,0:T(8,128)(2,1)S(1)} %fusion.2.refs_1_), channel_id=1, source_target_pairs={{0,1},{1,0},{2,3},{3,2},{4,5},{5,4},{6,7},{7,6},{8,9},{9,8},{10,11... | collective-permute-start | bytes 393224 | tf_op jit(solution)/shard_map/ppermute | solution.py:28
  91.5 1.3 %collective-permute-start.30 = (bf16[128,512]{1,0:T(8,128)(2,1)S(1)}, bf16[128,512]{1,0:T(8,128)(2,1)S(1)}, u32[]{:S(2)}, u32[]{:S(2)}) collective-permute-start(bf16[128,512]{1,0:T(8,128)(2,1)S(1)} %collective-permute-done.25.refs_2_), channel_id=1, source_target_pairs={{0,1},{1,0},{2,3},{3,2},{4,5},{5,4},{6,7},{7,6},{8,9},{9,8},{10,11... | collective-permute-start | bytes 393224 | tf_op jit(solution)/shard_map/ppermute | solution.py:28
  91.5 1.5 %collective-permute-start.31 = (bf16[128,512]{1,0:T(8,128)(2,1)S(1)}, bf16[128,512]{1,0:T(8,128)(2,1)S(1)}, u32[]{:S(2)}, u32[]{:S(2)}) collective-permute-start(bf16[128,512]{1,0:T(8,128)(2,1)S(1)} %collective-permute-done.26.refs_3_), channel_id=1, source_target_pairs={{0,1},{1,0},{2,3},{3,2},{4,5},{5,4},{6,7},{7,6},{8,9},{9,8},{10,11... | collective-permute-start | bytes 393224 | tf_op jit(solution)/shard_map/ppermute | solution.py:28
  (7 other events, 30.2 us)

commit v4 on v3

--- a/solution.py
+++ b/solution.py
@@ -132,7 +132,7 @@
     return pl.ds(pl.multiple_of(start, lanes), lanes)
 
 
-def call(body, name, out, operands, scratch=(), flops=0):
+def call(body, name, out, operands, scratch=(), flops=0, space=pltpu.VMEM):
     specs = [pl.BlockSpec(memory_space=pltpu.SMEM)]
     specs += [pl.BlockSpec(memory_space=pltpu.VMEM)] * (len(operands) - 1)
     moved = sum(a.size * a.dtype.itemsize for a in (*operands, *out))
@@ -141,7 +141,7 @@
         name=name,
         out_shape=out,
         in_specs=specs,
-        out_specs=[pl.BlockSpec(memory_space=pltpu.VMEM)] * len(out),
+        out_specs=[pl.BlockSpec(memory_space=space)] * len(out),
         scratch_shapes=list(scratch),
         compiler_params=pltpu.CompilerParams(vmem_limit_bytes=40 * 1024 * 1024),
         cost_estimate=pl.CostEstimate(flops=flops, bytes_accessed=moved, transcendentals=0),
@@ -150,12 +150,6 @@
 
 def shaped(shape, dtype):
     return jax.ShapeDtypeStruct(shape, dtype)
-
-
-def pack_kernel(where, gate, up, out):
-    cols = gate.shape[0]
-    out[:cols, :] = gate[...]
-    out[cols:, :] = up[...]
 
 
 def upstream_kernel(n_dp, where, *refs):
@@ -195,16 +189,13 @@
             outs[k - 1][:, units:] = ups[k - 1][...]
 
 
-def gate_and_up(packs, k, cols, start, rows):
-    if k < len(packs) - 2:
-        pieces = [packs[k][aligned(s * cols + start, rows), :] for s in (0, 1)]
-    else:
-        pieces = [pack[aligned(start, rows), :] for pack in packs[-2:]]
+def gate_and_up(packs, k, start, rows):
+    pieces = [pack[aligned(start, rows), :] for pack in (packs[k], packs[len(packs) // 2 + k])]
     return jnp.concatenate(pieces, axis=1)
 
 
 def forward_kernel(n_dp, where, *refs):
-    packs, (x_mine, x_other, gain, resid, scale, pre, normed) = refs[: n_dp + 1], refs[n_dp + 1 :]
+    packs, (x_mine, x_other, gain, resid, scale, pre, last, normed) = refs[: 2 * (n_dp - 1)], refs[2 * (n_dp - 1) :]
     ten = where[2]
     half = x_mine.shape[1]
     resid[:, aligned(ten * half, half)] = x_mine[...]
@@ -215,9 +206,10 @@
     normed[...] = (values_in * row_scale * gain[...].astype(F32)).astype(BF16)
     cols = resid.shape[1] // n_dp
     result = jnp.zeros(pre.shape, F32)
-    for k in range(n_dp):
+    for k in range(n_dp - 1):
         left = normed[:, aligned((where[0] ^ k) * cols, cols)]
-        result += jnp.dot(left, gate_and_up(packs, k, cols, 0, cols), preferred_element_type=F32)
+        result += jnp.dot(left, gate_and_up(packs, k, 0, cols), preferred_element_type=F32)
+    last[...] = normed[:, aligned((where[0] ^ (n_dp - 1)) * cols, cols)]
     pre[...] = result
 
 
@@ -225,12 +217,14 @@
     terms, upstream, rest = refs[:n_dp], refs[n_dp], refs[n_dp + 1 :]
     units = terms[0].shape[1]
     ups = [upstream] + [term.at[:, units:] for term in terms[1:]]
-    packs, (pre, scale, resid, gain, other, mine) = rest[: n_dp + 1], rest[n_dp + 1 :]
+    packs, (pre, last, scale, resid, gain, other, mine) = rest[: 2 * n_dp], rest[2 * n_dp :]
     pipe, ten = where[1], where[2]
     hidden_grad = terms[0][...]
     for term in terms[1:]:
         hidden_grad = hidden_grad + term[:, :units].astype(F32)
-    gate_pre, up_pre = pre[:, :units], pre[:, units:]
+    both = gate_and_up(packs, n_dp - 1, 0, last.shape[1])
+    pre_here = pre[...] + jnp.dot(last[...], both, preferred_element_type=F32)
+    gate_pre, up_pre = pre_here[:, :units], pre_here[:, units:]
     gelu_value, gelu_slope = gelu_parts(gate_pre)
     gate_grad = hidden_grad * up_pre * gelu_slope
     up_grad = hidden_grad * gelu_value
@@ -247,7 +241,7 @@
         for k in range(n_dp):
             i = where[0] ^ k
             spot = aligned(i * cols + start, half)
-            part = dot_nt(grads, gate_and_up(packs, k, cols, start, half))
+            part = dot_nt(grads, gate_and_up(packs, k, start, half))
             part = row_scale * (gain[:, spot].astype(F32) * part) - resid[:, spot].astype(F32) * pull
             if step == 0:
                 part = part + ups[k][...].astype(F32)
@@ -257,15 +251,22 @@
 
 
 def assemble_kernel(n_dp, n_pipe, n_ten, where, *refs):
-    parts, out = refs[:-1], refs[-1]
+    parts, (out, held, sems) = refs[:-3], refs[-3:]
     pipe, ten = where[1], where[2]
     share = parts[0].shape[1] // n_dp
-    for core in range(n_ten):
-        for k in range(n_pipe):
-            part = parts[core * n_pipe + k]
-            for i in range(n_dp):
-                start = ((i * n_ten + (ten ^ core)) * n_pipe + (pipe ^ k)) * share
-                out[:, aligned(start, share)] = part[:, i * share : (i + 1) * share]
+    width = share * n_pipe
+    copies = []
+    for i in range(n_dp):
+        for core in range(n_ten):
+            at = i * n_ten + core
+            for k in range(n_pipe):
+                part = parts[core * n_pipe + k]
+                held[at, :, aligned((pipe ^ k) * share, share)] = part[:, i * share : (i + 1) * share]
+            spot = aligned((i * n_ten + (ten ^ core)) * width, width)
+            copies.append(pltpu.make_async_copy(held.at[at], out.at[:, spot], sems.at[at]))
+            copies[-1].start()
+    for copy in copies:
+        copy.wait()
 
 
 def encoded_kernel(n_dp, n_ten, where, mine, other, own, near, far):
@@ -316,11 +317,8 @@
     grads = gather(grad_kv.reshape(tok, -1), DP)
     x_other = send(mlp_input, TENSOR, 1)
     far, near = send(down_weight, PIPE, 2), send(down_weight, PIPE, 1)
-    (both,) = call(
-        pack_kernel, "gate_and_up", [shaped((2 * cols, units), BF16)], [where, gate_weight, up_weight]
-    )
-    grads, both = lax.optimization_barrier((grads, both))
-    packs = [both, send(both, DP, 1), send(both, DP, 2)]
+    grads, gate, up = lax.optimization_barrier((grads, gate_weight, up_weight))
+    gates, ups = [[value] + [send(value, DP, k) for k in (1, 2)] for value in (gate, up)]
     grads, far, near = lax.optimization_barrier((grads, far, near))
     downs = [down_weight, near, far, send(far, PIPE, 1)]
 
@@ -349,15 +347,24 @@
         flops=2 * n_dp * tok * cols * group,
     )
     terms = [send(out, PIPE, k) for k, out in enumerate(outs[:n_pipe])]
-    packs = lax.optimization_barrier((terms[1], packs))[1]
-    packs += [send(packs[1][:cols], DP, 2), send(packs[2][cols:], DP, 1)]
-    hidden, *ups = call(
+    gain_row = norm_gain.reshape(1, width)
+    resid, scale, pre, last = call(
+        lambda *refs: forward_kernel(n_dp, *refs),
+        "mlp_forward",
+        [shaped((tok, width), BF16), shaped((tok, 128), F32), shaped((tok, 2 * units), F32), shaped((tok, cols), BF16)],
+        [where, *gates, *ups, mlp_input, x_other, gain_row],
+        [pltpu.VMEM((tok, width), BF16)],
+        flops=4 * tok * width * units,
+    )
+    packs = [*gates, send(gates[1], DP, 2), *ups, send(ups[2], DP, 1)]
+    terms, resid, scale, pre, last = lax.optimization_barrier((terms, resid, scale, pre, last))
+    hidden, *sums = call(
         lambda *refs: owner_kernel(n_dp, n_pipe, *refs),
         "hidden_sums",
         [shaped((tok, units), F32)] + [shaped((tok, units + half), BF16)] * (n_dp - 1),
         [where, *terms, *outs[n_pipe + 1 :]],
     )
-    terms = [hidden] + [send(up, DP, k) for k, up in enumerate(ups, 1)]
+    terms = [hidden] + [send(part, DP, k) for k, part in enumerate(sums, 1)]
     encoded = [enc_out, enc_other]
     encoded = call(
         lambda *refs: encoded_kernel(n_dp, n_ten, *refs),
@@ -367,20 +374,11 @@
     )
     terms, encoded = lax.optimization_barrier((terms, encoded))
 
-    gain_row = norm_gain.reshape(1, width)
-    resid, scale, pre = call(
-        lambda *refs: forward_kernel(n_dp, *refs),
-        "mlp_forward",
-        [shaped((tok, width), BF16), shaped((tok, 128), F32), shaped((tok, 2 * units), F32)],
-        [where, *packs, mlp_input, x_other, gain_row],
-        [pltpu.VMEM((tok, width), BF16)],
-        flops=4 * tok * width * units,
-    )
     other, mine = call(
         lambda *refs: backward_kernel(n_dp, n_pipe, n_ten, *refs),
         "mlp_backward",
         [shaped((n_pipe, tok, n_dp * share), BF16), shaped((n_pipe, tok, n_dp * share), F32)],
-        [where, *terms, outs[n_pipe], *packs, pre, scale, resid, gain_row],
+        [where, *terms, outs[n_pipe], *packs, pre, last, scale, resid, gain_row],
         flops=4 * tok * width * units,
     )
     mine = mine + send(other, TENSOR, 1).astype(F32)
@@ -406,13 +404,19 @@
         flops=2 * n_dp * tok * section.size,
     )
     kv_grad = kv_grad.reshape(kv_weight.shape)
-    parts, kv_grad = lax.optimization_barrier((parts, kv_grad))
-    parts = parts + [send(part, TENSOR, 1) for part in parts]
+    swapped = send(part, TENSOR, 1)
+    parts, swapped, kv_grad = lax.optimization_barrier((parts, swapped, kv_grad))
+    parts = parts + [swapped] + [send(part, TENSOR, 1) for part in parts[1:]]
     (input_grad,) = call(
         lambda *refs: assemble_kernel(n_dp, n_pipe, n_ten, *refs),
         "input_grad",
         [shaped((tok, width), BF16)],
         [where, *parts],
+        [
+            pltpu.VMEM((n_dp * n_ten, tok, width // (n_dp * n_ten)), BF16),
+            pltpu.SemaphoreType.DMA((n_dp * n_ten,)),
+        ],
+        space=pl.ANY,
     )
     return (input_grad, kv_grad)
 

time: 95.3 us -> 91.4 us (0.959)
  waiting for transfers between devices: 48.2 us -> 44 us
    ppermute x33 -> x35, waiting for transfers between devices: 48.2 us -> 44 us  [send(): return lax.ppermute(value, axis, [(src, src ^ step) for src in range(size)])]
    ppermute x33 -> x35, starting transfers between devices: 31.4 us -> 32.3 us  [send(): return lax.ppermute(value, axis, [(src, src ^ step) for src in range(size)])]
    pallas_call x9 -> x8, Pallas kernels: 10.7 us -> 10.1 us  [call(): pl.pallas_call(body, name=name, out_shape=out, in_specs=specs, out_specs=...]
  transfers between devices with their start and end apart: 33 -> 35, of which waited for: 23 -> 21; matrix products, arithmetic and copies ran while one was open for 4% -> 4% of each run, Pallas kernels for 8% -> 8%
where the time goes in v4:
time: 91.4 us; the launch traced here: 91.2 us
  waiting for transfers between devices  44 us (48%)
  starting transfers between devices  32.3 us (35%)
  Pallas kernels  10.1 us (11%)
  local copies, waits for them, and re-layouts  3.56 us (4%)
    ppermute x35, waiting for transfers between devices, send(): return lax.ppermute(value, axis, [(src, src ^ step) for src in range(size)])  44 us
    ppermute x35, starting transfers between devices, send(): return lax.ppermute(value, axis, [(src, src ^ step) for src in range(size)])  32.3 us
    pallas_call x8, Pallas kernels, call(): pl.pallas_call(body, name=name, out_shape=out, in_specs=specs, out_specs=...  10.1 us
    unnamed x14, local copies, waits for them, and re-layouts  2.39 us
  transfers between devices with their start and end apart: 35, of which 21 were waited for; matrix products, arithmetic and copies ran while one was open for 4% of the time, Pallas kernels for 8%

profile of v4, /device:TPU:9, one launch (start us, length us, event | category | flops | bytes accessed | tf_op | source)
XLA Modules:
  0.0 91.2 jit_solution(1610520363064125767)
XLA Ops:
  0.6 2.4 %collective-permute-start.3 = (bf16[128,1024]{1,0:T(8,128)(2,1)}, bf16[128,1024]{1,0:T(8,128)(2,1)S(1)}, u32[]{:S(2)}, u32[]{:S(2)}) collective-permute-start(bf16[128,1024]{1,0:T(8,128)(2,1)} %refs_3_.1), channel_id=1, source_target_pairs={{0,4},{2,6},{4,0},{6,2},{1,5},{3,7},{5,1},{7,3},{8,12},{10,14},{12... | collective-permute-start | bytes 786440 | tf_op jit(solution)/shard_map/ppermute | solution.py:28
  4.1 1.3 %collective-permute-start = (bf16[128,512]{1,0:T(8,128)(2,1)S(1)}, bf16[128,512]{1,0:T(8,128)(2,1)S(1)}, u32[]{:S(2)}, u32[]{:S(2)}) collective-permute-start(bf16[128,512]{1,0:T(8,128)(2,1)S(1)} %bitcast.27), channel_id=1, source_target_pairs={{0,8},{8,0},{16,24},{24,16},{1,9},{9,1},{17,25},{25,17},{2,10},{10... | collective-permute-start | bytes 393224 | tf_op jit(solution)/shard_map/ppermute | solution.py:28
  5.4 1.2 %collective-permute-start.1 = (bf16[128,512]{1,0:T(8,128)(2,1)S(1)}, bf16[128,512]{1,0:T(8,128)(2,1)S(1)}, u32[]{:S(2)}, u32[]{:S(2)}) collective-permute-start(bf16[128,512]{1,0:T(8,128)(2,1)S(1)} %bitcast.28), channel_id=1, source_target_pairs={{0,16},{8,24},{16,0},{24,8},{1,17},{9,25},{17,1},{25,9},{2,18},{10... | collective-permute-start | bytes 393224 | tf_op jit(solution)/shard_map/ppermute | solution.py:28
  6.8 1.4 %copy.12 = bf16[128,8,2,256]{3,1,2,0:T(8,128)(2,1)S(1)} copy(bf16[128,8,2,256]{3,2,1,0:T(2,128)(2,1)} %bitcast.32) | data formatting | bytes 2097152
  9.5 2.6 %collective-permute-done.2.refs_4_ = bf16[128,512]{1,0:T(8,128)(2,1)S(1)} collective-permute-done((bf16[128,512]{1,0:T(8,128)(2,1)S(1)}, bf16[128,512]{1,0:T(8,128)(2,1)S(1)}, u32[]{:S(2)}, u32[]{:S(2)}) %collective-permute-start.2) | collective-permute-done | bytes 131104 | tf_op jit(solution)/shard_map/ppermute | solution.py:28
  12.1 2.8 %collective-permute-done.3.refs_5_ = bf16[128,1024]{1,0:T(8,128)(2,1)S(1)} collective-permute-done((bf16[128,1024]{1,0:T(8,128)(2,1)}, bf16[128,1024]{1,0:T(8,128)(2,1)S(1)}, u32[]{:S(2)}, u32[]{:S(2)}) %collective-permute-start.3) | collective-permute-done | bytes 262176 | tf_op jit(solution)/shard_map/ppermute | solution.py:28
  14.9 1.3 %upstream_terms.1.refs_1_ = bf16[512,1024]{1,0:T(8,128)(2,1)S(1)} custom-call(s32[3]{0:T(128)S(1)} %pad_add_fusion.refs_0_, bf16[128,512]{1,0:T(8,128)(2,1)S(1)} %bitcast.30, bf16[128,512]{1,0:T(8,128)(2,1)S(1)} %collective-permute-done.refs_2_, bf16[128,512]{1,0:T(8,128)(2,1)S(1)} %collective-permute-done.1.refs_3_, ...), custom_call_target="tpu_custom_call" | custom-call | flops 536870912 | bytes 2621452 | tf_op jit(solution)/shard_map/upstream_terms/pallas_call | solution.py:139
  16.2 1.5 %collective-permute-start.5 = (bf16[512,1024]{1,0:T(8,128)(2,1)S(1)}, bf16[512,1024]{1,0:T(8,128)(2,1)S(1)}, u32[]{:S(2)}, u32[]{:S(2)}) collective-permute-start(bf16[512,1024]{1,0:T(8,128)(2,1)S(1)} %upstream_terms.1.refs_1_), channel_id=1, source_target_pairs={{0,1},{1,0},{2,3},{3,2},{4,5},{5,4},{6,7},{7,6},{8,9},{9,8},{10,11... | collective-permute-start | bytes 3145736 | tf_op jit(solution)/shard_map/ppermute | solution.py:28
  18.5 1.3 %collective-permute-start.12 = (bf16[1024,128]{1,0:T(8,128)(2,1)S(1)}, bf16[1024,128]{1,0:T(8,128)(2,1)S(1)}, u32[]{:S(2)}, u32[]{:S(2)}) collective-permute-start(bf16[1024,128]{1,0:T(8,128)(2,1)S(1)} %copy-done), channel_id=1, source_target_pairs={{0,8},{8,0},{16,24},{24,16},{1,9},{9,1},{17,25},{25,17},{2,10},{10... | collective-permute-start | bytes 786440 | tf_op jit(solution)/shard_map/ppermute | solution.py:28
  20.7 1.2 %collective-permute-start.13 = (bf16[1024,128]{1,0:T(8,128)(2,1)S(1)}, bf16[1024,128]{1,0:T(8,128)(2,1)S(1)}, u32[]{:S(2)}, u32[]{:S(2)}) collective-permute-start(bf16[1024,128]{1,0:T(8,128)(2,1)S(1)} %copy-done), channel_id=1, source_target_pairs={{0,16},{8,24},{16,0},{24,8},{1,17},{9,25},{17,1},{25,9},{2,18},{10... | collective-permute-start | bytes 786440 | tf_op jit(solution)/shard_map/ppermute | solution.py:28
  23.9 2.1 %collective-permute-done.8.refs_6_ = bf16[128,1024]{1,0:T(8,128)(2,1)S(1)} collective-permute-done((bf16[128,1024]{1,0:T(8,128)(2,1)S(1)}, bf16[128,1024]{1,0:T(8,128)(2,1)S(1)}, u32[]{:S(2)}, u32[]{:S(2)}) %collective-permute-start.8) | collective-permute-done | bytes 262176 | tf_op jit(solution)/shard_map/ppermute | solution.py:28
  26.1 1.3 %hidden_terms.1 = (f32[512,128]{1,0:T(8,128)S(1)}, bf16[512,128]{1,0:T(8,128)(2,1)S(1)}, bf16[512,128]{1,0:T(8,128)(2,1)S(1)}, bf16[512,128]{1,0:T(8,128)(2,1)S(...) custom-call(s32[3]{0:T(128)S(1)} %pad_add_fusion.refs_0_, ...), custom_call_target="tpu_custom_call" | custom-call | flops 536870912 | bytes 4325388 | tf_op jit(solution)/shard_map/hidden_terms/pallas_call | solution.py:139
  27.7 2.0 %collective-permute-start.10 = (bf16[512,128]{1,0:T(8,128)(2,1)S(1)}, bf16[512,128]{1,0:T(8,128)(2,1)S(1)}, u32[]{:S(2)}, u32[]{:S(2)}) collective-permute-start(bf16[512,128]{1,0:T(8,128)(2,1)S(1)} %get-tuple-element.76), channel_id=1, source_target_pairs={{0,4},{2,6},{4,0},{6,2},{1,5},{3,7},{5,1},{7,3},{8,12},{10,14},{12... | collective-permute-start | bytes 393224 | tf_op jit(solution)/shard_map/ppermute | solution.py:28
  30.1 1.5 %collective-permute-done.14.refs_5_.refs_11_ = bf16[1024,128]{1,0:T(8,128)(2,1)S(1)} collective-permute-done((bf16[1024,128]{1,0:T(8,128)(2,1)S(1)}, bf16[1024,128]{1,0:T(8,128)(2,1)S(1)}, u32[]{:S(2)}, u32[]{:S(2)}) %collective-permute-start.14) | collective-permute-done | bytes 262176 | tf_op jit(solution)/shard_map/ppermute | solution.py:28
  31.6 1.3 %collective-permute-start.19 = (bf16[1024,128]{1,0:T(8,128)(2,1)S(1)}, bf16[1024,128]{1,0:T(8,128)(2,1)S(1)}, u32[]{:S(2)}, u32[]{:S(2)}) collective-permute-start(bf16[1024,128]{1,0:T(8,128)(2,1)S(1)} %collective-permute-done.12.refs_2_.refs_7_), channel_id=1, source_target_pairs={{0,16},{8,24},{16,0},{24,8},{1,17},{9,25},{17,1},{25,9},{2,18},{10... | collective-permute-start | bytes 786440 | tf_op jit(solution)/shard_map/ppermute | solution.py:28
  33.9 1.2 %collective-permute-start.20 = (bf16[1024,128]{1,0:T(8,128)(2,1)S(1)}, bf16[1024,128]{1,0:T(8,128)(2,1)S(1)}, u32[]{:S(2)}, u32[]{:S(2)}) collective-permute-start(bf16[1024,128]{1,0:T(8,128)(2,1)S(1)} %collective-permute-done.15.refs_6_.refs_12_), channel_id=1, source_target_pairs={{0,8},{8,0},{16,24},{24,16},{1,9},{9,1},{17,25},{25,17},{2,10},{10... | collective-permute-start | bytes 786440 | tf_op jit(solution)/shard_map/ppermute | solution.py:28
  35.1 1.5 %mlp_forward.1 = (bf16[128,4096]{1,0:T(8,128)(2,1)S(1)}, f32[128,128]{1,0:T(8,128)S(1)}, f32[128,256]{1,0:T(8,128)S(1)}, bf16[128,1024]{1,0:T(8,128)(2,1)S(1)}) custom-call(s32[3]{0:T(128)S(1)} %pad_add_fusion.refs_0_, bf16[1024,128]{1,0:T(8,128)(2,1)S(1)} %copy-done, bf16[1024,128]{1,0:T(8,128)(2,1)S(1)} %collective-permute-done.12.refs_2_.refs_7_, ...), custom_call_target="tpu_custom_call" | custom-call | flops 268435456 | bytes 4136972 | tf_op jit(solution)/shard_map/mlp_forward/pallas_call | solution.py:139
  36.6 4.6 %collective-permute-done.11.refs_4_ = bf16[512,128]{1,0:T(8,128)(2,1)S(1)} collective-permute-done((bf16[512,128]{1,0:T(8,128)(2,1)S(1)}, bf16[512,128]{1,0:T(8,128)(2,1)S(1)}, u32[]{:S(2)}, u32[]{:S(2)}) %collective-permute-start.11) | collective-permute-done | bytes 131104 | tf_op jit(solution)/shard_map/ppermute | solution.py:28
  41.8 1.3 %collective-permute-start.16 = (bf16[128,640]{1,0:T(8,128)(2,1)S(1)}, bf16[128,640]{1,0:T(8,128)(2,1)S(1)}, u32[]{:S(2)}, u32[]{:S(2)}) collective-permute-start(bf16[128,640]{1,0:T(8,128)(2,1)S(1)} %get-tuple-element.93), channel_id=1, source_target_pairs={{0,8},{8,0},{16,24},{24,16},{1,9},{9,1},{17,25},{25,17},{2,10},{10... | collective-permute-start | bytes 491528 | tf_op jit(solution)/shard_map/ppermute | solution.py:28
  43.1 1.2 %collective-permute-start.17 = (bf16[128,640]{1,0:T(8,128)(2,1)S(1)}, bf16[128,640]{1,0:T(8,128)(2,1)S(1)}, u32[]{:S(2)}, u32[]{:S(2)}) collective-permute-start(bf16[128,640]{1,0:T(8,128)(2,1)S(1)} %get-tuple-element.94), channel_id=1, source_target_pairs={{0,16},{8,24},{16,0},{24,8},{1,17},{9,25},{17,1},{25,9},{2,18},{10... | collective-permute-start | bytes 491528 | tf_op jit(solution)/shard_map/ppermute | solution.py:28
  46.0 1.5 %collective-permute-done.17.refs_3_ = bf16[128,640]{1,0:T(8,128)(2,1)S(1)} collective-permute-done((bf16[128,640]{1,0:T(8,128)(2,1)S(1)}, bf16[128,640]{1,0:T(8,128)(2,1)S(1)}, u32[]{:S(2)}, u32[]{:S(2)}) %collective-permute-start.17) | collective-permute-done | bytes 163872 | tf_op jit(solution)/shard_map/ppermute | solution.py:28
  47.6 3.9 %collective-permute-done.18.refs_4_ = bf16[128,640]{1,0:T(8,128)(2,1)S(1)} collective-permute-done((bf16[128,640]{1,0:T(8,128)(2,1)S(1)}, bf16[128,640]{1,0:T(8,128)(2,1)S(1)}, u32[]{:S(2)}, u32[]{:S(2)}) %collective-permute-start.18) | collective-permute-done | bytes 163872 | tf_op jit(solution)/shard_map/ppermute | solution.py:28
  51.5 1.8 %mlp_backward.1 = (bf16[4,128,512]{2,1,0:T(8,128)(2,1)S(1)}, f32[4,128,512]{2,1,0:T(8,128)S(1)}) custom-call(s32[3]{0:T(128)S(1)} %pad_add_fusion.refs_0_, f32[128,128]{1,0:T(8,128)S(1)} %get-tuple-element.100.refs_1_, bf16[128,640]{1,0:T(8,128)(2,1)S(1)} %collective-permute-done.16.refs_2_, bf16[128,640]{1,0:T(8,128)(2,1)S(1)} %collective-permute-done.17.refs_3_, ...), custom_call_target="tpu_custom_call" | custom-call | flops 268435456 | bytes 5873676 | tf_op jit(solution)/shard_map/mlp_backward/pallas_call | solution.py:139
  53.3 3.0 %collective-permute-start.21 = (bf16[4,128,512]{2,1,0:T(8,128)(2,1)S(1)}, bf16[4,128,512]{2,1,0:T(8,128)(2,1)S(1)}, u32[]{:S(2)}, u32[]{:S(2)}) collective-permute-start(bf16[4,128,512]{2,1,0:T(8,128)(2,1)S(1)} %get-tuple-element.110), channel_id=1, source_target_pairs={{0,1},{1,0},{2,3},{3,2},{4,5},{5,4},{6,7},{7,6},{8,9},{9,8},{10,11... | collective-permute-start | bytes 1572872 | tf_op jit(solution)/shard_map/ppermute | solution.py:28
  58.2 1.4 %collective-permute-start.25 = (bf16[128,512]{1,0:T(8,128)(2,1)S(1)}, bf16[128,512]{1,0:T(8,128)(2,1)S(1)}, u32[]{:S(2)}, u32[]{:S(2)}) collective-permute-start(bf16[128,512]{1,0:T(8,128)(2,1)S(1)} %get-tuple-element.127), channel_id=1, source_target_pairs={{0,6},{2,4},{4,2},{6,0},{1,7},{3,5},{5,3},{7,1},{8,14},{10,12},{12... | collective-permute-start | bytes 393224 | tf_op jit(solution)/shard_map/ppermute | solution.py:28
  61.4 6.8 %collective-permute-done.25 = bf16[128,512]{1,0:T(8,128)(2,1)S(1)} collective-permute-done((bf16[128,512]{1,0:T(8,128)(2,1)S(1)}, bf16[128,512]{1,0:T(8,128)(2,1)S(1)}, u32[]{:S(2)}, u32[]{:S(2)}) %collective-permute-start.25) | collective-permute-done | bytes 131104 | tf_op jit(solution)/shard_map/ppermute | solution.py:28
  68.3 2.8 %collective-permute-done.24 = bf16[128,512]{1,0:T(8,128)(2,1)S(1)} collective-permute-done((bf16[128,512]{1,0:T(8,128)(2,1)S(1)}, bf16[128,512]{1,0:T(8,128)(2,1)S(1)}, u32[]{:S(2)}, u32[]{:S(2)}) %collective-permute-start.24) | collective-permute-done | bytes 131104 | tf_op jit(solution)/shard_map/ppermute | solution.py:28
  71.8 2.2 %collective-permute-start.27 = (bf16[128,512]{1,0:T(8,128)(2,1)S(1)}, bf16[128,512]{1,0:T(8,128)(2,1)S(1)}, u32[]{:S(2)}, u32[]{:S(2)}) collective-permute-start(bf16[128,512]{1,0:T(8,128)(2,1)S(1)} %fusion.2.refs_1_), channel_id=1, source_target_pairs={{0,2},{2,0},{4,6},{6,4},{1,3},{3,1},{5,7},{7,5},{8,10},{10,8},{12,... | collective-permute-start | bytes 393224 | tf_op jit(solution)/shard_map/ppermute | solution.py:28
  75.9 1.3 %kv_grad.1 = bf16[1024,512]{1,0:T(8,128)(2,1)S(1)} custom-call(s32[3]{0:T(128)S(1)} %pad_add_fusion.refs_0_, bf16[128,512]{1,0:T(8,128)(2,1)S(1)} %bitcast.31, bf16[128,512]{1,0:T(8,128)(2,1)S(1)} %collective-permute-done.refs_2_, bf16[128,512]{1,0:T(8,128)(2,1)S(1)} %collective-permute-done.1.refs_3_, bf16[128,512]{1,0:T(8,128)(2,1)S(1)} %collective-permute-done.2.refs_4_, ...), custom_call_target="tpu_custom_call" | custom-call | flops 536870912 | bytes 2621452 | tf_op jit(solution)/shard_map/kv_grad/pallas_call | solution.py:139
  79.3 3.9 %collective-permute-done.28.refs_3_ = bf16[128,512]{1,0:T(8,128)(2,1)S(1)} collective-permute-done((bf16[128,512]{1,0:T(8,128)(2,1)S(1)}, bf16[128,512]{1,0:T(8,128)(2,1)S(1)}, u32[]{:S(2)}, u32[]{:S(2)}) %collective-permute-start.28) | collective-permute-done | bytes 131104 | tf_op jit(solution)/shard_map/ppermute | solution.py:28
  83.1 4.0 %collective-permute-done.29.refs_4_ = bf16[128,512]{1,0:T(8,128)(2,1)S(1)} collective-permute-done((bf16[128,512]{1,0:T(8,128)(2,1)S(1)}, bf16[128,512]{1,0:T(8,128)(2,1)S(1)}, u32[]{:S(2)}, u32[]{:S(2)}) %collective-permute-start.29) | collective-permute-done | bytes 131104 | tf_op jit(solution)/shard_map/ppermute | solution.py:28
  89.6 1.6 %input_grad.1 = bf16[128,4096]{1,0:T(8,128)(2,1)} custom-call(s32[3]{0:T(128)S(1)} %pad_add_fusion.refs_0_, bf16[128,512]{1,0:T(8,128)(2,1)S(1)} %fusion.2.refs_1_, bf16[128,512]{1,0:T(8,128)(2,1)S(1)} %collective-permute-done.27.refs_2_, bf16[128,512]{1,0:T(8,128)(2,1)S(1)} %collective-permute-done.28.refs_3_, ...), custom_call_target="tpu_custom_call" | custom-call | bytes 2097164 | tf_op jit(solution)/shard_map/input_grad/pallas_call | solution.py:139
  (70 shorter events, 21.1 us)
Async XLA Ops:
  0.6 14.2 %collective-permute-start.3 = (bf16[128,1024]{1,0:T(8,128)(2,1)}, bf16[128,1024]{1,0:T(8,128)(2,1)S(1)}, u32[]{:S(2)}, u32[]{:S(2)}) collective-permute-start(bf16[128,1024]{1,0:T(8,128)(2,1)} %refs_3_.1), channel_id=1, source_target_pairs={{0,4},{2,6},{4,0},{6,2},{1,5},{3,7},{5,1},{7,3},{8,12},{10,14},{12... | collective-permute-start | bytes 786440 | tf_op jit(solution)/shard_map/ppermute | solution.py:28
  3.0 11.8 %collective-permute-start.4 = (bf16[128,1024]{1,0:T(8,128)(2,1)}, bf16[128,1024]{1,0:T(8,128)(2,1)S(1)}, u32[]{:S(2)}, u32[]{:S(2)}) collective-permute-start(bf16[128,1024]{1,0:T(8,128)(2,1)} %refs_3_.1), channel_id=1, source_target_pairs={{0,2},{2,0},{4,6},{6,4},{1,3},{3,1},{5,7},{7,5},{8,10},{10,8},{12,... | collective-permute-start | bytes 786440 | tf_op jit(solution)/shard_map/ppermute | solution.py:28
  4.1 4.3 %collective-permute-start = (bf16[128,512]{1,0:T(8,128)(2,1)S(1)}, bf16[128,512]{1,0:T(8,128)(2,1)S(1)}, u32[]{:S(2)}, u32[]{:S(2)}) collective-permute-start(bf16[128,512]{1,0:T(8,128)(2,1)S(1)} %bitcast.27), channel_id=1, source_target_pairs={{0,8},{8,0},{16,24},{24,16},{1,9},{9,1},{17,25},{25,17},{2,10},{10... | collective-permute-start | bytes 393224 | tf_op jit(solution)/shard_map/ppermute | solution.py:28
  5.4 4.1 %collective-permute-start.1 = (bf16[128,512]{1,0:T(8,128)(2,1)S(1)}, bf16[128,512]{1,0:T(8,128)(2,1)S(1)}, u32[]{:S(2)}, u32[]{:S(2)}) collective-permute-start(bf16[128,512]{1,0:T(8,128)(2,1)S(1)} %bitcast.28), channel_id=1, source_target_pairs={{0,16},{8,24},{16,0},{24,8},{1,17},{9,25},{17,1},{25,9},{2,18},{10... | collective-permute-start | bytes 393224 | tf_op jit(solution)/shard_map/ppermute | solution.py:28
  6.6 5.5 %collective-permute-start.2 = (bf16[128,512]{1,0:T(8,128)(2,1)S(1)}, bf16[128,512]{1,0:T(8,128)(2,1)S(1)}, u32[]{:S(2)}, u32[]{:S(2)}) collective-permute-start(bf16[128,512]{1,0:T(8,128)(2,1)S(1)} %bitcast.29), channel_id=1, source_target_pairs={{0,24},{8,16},{16,8},{24,0},{1,25},{9,17},{17,9},{25,1},{2,26},{10... | collective-permute-start | bytes 393224 | tf_op jit(solution)/shard_map/ppermute | solution.py:28
  16.2 7.0 %collective-permute-start.5 = (bf16[512,1024]{1,0:T(8,128)(2,1)S(1)}, bf16[512,1024]{1,0:T(8,128)(2,1)S(1)}, u32[]{:S(2)}, u32[]{:S(2)}) collective-permute-start(bf16[512,1024]{1,0:T(8,128)(2,1)S(1)} %upstream_terms.1.refs_1_), channel_id=1, source_target_pairs={{0,1},{1,0},{2,3},{3,2},{4,5},{5,4},{6,7},{7,6},{8,9},{9,8},{10,11... | collective-permute-start | bytes 3145736 | tf_op jit(solution)/shard_map/ppermute | solution.py:28
  17.7 3.0 %collective-permute-start.6 = (bf16[128,2048]{1,0:T(8,128)(2,1)S(1)}, bf16[128,2048]{1,0:T(8,128)(2,1)S(1)}, u32[]{:S(2)}, u32[]{:S(2)}) collective-permute-start(bf16[128,2048]{1,0:T(8,128)(2,1)S(1)} %copy-done.3), channel_id=1, source_target_pairs={{0,1},{1,0},{2,3},{3,2},{4,5},{5,4},{6,7},{7,6},{8,9},{9,8},{10,11... | collective-permute-start | bytes 1572872 | tf_op jit(solution)/shard_map/ppermute | solution.py:28
  17.8 4.2 %collective-permute-start.7 = (bf16[128,2048]{1,0:T(8,128)(2,1)S(1)}, bf16[128,2048]{1,0:T(8,128)(2,1)S(1)}, u32[]{:S(2)}, u32[]{:S(2)}) collective-permute-start(bf16[128,2048]{1,0:T(8,128)(2,1)S(1)} %copy-done.2), channel_id=1, source_target_pairs={{0,1},{1,0},{2,3},{3,2},{4,5},{5,4},{6,7},{7,6},{8,9},{9,8},{10,11... | collective-permute-start | bytes 1572872 | tf_op jit(solution)/shard_map/ppermute | solution.py:28
  18.2 7.9 %collective-permute-start.8 = (bf16[128,1024]{1,0:T(8,128)(2,1)S(1)}, bf16[128,1024]{1,0:T(8,128)(2,1)S(1)}, u32[]{:S(2)}, u32[]{:S(2)}) collective-permute-start(bf16[128,1024]{1,0:T(8,128)(2,1)S(1)} %collective-permute-done.3.refs_5_), channel_id=1, source_target_pairs={{0,2},{2,0},{4,6},{6,4},{1,3},{3,1},{5,7},{7,5},{8,10},{10,8},{12,... | collective-permute-start | bytes 786440 | tf_op jit(solution)/shard_map/ppermute | solution.py:28
  18.5 9.3 %collective-permute-start.12 = (bf16[1024,128]{1,0:T(8,128)(2,1)S(1)}, bf16[1024,128]{1,0:T(8,128)(2,1)S(1)}, u32[]{:S(2)}, u32[]{:S(2)}) collective-permute-start(bf16[1024,128]{1,0:T(8,128)(2,1)S(1)} %copy-done), channel_id=1, source_target_pairs={{0,8},{8,0},{16,24},{24,16},{1,9},{9,1},{17,25},{25,17},{2,10},{10... | collective-permute-start | bytes 786440 | tf_op jit(solution)/shard_map/ppermute | solution.py:28
  20.7 9.0 %collective-permute-start.13 = (bf16[1024,128]{1,0:T(8,128)(2,1)S(1)}, bf16[1024,128]{1,0:T(8,128)(2,1)S(1)}, u32[]{:S(2)}, u32[]{:S(2)}) collective-permute-start(bf16[1024,128]{1,0:T(8,128)(2,1)S(1)} %copy-done), channel_id=1, source_target_pairs={{0,16},{8,24},{16,0},{24,8},{1,17},{9,25},{17,1},{25,9},{2,18},{10... | collective-permute-start | bytes 786440 | tf_op jit(solution)/shard_map/ppermute | solution.py:28
  22.0 9.7 %collective-permute-start.14 = (bf16[1024,128]{1,0:T(8,128)(2,1)S(1)}, bf16[1024,128]{1,0:T(8,128)(2,1)S(1)}, u32[]{:S(2)}, u32[]{:S(2)}) collective-permute-start(bf16[1024,128]{1,0:T(8,128)(2,1)S(1)} %copy-done.1), channel_id=1, source_target_pairs={{0,8},{8,0},{16,24},{24,16},{1,9},{9,1},{17,25},{25,17},{2,10},{10... | collective-permute-start | bytes 786440 | tf_op jit(solution)/shard_map/ppermute | solution.py:28
  23.2 10.7 %collective-permute-start.15 = (bf16[1024,128]{1,0:T(8,128)(2,1)S(1)}, bf16[1024,128]{1,0:T(8,128)(2,1)S(1)}, u32[]{:S(2)}, u32[]{:S(2)}) collective-permute-start(bf16[1024,128]{1,0:T(8,128)(2,1)S(1)} %copy-done.1), channel_id=1, source_target_pairs={{0,16},{8,24},{16,0},{24,8},{1,17},{9,25},{17,1},{25,9},{2,18},{10... | collective-permute-start | bytes 786440 | tf_op jit(solution)/shard_map/ppermute | solution.py:28
  27.4 9.2 %collective-permute-start.9 = (bf16[512,128]{1,0:T(8,128)(2,1)S(1)}, bf16[512,128]{1,0:T(8,128)(2,1)S(1)}, u32[]{:S(2)}, u32[]{:S(2)}) collective-permute-start(bf16[512,128]{1,0:T(8,128)(2,1)S(1)} %get-tuple-element.75), channel_id=1, source_target_pairs={{0,2},{2,0},{4,6},{6,4},{1,3},{3,1},{5,7},{7,5},{8,10},{10,8},{12,... | collective-permute-start | bytes 393224 | tf_op jit(solution)/shard_map/ppermute | solution.py:28
  27.7 8.9 %collective-permute-start.10 = (bf16[512,128]{1,0:T(8,128)(2,1)S(1)}, bf16[512,128]{1,0:T(8,128)(2,1)S(1)}, u32[]{:S(2)}, u32[]{:S(2)}) collective-permute-start(bf16[512,128]{1,0:T(8,128)(2,1)S(1)} %get-tuple-element.76), channel_id=1, source_target_pairs={{0,4},{2,6},{4,0},{6,2},{1,5},{3,7},{5,1},{7,3},{8,12},{10,14},{12... | collective-permute-start | bytes 393224 | tf_op jit(solution)/shard_map/ppermute | solution.py:28
  29.7 11.5 %collective-permute-start.11 = (bf16[512,128]{1,0:T(8,128)(2,1)S(1)}, bf16[512,128]{1,0:T(8,128)(2,1)S(1)}, u32[]{:S(2)}, u32[]{:S(2)}) collective-permute-start(bf16[512,128]{1,0:T(8,128)(2,1)S(1)} %get-tuple-element.77), channel_id=1, source_target_pairs={{0,6},{2,4},{4,2},{6,0},{1,7},{3,5},{5,3},{7,1},{8,14},{10,12},{12... | collective-permute-start | bytes 393224 | tf_op jit(solution)/shard_map/ppermute | solution.py:28
  31.6 19.8 %collective-permute-start.19 = (bf16[1024,128]{1,0:T(8,128)(2,1)S(1)}, bf16[1024,128]{1,0:T(8,128)(2,1)S(1)}, u32[]{:S(2)}, u32[]{:S(2)}) collective-permute-start(bf16[1024,128]{1,0:T(8,128)(2,1)S(1)} %collective-permute-done.12.refs_2_.refs_7_), channel_id=1, source_target_pairs={{0,16},{8,24},{16,0},{24,8},{1,17},{9,25},{17,1},{25,9},{2,18},{10... | collective-permute-start | bytes 786440 | tf_op jit(solution)/shard_map/ppermute | solution.py:28
  33.9 17.6 %collective-permute-start.20 = (bf16[1024,128]{1,0:T(8,128)(2,1)S(1)}, bf16[1024,128]{1,0:T(8,128)(2,1)S(1)}, u32[]{:S(2)}, u32[]{:S(2)}) collective-permute-start(bf16[1024,128]{1,0:T(8,128)(2,1)S(1)} %collective-permute-done.15.refs_6_.refs_12_), channel_id=1, source_target_pairs={{0,8},{8,0},{16,24},{24,16},{1,9},{9,1},{17,25},{25,17},{2,10},{10... | collective-permute-start | bytes 786440 | tf_op jit(solution)/shard_map/ppermute | solution.py:28
  41.8 4.2 %collective-permute-start.16 = (bf16[128,640]{1,0:T(8,128)(2,1)S(1)}, bf16[128,640]{1,0:T(8,128)(2,1)S(1)}, u32[]{:S(2)}, u32[]{:S(2)}) collective-permute-start(bf16[128,640]{1,0:T(8,128)(2,1)S(1)} %get-tuple-element.93), channel_id=1, source_target_pairs={{0,8},{8,0},{16,24},{24,16},{1,9},{9,1},{17,25},{25,17},{2,10},{10... | collective-permute-start | bytes 491528 | tf_op jit(solution)/shard_map/ppermute | solution.py:28
  43.1 4.5 %collective-permute-start.17 = (bf16[128,640]{1,0:T(8,128)(2,1)S(1)}, bf16[128,640]{1,0:T(8,128)(2,1)S(1)}, u32[]{:S(2)}, u32[]{:S(2)}) collective-permute-start(bf16[128,640]{1,0:T(8,128)(2,1)S(1)} %get-tuple-element.94), channel_id=1, source_target_pairs={{0,16},{8,24},{16,0},{24,8},{1,17},{9,25},{17,1},{25,9},{2,18},{10... | collective-permute-start | bytes 491528 | tf_op jit(solution)/shard_map/ppermute | solution.py:28
  44.3 7.1 %collective-permute-start.18 = (bf16[128,640]{1,0:T(8,128)(2,1)S(1)}, bf16[128,640]{1,0:T(8,128)(2,1)S(1)}, u32[]{:S(2)}, u32[]{:S(2)}) collective-permute-start(bf16[128,640]{1,0:T(8,128)(2,1)S(1)} %get-tuple-element.95), channel_id=1, source_target_pairs={{0,24},{8,16},{16,8},{24,0},{1,25},{9,17},{17,9},{25,1},{2,26},{10... | collective-permute-start | bytes 491528 | tf_op jit(solution)/shard_map/ppermute | solution.py:28
  51.4 5.2 %collective-permute-start.22 = (bf16[256,512]{1,0:T(8,128)(2,1)S(1)}, bf16[256,512]{1,0:T(8,128)(2,1)S(1)}, u32[]{:S(2)}, u32[]{:S(2)}) collective-permute-start(bf16[256,512]{1,0:T(8,128)(2,1)S(1)} %get-tuple-element.112), channel_id=1, source_target_pairs={{0,8},{8,0},{16,24},{24,16},{1,9},{9,1},{17,25},{25,17},{2,10},{10... | collective-permute-start | bytes 786440 | tf_op jit(solution)/shard_map/ppermute | solution.py:28
  53.3 4.6 %collective-permute-start.21 = (bf16[4,128,512]{2,1,0:T(8,128)(2,1)S(1)}, bf16[4,128,512]{2,1,0:T(8,128)(2,1)S(1)}, u32[]{:S(2)}, u32[]{:S(2)}) collective-permute-start(bf16[4,128,512]{2,1,0:T(8,128)(2,1)S(1)} %get-tuple-element.110), channel_id=1, source_target_pairs={{0,1},{1,0},{2,3},{3,2},{4,5},{5,4},{6,7},{7,6},{8,9},{9,8},{10,11... | collective-permute-start | bytes 1572872 | tf_op jit(solution)/shard_map/ppermute | solution.py:28
  58.2 10.1 %collective-permute-start.25 = (bf16[128,512]{1,0:T(8,128)(2,1)S(1)}, bf16[128,512]{1,0:T(8,128)(2,1)S(1)}, u32[]{:S(2)}, u32[]{:S(2)}) collective-permute-start(bf16[128,512]{1,0:T(8,128)(2,1)S(1)} %get-tuple-element.127), channel_id=1, source_target_pairs={{0,6},{2,4},{4,2},{6,0},{1,7},{3,5},{5,3},{7,1},{8,14},{10,12},{12... | collective-permute-start | bytes 393224 | tf_op jit(solution)/shard_map/ppermute | solution.py:28
  59.6 11.5 %collective-permute-start.24 = (bf16[128,512]{1,0:T(8,128)(2,1)S(1)}, bf16[128,512]{1,0:T(8,128)(2,1)S(1)}, u32[]{:S(2)}, u32[]{:S(2)}) collective-permute-start(bf16[128,512]{1,0:T(8,128)(2,1)S(1)} %get-tuple-element.128), channel_id=1, source_target_pairs={{0,4},{2,6},{4,0},{6,2},{1,5},{3,7},{5,1},{7,3},{8,12},{10,14},{12... | collective-permute-start | bytes 393224 | tf_op jit(solution)/shard_map/ppermute | solution.py:28
  60.6 10.5 %collective-permute-start.23 = (bf16[128,512]{1,0:T(8,128)(2,1)S(1)}, bf16[128,512]{1,0:T(8,128)(2,1)S(1)}, u32[]{:S(2)}, u32[]{:S(2)}) collective-permute-start(bf16[128,512]{1,0:T(8,128)(2,1)S(1)} %get-tuple-element.126), channel_id=1, source_target_pairs={{0,2},{2,0},{4,6},{6,4},{1,3},{3,1},{5,7},{7,5},{8,10},{10,8},{12,... | collective-permute-start | bytes 393224 | tf_op jit(solution)/shard_map/ppermute | solution.py:28
  60.9 10.3 %collective-permute-start.26 = (bf16[256,512]{1,0:T(8,128)(2,1)S(1)}, bf16[256,512]{1,0:T(8,128)(2,1)S(1)}, u32[]{:S(2)}, u32[]{:S(2)}) collective-permute-start(bf16[256,512]{1,0:T(8,128)(2,1)S(1)} %pad_maximum_fusion.1), channel_id=1, source_target_pairs={{0,16},{8,24},{16,0},{24,8},{1,17},{9,25},{17,1},{25,9},{2,18},{10... | collective-permute-start | bytes 786440 | tf_op jit(solution)/shard_map/ppermute | solution.py:28
  71.2 4.7 %collective-permute-start.31 = (bf16[512,512]{1,0:T(8,128)(2,1)S(1)}, bf16[512,512]{1,0:T(8,128)(2,1)S(1)}, u32[]{:S(2)}, u32[]{:S(2)}) collective-permute-start(bf16[512,512]{1,0:T(8,128)(2,1)S(1)} %pad_maximum_fusion.refs_5_), channel_id=1, source_target_pairs={{0,1},{1,0},{2,3},{3,2},{4,5},{5,4},{6,7},{7,6},{8,9},{9,8},{10,11... | collective-permute-start | bytes 1572872 | tf_op jit(solution)/shard_map/ppermute | solution.py:28
  71.8 7.5 %collective-permute-start.27 = (bf16[128,512]{1,0:T(8,128)(2,1)S(1)}, bf16[128,512]{1,0:T(8,128)(2,1)S(1)}, u32[]{:S(2)}, u32[]{:S(2)}) collective-permute-start(bf16[128,512]{1,0:T(8,128)(2,1)S(1)} %fusion.2.refs_1_), channel_id=1, source_target_pairs={{0,2},{2,0},{4,6},{6,4},{1,3},{3,1},{5,7},{7,5},{8,10},{10,8},{12,... | collective-permute-start | bytes 393224 | tf_op jit(solution)/shard_map/ppermute | solution.py:28
  74.0 9.2 %collective-permute-start.28 = (bf16[128,512]{1,0:T(8,128)(2,1)S(1)}, bf16[128,512]{1,0:T(8,128)(2,1)S(1)}, u32[]{:S(2)}, u32[]{:S(2)}) collective-permute-start(bf16[128,512]{1,0:T(8,128)(2,1)S(1)} %fusion.2.refs_1_), channel_id=1, source_target_pairs={{0,4},{2,6},{4,0},{6,2},{1,5},{3,7},{5,1},{7,3},{8,12},{10,14},{12... | collective-permute-start | bytes 393224 | tf_op jit(solution)/shard_map/ppermute | solution.py:28
  74.9 12.3 %collective-permute-start.29 = (bf16[128,512]{1,0:T(8,128)(2,1)S(1)}, bf16[128,512]{1,0:T(8,128)(2,1)S(1)}, u32[]{:S(2)}, u32[]{:S(2)}) collective-permute-start(bf16[128,512]{1,0:T(8,128)(2,1)S(1)} %fusion.2.refs_1_), channel_id=1, source_target_pairs={{0,6},{2,4},{4,2},{6,0},{1,7},{3,5},{5,3},{7,1},{8,14},{10,12},{12... | collective-permute-start | bytes 393224 | tf_op jit(solution)/shard_map/ppermute | solution.py:28
  75.2 12.0 %collective-permute-start.30 = (bf16[128,512]{1,0:T(8,128)(2,1)S(1)}, bf16[128,512]{1,0:T(8,128)(2,1)S(1)}, u32[]{:S(2)}, u32[]{:S(2)}) collective-permute-start(bf16[128,512]{1,0:T(8,128)(2,1)S(1)} %fusion.2.refs_1_), channel_id=1, source_target_pairs={{0,1},{1,0},{2,3},{3,2},{4,5},{5,4},{6,7},{7,6},{8,9},{9,8},{10,11... | collective-permute-start | bytes 393224 | tf_op jit(solution)/shard_map/ppermute | solution.py:28
  (9 other events, 41.5 us)

commit v5 on v4

--- a/solution.py
+++ b/solution.py
@@ -1,3 +1,4 @@
+import functools
 import math
 
 import jax
@@ -132,9 +133,11 @@
     return pl.ds(pl.multiple_of(start, lanes), lanes)
 
 
-def call(body, name, out, operands, scratch=(), flops=0, space=pltpu.VMEM):
+def call(body, name, out, operands, scratch=(), flops=0, space=pltpu.VMEM, onto=False):
     specs = [pl.BlockSpec(memory_space=pltpu.SMEM)]
     specs += [pl.BlockSpec(memory_space=pltpu.VMEM)] * (len(operands) - 1)
+    if onto:
+        specs[-1] = pl.BlockSpec(memory_space=space)
     moved = sum(a.size * a.dtype.itemsize for a in (*operands, *out))
     return pl.pallas_call(
         body,
@@ -143,6 +146,7 @@
         in_specs=specs,
         out_specs=[pl.BlockSpec(memory_space=space)] * len(out),
         scratch_shapes=list(scratch),
+        input_output_aliases={len(operands) - 1: 0} if onto else {},
         compiler_params=pltpu.CompilerParams(vmem_limit_bytes=40 * 1024 * 1024),
         cost_estimate=pl.CostEstimate(flops=flops, bytes_accessed=moved, transcendentals=0),
     )(*operands)
@@ -213,12 +217,28 @@
     pre[...] = result
 
 
+def terms_half(n_dp, n_pipe, n_ten, step, where, grads, pull, packs, scale, resid, gain, out, extra):
+    pipe, ten = where[1], where[2]
+    cols = resid.shape[1] // n_dp
+    half = cols // n_ten
+    share = half // n_pipe
+    start = (ten ^ step) * half
+    for k in range(n_dp):
+        i = where[0] ^ k
+        spot = aligned(i * cols + start, half)
+        part = dot_nt(grads, gate_and_up(packs, k, start, half))
+        part = scale * (gain[:, spot].astype(F32) * part) - resid[:, spot].astype(F32) * pull
+        if extra is not None:
+            part = part + extra[k][...].astype(F32)
+        part = part.astype(out.dtype)
+        for j in range(n_pipe):
+            out[pipe ^ j, :, aligned(i * share, share)] = part[:, j * share : (j + 1) * share]
+
+
 def backward_kernel(n_dp, n_pipe, n_ten, where, *refs):
-    terms, upstream, rest = refs[:n_dp], refs[n_dp], refs[n_dp + 1 :]
+    terms, packs = refs[:n_dp], refs[n_dp : 3 * n_dp]
+    pre, last, scale, resid, gain, other, grads, pull = refs[3 * n_dp :]
     units = terms[0].shape[1]
-    ups = [upstream] + [term.at[:, units:] for term in terms[1:]]
-    packs, (pre, last, scale, resid, gain, other, mine) = rest[: 2 * n_dp], rest[2 * n_dp :]
-    pipe, ten = where[1], where[2]
     hidden_grad = terms[0][...]
     for term in terms[1:]:
         hidden_grad = hidden_grad + term[:, :units].astype(F32)
@@ -229,25 +249,23 @@
     gate_grad = hidden_grad * up_pre * gelu_slope
     up_grad = hidden_grad * gelu_value
     dotted = jnp.sum(gate_grad * gate_pre + up_grad * up_pre, axis=1, keepdims=True)
-    grads = jnp.concatenate([gate_grad, up_grad], axis=1).astype(BF16)
+    grads[...] = jnp.concatenate([gate_grad, up_grad], axis=1).astype(BF16)
     row_scale = scale[:, :1]
-    width = resid.shape[1]
-    pull = row_scale * row_scale * (dotted / width)
-    cols = width // n_dp
-    half = cols // n_ten
-    share = half // n_pipe
-    for step, out in ((1, other), (0, mine)):
-        start = (ten ^ step) * half
-        for k in range(n_dp):
-            i = where[0] ^ k
-            spot = aligned(i * cols + start, half)
-            part = dot_nt(grads, gate_and_up(packs, k, start, half))
-            part = row_scale * (gain[:, spot].astype(F32) * part) - resid[:, spot].astype(F32) * pull
-            if step == 0:
-                part = part + ups[k][...].astype(F32)
-            part = part.astype(out.dtype)
-            for j in range(n_pipe):
-                out[pipe ^ j, :, aligned(i * share, share)] = part[:, j * share : (j + 1) * share]
+    pull_here = row_scale * row_scale * (dotted / resid.shape[1])
+    pull[...] = jnp.broadcast_to(pull_here, pull.shape)
+    terms_half(
+        n_dp, n_pipe, n_ten, 1, where, grads[...], pull_here, packs, row_scale, resid, gain, other, None
+    )
+
+
+def own_kernel(n_dp, n_pipe, n_ten, where, grads, pull, *refs):
+    terms, upstream, packs = refs[: n_dp - 1], refs[n_dp - 1], refs[n_dp : 3 * n_dp]
+    scale, resid, gain, mine = refs[3 * n_dp :]
+    half = upstream.shape[1]
+    extra = [upstream] + [term.at[:, term.shape[1] - half :] for term in terms]
+    terms_half(
+        n_dp, n_pipe, n_ten, 0, where, grads[...], pull[:, :1], packs, scale[:, :1], resid, gain, mine, extra
+    )
 
 
 def assemble_kernel(n_dp, n_pipe, n_ten, where, *refs):
@@ -318,7 +336,9 @@
     x_other = send(mlp_input, TENSOR, 1)
     far, near = send(down_weight, PIPE, 2), send(down_weight, PIPE, 1)
     grads, gate, up = lax.optimization_barrier((grads, gate_weight, up_weight))
-    gates, ups = [[value] + [send(value, DP, k) for k in (1, 2)] for value in (gate, up)]
+    near, first_gate, first_up = lax.optimization_barrier((near, gate_weight, up_weight))
+    gates = [gate, send(first_gate, DP, 1), send(gate, DP, 2)]
+    ups = [up, send(up, DP, 1), send(first_up, DP, 2)]
     grads, far, near = lax.optimization_barrier((grads, far, near))
     downs = [down_weight, near, far, send(far, PIPE, 1)]
 
@@ -374,12 +394,19 @@
     )
     terms, encoded = lax.optimization_barrier((terms, encoded))
 
-    other, mine = call(
+    other, grads_both, pull = call(
         lambda *refs: backward_kernel(n_dp, n_pipe, n_ten, *refs),
         "mlp_backward",
-        [shaped((n_pipe, tok, n_dp * share), BF16), shaped((n_pipe, tok, n_dp * share), F32)],
-        [where, *terms, outs[n_pipe], *packs, pre, last, scale, resid, gain_row],
-        flops=4 * tok * width * units,
+        [shaped((n_pipe, tok, n_dp * share), BF16), shaped((tok, 2 * units), BF16), shaped((tok, 128), F32)],
+        [where, *terms, *packs, pre, last, scale, resid, gain_row],
+        flops=2 * tok * width * units,
+    )
+    (mine,) = call(
+        lambda *refs: own_kernel(n_dp, n_pipe, n_ten, *refs),
+        "own_terms",
+        [shaped((n_pipe, tok, n_dp * share), F32)],
+        [where, grads_both, pull, *terms[1:], outs[n_pipe], *packs, scale, resid, gain_row],
+        flops=2 * tok * width * units,
     )
     mine = mine + send(other, TENSOR, 1).astype(F32)
     first = send(encoded[1], DP, 1)

time: 91.4 us -> 90.9 us (level)
  waiting for transfers between devices: 44 us -> 40.5 us
  starting transfers between devices: 32.3 us -> 34.6 us
    ppermute x35, waiting for transfers between devices: 44 us -> 40.5 us  [send(): return lax.ppermute(value, axis, [(src, src ^ step) for src in range(size)])]
    ppermute x35, starting transfers between devices: 32.3 us -> 34.6 us  [send(): return lax.ppermute(value, axis, [(src, src ^ step) for src in range(size)])]
    pallas_call x8 -> x9, Pallas kernels: 10.1 us -> 10.7 us  [call(): pl.pallas_call(body, name=name, out_shape=out, in_specs=specs, out_specs=...]
  transfers between devices with their start and end apart: 35 -> 35, of which waited for: 21 -> 18; matrix products, arithmetic and copies ran while one was open for 4% -> 4% of each run, Pallas kernels for 8% -> 9%
where the time goes in v5:
time: 90.9 us; the launch traced here: 90.7 us
  waiting for transfers between devices  40.5 us (45%)
  starting transfers between devices  34.6 us (38%)
  Pallas kernels  10.7 us (12%)
  local copies, waits for them, and re-layouts  3.56 us (4%)
    ppermute x35, waiting for transfers between devices, send(): return lax.ppermute(value, axis, [(src, src ^ step) for src in range(size)])  40.5 us
    ppermute x35, starting transfers between devices, send(): return lax.ppermute(value, axis, [(src, src ^ step) for src in range(size)])  34.6 us
    pallas_call x9, Pallas kernels, call(): pl.pallas_call(body, name=name, out_shape=out, in_specs=specs, out_specs=...  10.7 us
    unnamed x14, local copies, waits for them, and re-layouts  2.39 us
  transfers between devices with their start and end apart: 35, of which 18 were waited for; matrix products, arithmetic and copies ran while one was open for 4% of the time, Pallas kernels for 9%

profile of v5, /device:TPU:9, one launch (start us, length us, event | category | flops | bytes accessed | tf_op | source)
XLA Modules:
  0.0 90.7 jit_solution(1157121485232954795)
XLA Ops:
  0.7 2.5 %collective-permute-start.3 = (bf16[128,1024]{1,0:T(8,128)(2,1)}, bf16[128,1024]{1,0:T(8,128)(2,1)S(1)}, u32[]{:S(2)}, u32[]{:S(2)}) collective-permute-start(bf16[128,1024]{1,0:T(8,128)(2,1)} %refs_3_.1), channel_id=1, source_target_pairs={{0,4},{2,6},{4,0},{6,2},{1,5},{3,7},{5,1},{7,3},{8,12},{10,14},{12... | collective-permute-start | bytes 786440 | tf_op jit(solution)/shard_map/ppermute | solution.py:29
  4.1 1.3 %collective-permute-start = (bf16[128,512]{1,0:T(8,128)(2,1)S(1)}, bf16[128,512]{1,0:T(8,128)(2,1)S(1)}, u32[]{:S(2)}, u32[]{:S(2)}) collective-permute-start(bf16[128,512]{1,0:T(8,128)(2,1)S(1)} %bitcast.27), channel_id=1, source_target_pairs={{0,8},{8,0},{16,24},{24,16},{1,9},{9,1},{17,25},{25,17},{2,10},{10... | collective-permute-start | bytes 393224 | tf_op jit(solution)/shard_map/ppermute | solution.py:29
  6.8 1.4 %copy.12 = bf16[128,8,2,256]{3,1,2,0:T(8,128)(2,1)S(1)} copy(bf16[128,8,2,256]{3,2,1,0:T(2,128)(2,1)} %bitcast.32) | data formatting | bytes 2097152
  9.5 2.8 %collective-permute-done.2.refs_4_ = bf16[128,512]{1,0:T(8,128)(2,1)S(1)} collective-permute-done((bf16[128,512]{1,0:T(8,128)(2,1)S(1)}, bf16[128,512]{1,0:T(8,128)(2,1)S(1)}, u32[]{:S(2)}, u32[]{:S(2)}) %collective-permute-start.2) | collective-permute-done | bytes 131104 | tf_op jit(solution)/shard_map/ppermute | solution.py:29
  12.3 2.4 %collective-permute-done.3.refs_5_ = bf16[128,1024]{1,0:T(8,128)(2,1)S(1)} collective-permute-done((bf16[128,1024]{1,0:T(8,128)(2,1)}, bf16[128,1024]{1,0:T(8,128)(2,1)S(1)}, u32[]{:S(2)}, u32[]{:S(2)}) %collective-permute-start.3) | collective-permute-done | bytes 262176 | tf_op jit(solution)/shard_map/ppermute | solution.py:29
  14.8 1.3 %upstream_terms.1.refs_1_ = bf16[512,1024]{1,0:T(8,128)(2,1)S(1)} custom-call(s32[3]{0:T(128)S(1)} %pad_add_fusion.refs_0_, bf16[128,512]{1,0:T(8,128)(2,1)S(1)} %bitcast.30, bf16[128,512]{1,0:T(8,128)(2,1)S(1)} %collective-permute-done.refs_2_, bf16[128,512]{1,0:T(8,128)(2,1)S(1)} %collective-permute-done.1.refs_3_, ...), custom_call_target="tpu_custom_call" | custom-call | flops 536870912 | bytes 2621452 | tf_op jit(solution)/shard_map/upstream_terms/pallas_call | solution.py:142
  16.1 1.7 %collective-permute-start.5 = (bf16[512,1024]{1,0:T(8,128)(2,1)S(1)}, bf16[512,1024]{1,0:T(8,128)(2,1)S(1)}, u32[]{:S(2)}, u32[]{:S(2)}) collective-permute-start(bf16[512,1024]{1,0:T(8,128)(2,1)S(1)} %upstream_terms.1.refs_1_), channel_id=1, source_target_pairs={{0,1},{1,0},{2,3},{3,2},{4,5},{5,4},{6,7},{7,6},{8,9},{9,8},{10,11... | collective-permute-start | bytes 3145736 | tf_op jit(solution)/shard_map/ppermute | solution.py:29
  18.3 1.3 %collective-permute-start.8 = (bf16[128,1024]{1,0:T(8,128)(2,1)S(1)}, bf16[128,1024]{1,0:T(8,128)(2,1)S(1)}, u32[]{:S(2)}, u32[]{:S(2)}) collective-permute-start(bf16[128,1024]{1,0:T(8,128)(2,1)S(1)} %collective-permute-done.3.refs_5_), channel_id=1, source_target_pairs={{0,2},{2,0},{4,6},{6,4},{1,3},{3,1},{5,7},{7,5},{8,10},{10,8},{12,... | collective-permute-start | bytes 786440 | tf_op jit(solution)/shard_map/ppermute | solution.py:29
  19.6 1.2 %collective-permute-start.13 = (bf16[1024,128]{1,0:T(8,128)(2,1)S(1)}, bf16[1024,128]{1,0:T(8,128)(2,1)S(1)}, u32[]{:S(2)}, u32[]{:S(2)}) collective-permute-start(bf16[1024,128]{1,0:T(8,128)(2,1)S(1)} %copy-done), channel_id=1, source_target_pairs={{0,16},{8,24},{16,0},{24,8},{1,17},{9,25},{17,1},{25,9},{2,18},{10... | collective-permute-start | bytes 786440 | tf_op jit(solution)/shard_map/ppermute | solution.py:29
  22.7 1.2 %collective-permute-start.15 = (bf16[1024,128]{1,0:T(8,128)(2,1)S(1)}, bf16[1024,128]{1,0:T(8,128)(2,1)S(1)}, u32[]{:S(2)}, u32[]{:S(2)}) collective-permute-start(bf16[1024,128]{1,0:T(8,128)(2,1)S(1)} %copy-done.1), channel_id=1, source_target_pairs={{0,16},{8,24},{16,0},{24,8},{1,17},{9,25},{17,1},{25,9},{2,18},{10... | collective-permute-start | bytes 786440 | tf_op jit(solution)/shard_map/ppermute | solution.py:29
  24.0 2.1 %collective-permute-done.8.refs_6_ = bf16[128,1024]{1,0:T(8,128)(2,1)S(1)} collective-permute-done((bf16[128,1024]{1,0:T(8,128)(2,1)S(1)}, bf16[128,1024]{1,0:T(8,128)(2,1)S(1)}, u32[]{:S(2)}, u32[]{:S(2)}) %collective-permute-start.8) | collective-permute-done | bytes 262176 | tf_op jit(solution)/shard_map/ppermute | solution.py:29
  26.1 1.3 %hidden_terms.1 = (f32[512,128]{1,0:T(8,128)S(1)}, bf16[512,128]{1,0:T(8,128)(2,1)S(1)}, bf16[512,128]{1,0:T(8,128)(2,1)S(1)}, bf16[512,128]{1,0:T(8,128)(2,1)S(...) custom-call(s32[3]{0:T(128)S(1)} %pad_add_fusion.refs_0_, ...), custom_call_target="tpu_custom_call" | custom-call | flops 536870912 | bytes 4325388 | tf_op jit(solution)/shard_map/hidden_terms/pallas_call | solution.py:142
  27.5 1.4 %collective-permute-start.9 = (bf16[512,128]{1,0:T(8,128)(2,1)S(1)}, bf16[512,128]{1,0:T(8,128)(2,1)S(1)}, u32[]{:S(2)}, u32[]{:S(2)}) collective-permute-start(bf16[512,128]{1,0:T(8,128)(2,1)S(1)} %get-tuple-element.80), channel_id=1, source_target_pairs={{0,2},{2,0},{4,6},{6,4},{1,3},{3,1},{5,7},{7,5},{8,10},{10,8},{12,... | collective-permute-start | bytes 393224 | tf_op jit(solution)/shard_map/ppermute | solution.py:29
  30.2 3.5 %collective-permute-done.12.refs_2_.refs_6_.refs_8_ = bf16[1024,128]{1,0:T(8,128)(2,1)S(1)} collective-permute-done((bf16[1024,128]{1,0:T(8,128)(2,1)S(1)}, bf16[1024,128]{1,0:T(8,128)(2,1)S(1)}, u32[]{:S(2)}, u32[]{:S(2)}) %collective-permute-start.12) | collective-permute-done | bytes 262176 | tf_op jit(solution)/shard_map/ppermute | solution.py:29
  33.7 1.5 %collective-permute-start.19 = (bf16[1024,128]{1,0:T(8,128)(2,1)S(1)}, bf16[1024,128]{1,0:T(8,128)(2,1)S(1)}, u32[]{:S(2)}, u32[]{:S(2)}) collective-permute-start(bf16[1024,128]{1,0:T(8,128)(2,1)S(1)} %collective-permute-done.12.refs_2_.refs_6_.refs_8_), channel_id=1, source_target_pairs={{0,16},{8,24},{16,0},{24,8},{1,17},{9,25},{17,1},{25,9},{2,18},{10... | collective-permute-start | bytes 786440 | tf_op jit(solution)/shard_map/ppermute | solution.py:29
  36.4 1.5 %mlp_forward.1 = (bf16[128,4096]{1,0:T(8,128)(2,1)S(1)}, f32[128,128]{1,0:T(8,128)S(1)}, f32[128,256]{1,0:T(8,128)S(1)}, bf16[128,1024]{1,0:T(8,128)(2,1)S(1)}) custom-call(s32[3]{0:T(128)S(1)} %pad_add_fusion.refs_0_, bf16[1024,128]{1,0:T(8,128)(2,1)S(1)} %copy-done, bf16[1024,128]{1,0:T(8,128)(2,1)S(1)} %collective-permute-done.12.refs_2_.refs_6_.refs_8_, ...), custom_call_target="tpu_custom_call" | custom-call | flops 268435456 | bytes 4136972 | tf_op jit(solution)/shard_map/mlp_forward/pallas_call | solution.py:142
  37.9 3.2 %collective-permute-done.11.refs_4_ = bf16[512,128]{1,0:T(8,128)(2,1)S(1)} collective-permute-done((bf16[512,128]{1,0:T(8,128)(2,1)S(1)}, bf16[512,128]{1,0:T(8,128)(2,1)S(1)}, u32[]{:S(2)}, u32[]{:S(2)}) %collective-permute-start.11) | collective-permute-done | bytes 131104 | tf_op jit(solution)/shard_map/ppermute | solution.py:29
  41.7 1.3 %collective-permute-start.16 = (bf16[128,640]{1,0:T(8,128)(2,1)S(1)}, bf16[128,640]{1,0:T(8,128)(2,1)S(1)}, u32[]{:S(2)}, u32[]{:S(2)}) collective-permute-start(bf16[128,640]{1,0:T(8,128)(2,1)S(1)} %get-tuple-element.100), channel_id=1, source_target_pairs={{0,8},{8,0},{16,24},{24,16},{1,9},{9,1},{17,25},{25,17},{2,10},{10... | collective-permute-start | bytes 491528 | tf_op jit(solution)/shard_map/ppermute | solution.py:29
  43.0 1.2 %collective-permute-start.17 = (bf16[128,640]{1,0:T(8,128)(2,1)S(1)}, bf16[128,640]{1,0:T(8,128)(2,1)S(1)}, u32[]{:S(2)}, u32[]{:S(2)}) collective-permute-start(bf16[128,640]{1,0:T(8,128)(2,1)S(1)} %get-tuple-element.101), channel_id=1, source_target_pairs={{0,16},{8,24},{16,0},{24,8},{1,17},{9,25},{17,1},{25,9},{2,18},{10... | collective-permute-start | bytes 491528 | tf_op jit(solution)/shard_map/ppermute | solution.py:29
  46.0 1.5 %collective-permute-done.17.refs_3_.refs_4_ = bf16[128,640]{1,0:T(8,128)(2,1)S(1)} collective-permute-done((bf16[128,640]{1,0:T(8,128)(2,1)S(1)}, bf16[128,640]{1,0:T(8,128)(2,1)S(1)}, u32[]{:S(2)}, u32[]{:S(2)}) %collective-permute-start.17) | collective-permute-done | bytes 163872 | tf_op jit(solution)/shard_map/ppermute | solution.py:29
  47.5 3.6 %collective-permute-done.18.refs_4_.refs_5_ = bf16[128,640]{1,0:T(8,128)(2,1)S(1)} collective-permute-done((bf16[128,640]{1,0:T(8,128)(2,1)S(1)}, bf16[128,640]{1,0:T(8,128)(2,1)S(1)}, u32[]{:S(2)}, u32[]{:S(2)}) %collective-permute-start.18) | collective-permute-done | bytes 163872 | tf_op jit(solution)/shard_map/ppermute | solution.py:29
  51.1 1.4 %mlp_backward.1 = (bf16[4,128,512]{2,1,0:T(8,128)(2,1)S(1)}, bf16[128,256]{1,0:T(8,128)(2,1)S(1)}, f32[128,128]{1,0:T(8,128)S(1)}) custom-call(s32[3]{0:T(128)S(1)} %pad_add_fusion.refs_0_, f32[128,128]{1,0:T(8,128)S(1)} %get-tuple-element.107.refs_1_, bf16[128,640]{1,0:T(8,128)(2,1)S(1)} %collective-permute-done.16.refs_2_.refs_3_, ...), custom_call_target="tpu_custom_call" | custom-call | flops 134217728 | bytes 4825100 | tf_op jit(solution)/shard_map/mlp_backward/pallas_call | solution.py:142
  52.5 3.4 %collective-permute-start.21 = (bf16[4,128,512]{2,1,0:T(8,128)(2,1)S(1)}, bf16[4,128,512]{2,1,0:T(8,128)(2,1)S(1)}, u32[]{:S(2)}, u32[]{:S(2)}) collective-permute-start(bf16[4,128,512]{2,1,0:T(8,128)(2,1)S(1)} %get-tuple-element.118), channel_id=1, source_target_pairs={{0,1},{1,0},{2,3},{3,2},{4,5},{5,4},{6,7},{7,6},{8,9},{9,8},{10,11... | collective-permute-start | bytes 1572872 | tf_op jit(solution)/shard_map/ppermute | solution.py:29
  57.7 1.7 %collective-permute-start.25 = (bf16[128,512]{1,0:T(8,128)(2,1)S(1)}, bf16[128,512]{1,0:T(8,128)(2,1)S(1)}, u32[]{:S(2)}, u32[]{:S(2)}) collective-permute-start(bf16[128,512]{1,0:T(8,128)(2,1)S(1)} %get-tuple-element.135), channel_id=1, source_target_pairs={{0,6},{2,4},{4,2},{6,0},{1,7},{3,5},{5,3},{7,1},{8,14},{10,12},{12... | collective-permute-start | bytes 393224 | tf_op jit(solution)/shard_map/ppermute | solution.py:29
  59.4 1.3 %collective-permute-start.23 = (bf16[128,512]{1,0:T(8,128)(2,1)S(1)}, bf16[128,512]{1,0:T(8,128)(2,1)S(1)}, u32[]{:S(2)}, u32[]{:S(2)}) collective-permute-start(bf16[128,512]{1,0:T(8,128)(2,1)S(1)} %get-tuple-element.134), channel_id=1, source_target_pairs={{0,2},{2,0},{4,6},{6,4},{1,3},{3,1},{5,7},{7,5},{8,10},{10,8},{12,... | collective-permute-start | bytes 393224 | tf_op jit(solution)/shard_map/ppermute | solution.py:29
  61.2 5.9 %collective-permute-done.25 = bf16[128,512]{1,0:T(8,128)(2,1)S(1)} collective-permute-done((bf16[128,512]{1,0:T(8,128)(2,1)S(1)}, bf16[128,512]{1,0:T(8,128)(2,1)S(1)}, u32[]{:S(2)}, u32[]{:S(2)}) %collective-permute-start.25) | collective-permute-done | bytes 131104 | tf_op jit(solution)/shard_map/ppermute | solution.py:29
  67.1 3.0 %collective-permute-done.24 = bf16[128,512]{1,0:T(8,128)(2,1)S(1)} collective-permute-done((bf16[128,512]{1,0:T(8,128)(2,1)S(1)}, bf16[128,512]{1,0:T(8,128)(2,1)S(1)}, u32[]{:S(2)}, u32[]{:S(2)}) %collective-permute-start.24) | collective-permute-done | bytes 131104 | tf_op jit(solution)/shard_map/ppermute | solution.py:29
  71.2 2.1 %collective-permute-start.27 = (bf16[128,512]{1,0:T(8,128)(2,1)S(1)}, bf16[128,512]{1,0:T(8,128)(2,1)S(1)}, u32[]{:S(2)}, u32[]{:S(2)}) collective-permute-start(bf16[128,512]{1,0:T(8,128)(2,1)S(1)} %fusion.2.refs_1_), channel_id=1, source_target_pairs={{0,2},{2,0},{4,6},{6,4},{1,3},{3,1},{5,7},{7,5},{8,10},{10,8},{12,... | collective-permute-start | bytes 393224 | tf_op jit(solution)/shard_map/ppermute | solution.py:29
  75.3 1.3 %kv_grad.1 = bf16[1024,512]{1,0:T(8,128)(2,1)S(1)} custom-call(s32[3]{0:T(128)S(1)} %pad_add_fusion.refs_0_, bf16[128,512]{1,0:T(8,128)(2,1)S(1)} %bitcast.31, bf16[128,512]{1,0:T(8,128)(2,1)S(1)} %collective-permute-done.refs_2_, bf16[128,512]{1,0:T(8,128)(2,1)S(1)} %collective-permute-done.1.refs_3_, bf16[128,512]{1,0:T(8,128)(2,1)S(1)} %collective-permute-done.2.refs_4_, ...), custom_call_target="tpu_custom_call" | custom-call | flops 536870912 | bytes 2621452 | tf_op jit(solution)/shard_map/kv_grad/pallas_call | solution.py:142
  78.7 3.9 %collective-permute-done.28.refs_3_ = bf16[128,512]{1,0:T(8,128)(2,1)S(1)} collective-permute-done((bf16[128,512]{1,0:T(8,128)(2,1)S(1)}, bf16[128,512]{1,0:T(8,128)(2,1)S(1)}, u32[]{:S(2)}, u32[]{:S(2)}) %collective-permute-start.28) | collective-permute-done | bytes 131104 | tf_op jit(solution)/shard_map/ppermute | solution.py:29
  82.6 4.1 %collective-permute-done.29.refs_4_ = bf16[128,512]{1,0:T(8,128)(2,1)S(1)} collective-permute-done((bf16[128,512]{1,0:T(8,128)(2,1)S(1)}, bf16[128,512]{1,0:T(8,128)(2,1)S(1)}, u32[]{:S(2)}, u32[]{:S(2)}) %collective-permute-start.29) | collective-permute-done | bytes 131104 | tf_op jit(solution)/shard_map/ppermute | solution.py:29
  89.1 1.6 %input_grad.1 = bf16[128,4096]{1,0:T(8,128)(2,1)} custom-call(s32[3]{0:T(128)S(1)} %pad_add_fusion.refs_0_, bf16[128,512]{1,0:T(8,128)(2,1)S(1)} %fusion.2.refs_1_, bf16[128,512]{1,0:T(8,128)(2,1)S(1)} %collective-permute-done.27.refs_2_, bf16[128,512]{1,0:T(8,128)(2,1)S(1)} %collective-permute-done.28.refs_3_, ...), custom_call_target="tpu_custom_call" | custom-call | bytes 2097164 | tf_op jit(solution)/shard_map/input_grad/pallas_call | solution.py:142
  (71 shorter events, 20.9 us)
Async XLA Ops:
  0.6 11.7 %collective-permute-start.4 = (bf16[128,1024]{1,0:T(8,128)(2,1)}, bf16[128,1024]{1,0:T(8,128)(2,1)S(1)}, u32[]{:S(2)}, u32[]{:S(2)}) collective-permute-start(bf16[128,1024]{1,0:T(8,128)(2,1)} %refs_3_.1), channel_id=1, source_target_pairs={{0,2},{2,0},{4,6},{6,4},{1,3},{3,1},{5,7},{7,5},{8,10},{10,8},{12,... | collective-permute-start | bytes 786440 | tf_op jit(solution)/shard_map/ppermute | solution.py:29
  0.7 14.0 %collective-permute-start.3 = (bf16[128,1024]{1,0:T(8,128)(2,1)}, bf16[128,1024]{1,0:T(8,128)(2,1)S(1)}, u32[]{:S(2)}, u32[]{:S(2)}) collective-permute-start(bf16[128,1024]{1,0:T(8,128)(2,1)} %refs_3_.1), channel_id=1, source_target_pairs={{0,4},{2,6},{4,0},{6,2},{1,5},{3,7},{5,1},{7,3},{8,12},{10,14},{12... | collective-permute-start | bytes 786440 | tf_op jit(solution)/shard_map/ppermute | solution.py:29
  4.1 4.3 %collective-permute-start = (bf16[128,512]{1,0:T(8,128)(2,1)S(1)}, bf16[128,512]{1,0:T(8,128)(2,1)S(1)}, u32[]{:S(2)}, u32[]{:S(2)}) collective-permute-start(bf16[128,512]{1,0:T(8,128)(2,1)S(1)} %bitcast.27), channel_id=1, source_target_pairs={{0,8},{8,0},{16,24},{24,16},{1,9},{9,1},{17,25},{25,17},{2,10},{10... | collective-permute-start | bytes 393224 | tf_op jit(solution)/shard_map/ppermute | solution.py:29
  5.4 4.1 %collective-permute-start.1 = (bf16[128,512]{1,0:T(8,128)(2,1)S(1)}, bf16[128,512]{1,0:T(8,128)(2,1)S(1)}, u32[]{:S(2)}, u32[]{:S(2)}) collective-permute-start(bf16[128,512]{1,0:T(8,128)(2,1)S(1)} %bitcast.28), channel_id=1, source_target_pairs={{0,16},{8,24},{16,0},{24,8},{1,17},{9,25},{17,1},{25,9},{2,18},{10... | collective-permute-start | bytes 393224 | tf_op jit(solution)/shard_map/ppermute | solution.py:29
  6.6 5.7 %collective-permute-start.2 = (bf16[128,512]{1,0:T(8,128)(2,1)S(1)}, bf16[128,512]{1,0:T(8,128)(2,1)S(1)}, u32[]{:S(2)}, u32[]{:S(2)}) collective-permute-start(bf16[128,512]{1,0:T(8,128)(2,1)S(1)} %bitcast.29), channel_id=1, source_target_pairs={{0,24},{8,16},{16,8},{24,0},{1,25},{9,17},{17,9},{25,1},{2,26},{10... | collective-permute-start | bytes 393224 | tf_op jit(solution)/shard_map/ppermute | solution.py:29
  16.1 6.7 %collective-permute-start.5 = (bf16[512,1024]{1,0:T(8,128)(2,1)S(1)}, bf16[512,1024]{1,0:T(8,128)(2,1)S(1)}, u32[]{:S(2)}, u32[]{:S(2)}) collective-permute-start(bf16[512,1024]{1,0:T(8,128)(2,1)S(1)} %upstream_terms.1.refs_1_), channel_id=1, source_target_pairs={{0,1},{1,0},{2,3},{3,2},{4,5},{5,4},{6,7},{7,6},{8,9},{9,8},{10,11... | collective-permute-start | bytes 3145736 | tf_op jit(solution)/shard_map/ppermute | solution.py:29
  17.7 3.1 %collective-permute-start.6 = (bf16[128,2048]{1,0:T(8,128)(2,1)S(1)}, bf16[128,2048]{1,0:T(8,128)(2,1)S(1)}, u32[]{:S(2)}, u32[]{:S(2)}) collective-permute-start(bf16[128,2048]{1,0:T(8,128)(2,1)S(1)} %copy-done.3), channel_id=1, source_target_pairs={{0,1},{1,0},{2,3},{3,2},{4,5},{5,4},{6,7},{7,6},{8,9},{9,8},{10,11... | collective-permute-start | bytes 1572872 | tf_op jit(solution)/shard_map/ppermute | solution.py:29
  17.8 4.2 %collective-permute-start.7 = (bf16[128,2048]{1,0:T(8,128)(2,1)S(1)}, bf16[128,2048]{1,0:T(8,128)(2,1)S(1)}, u32[]{:S(2)}, u32[]{:S(2)}) collective-permute-start(bf16[128,2048]{1,0:T(8,128)(2,1)S(1)} %copy-done.2), channel_id=1, source_target_pairs={{0,1},{1,0},{2,3},{3,2},{4,5},{5,4},{6,7},{7,6},{8,9},{9,8},{10,11... | collective-permute-start | bytes 1572872 | tf_op jit(solution)/shard_map/ppermute | solution.py:29
  18.3 7.9 %collective-permute-start.8 = (bf16[128,1024]{1,0:T(8,128)(2,1)S(1)}, bf16[128,1024]{1,0:T(8,128)(2,1)S(1)}, u32[]{:S(2)}, u32[]{:S(2)}) collective-permute-start(bf16[128,1024]{1,0:T(8,128)(2,1)S(1)} %collective-permute-done.3.refs_5_), channel_id=1, source_target_pairs={{0,2},{2,0},{4,6},{6,4},{1,3},{3,1},{5,7},{7,5},{8,10},{10,8},{12,... | collective-permute-start | bytes 786440 | tf_op jit(solution)/shard_map/ppermute | solution.py:29
  19.6 9.3 %collective-permute-start.13 = (bf16[1024,128]{1,0:T(8,128)(2,1)S(1)}, bf16[1024,128]{1,0:T(8,128)(2,1)S(1)}, u32[]{:S(2)}, u32[]{:S(2)}) collective-permute-start(bf16[1024,128]{1,0:T(8,128)(2,1)S(1)} %copy-done), channel_id=1, source_target_pairs={{0,16},{8,24},{16,0},{24,8},{1,17},{9,25},{17,1},{25,9},{2,18},{10... | collective-permute-start | bytes 786440 | tf_op jit(solution)/shard_map/ppermute | solution.py:29
  20.8 9.2 %collective-permute-start.14 = (bf16[1024,128]{1,0:T(8,128)(2,1)S(1)}, bf16[1024,128]{1,0:T(8,128)(2,1)S(1)}, u32[]{:S(2)}, u32[]{:S(2)}) collective-permute-start(bf16[1024,128]{1,0:T(8,128)(2,1)S(1)} %copy-done.1), channel_id=1, source_target_pairs={{0,8},{8,0},{16,24},{24,16},{1,9},{9,1},{17,25},{25,17},{2,10},{10... | collective-permute-start | bytes 786440 | tf_op jit(solution)/shard_map/ppermute | solution.py:29
  22.1 11.6 %collective-permute-start.12 = (bf16[1024,128]{1,0:T(8,128)(2,1)S(1)}, bf16[1024,128]{1,0:T(8,128)(2,1)S(1)}, u32[]{:S(2)}, u32[]{:S(2)}) collective-permute-start(bf16[1024,128]{1,0:T(8,128)(2,1)S(1)} %copy-done), channel_id=1, source_target_pairs={{0,8},{8,0},{16,24},{24,16},{1,9},{9,1},{17,25},{25,17},{2,10},{10... | collective-permute-start | bytes 786440 | tf_op jit(solution)/shard_map/ppermute | solution.py:29
  22.7 12.4 %collective-permute-start.15 = (bf16[1024,128]{1,0:T(8,128)(2,1)S(1)}, bf16[1024,128]{1,0:T(8,128)(2,1)S(1)}, u32[]{:S(2)}, u32[]{:S(2)}) collective-permute-start(bf16[1024,128]{1,0:T(8,128)(2,1)S(1)} %copy-done.1), channel_id=1, source_target_pairs={{0,16},{8,24},{16,0},{24,8},{1,17},{9,25},{17,1},{25,9},{2,18},{10... | collective-permute-start | bytes 786440 | tf_op jit(solution)/shard_map/ppermute | solution.py:29
  27.5 10.4 %collective-permute-start.9 = (bf16[512,128]{1,0:T(8,128)(2,1)S(1)}, bf16[512,128]{1,0:T(8,128)(2,1)S(1)}, u32[]{:S(2)}, u32[]{:S(2)}) collective-permute-start(bf16[512,128]{1,0:T(8,128)(2,1)S(1)} %get-tuple-element.80), channel_id=1, source_target_pairs={{0,2},{2,0},{4,6},{6,4},{1,3},{3,1},{5,7},{7,5},{8,10},{10,8},{12,... | collective-permute-start | bytes 393224 | tf_op jit(solution)/shard_map/ppermute | solution.py:29
  28.8 9.1 %collective-permute-start.10 = (bf16[512,128]{1,0:T(8,128)(2,1)S(1)}, bf16[512,128]{1,0:T(8,128)(2,1)S(1)}, u32[]{:S(2)}, u32[]{:S(2)}) collective-permute-start(bf16[512,128]{1,0:T(8,128)(2,1)S(1)} %get-tuple-element.81), channel_id=1, source_target_pairs={{0,4},{2,6},{4,0},{6,2},{1,5},{3,7},{5,1},{7,3},{8,12},{10,14},{12... | collective-permute-start | bytes 393224 | tf_op jit(solution)/shard_map/ppermute | solution.py:29
  30.0 11.1 %collective-permute-start.11 = (bf16[512,128]{1,0:T(8,128)(2,1)S(1)}, bf16[512,128]{1,0:T(8,128)(2,1)S(1)}, u32[]{:S(2)}, u32[]{:S(2)}) collective-permute-start(bf16[512,128]{1,0:T(8,128)(2,1)S(1)} %get-tuple-element.82), channel_id=1, source_target_pairs={{0,6},{2,4},{4,2},{6,0},{1,7},{3,5},{5,3},{7,1},{8,14},{10,12},{12... | collective-permute-start | bytes 393224 | tf_op jit(solution)/shard_map/ppermute | solution.py:29
  33.7 17.4 %collective-permute-start.19 = (bf16[1024,128]{1,0:T(8,128)(2,1)S(1)}, bf16[1024,128]{1,0:T(8,128)(2,1)S(1)}, u32[]{:S(2)}, u32[]{:S(2)}) collective-permute-start(bf16[1024,128]{1,0:T(8,128)(2,1)S(1)} %collective-permute-done.12.refs_2_.refs_6_.refs_8_), channel_id=1, source_target_pairs={{0,16},{8,24},{16,0},{24,8},{1,17},{9,25},{17,1},{25,9},{2,18},{10... | collective-permute-start | bytes 786440 | tf_op jit(solution)/shard_map/ppermute | solution.py:29
  35.2 15.9 %collective-permute-start.20 = (bf16[1024,128]{1,0:T(8,128)(2,1)S(1)}, bf16[1024,128]{1,0:T(8,128)(2,1)S(1)}, u32[]{:S(2)}, u32[]{:S(2)}) collective-permute-start(bf16[1024,128]{1,0:T(8,128)(2,1)S(1)} %collective-permute-done.15.refs_6_.refs_11_.refs_13_), channel_id=1, source_target_pairs={{0,8},{8,0},{16,24},{24,16},{1,9},{9,1},{17,25},{25,17},{2,10},{10... | collective-permute-start | bytes 786440 | tf_op jit(solution)/shard_map/ppermute | solution.py:29
  41.7 4.2 %collective-permute-start.16 = (bf16[128,640]{1,0:T(8,128)(2,1)S(1)}, bf16[128,640]{1,0:T(8,128)(2,1)S(1)}, u32[]{:S(2)}, u32[]{:S(2)}) collective-permute-start(bf16[128,640]{1,0:T(8,128)(2,1)S(1)} %get-tuple-element.100), channel_id=1, source_target_pairs={{0,8},{8,0},{16,24},{24,16},{1,9},{9,1},{17,25},{25,17},{2,10},{10... | collective-permute-start | bytes 491528 | tf_op jit(solution)/shard_map/ppermute | solution.py:29
  43.0 4.5 %collective-permute-start.17 = (bf16[128,640]{1,0:T(8,128)(2,1)S(1)}, bf16[128,640]{1,0:T(8,128)(2,1)S(1)}, u32[]{:S(2)}, u32[]{:S(2)}) collective-permute-start(bf16[128,640]{1,0:T(8,128)(2,1)S(1)} %get-tuple-element.101), channel_id=1, source_target_pairs={{0,16},{8,24},{16,0},{24,8},{1,17},{9,25},{17,1},{25,9},{2,18},{10... | collective-permute-start | bytes 491528 | tf_op jit(solution)/shard_map/ppermute | solution.py:29
  44.3 6.8 %collective-permute-start.18 = (bf16[128,640]{1,0:T(8,128)(2,1)S(1)}, bf16[128,640]{1,0:T(8,128)(2,1)S(1)}, u32[]{:S(2)}, u32[]{:S(2)}) collective-permute-start(bf16[128,640]{1,0:T(8,128)(2,1)S(1)} %get-tuple-element.102), channel_id=1, source_target_pairs={{0,24},{8,16},{16,8},{24,0},{1,25},{9,17},{17,9},{25,1},{2,26},{10... | collective-permute-start | bytes 491528 | tf_op jit(solution)/shard_map/ppermute | solution.py:29
  51.1 5.9 %collective-permute-start.22 = (bf16[256,512]{1,0:T(8,128)(2,1)S(1)}, bf16[256,512]{1,0:T(8,128)(2,1)S(1)}, u32[]{:S(2)}, u32[]{:S(2)}) collective-permute-start(bf16[256,512]{1,0:T(8,128)(2,1)S(1)} %get-tuple-element.120), channel_id=1, source_target_pairs={{0,8},{8,0},{16,24},{24,16},{1,9},{9,1},{17,25},{25,17},{2,10},{10... | collective-permute-start | bytes 786440 | tf_op jit(solution)/shard_map/ppermute | solution.py:29
  52.5 4.9 %collective-permute-start.21 = (bf16[4,128,512]{2,1,0:T(8,128)(2,1)S(1)}, bf16[4,128,512]{2,1,0:T(8,128)(2,1)S(1)}, u32[]{:S(2)}, u32[]{:S(2)}) collective-permute-start(bf16[4,128,512]{2,1,0:T(8,128)(2,1)S(1)} %get-tuple-element.118), channel_id=1, source_target_pairs={{0,1},{1,0},{2,3},{3,2},{4,5},{5,4},{6,7},{7,6},{8,9},{9,8},{10,11... | collective-permute-start | bytes 1572872 | tf_op jit(solution)/shard_map/ppermute | solution.py:29
  57.7 9.4 %collective-permute-start.25 = (bf16[128,512]{1,0:T(8,128)(2,1)S(1)}, bf16[128,512]{1,0:T(8,128)(2,1)S(1)}, u32[]{:S(2)}, u32[]{:S(2)}) collective-permute-start(bf16[128,512]{1,0:T(8,128)(2,1)S(1)} %get-tuple-element.135), channel_id=1, source_target_pairs={{0,6},{2,4},{4,2},{6,0},{1,7},{3,5},{5,3},{7,1},{8,14},{10,12},{12... | collective-permute-start | bytes 393224 | tf_op jit(solution)/shard_map/ppermute | solution.py:29
  59.4 10.6 %collective-permute-start.24 = (bf16[128,512]{1,0:T(8,128)(2,1)S(1)}, bf16[128,512]{1,0:T(8,128)(2,1)S(1)}, u32[]{:S(2)}, u32[]{:S(2)}) collective-permute-start(bf16[128,512]{1,0:T(8,128)(2,1)S(1)} %get-tuple-element.136), channel_id=1, source_target_pairs={{0,4},{2,6},{4,0},{6,2},{1,5},{3,7},{5,1},{7,3},{8,12},{10,14},{12... | collective-permute-start | bytes 393224 | tf_op jit(solution)/shard_map/ppermute | solution.py:29
  59.4 10.6 %collective-permute-start.23 = (bf16[128,512]{1,0:T(8,128)(2,1)S(1)}, bf16[128,512]{1,0:T(8,128)(2,1)S(1)}, u32[]{:S(2)}, u32[]{:S(2)}) collective-permute-start(bf16[128,512]{1,0:T(8,128)(2,1)S(1)} %get-tuple-element.134), channel_id=1, source_target_pairs={{0,2},{2,0},{4,6},{6,4},{1,3},{3,1},{5,7},{7,5},{8,10},{10,8},{12,... | collective-permute-start | bytes 393224 | tf_op jit(solution)/shard_map/ppermute | solution.py:29
  60.7 9.5 %collective-permute-start.26 = (bf16[256,512]{1,0:T(8,128)(2,1)S(1)}, bf16[256,512]{1,0:T(8,128)(2,1)S(1)}, u32[]{:S(2)}, u32[]{:S(2)}) collective-permute-start(bf16[256,512]{1,0:T(8,128)(2,1)S(1)} %pad_maximum_fusion.1), channel_id=1, source_target_pairs={{0,16},{8,24},{16,0},{24,8},{1,17},{9,25},{17,1},{25,9},{2,18},{10... | collective-permute-start | bytes 786440 | tf_op jit(solution)/shard_map/ppermute | solution.py:29
  70.2 5.1 %collective-permute-start.31 = (bf16[512,512]{1,0:T(8,128)(2,1)S(1)}, bf16[512,512]{1,0:T(8,128)(2,1)S(1)}, u32[]{:S(2)}, u32[]{:S(2)}) collective-permute-start(bf16[512,512]{1,0:T(8,128)(2,1)S(1)} %pad_maximum_fusion.refs_5_), channel_id=1, source_target_pairs={{0,1},{1,0},{2,3},{3,2},{4,5},{5,4},{6,7},{7,6},{8,9},{9,8},{10,11... | collective-permute-start | bytes 1572872 | tf_op jit(solution)/shard_map/ppermute | solution.py:29
  71.2 7.4 %collective-permute-start.27 = (bf16[128,512]{1,0:T(8,128)(2,1)S(1)}, bf16[128,512]{1,0:T(8,128)(2,1)S(1)}, u32[]{:S(2)}, u32[]{:S(2)}) collective-permute-start(bf16[128,512]{1,0:T(8,128)(2,1)S(1)} %fusion.2.refs_1_), channel_id=1, source_target_pairs={{0,2},{2,0},{4,6},{6,4},{1,3},{3,1},{5,7},{7,5},{8,10},{10,8},{12,... | collective-permute-start | bytes 393224 | tf_op jit(solution)/shard_map/ppermute | solution.py:29
  73.4 9.3 %collective-permute-start.28 = (bf16[128,512]{1,0:T(8,128)(2,1)S(1)}, bf16[128,512]{1,0:T(8,128)(2,1)S(1)}, u32[]{:S(2)}, u32[]{:S(2)}) collective-permute-start(bf16[128,512]{1,0:T(8,128)(2,1)S(1)} %fusion.2.refs_1_), channel_id=1, source_target_pairs={{0,4},{2,6},{4,0},{6,2},{1,5},{3,7},{5,1},{7,3},{8,12},{10,14},{12... | collective-permute-start | bytes 393224 | tf_op jit(solution)/shard_map/ppermute | solution.py:29
  74.3 12.4 %collective-permute-start.29 = (bf16[128,512]{1,0:T(8,128)(2,1)S(1)}, bf16[128,512]{1,0:T(8,128)(2,1)S(1)}, u32[]{:S(2)}, u32[]{:S(2)}) collective-permute-start(bf16[128,512]{1,0:T(8,128)(2,1)S(1)} %fusion.2.refs_1_), channel_id=1, source_target_pairs={{0,6},{2,4},{4,2},{6,0},{1,7},{3,5},{5,3},{7,1},{8,14},{10,12},{12... | collective-permute-start | bytes 393224 | tf_op jit(solution)/shard_map/ppermute | solution.py:29
  74.6 12.1 %collective-permute-start.30 = (bf16[128,512]{1,0:T(8,128)(2,1)S(1)}, bf16[128,512]{1,0:T(8,128)(2,1)S(1)}, u32[]{:S(2)}, u32[]{:S(2)}) collective-permute-start(bf16[128,512]{1,0:T(8,128)(2,1)S(1)} %fusion.2.refs_1_), channel_id=1, source_target_pairs={{0,1},{1,0},{2,3},{3,2},{4,5},{5,4},{6,7},{7,6},{8,9},{9,8},{10,11... | collective-permute-start | bytes 393224 | tf_op jit(solution)/shard_map/ppermute | solution.py:29
  (9 other events, 37.1 us)

commit v6 on v5

--- a/solution.py
+++ b/solution.py
@@ -1,4 +1,3 @@
-import functools
 import math
 
 import jax
@@ -31,11 +30,6 @@
 
 def gather(value, axis):
     return [send(value, axis, step) for step in range(lax.axis_size(axis))]
-
-
-def relayed(value, axis):
-    far, near = send(value, axis, 2), send(value, axis, 1)
-    return [value, near, far, send(far, axis, 1)]
 
 
 def natural(parts, axis, dim):
@@ -133,11 +127,9 @@
     return pl.ds(pl.multiple_of(start, lanes), lanes)
 
 
-def call(body, name, out, operands, scratch=(), flops=0, space=pltpu.VMEM, onto=False):
+def call(body, name, out, operands, scratch=(), flops=0, space=pltpu.VMEM):
     specs = [pl.BlockSpec(memory_space=pltpu.SMEM)]
     specs += [pl.BlockSpec(memory_space=pltpu.VMEM)] * (len(operands) - 1)
-    if onto:
-        specs[-1] = pl.BlockSpec(memory_space=space)
     moved = sum(a.size * a.dtype.itemsize for a in (*operands, *out))
     return pl.pallas_call(
         body,
@@ -146,7 +138,6 @@
         in_specs=specs,
         out_specs=[pl.BlockSpec(memory_space=space)] * len(out),
         scratch_shapes=list(scratch),
-        input_output_aliases={len(operands) - 1: 0} if onto else {},
         compiler_params=pltpu.CompilerParams(vmem_limit_bytes=40 * 1024 * 1024),
         cost_estimate=pl.CostEstimate(flops=flops, bytes_accessed=moved, transcendentals=0),
     )(*operands)
@@ -326,7 +317,8 @@
     cols = kv_weight.shape[0]
     units = gate_weight.shape[1]
     share = cols // (n_pipe * n_ten)
-    if (n_dp, n_pipe, n_ten) != (4, 4, 2) or share % 128 or tok % 128 or units % 128:
+    squares = n_dp == n_pipe == n_ten * n_ten and n_ten == 2
+    if not squares or share % 128 or tok % 128 or units % 128:
         return on_device_any(
             enc_out, mlp_input, grad_kv, kv_weight, gate_weight, up_weight, down_weight, norm_gain
         )
@@ -431,9 +423,9 @@
         flops=2 * n_dp * tok * section.size,
     )
     kv_grad = kv_grad.reshape(kv_weight.shape)
-    swapped = send(part, TENSOR, 1)
-    parts, swapped, kv_grad = lax.optimization_barrier((parts, swapped, kv_grad))
-    parts = parts + [swapped] + [send(part, TENSOR, 1) for part in parts[1:]]
+    swapped = [send(part, TENSOR, 1) for part in parts[:2]]
+    far, last, kv_grad = lax.optimization_barrier((*parts[2:], kv_grad))
+    parts = [*parts[:2], far, last, *swapped, send(far, TENSOR, 1), send(last, TENSOR, 1)]
     (input_grad,) = call(
         lambda *refs: assemble_kernel(n_dp, n_pipe, n_ten, *refs),
         "input_grad",

time: 90.9 us -> 90.7 us (level)
  transfers between devices with their start and end apart: 35 -> 35, of which waited for: 18 -> 17; matrix products, arithmetic and copies ran while one was open for 4% -> 4% of each run, Pallas kernels for 9% -> 9%
where the time goes in v6:
time: 90.7 us; the launch traced here: 90.5 us
  waiting for transfers between devices  39.9 us (44%)
  starting transfers between devices  35 us (39%)
  Pallas kernels  10.7 us (12%)
  local copies, waits for them, and re-layouts  3.56 us (4%)
    ppermute x35, waiting for transfers between devices, send(): return lax.ppermute(value, axis, [(src, src ^ step) for src in range(size)])  39.9 us
    ppermute x35, starting transfers between devices, send(): return lax.ppermute(value, axis, [(src, src ^ step) for src in range(size)])  35 us
    pallas_call x9, Pallas kernels, call(): pl.pallas_call(body, name=name, out_shape=out, in_specs=specs, out_specs=...  10.7 us
    unnamed x14, local copies, waits for them, and re-layouts  2.39 us
  transfers between devices with their start and end apart: 35, of which 17 were waited for; matrix products, arithmetic and copies ran while one was open for 4% of the time, Pallas kernels for 9%

profile of v6, /device:TPU:9, one launch (start us, length us, event | category | flops | bytes accessed | tf_op | source)
XLA Modules:
  0.0 90.5 jit_solution(15801062916045619609)
XLA Ops:
  0.7 2.5 %collective-permute-start.3 = (bf16[128,1024]{1,0:T(8,128)(2,1)}, bf16[128,1024]{1,0:T(8,128)(2,1)S(1)}, u32[]{:S(2)}, u32[]{:S(2)}) collective-permute-start(bf16[128,1024]{1,0:T(8,128)(2,1)} %refs_3_.1), channel_id=1, source_target_pairs={{0,4},{2,6},{4,0},{6,2},{1,5},{3,7},{5,1},{7,3},{8,12},{10,14},{12... | collective-permute-start | bytes 786440 | tf_op jit(solution)/shard_map/ppermute | solution.py:28
  4.1 1.3 %collective-permute-start = (bf16[128,512]{1,0:T(8,128)(2,1)S(1)}, bf16[128,512]{1,0:T(8,128)(2,1)S(1)}, u32[]{:S(2)}, u32[]{:S(2)}) collective-permute-start(bf16[128,512]{1,0:T(8,128)(2,1)S(1)} %bitcast.27), channel_id=1, source_target_pairs={{0,8},{8,0},{16,24},{24,16},{1,9},{9,1},{17,25},{25,17},{2,10},{10... | collective-permute-start | bytes 393224 | tf_op jit(solution)/shard_map/ppermute | solution.py:28
  6.8 1.4 %copy.12 = bf16[128,8,2,256]{3,1,2,0:T(8,128)(2,1)S(1)} copy(bf16[128,8,2,256]{3,2,1,0:T(2,128)(2,1)} %bitcast.32) | data formatting | bytes 2097152
  9.5 2.8 %collective-permute-done.2.refs_4_ = bf16[128,512]{1,0:T(8,128)(2,1)S(1)} collective-permute-done((bf16[128,512]{1,0:T(8,128)(2,1)S(1)}, bf16[128,512]{1,0:T(8,128)(2,1)S(1)}, u32[]{:S(2)}, u32[]{:S(2)}) %collective-permute-start.2) | collective-permute-done | bytes 131104 | tf_op jit(solution)/shard_map/ppermute | solution.py:28
  12.3 2.4 %collective-permute-done.3.refs_5_ = bf16[128,1024]{1,0:T(8,128)(2,1)S(1)} collective-permute-done((bf16[128,1024]{1,0:T(8,128)(2,1)}, bf16[128,1024]{1,0:T(8,128)(2,1)S(1)}, u32[]{:S(2)}, u32[]{:S(2)}) %collective-permute-start.3) | collective-permute-done | bytes 262176 | tf_op jit(solution)/shard_map/ppermute | solution.py:28
  14.8 1.3 %upstream_terms.1.refs_1_ = bf16[512,1024]{1,0:T(8,128)(2,1)S(1)} custom-call(s32[3]{0:T(128)S(1)} %pad_add_fusion.refs_0_, bf16[128,512]{1,0:T(8,128)(2,1)S(1)} %bitcast.30, bf16[128,512]{1,0:T(8,128)(2,1)S(1)} %collective-permute-done.refs_2_, bf16[128,512]{1,0:T(8,128)(2,1)S(1)} %collective-permute-done.1.refs_3_, ...), custom_call_target="tpu_custom_call" | custom-call | flops 536870912 | bytes 2621452 | tf_op jit(solution)/shard_map/upstream_terms/pallas_call | solution.py:134
  16.1 1.7 %collective-permute-start.5 = (bf16[512,1024]{1,0:T(8,128)(2,1)S(1)}, bf16[512,1024]{1,0:T(8,128)(2,1)S(1)}, u32[]{:S(2)}, u32[]{:S(2)}) collective-permute-start(bf16[512,1024]{1,0:T(8,128)(2,1)S(1)} %upstream_terms.1.refs_1_), channel_id=1, source_target_pairs={{0,1},{1,0},{2,3},{3,2},{4,5},{5,4},{6,7},{7,6},{8,9},{9,8},{10,11... | collective-permute-start | bytes 3145736 | tf_op jit(solution)/shard_map/ppermute | solution.py:28
  18.3 1.3 %collective-permute-start.8 = (bf16[128,1024]{1,0:T(8,128)(2,1)S(1)}, bf16[128,1024]{1,0:T(8,128)(2,1)S(1)}, u32[]{:S(2)}, u32[]{:S(2)}) collective-permute-start(bf16[128,1024]{1,0:T(8,128)(2,1)S(1)} %collective-permute-done.3.refs_5_), channel_id=1, source_target_pairs={{0,2},{2,0},{4,6},{6,4},{1,3},{3,1},{5,7},{7,5},{8,10},{10,8},{12,... | collective-permute-start | bytes 786440 | tf_op jit(solution)/shard_map/ppermute | solution.py:28
  19.6 1.2 %collective-permute-start.13 = (bf16[1024,128]{1,0:T(8,128)(2,1)S(1)}, bf16[1024,128]{1,0:T(8,128)(2,1)S(1)}, u32[]{:S(2)}, u32[]{:S(2)}) collective-permute-start(bf16[1024,128]{1,0:T(8,128)(2,1)S(1)} %copy-done), channel_id=1, source_target_pairs={{0,16},{8,24},{16,0},{24,8},{1,17},{9,25},{17,1},{25,9},{2,18},{10... | collective-permute-start | bytes 786440 | tf_op jit(solution)/shard_map/ppermute | solution.py:28
  22.7 1.2 %collective-permute-start.15 = (bf16[1024,128]{1,0:T(8,128)(2,1)S(1)}, bf16[1024,128]{1,0:T(8,128)(2,1)S(1)}, u32[]{:S(2)}, u32[]{:S(2)}) collective-permute-start(bf16[1024,128]{1,0:T(8,128)(2,1)S(1)} %copy-done.1), channel_id=1, source_target_pairs={{0,16},{8,24},{16,0},{24,8},{1,17},{9,25},{17,1},{25,9},{2,18},{10... | collective-permute-start | bytes 786440 | tf_op jit(solution)/shard_map/ppermute | solution.py:28
  24.0 2.1 %collective-permute-done.8.refs_6_ = bf16[128,1024]{1,0:T(8,128)(2,1)S(1)} collective-permute-done((bf16[128,1024]{1,0:T(8,128)(2,1)S(1)}, bf16[128,1024]{1,0:T(8,128)(2,1)S(1)}, u32[]{:S(2)}, u32[]{:S(2)}) %collective-permute-start.8) | collective-permute-done | bytes 262176 | tf_op jit(solution)/shard_map/ppermute | solution.py:28
  26.1 1.3 %hidden_terms.1 = (f32[512,128]{1,0:T(8,128)S(1)}, bf16[512,128]{1,0:T(8,128)(2,1)S(1)}, bf16[512,128]{1,0:T(8,128)(2,1)S(1)}, bf16[512,128]{1,0:T(8,128)(2,1)S(...) custom-call(s32[3]{0:T(128)S(1)} %pad_add_fusion.refs_0_, ...), custom_call_target="tpu_custom_call" | custom-call | flops 536870912 | bytes 4325388 | tf_op jit(solution)/shard_map/hidden_terms/pallas_call | solution.py:134
  27.5 1.4 %collective-permute-start.9 = (bf16[512,128]{1,0:T(8,128)(2,1)S(1)}, bf16[512,128]{1,0:T(8,128)(2,1)S(1)}, u32[]{:S(2)}, u32[]{:S(2)}) collective-permute-start(bf16[512,128]{1,0:T(8,128)(2,1)S(1)} %get-tuple-element.77), channel_id=1, source_target_pairs={{0,2},{2,0},{4,6},{6,4},{1,3},{3,1},{5,7},{7,5},{8,10},{10,8},{12,... | collective-permute-start | bytes 393224 | tf_op jit(solution)/shard_map/ppermute | solution.py:28
  30.2 3.5 %collective-permute-done.12.refs_2_.refs_6_.refs_8_ = bf16[1024,128]{1,0:T(8,128)(2,1)S(1)} collective-permute-done((bf16[1024,128]{1,0:T(8,128)(2,1)S(1)}, bf16[1024,128]{1,0:T(8,128)(2,1)S(1)}, u32[]{:S(2)}, u32[]{:S(2)}) %collective-permute-start.12) | collective-permute-done | bytes 262176 | tf_op jit(solution)/shard_map/ppermute | solution.py:28
  33.7 1.5 %collective-permute-start.19 = (bf16[1024,128]{1,0:T(8,128)(2,1)S(1)}, bf16[1024,128]{1,0:T(8,128)(2,1)S(1)}, u32[]{:S(2)}, u32[]{:S(2)}) collective-permute-start(bf16[1024,128]{1,0:T(8,128)(2,1)S(1)} %collective-permute-done.12.refs_2_.refs_6_.refs_8_), channel_id=1, source_target_pairs={{0,16},{8,24},{16,0},{24,8},{1,17},{9,25},{17,1},{25,9},{2,18},{10... | collective-permute-start | bytes 786440 | tf_op jit(solution)/shard_map/ppermute | solution.py:28
  36.4 1.5 %mlp_forward.1 = (bf16[128,4096]{1,0:T(8,128)(2,1)S(1)}, f32[128,128]{1,0:T(8,128)S(1)}, f32[128,256]{1,0:T(8,128)S(1)}, bf16[128,1024]{1,0:T(8,128)(2,1)S(1)}) custom-call(s32[3]{0:T(128)S(1)} %pad_add_fusion.refs_0_, bf16[1024,128]{1,0:T(8,128)(2,1)S(1)} %copy-done, bf16[1024,128]{1,0:T(8,128)(2,1)S(1)} %collective-permute-done.12.refs_2_.refs_6_.refs_8_, ...), custom_call_target="tpu_custom_call" | custom-call | flops 268435456 | bytes 4136972 | tf_op jit(solution)/shard_map/mlp_forward/pallas_call | solution.py:134
  37.9 3.2 %collective-permute-done.11.refs_4_ = bf16[512,128]{1,0:T(8,128)(2,1)S(1)} collective-permute-done((bf16[512,128]{1,0:T(8,128)(2,1)S(1)}, bf16[512,128]{1,0:T(8,128)(2,1)S(1)}, u32[]{:S(2)}, u32[]{:S(2)}) %collective-permute-start.11) | collective-permute-done | bytes 131104 | tf_op jit(solution)/shard_map/ppermute | solution.py:28
  41.7 1.3 %collective-permute-start.16 = (bf16[128,640]{1,0:T(8,128)(2,1)S(1)}, bf16[128,640]{1,0:T(8,128)(2,1)S(1)}, u32[]{:S(2)}, u32[]{:S(2)}) collective-permute-start(bf16[128,640]{1,0:T(8,128)(2,1)S(1)} %get-tuple-element.97), channel_id=1, source_target_pairs={{0,8},{8,0},{16,24},{24,16},{1,9},{9,1},{17,25},{25,17},{2,10},{10... | collective-permute-start | bytes 491528 | tf_op jit(solution)/shard_map/ppermute | solution.py:28
  43.0 1.2 %collective-permute-start.17 = (bf16[128,640]{1,0:T(8,128)(2,1)S(1)}, bf16[128,640]{1,0:T(8,128)(2,1)S(1)}, u32[]{:S(2)}, u32[]{:S(2)}) collective-permute-start(bf16[128,640]{1,0:T(8,128)(2,1)S(1)} %get-tuple-element.98), channel_id=1, source_target_pairs={{0,16},{8,24},{16,0},{24,8},{1,17},{9,25},{17,1},{25,9},{2,18},{10... | collective-permute-start | bytes 491528 | tf_op jit(solution)/shard_map/ppermute | solution.py:28
  46.0 1.5 %collective-permute-done.17.refs_3_.refs_4_ = bf16[128,640]{1,0:T(8,128)(2,1)S(1)} collective-permute-done((bf16[128,640]{1,0:T(8,128)(2,1)S(1)}, bf16[128,640]{1,0:T(8,128)(2,1)S(1)}, u32[]{:S(2)}, u32[]{:S(2)}) %collective-permute-start.17) | collective-permute-done | bytes 163872 | tf_op jit(solution)/shard_map/ppermute | solution.py:28
  47.5 3.6 %collective-permute-done.18.refs_4_.refs_5_ = bf16[128,640]{1,0:T(8,128)(2,1)S(1)} collective-permute-done((bf16[128,640]{1,0:T(8,128)(2,1)S(1)}, bf16[128,640]{1,0:T(8,128)(2,1)S(1)}, u32[]{:S(2)}, u32[]{:S(2)}) %collective-permute-start.18) | collective-permute-done | bytes 163872 | tf_op jit(solution)/shard_map/ppermute | solution.py:28
  51.1 1.4 %mlp_backward.1 = (bf16[4,128,512]{2,1,0:T(8,128)(2,1)S(1)}, bf16[128,256]{1,0:T(8,128)(2,1)S(1)}, f32[128,128]{1,0:T(8,128)S(1)}) custom-call(s32[3]{0:T(128)S(1)} %pad_add_fusion.refs_0_, f32[128,128]{1,0:T(8,128)S(1)} %get-tuple-element.104.refs_1_, bf16[128,640]{1,0:T(8,128)(2,1)S(1)} %collective-permute-done.16.refs_2_.refs_3_, ...), custom_call_target="tpu_custom_call" | custom-call | flops 134217728 | bytes 4825100 | tf_op jit(solution)/shard_map/mlp_backward/pallas_call | solution.py:134
  52.5 3.4 %collective-permute-start.21 = (bf16[4,128,512]{2,1,0:T(8,128)(2,1)S(1)}, bf16[4,128,512]{2,1,0:T(8,128)(2,1)S(1)}, u32[]{:S(2)}, u32[]{:S(2)}) collective-permute-start(bf16[4,128,512]{2,1,0:T(8,128)(2,1)S(1)} %get-tuple-element.115), channel_id=1, source_target_pairs={{0,1},{1,0},{2,3},{3,2},{4,5},{5,4},{6,7},{7,6},{8,9},{9,8},{10,11... | collective-permute-start | bytes 1572872 | tf_op jit(solution)/shard_map/ppermute | solution.py:28
  57.7 1.7 %collective-permute-start.25 = (bf16[128,512]{1,0:T(8,128)(2,1)S(1)}, bf16[128,512]{1,0:T(8,128)(2,1)S(1)}, u32[]{:S(2)}, u32[]{:S(2)}) collective-permute-start(bf16[128,512]{1,0:T(8,128)(2,1)S(1)} %get-tuple-element.129), channel_id=1, source_target_pairs={{0,6},{2,4},{4,2},{6,0},{1,7},{3,5},{5,3},{7,1},{8,14},{10,12},{12... | collective-permute-start | bytes 393224 | tf_op jit(solution)/shard_map/ppermute | solution.py:28
  59.4 1.3 %collective-permute-start.23 = (bf16[128,512]{1,0:T(8,128)(2,1)S(1)}, bf16[128,512]{1,0:T(8,128)(2,1)S(1)}, u32[]{:S(2)}, u32[]{:S(2)}) collective-permute-start(bf16[128,512]{1,0:T(8,128)(2,1)S(1)} %get-tuple-element.128), channel_id=1, source_target_pairs={{0,2},{2,0},{4,6},{6,4},{1,3},{3,1},{5,7},{7,5},{8,10},{10,8},{12,... | collective-permute-start | bytes 393224 | tf_op jit(solution)/shard_map/ppermute | solution.py:28
  61.2 5.9 %collective-permute-done.25 = bf16[128,512]{1,0:T(8,128)(2,1)S(1)} collective-permute-done((bf16[128,512]{1,0:T(8,128)(2,1)S(1)}, bf16[128,512]{1,0:T(8,128)(2,1)S(1)}, u32[]{:S(2)}, u32[]{:S(2)}) %collective-permute-start.25) | collective-permute-done | bytes 131104 | tf_op jit(solution)/shard_map/ppermute | solution.py:28
  67.1 3.0 %collective-permute-done.24 = bf16[128,512]{1,0:T(8,128)(2,1)S(1)} collective-permute-done((bf16[128,512]{1,0:T(8,128)(2,1)S(1)}, bf16[128,512]{1,0:T(8,128)(2,1)S(1)}, u32[]{:S(2)}, u32[]{:S(2)}) %collective-permute-start.24) | collective-permute-done | bytes 131104 | tf_op jit(solution)/shard_map/ppermute | solution.py:28
  71.2 2.1 %collective-permute-start.27 = (bf16[128,512]{1,0:T(8,128)(2,1)S(1)}, bf16[128,512]{1,0:T(8,128)(2,1)S(1)}, u32[]{:S(2)}, u32[]{:S(2)}) collective-permute-start(bf16[128,512]{1,0:T(8,128)(2,1)S(1)} %fusion.2.refs_1_), channel_id=1, source_target_pairs={{0,2},{2,0},{4,6},{6,4},{1,3},{3,1},{5,7},{7,5},{8,10},{10,8},{12,... | collective-permute-start | bytes 393224 | tf_op jit(solution)/shard_map/ppermute | solution.py:28
  75.3 3.4 %collective-permute-done.27.refs_2_ = bf16[128,512]{1,0:T(8,128)(2,1)S(1)} collective-permute-done((bf16[128,512]{1,0:T(8,128)(2,1)S(1)}, bf16[128,512]{1,0:T(8,128)(2,1)S(1)}, u32[]{:S(2)}, u32[]{:S(2)}) %collective-permute-start.27) | collective-permute-done | bytes 131104 | tf_op jit(solution)/shard_map/ppermute | solution.py:28
  79.5 1.3 %kv_grad.1 = bf16[1024,512]{1,0:T(8,128)(2,1)S(1)} custom-call(s32[3]{0:T(128)S(1)} %pad_add_fusion.refs_0_, bf16[128,512]{1,0:T(8,128)(2,1)S(1)} %bitcast.31, bf16[128,512]{1,0:T(8,128)(2,1)S(1)} %collective-permute-done.refs_2_, bf16[128,512]{1,0:T(8,128)(2,1)S(1)} %collective-permute-done.1.refs_3_, bf16[128,512]{1,0:T(8,128)(2,1)S(1)} %collective-permute-done.2.refs_4_, ...), custom_call_target="tpu_custom_call" | custom-call | flops 536870912 | bytes 2621452 | tf_op jit(solution)/shard_map/kv_grad/pallas_call | solution.py:134
  82.6 4.1 %collective-permute-done.29.refs_4_ = bf16[128,512]{1,0:T(8,128)(2,1)S(1)} collective-permute-done((bf16[128,512]{1,0:T(8,128)(2,1)S(1)}, bf16[128,512]{1,0:T(8,128)(2,1)S(1)}, u32[]{:S(2)}, u32[]{:S(2)}) %collective-permute-start.29) | collective-permute-done | bytes 131104 | tf_op jit(solution)/shard_map/ppermute | solution.py:28
  88.9 1.6 %input_grad.1 = bf16[128,4096]{1,0:T(8,128)(2,1)} custom-call(s32[3]{0:T(128)S(1)} %pad_add_fusion.refs_0_, bf16[128,512]{1,0:T(8,128)(2,1)S(1)} %fusion.2.refs_1_, bf16[128,512]{1,0:T(8,128)(2,1)S(1)} %collective-permute-done.27.refs_2_, bf16[128,512]{1,0:T(8,128)(2,1)S(1)} %collective-permute-done.28.refs_3_, ...), custom_call_target="tpu_custom_call" | custom-call | bytes 2097164 | tf_op jit(solution)/shard_map/input_grad/pallas_call | solution.py:134
  (71 shorter events, 21.2 us)
Async XLA Ops:
  0.6 11.7 %collective-permute-start.4 = (bf16[128,1024]{1,0:T(8,128)(2,1)}, bf16[128,1024]{1,0:T(8,128)(2,1)S(1)}, u32[]{:S(2)}, u32[]{:S(2)}) collective-permute-start(bf16[128,1024]{1,0:T(8,128)(2,1)} %refs_3_.1), channel_id=1, source_target_pairs={{0,2},{2,0},{4,6},{6,4},{1,3},{3,1},{5,7},{7,5},{8,10},{10,8},{12,... | collective-permute-start | bytes 786440 | tf_op jit(solution)/shard_map/ppermute | solution.py:28
  0.7 14.0 %collective-permute-start.3 = (bf16[128,1024]{1,0:T(8,128)(2,1)}, bf16[128,1024]{1,0:T(8,128)(2,1)S(1)}, u32[]{:S(2)}, u32[]{:S(2)}) collective-permute-start(bf16[128,1024]{1,0:T(8,128)(2,1)} %refs_3_.1), channel_id=1, source_target_pairs={{0,4},{2,6},{4,0},{6,2},{1,5},{3,7},{5,1},{7,3},{8,12},{10,14},{12... | collective-permute-start | bytes 786440 | tf_op jit(solution)/shard_map/ppermute | solution.py:28
  4.1 4.3 %collective-permute-start = (bf16[128,512]{1,0:T(8,128)(2,1)S(1)}, bf16[128,512]{1,0:T(8,128)(2,1)S(1)}, u32[]{:S(2)}, u32[]{:S(2)}) collective-permute-start(bf16[128,512]{1,0:T(8,128)(2,1)S(1)} %bitcast.27), channel_id=1, source_target_pairs={{0,8},{8,0},{16,24},{24,16},{1,9},{9,1},{17,25},{25,17},{2,10},{10... | collective-permute-start | bytes 393224 | tf_op jit(solution)/shard_map/ppermute | solution.py:28
  5.4 4.1 %collective-permute-start.1 = (bf16[128,512]{1,0:T(8,128)(2,1)S(1)}, bf16[128,512]{1,0:T(8,128)(2,1)S(1)}, u32[]{:S(2)}, u32[]{:S(2)}) collective-permute-start(bf16[128,512]{1,0:T(8,128)(2,1)S(1)} %bitcast.28), channel_id=1, source_target_pairs={{0,16},{8,24},{16,0},{24,8},{1,17},{9,25},{17,1},{25,9},{2,18},{10... | collective-permute-start | bytes 393224 | tf_op jit(solution)/shard_map/ppermute | solution.py:28
  6.6 5.7 %collective-permute-start.2 = (bf16[128,512]{1,0:T(8,128)(2,1)S(1)}, bf16[128,512]{1,0:T(8,128)(2,1)S(1)}, u32[]{:S(2)}, u32[]{:S(2)}) collective-permute-start(bf16[128,512]{1,0:T(8,128)(2,1)S(1)} %bitcast.29), channel_id=1, source_target_pairs={{0,24},{8,16},{16,8},{24,0},{1,25},{9,17},{17,9},{25,1},{2,26},{10... | collective-permute-start | bytes 393224 | tf_op jit(solution)/shard_map/ppermute | solution.py:28
  16.1 6.7 %collective-permute-start.5 = (bf16[512,1024]{1,0:T(8,128)(2,1)S(1)}, bf16[512,1024]{1,0:T(8,128)(2,1)S(1)}, u32[]{:S(2)}, u32[]{:S(2)}) collective-permute-start(bf16[512,1024]{1,0:T(8,128)(2,1)S(1)} %upstream_terms.1.refs_1_), channel_id=1, source_target_pairs={{0,1},{1,0},{2,3},{3,2},{4,5},{5,4},{6,7},{7,6},{8,9},{9,8},{10,11... | collective-permute-start | bytes 3145736 | tf_op jit(solution)/shard_map/ppermute | solution.py:28
  17.8 4.2 %collective-permute-start.7 = (bf16[128,2048]{1,0:T(8,128)(2,1)S(1)}, bf16[128,2048]{1,0:T(8,128)(2,1)S(1)}, u32[]{:S(2)}, u32[]{:S(2)}) collective-permute-start(bf16[128,2048]{1,0:T(8,128)(2,1)S(1)} %copy-done.2), channel_id=1, source_target_pairs={{0,1},{1,0},{2,3},{3,2},{4,5},{5,4},{6,7},{7,6},{8,9},{9,8},{10,11... | collective-permute-start | bytes 1572872 | tf_op jit(solution)/shard_map/ppermute | solution.py:28
  18.3 7.9 %collective-permute-start.8 = (bf16[128,1024]{1,0:T(8,128)(2,1)S(1)}, bf16[128,1024]{1,0:T(8,128)(2,1)S(1)}, u32[]{:S(2)}, u32[]{:S(2)}) collective-permute-start(bf16[128,1024]{1,0:T(8,128)(2,1)S(1)} %collective-permute-done.3.refs_5_), channel_id=1, source_target_pairs={{0,2},{2,0},{4,6},{6,4},{1,3},{3,1},{5,7},{7,5},{8,10},{10,8},{12,... | collective-permute-start | bytes 786440 | tf_op jit(solution)/shard_map/ppermute | solution.py:28
  19.6 9.3 %collective-permute-start.13 = (bf16[1024,128]{1,0:T(8,128)(2,1)S(1)}, bf16[1024,128]{1,0:T(8,128)(2,1)S(1)}, u32[]{:S(2)}, u32[]{:S(2)}) collective-permute-start(bf16[1024,128]{1,0:T(8,128)(2,1)S(1)} %copy-done), channel_id=1, source_target_pairs={{0,16},{8,24},{16,0},{24,8},{1,17},{9,25},{17,1},{25,9},{2,18},{10... | collective-permute-start | bytes 786440 | tf_op jit(solution)/shard_map/ppermute | solution.py:28
  20.8 9.2 %collective-permute-start.14 = (bf16[1024,128]{1,0:T(8,128)(2,1)S(1)}, bf16[1024,128]{1,0:T(8,128)(2,1)S(1)}, u32[]{:S(2)}, u32[]{:S(2)}) collective-permute-start(bf16[1024,128]{1,0:T(8,128)(2,1)S(1)} %copy-done.1), channel_id=1, source_target_pairs={{0,8},{8,0},{16,24},{24,16},{1,9},{9,1},{17,25},{25,17},{2,10},{10... | collective-permute-start | bytes 786440 | tf_op jit(solution)/shard_map/ppermute | solution.py:28
  22.1 11.6 %collective-permute-start.12 = (bf16[1024,128]{1,0:T(8,128)(2,1)S(1)}, bf16[1024,128]{1,0:T(8,128)(2,1)S(1)}, u32[]{:S(2)}, u32[]{:S(2)}) collective-permute-start(bf16[1024,128]{1,0:T(8,128)(2,1)S(1)} %copy-done), channel_id=1, source_target_pairs={{0,8},{8,0},{16,24},{24,16},{1,9},{9,1},{17,25},{25,17},{2,10},{10... | collective-permute-start | bytes 786440 | tf_op jit(solution)/shard_map/ppermute | solution.py:28
  22.7 12.4 %collective-permute-start.15 = (bf16[1024,128]{1,0:T(8,128)(2,1)S(1)}, bf16[1024,128]{1,0:T(8,128)(2,1)S(1)}, u32[]{:S(2)}, u32[]{:S(2)}) collective-permute-start(bf16[1024,128]{1,0:T(8,128)(2,1)S(1)} %copy-done.1), channel_id=1, source_target_pairs={{0,16},{8,24},{16,0},{24,8},{1,17},{9,25},{17,1},{25,9},{2,18},{10... | collective-permute-start | bytes 786440 | tf_op jit(solution)/shard_map/ppermute | solution.py:28
  27.5 10.4 %collective-permute-start.9 = (bf16[512,128]{1,0:T(8,128)(2,1)S(1)}, bf16[512,128]{1,0:T(8,128)(2,1)S(1)}, u32[]{:S(2)}, u32[]{:S(2)}) collective-permute-start(bf16[512,128]{1,0:T(8,128)(2,1)S(1)} %get-tuple-element.77), channel_id=1, source_target_pairs={{0,2},{2,0},{4,6},{6,4},{1,3},{3,1},{5,7},{7,5},{8,10},{10,8},{12,... | collective-permute-start | bytes 393224 | tf_op jit(solution)/shard_map/ppermute | solution.py:28
  28.8 9.1 %collective-permute-start.10 = (bf16[512,128]{1,0:T(8,128)(2,1)S(1)}, bf16[512,128]{1,0:T(8,128)(2,1)S(1)}, u32[]{:S(2)}, u32[]{:S(2)}) collective-permute-start(bf16[512,128]{1,0:T(8,128)(2,1)S(1)} %get-tuple-element.78), channel_id=1, source_target_pairs={{0,4},{2,6},{4,0},{6,2},{1,5},{3,7},{5,1},{7,3},{8,12},{10,14},{12... | collective-permute-start | bytes 393224 | tf_op jit(solution)/shard_map/ppermute | solution.py:28
  30.0 11.1 %collective-permute-start.11 = (bf16[512,128]{1,0:T(8,128)(2,1)S(1)}, bf16[512,128]{1,0:T(8,128)(2,1)S(1)}, u32[]{:S(2)}, u32[]{:S(2)}) collective-permute-start(bf16[512,128]{1,0:T(8,128)(2,1)S(1)} %get-tuple-element.79), channel_id=1, source_target_pairs={{0,6},{2,4},{4,2},{6,0},{1,7},{3,5},{5,3},{7,1},{8,14},{10,12},{12... | collective-permute-start | bytes 393224 | tf_op jit(solution)/shard_map/ppermute | solution.py:28
  33.7 17.4 %collective-permute-start.19 = (bf16[1024,128]{1,0:T(8,128)(2,1)S(1)}, bf16[1024,128]{1,0:T(8,128)(2,1)S(1)}, u32[]{:S(2)}, u32[]{:S(2)}) collective-permute-start(bf16[1024,128]{1,0:T(8,128)(2,1)S(1)} %collective-permute-done.12.refs_2_.refs_6_.refs_8_), channel_id=1, source_target_pairs={{0,16},{8,24},{16,0},{24,8},{1,17},{9,25},{17,1},{25,9},{2,18},{10... | collective-permute-start | bytes 786440 | tf_op jit(solution)/shard_map/ppermute | solution.py:28
  35.2 15.9 %collective-permute-start.20 = (bf16[1024,128]{1,0:T(8,128)(2,1)S(1)}, bf16[1024,128]{1,0:T(8,128)(2,1)S(1)}, u32[]{:S(2)}, u32[]{:S(2)}) collective-permute-start(bf16[1024,128]{1,0:T(8,128)(2,1)S(1)} %collective-permute-done.15.refs_6_.refs_11_.refs_13_), channel_id=1, source_target_pairs={{0,8},{8,0},{16,24},{24,16},{1,9},{9,1},{17,25},{25,17},{2,10},{10... | collective-permute-start | bytes 786440 | tf_op jit(solution)/shard_map/ppermute | solution.py:28
  41.7 4.2 %collective-permute-start.16 = (bf16[128,640]{1,0:T(8,128)(2,1)S(1)}, bf16[128,640]{1,0:T(8,128)(2,1)S(1)}, u32[]{:S(2)}, u32[]{:S(2)}) collective-permute-start(bf16[128,640]{1,0:T(8,128)(2,1)S(1)} %get-tuple-element.97), channel_id=1, source_target_pairs={{0,8},{8,0},{16,24},{24,16},{1,9},{9,1},{17,25},{25,17},{2,10},{10... | collective-permute-start | bytes 491528 | tf_op jit(solution)/shard_map/ppermute | solution.py:28
  43.0 4.5 %collective-permute-start.17 = (bf16[128,640]{1,0:T(8,128)(2,1)S(1)}, bf16[128,640]{1,0:T(8,128)(2,1)S(1)}, u32[]{:S(2)}, u32[]{:S(2)}) collective-permute-start(bf16[128,640]{1,0:T(8,128)(2,1)S(1)} %get-tuple-element.98), channel_id=1, source_target_pairs={{0,16},{8,24},{16,0},{24,8},{1,17},{9,25},{17,1},{25,9},{2,18},{10... | collective-permute-start | bytes 491528 | tf_op jit(solution)/shard_map/ppermute | solution.py:28
  44.3 6.8 %collective-permute-start.18 = (bf16[128,640]{1,0:T(8,128)(2,1)S(1)}, bf16[128,640]{1,0:T(8,128)(2,1)S(1)}, u32[]{:S(2)}, u32[]{:S(2)}) collective-permute-start(bf16[128,640]{1,0:T(8,128)(2,1)S(1)} %get-tuple-element.99), channel_id=1, source_target_pairs={{0,24},{8,16},{16,8},{24,0},{1,25},{9,17},{17,9},{25,1},{2,26},{10... | collective-permute-start | bytes 491528 | tf_op jit(solution)/shard_map/ppermute | solution.py:28
  51.1 5.9 %collective-permute-start.22 = (bf16[256,512]{1,0:T(8,128)(2,1)S(1)}, bf16[256,512]{1,0:T(8,128)(2,1)S(1)}, u32[]{:S(2)}, u32[]{:S(2)}) collective-permute-start(bf16[256,512]{1,0:T(8,128)(2,1)S(1)} %get-tuple-element.117), channel_id=1, source_target_pairs={{0,8},{8,0},{16,24},{24,16},{1,9},{9,1},{17,25},{25,17},{2,10},{10... | collective-permute-start | bytes 786440 | tf_op jit(solution)/shard_map/ppermute | solution.py:28
  52.5 4.9 %collective-permute-start.21 = (bf16[4,128,512]{2,1,0:T(8,128)(2,1)S(1)}, bf16[4,128,512]{2,1,0:T(8,128)(2,1)S(1)}, u32[]{:S(2)}, u32[]{:S(2)}) collective-permute-start(bf16[4,128,512]{2,1,0:T(8,128)(2,1)S(1)} %get-tuple-element.115), channel_id=1, source_target_pairs={{0,1},{1,0},{2,3},{3,2},{4,5},{5,4},{6,7},{7,6},{8,9},{9,8},{10,11... | collective-permute-start | bytes 1572872 | tf_op jit(solution)/shard_map/ppermute | solution.py:28
  57.7 9.4 %collective-permute-start.25 = (bf16[128,512]{1,0:T(8,128)(2,1)S(1)}, bf16[128,512]{1,0:T(8,128)(2,1)S(1)}, u32[]{:S(2)}, u32[]{:S(2)}) collective-permute-start(bf16[128,512]{1,0:T(8,128)(2,1)S(1)} %get-tuple-element.129), channel_id=1, source_target_pairs={{0,6},{2,4},{4,2},{6,0},{1,7},{3,5},{5,3},{7,1},{8,14},{10,12},{12... | collective-permute-start | bytes 393224 | tf_op jit(solution)/shard_map/ppermute | solution.py:28
  59.4 10.6 %collective-permute-start.24 = (bf16[128,512]{1,0:T(8,128)(2,1)S(1)}, bf16[128,512]{1,0:T(8,128)(2,1)S(1)}, u32[]{:S(2)}, u32[]{:S(2)}) collective-permute-start(bf16[128,512]{1,0:T(8,128)(2,1)S(1)} %get-tuple-element.130), channel_id=1, source_target_pairs={{0,4},{2,6},{4,0},{6,2},{1,5},{3,7},{5,1},{7,3},{8,12},{10,14},{12... | collective-permute-start | bytes 393224 | tf_op jit(solution)/shard_map/ppermute | solution.py:28
  59.4 10.6 %collective-permute-start.23 = (bf16[128,512]{1,0:T(8,128)(2,1)S(1)}, bf16[128,512]{1,0:T(8,128)(2,1)S(1)}, u32[]{:S(2)}, u32[]{:S(2)}) collective-permute-start(bf16[128,512]{1,0:T(8,128)(2,1)S(1)} %get-tuple-element.128), channel_id=1, source_target_pairs={{0,2},{2,0},{4,6},{6,4},{1,3},{3,1},{5,7},{7,5},{8,10},{10,8},{12,... | collective-permute-start | bytes 393224 | tf_op jit(solution)/shard_map/ppermute | solution.py:28
  60.7 9.5 %collective-permute-start.26 = (bf16[256,512]{1,0:T(8,128)(2,1)S(1)}, bf16[256,512]{1,0:T(8,128)(2,1)S(1)}, u32[]{:S(2)}, u32[]{:S(2)}) collective-permute-start(bf16[256,512]{1,0:T(8,128)(2,1)S(1)} %pad_maximum_fusion.1), channel_id=1, source_target_pairs={{0,16},{8,24},{16,0},{24,8},{1,17},{9,25},{17,1},{25,9},{2,18},{10... | collective-permute-start | bytes 786440 | tf_op jit(solution)/shard_map/ppermute | solution.py:28
  70.2 9.4 %collective-permute-start.30 = (bf16[512,512]{1,0:T(8,128)(2,1)S(1)}, bf16[512,512]{1,0:T(8,128)(2,1)S(1)}, u32[]{:S(2)}, u32[]{:S(2)}) collective-permute-start(bf16[512,512]{1,0:T(8,128)(2,1)S(1)} %pad_maximum_fusion.refs_5_), channel_id=1, source_target_pairs={{0,1},{1,0},{2,3},{3,2},{4,5},{5,4},{6,7},{7,6},{8,9},{9,8},{10,11... | collective-permute-start | bytes 1572872 | tf_op jit(solution)/shard_map/ppermute | solution.py:28
  71.2 7.4 %collective-permute-start.27 = (bf16[128,512]{1,0:T(8,128)(2,1)S(1)}, bf16[128,512]{1,0:T(8,128)(2,1)S(1)}, u32[]{:S(2)}, u32[]{:S(2)}) collective-permute-start(bf16[128,512]{1,0:T(8,128)(2,1)S(1)} %fusion.2.refs_1_), channel_id=1, source_target_pairs={{0,2},{2,0},{4,6},{6,4},{1,3},{3,1},{5,7},{7,5},{8,10},{10,8},{12,... | collective-permute-start | bytes 393224 | tf_op jit(solution)/shard_map/ppermute | solution.py:28
  73.4 9.3 %collective-permute-start.28 = (bf16[128,512]{1,0:T(8,128)(2,1)S(1)}, bf16[128,512]{1,0:T(8,128)(2,1)S(1)}, u32[]{:S(2)}, u32[]{:S(2)}) collective-permute-start(bf16[128,512]{1,0:T(8,128)(2,1)S(1)} %fusion.2.refs_1_), channel_id=1, source_target_pairs={{0,4},{2,6},{4,0},{6,2},{1,5},{3,7},{5,1},{7,3},{8,12},{10,14},{12... | collective-permute-start | bytes 393224 | tf_op jit(solution)/shard_map/ppermute | solution.py:28
  74.3 12.4 %collective-permute-start.29 = (bf16[128,512]{1,0:T(8,128)(2,1)S(1)}, bf16[128,512]{1,0:T(8,128)(2,1)S(1)}, u32[]{:S(2)}, u32[]{:S(2)}) collective-permute-start(bf16[128,512]{1,0:T(8,128)(2,1)S(1)} %fusion.2.refs_1_), channel_id=1, source_target_pairs={{0,6},{2,4},{4,2},{6,0},{1,7},{3,5},{5,3},{7,1},{8,14},{10,12},{12... | collective-permute-start | bytes 393224 | tf_op jit(solution)/shard_map/ppermute | solution.py:28
  74.6 12.9 %collective-permute-start.31 = (bf16[128,512]{1,0:T(8,128)(2,1)S(1)}, bf16[128,512]{1,0:T(8,128)(2,1)S(1)}, u32[]{:S(2)}, u32[]{:S(2)}) collective-permute-start(bf16[128,512]{1,0:T(8,128)(2,1)S(1)} %fusion.2.refs_1_), channel_id=1, source_target_pairs={{0,1},{1,0},{2,3},{3,2},{4,5},{5,4},{6,7},{7,6},{8,9},{9,8},{10,11... | collective-permute-start | bytes 393224 | tf_op jit(solution)/shard_map/ppermute | solution.py:28
  78.7 8.9 %collective-permute-start.32 = (bf16[128,512]{1,0:T(8,128)(2,1)S(1)}, bf16[128,512]{1,0:T(8,128)(2,1)S(1)}, u32[]{:S(2)}, u32[]{:S(2)}) collective-permute-start(bf16[128,512]{1,0:T(8,128)(2,1)S(1)} %collective-permute-done.27.refs_2_), channel_id=1, source_target_pairs={{0,1},{1,0},{2,3},{3,2},{4,5},{5,4},{6,7},{7,6},{8,9},{9,8},{10,11... | collective-permute-start | bytes 393224 | tf_op jit(solution)/shard_map/ppermute | solution.py:28
  (9 other events, 38.7 us)

commit v7 on v6

--- a/solution.py
+++ b/solution.py
@@ -155,8 +155,8 @@
     out[...] = dot_nt(grads[...], section[...]).astype(out.dtype)
 
 
-def hidden_kernel(n_dp, n_pipe, n_ten, where, mine, other, *refs):
-    downs, hidden, outs = refs[:n_pipe], refs[n_pipe : 2 * n_pipe], refs[2 * n_pipe : 2 * n_pipe + n_dp]
+def hidden_kernel(n_parts, n_ten, where, mine, other, *refs):
+    downs, hidden, outs = refs[:n_parts], refs[n_parts : 2 * n_parts], refs[2 * n_parts : -2]
     upstream, down = refs[-2:]
     upstream[...] = (mine[...].astype(F32) + other[...].astype(F32)).astype(BF16)
     units = downs[0].shape[0]
@@ -165,8 +165,8 @@
     result = dot_nt(upstream[...], down[...])
     for k, out in enumerate(hidden):
         out[...] = result[:, k * units : (k + 1) * units].astype(out.dtype)
-    tok, half = outs[0].shape
     for k, out in enumerate(outs):
+        tok, half = out.shape
         out[...] = upstream[k * tok : (k + 1) * tok, aligned(where[2] * half, half)]
 
 
@@ -328,9 +328,8 @@
     x_other = send(mlp_input, TENSOR, 1)
     far, near = send(down_weight, PIPE, 2), send(down_weight, PIPE, 1)
     grads, gate, up = lax.optimization_barrier((grads, gate_weight, up_weight))
-    near, first_gate, first_up = lax.optimization_barrier((near, gate_weight, up_weight))
-    gates = [gate, send(first_gate, DP, 1), send(gate, DP, 2)]
-    ups = [up, send(up, DP, 1), send(first_up, DP, 2)]
+    gates = [gate, send(gate, DP, 1), send(gate, DP, 2)]
+    ups = [up, send(up, DP, 1), send(up, DP, 2)]
     grads, far, near = lax.optimization_barrier((grads, far, near))
     downs = [down_weight, near, far, send(far, PIPE, 1)]
 
@@ -349,15 +348,24 @@
     other, x_other, enc_other = lax.optimization_barrier((other, x_other, enc_other))
     group = n_pipe * units
     outs = call(
-        lambda *refs: hidden_kernel(n_dp, n_pipe, n_ten, *refs),
+        lambda *refs: hidden_kernel(n_pipe - 1, n_ten, *refs),
         "hidden_terms",
         [shaped((n_dp * tok, units), F32)]
-        + [shaped((n_dp * tok, units), BF16)] * (n_pipe - 1)
+        + [shaped((n_dp * tok, units), BF16)] * (n_pipe - 2)
         + [shaped((tok, half), BF16)] * n_dp,
-        [where, mine, other, *downs],
-        [pltpu.VMEM((n_dp * tok, cols), BF16), pltpu.VMEM((group, cols), BF16)],
+        [where, mine, other, *downs[:-1]],
+        [pltpu.VMEM((n_dp * tok, cols), BF16), pltpu.VMEM((group - units, cols), BF16)],
         flops=2 * n_dp * tok * cols * group,
     )
+    (last_out,) = call(
+        lambda *refs: hidden_kernel(1, n_ten, *refs),
+        "hidden_last",
+        [shaped((n_dp * tok, units), BF16)],
+        [where, mine, other, downs[-1]],
+        [pltpu.VMEM((n_dp * tok, cols), BF16), pltpu.VMEM((units, cols), BF16)],
+        flops=2 * n_dp * tok * cols * units,
+    )
+    outs = [*outs[: n_pipe - 1], last_out, *outs[n_pipe - 1 :]]
     terms = [send(out, PIPE, k) for k, out in enumerate(outs[:n_pipe])]
     gain_row = norm_gain.reshape(1, width)
     resid, scale, pre, last = call(

time: 90.7 us -> 90.3 us (level)
  starting transfers between devices: 35 us -> 33.1 us
  Pallas kernels: 10.7 us -> 11.7 us
    ppermute x35, starting transfers between devices: 35 us -> 33.1 us  [send(): return lax.ppermute(value, axis, [(src, src ^ step) for src in range(size)])]
    pallas_call x9 -> x10, Pallas kernels: 10.7 us -> 11.7 us  [call(): pl.pallas_call(body, name=name, out_shape=out, in_specs=specs, out_specs=...]
  transfers between devices with their start and end apart: 35 -> 35, of which waited for: 17 -> 20; matrix products, arithmetic and copies ran while one was open for 4% -> 4% of each run, Pallas kernels for 9% -> 10%
where the time goes in v7:
time: 90.3 us; the launch traced here: 90.2 us
  waiting for transfers between devices  40.5 us (45%)
  starting transfers between devices  33.1 us (37%)
  Pallas kernels  11.7 us (13%)
  local copies, waits for them, and re-layouts  3.56 us (4%)
    ppermute x35, waiting for transfers between devices, send(): return lax.ppermute(value, axis, [(src, src ^ step) for src in range(size)])  40.5 us
    ppermute x35, starting transfers between devices, send(): return lax.ppermute(value, axis, [(src, src ^ step) for src in range(size)])  33.1 us
    pallas_call x10, Pallas kernels, call(): pl.pallas_call(body, name=name, out_shape=out, in_specs=specs, out_specs=...  11.7 us
    unnamed x14, local copies, waits for them, and re-layouts  2.39 us
  transfers between devices with their start and end apart: 35, of which 20 were waited for; matrix products, arithmetic and copies ran while one was open for 4% of the time, Pallas kernels for 10%

profile of v7, /device:TPU:9, one launch (start us, length us, event | category | flops | bytes accessed | tf_op | source)
XLA Modules:
  0.0 90.2 jit_solution(15075472119833494155)
XLA Ops:
  0.6 2.4 %collective-permute-start.3 = (bf16[128,1024]{1,0:T(8,128)(2,1)}, bf16[128,1024]{1,0:T(8,128)(2,1)S(1)}, u32[]{:S(2)}, u32[]{:S(2)}) collective-permute-start(bf16[128,1024]{1,0:T(8,128)(2,1)} %refs_3_.1), channel_id=1, source_target_pairs={{0,4},{2,6},{4,0},{6,2},{1,5},{3,7},{5,1},{7,3},{8,12},{10,14},{12... | collective-permute-start | bytes 786440 | tf_op jit(solution)/shard_map/ppermute | solution.py:28
  4.1 1.3 %collective-permute-start = (bf16[128,512]{1,0:T(8,128)(2,1)S(1)}, bf16[128,512]{1,0:T(8,128)(2,1)S(1)}, u32[]{:S(2)}, u32[]{:S(2)}) collective-permute-start(bf16[128,512]{1,0:T(8,128)(2,1)S(1)} %bitcast.27), channel_id=1, source_target_pairs={{0,8},{8,0},{16,24},{24,16},{1,9},{9,1},{17,25},{25,17},{2,10},{10... | collective-permute-start | bytes 393224 | tf_op jit(solution)/shard_map/ppermute | solution.py:28
  5.4 1.2 %collective-permute-start.1 = (bf16[128,512]{1,0:T(8,128)(2,1)S(1)}, bf16[128,512]{1,0:T(8,128)(2,1)S(1)}, u32[]{:S(2)}, u32[]{:S(2)}) collective-permute-start(bf16[128,512]{1,0:T(8,128)(2,1)S(1)} %bitcast.28), channel_id=1, source_target_pairs={{0,16},{8,24},{16,0},{24,8},{1,17},{9,25},{17,1},{25,9},{2,18},{10... | collective-permute-start | bytes 393224 | tf_op jit(solution)/shard_map/ppermute | solution.py:28
  6.8 1.4 %copy.12 = bf16[128,8,2,256]{3,1,2,0:T(8,128)(2,1)S(1)} copy(bf16[128,8,2,256]{3,2,1,0:T(2,128)(2,1)} %bitcast.32) | data formatting | bytes 2097152
  9.5 2.6 %collective-permute-done.2.refs_4_ = bf16[128,512]{1,0:T(8,128)(2,1)S(1)} collective-permute-done((bf16[128,512]{1,0:T(8,128)(2,1)S(1)}, bf16[128,512]{1,0:T(8,128)(2,1)S(1)}, u32[]{:S(2)}, u32[]{:S(2)}) %collective-permute-start.2) | collective-permute-done | bytes 131104 | tf_op jit(solution)/shard_map/ppermute | solution.py:28
  12.1 2.8 %collective-permute-done.3.refs_5_ = bf16[128,1024]{1,0:T(8,128)(2,1)S(1)} collective-permute-done((bf16[128,1024]{1,0:T(8,128)(2,1)}, bf16[128,1024]{1,0:T(8,128)(2,1)S(1)}, u32[]{:S(2)}, u32[]{:S(2)}) %collective-permute-start.3) | collective-permute-done | bytes 262176 | tf_op jit(solution)/shard_map/ppermute | solution.py:28
  14.9 1.3 %upstream_terms.1.refs_1_ = bf16[512,1024]{1,0:T(8,128)(2,1)S(1)} custom-call(s32[3]{0:T(128)S(1)} %pad_add_fusion.refs_0_, bf16[128,512]{1,0:T(8,128)(2,1)S(1)} %bitcast.30, bf16[128,512]{1,0:T(8,128)(2,1)S(1)} %collective-permute-done.refs_2_, bf16[128,512]{1,0:T(8,128)(2,1)S(1)} %collective-permute-done.1.refs_3_, ...), custom_call_target="tpu_custom_call" | custom-call | flops 536870912 | bytes 2621452 | tf_op jit(solution)/shard_map/upstream_terms/pallas_call | solution.py:134
  16.2 1.5 %collective-permute-start.5 = (bf16[512,1024]{1,0:T(8,128)(2,1)S(1)}, bf16[512,1024]{1,0:T(8,128)(2,1)S(1)}, u32[]{:S(2)}, u32[]{:S(2)}) collective-permute-start(bf16[512,1024]{1,0:T(8,128)(2,1)S(1)} %upstream_terms.1.refs_1_), channel_id=1, source_target_pairs={{0,1},{1,0},{2,3},{3,2},{4,5},{5,4},{6,7},{7,6},{8,9},{9,8},{10,11... | collective-permute-start | bytes 3145736 | tf_op jit(solution)/shard_map/ppermute | solution.py:28
  18.5 1.3 %collective-permute-start.12 = (bf16[1024,128]{1,0:T(8,128)(2,1)S(1)}, bf16[1024,128]{1,0:T(8,128)(2,1)S(1)}, u32[]{:S(2)}, u32[]{:S(2)}) collective-permute-start(bf16[1024,128]{1,0:T(8,128)(2,1)S(1)} %copy-done), channel_id=1, source_target_pairs={{0,8},{8,0},{16,24},{24,16},{1,9},{9,1},{17,25},{25,17},{2,10},{10... | collective-permute-start | bytes 786440 | tf_op jit(solution)/shard_map/ppermute | solution.py:28
  20.7 1.2 %collective-permute-start.13 = (bf16[1024,128]{1,0:T(8,128)(2,1)S(1)}, bf16[1024,128]{1,0:T(8,128)(2,1)S(1)}, u32[]{:S(2)}, u32[]{:S(2)}) collective-permute-start(bf16[1024,128]{1,0:T(8,128)(2,1)S(1)} %copy-done), channel_id=1, source_target_pairs={{0,16},{8,24},{16,0},{24,8},{1,17},{9,25},{17,1},{25,9},{2,18},{10... | collective-permute-start | bytes 786440 | tf_op jit(solution)/shard_map/ppermute | solution.py:28
  23.9 1.3 %hidden_terms.1 = (f32[512,128]{1,0:T(8,128)S(1)}, bf16[512,128]{1,0:T(8,128)(2,1)S(1)}, bf16[512,128]{1,0:T(8,128)(2,1)S(1)}, bf16[128,512]{1,0:T(8,128)(2,1)S(...) custom-call(s32[3]{0:T(128)S(1)} %pad_add_fusion.refs_0_, ...), custom_call_target="tpu_custom_call" | custom-call | flops 536870912 | bytes 3932172 | tf_op jit(solution)/shard_map/hidden_terms/pallas_call | solution.py:134
  27.3 2.1 %collective-permute-start.9 = (bf16[512,128]{1,0:T(8,128)(2,1)S(1)}, bf16[512,128]{1,0:T(8,128)(2,1)S(1)}, u32[]{:S(2)}, u32[]{:S(2)}) collective-permute-start(bf16[512,128]{1,0:T(8,128)(2,1)S(1)} %get-tuple-element.73), channel_id=1, source_target_pairs={{0,4},{2,6},{4,0},{6,2},{1,5},{3,7},{5,1},{7,3},{8,12},{10,14},{12... | collective-permute-start | bytes 393224 | tf_op jit(solution)/shard_map/ppermute | solution.py:28
  29.8 1.8 %collective-permute-done.14.refs_5_.refs_10_.refs_12_ = bf16[1024,128]{1,0:T(8,128)(2,1)S(1)} collective-permute-done((bf16[1024,128]{1,0:T(8,128)(2,1)S(1)}, bf16[1024,128]{1,0:T(8,128)(2,1)S(1)}, u32[]{:S(2)}, u32[]{:S(2)}) %collective-permute-start.14) | collective-permute-done | bytes 262176 | tf_op jit(solution)/shard_map/ppermute | solution.py:28
  31.6 1.3 %collective-permute-start.19 = (bf16[1024,128]{1,0:T(8,128)(2,1)S(1)}, bf16[1024,128]{1,0:T(8,128)(2,1)S(1)}, u32[]{:S(2)}, u32[]{:S(2)}) collective-permute-start(bf16[1024,128]{1,0:T(8,128)(2,1)S(1)} %collective-permute-done.12.refs_2_.refs_6_.refs_8_), channel_id=1, source_target_pairs={{0,16},{8,24},{16,0},{24,8},{1,17},{9,25},{17,1},{25,9},{2,18},{10... | collective-permute-start | bytes 786440 | tf_op jit(solution)/shard_map/ppermute | solution.py:28
  33.9 1.2 %collective-permute-start.20 = (bf16[1024,128]{1,0:T(8,128)(2,1)S(1)}, bf16[1024,128]{1,0:T(8,128)(2,1)S(1)}, u32[]{:S(2)}, u32[]{:S(2)}) collective-permute-start(bf16[1024,128]{1,0:T(8,128)(2,1)S(1)} %collective-permute-done.15.refs_6_.refs_11_.refs_13_), channel_id=1, source_target_pairs={{0,8},{8,0},{16,24},{24,16},{1,9},{9,1},{17,25},{25,17},{2,10},{10... | collective-permute-start | bytes 786440 | tf_op jit(solution)/shard_map/ppermute | solution.py:28
  35.1 1.5 %mlp_forward.1 = (bf16[128,4096]{1,0:T(8,128)(2,1)S(1)}, f32[128,128]{1,0:T(8,128)S(1)}, f32[128,256]{1,0:T(8,128)S(1)}, bf16[128,1024]{1,0:T(8,128)(2,1)S(1)}) custom-call(s32[3]{0:T(128)S(1)} %pad_add_fusion.refs_0_, bf16[1024,128]{1,0:T(8,128)(2,1)S(1)} %copy-done, bf16[1024,128]{1,0:T(8,128)(2,1)S(1)} %collective-permute-done.12.refs_2_.refs_6_.refs_8_, ...), custom_call_target="tpu_custom_call" | custom-call | flops 268435456 | bytes 4136972 | tf_op jit(solution)/shard_map/mlp_forward/pallas_call | solution.py:134
  37.1 4.2 %collective-permute-done.11.refs_4_ = bf16[512,128]{1,0:T(8,128)(2,1)S(1)} collective-permute-done((bf16[512,128]{1,0:T(8,128)(2,1)S(1)}, bf16[512,128]{1,0:T(8,128)(2,1)S(1)}, u32[]{:S(2)}, u32[]{:S(2)}) %collective-permute-start.11) | collective-permute-done | bytes 131104 | tf_op jit(solution)/shard_map/ppermute | solution.py:28
  41.9 1.3 %collective-permute-start.16 = (bf16[128,640]{1,0:T(8,128)(2,1)S(1)}, bf16[128,640]{1,0:T(8,128)(2,1)S(1)}, u32[]{:S(2)}, u32[]{:S(2)}) collective-permute-start(bf16[128,640]{1,0:T(8,128)(2,1)S(1)} %get-tuple-element.89), channel_id=1, source_target_pairs={{0,8},{8,0},{16,24},{24,16},{1,9},{9,1},{17,25},{25,17},{2,10},{10... | collective-permute-start | bytes 491528 | tf_op jit(solution)/shard_map/ppermute | solution.py:28
  43.2 1.2 %collective-permute-start.17 = (bf16[128,640]{1,0:T(8,128)(2,1)S(1)}, bf16[128,640]{1,0:T(8,128)(2,1)S(1)}, u32[]{:S(2)}, u32[]{:S(2)}) collective-permute-start(bf16[128,640]{1,0:T(8,128)(2,1)S(1)} %get-tuple-element.90), channel_id=1, source_target_pairs={{0,16},{8,24},{16,0},{24,8},{1,17},{9,25},{17,1},{25,9},{2,18},{10... | collective-permute-start | bytes 491528 | tf_op jit(solution)/shard_map/ppermute | solution.py:28
  46.2 1.5 %collective-permute-done.17.refs_3_.refs_4_ = bf16[128,640]{1,0:T(8,128)(2,1)S(1)} collective-permute-done((bf16[128,640]{1,0:T(8,128)(2,1)S(1)}, bf16[128,640]{1,0:T(8,128)(2,1)S(1)}, u32[]{:S(2)}, u32[]{:S(2)}) %collective-permute-start.17) | collective-permute-done | bytes 163872 | tf_op jit(solution)/shard_map/ppermute | solution.py:28
  47.7 3.8 %collective-permute-done.18.refs_4_.refs_5_ = bf16[128,640]{1,0:T(8,128)(2,1)S(1)} collective-permute-done((bf16[128,640]{1,0:T(8,128)(2,1)S(1)}, bf16[128,640]{1,0:T(8,128)(2,1)S(1)}, u32[]{:S(2)}, u32[]{:S(2)}) %collective-permute-start.18) | collective-permute-done | bytes 163872 | tf_op jit(solution)/shard_map/ppermute | solution.py:28
  51.7 1.4 %mlp_backward.1 = (bf16[4,128,512]{2,1,0:T(8,128)(2,1)S(1)}, bf16[128,256]{1,0:T(8,128)(2,1)S(1)}, f32[128,128]{1,0:T(8,128)S(1)}) custom-call(s32[3]{0:T(128)S(1)} %pad_add_fusion.refs_0_, f32[128,128]{1,0:T(8,128)S(1)} %get-tuple-element.96.refs_1_, bf16[128,640]{1,0:T(8,128)(2,1)S(1)} %collective-permute-done.16.refs_2_.refs_3_, ...), custom_call_target="tpu_custom_call" | custom-call | flops 134217728 | bytes 4825100 | tf_op jit(solution)/shard_map/mlp_backward/pallas_call | solution.py:134
  53.1 2.9 %collective-permute-start.21 = (bf16[4,128,512]{2,1,0:T(8,128)(2,1)S(1)}, bf16[4,128,512]{2,1,0:T(8,128)(2,1)S(1)}, u32[]{:S(2)}, u32[]{:S(2)}) collective-permute-start(bf16[4,128,512]{2,1,0:T(8,128)(2,1)S(1)} %get-tuple-element.107), channel_id=1, source_target_pairs={{0,1},{1,0},{2,3},{3,2},{4,5},{5,4},{6,7},{7,6},{8,9},{9,8},{10,11... | collective-permute-start | bytes 1572872 | tf_op jit(solution)/shard_map/ppermute | solution.py:28
  58.9 1.7 %collective-permute-start.23 = (bf16[128,512]{1,0:T(8,128)(2,1)S(1)}, bf16[128,512]{1,0:T(8,128)(2,1)S(1)}, u32[]{:S(2)}, u32[]{:S(2)}) collective-permute-start(bf16[128,512]{1,0:T(8,128)(2,1)S(1)} %get-tuple-element.120), channel_id=1, source_target_pairs={{0,2},{2,0},{4,6},{6,4},{1,3},{3,1},{5,7},{7,5},{8,10},{10,8},{12,... | collective-permute-start | bytes 393224 | tf_op jit(solution)/shard_map/ppermute | solution.py:28
  61.1 5.9 %collective-permute-done.25 = bf16[128,512]{1,0:T(8,128)(2,1)S(1)} collective-permute-done((bf16[128,512]{1,0:T(8,128)(2,1)S(1)}, bf16[128,512]{1,0:T(8,128)(2,1)S(1)}, u32[]{:S(2)}, u32[]{:S(2)}) %collective-permute-start.25) | collective-permute-done | bytes 131104 | tf_op jit(solution)/shard_map/ppermute | solution.py:28
  66.9 3.0 %collective-permute-done.24 = bf16[128,512]{1,0:T(8,128)(2,1)S(1)} collective-permute-done((bf16[128,512]{1,0:T(8,128)(2,1)S(1)}, bf16[128,512]{1,0:T(8,128)(2,1)S(1)}, u32[]{:S(2)}, u32[]{:S(2)}) %collective-permute-start.24) | collective-permute-done | bytes 131104 | tf_op jit(solution)/shard_map/ppermute | solution.py:28
  70.9 1.9 %collective-permute-start.27 = (bf16[128,512]{1,0:T(8,128)(2,1)S(1)}, bf16[128,512]{1,0:T(8,128)(2,1)S(1)}, u32[]{:S(2)}, u32[]{:S(2)}) collective-permute-start(bf16[128,512]{1,0:T(8,128)(2,1)S(1)} %fusion.2.refs_1_), channel_id=1, source_target_pairs={{0,2},{2,0},{4,6},{6,4},{1,3},{3,1},{5,7},{7,5},{8,10},{10,8},{12,... | collective-permute-start | bytes 393224 | tf_op jit(solution)/shard_map/ppermute | solution.py:28
  72.8 1.2 %collective-permute-start.28 = (bf16[128,512]{1,0:T(8,128)(2,1)S(1)}, bf16[128,512]{1,0:T(8,128)(2,1)S(1)}, u32[]{:S(2)}, u32[]{:S(2)}) collective-permute-start(bf16[128,512]{1,0:T(8,128)(2,1)S(1)} %fusion.2.refs_1_), channel_id=1, source_target_pairs={{0,4},{2,6},{4,0},{6,2},{1,5},{3,7},{5,1},{7,3},{8,12},{10,14},{12... | collective-permute-start | bytes 393224 | tf_op jit(solution)/shard_map/ppermute | solution.py:28
  74.9 3.0 %collective-permute-done.27.refs_2_ = bf16[128,512]{1,0:T(8,128)(2,1)S(1)} collective-permute-done((bf16[128,512]{1,0:T(8,128)(2,1)S(1)}, bf16[128,512]{1,0:T(8,128)(2,1)S(1)}, u32[]{:S(2)}, u32[]{:S(2)}) %collective-permute-start.27) | collective-permute-done | bytes 131104 | tf_op jit(solution)/shard_map/ppermute | solution.py:28
  79.0 1.3 %kv_grad.1 = bf16[1024,512]{1,0:T(8,128)(2,1)S(1)} custom-call(s32[3]{0:T(128)S(1)} %pad_add_fusion.refs_0_, bf16[128,512]{1,0:T(8,128)(2,1)S(1)} %bitcast.31, bf16[128,512]{1,0:T(8,128)(2,1)S(1)} %collective-permute-done.refs_2_, bf16[128,512]{1,0:T(8,128)(2,1)S(1)} %collective-permute-done.1.refs_3_, bf16[128,512]{1,0:T(8,128)(2,1)S(1)} %collective-permute-done.2.refs_4_, ...), custom_call_target="tpu_custom_call" | custom-call | flops 536870912 | bytes 2621452 | tf_op jit(solution)/shard_map/kv_grad/pallas_call | solution.py:134
  82.4 3.9 %collective-permute-done.29.refs_4_ = bf16[128,512]{1,0:T(8,128)(2,1)S(1)} collective-permute-done((bf16[128,512]{1,0:T(8,128)(2,1)S(1)}, bf16[128,512]{1,0:T(8,128)(2,1)S(1)}, u32[]{:S(2)}, u32[]{:S(2)}) %collective-permute-start.29) | collective-permute-done | bytes 131104 | tf_op jit(solution)/shard_map/ppermute | solution.py:28
  88.6 1.6 %input_grad.1 = bf16[128,4096]{1,0:T(8,128)(2,1)} custom-call(s32[3]{0:T(128)S(1)} %pad_add_fusion.refs_0_, bf16[128,512]{1,0:T(8,128)(2,1)S(1)} %fusion.2.refs_1_, bf16[128,512]{1,0:T(8,128)(2,1)S(1)} %collective-permute-done.27.refs_2_, bf16[128,512]{1,0:T(8,128)(2,1)S(1)} %collective-permute-done.28.refs_3_, ...), custom_call_target="tpu_custom_call" | custom-call | bytes 2097164 | tf_op jit(solution)/shard_map/input_grad/pallas_call | solution.py:134
  (72 shorter events, 23.3 us)
Async XLA Ops:
  0.6 14.2 %collective-permute-start.3 = (bf16[128,1024]{1,0:T(8,128)(2,1)}, bf16[128,1024]{1,0:T(8,128)(2,1)S(1)}, u32[]{:S(2)}, u32[]{:S(2)}) collective-permute-start(bf16[128,1024]{1,0:T(8,128)(2,1)} %refs_3_.1), channel_id=1, source_target_pairs={{0,4},{2,6},{4,0},{6,2},{1,5},{3,7},{5,1},{7,3},{8,12},{10,14},{12... | collective-permute-start | bytes 786440 | tf_op jit(solution)/shard_map/ppermute | solution.py:28
  3.0 11.8 %collective-permute-start.4 = (bf16[128,1024]{1,0:T(8,128)(2,1)}, bf16[128,1024]{1,0:T(8,128)(2,1)S(1)}, u32[]{:S(2)}, u32[]{:S(2)}) collective-permute-start(bf16[128,1024]{1,0:T(8,128)(2,1)} %refs_3_.1), channel_id=1, source_target_pairs={{0,2},{2,0},{4,6},{6,4},{1,3},{3,1},{5,7},{7,5},{8,10},{10,8},{12,... | collective-permute-start | bytes 786440 | tf_op jit(solution)/shard_map/ppermute | solution.py:28
  4.1 4.3 %collective-permute-start = (bf16[128,512]{1,0:T(8,128)(2,1)S(1)}, bf16[128,512]{1,0:T(8,128)(2,1)S(1)}, u32[]{:S(2)}, u32[]{:S(2)}) collective-permute-start(bf16[128,512]{1,0:T(8,128)(2,1)S(1)} %bitcast.27), channel_id=1, source_target_pairs={{0,8},{8,0},{16,24},{24,16},{1,9},{9,1},{17,25},{25,17},{2,10},{10... | collective-permute-start | bytes 393224 | tf_op jit(solution)/shard_map/ppermute | solution.py:28
  5.4 4.1 %collective-permute-start.1 = (bf16[128,512]{1,0:T(8,128)(2,1)S(1)}, bf16[128,512]{1,0:T(8,128)(2,1)S(1)}, u32[]{:S(2)}, u32[]{:S(2)}) collective-permute-start(bf16[128,512]{1,0:T(8,128)(2,1)S(1)} %bitcast.28), channel_id=1, source_target_pairs={{0,16},{8,24},{16,0},{24,8},{1,17},{9,25},{17,1},{25,9},{2,18},{10... | collective-permute-start | bytes 393224 | tf_op jit(solution)/shard_map/ppermute | solution.py:28
  6.6 5.5 %collective-permute-start.2 = (bf16[128,512]{1,0:T(8,128)(2,1)S(1)}, bf16[128,512]{1,0:T(8,128)(2,1)S(1)}, u32[]{:S(2)}, u32[]{:S(2)}) collective-permute-start(bf16[128,512]{1,0:T(8,128)(2,1)S(1)} %bitcast.29), channel_id=1, source_target_pairs={{0,24},{8,16},{16,8},{24,0},{1,25},{9,17},{17,9},{25,1},{2,26},{10... | collective-permute-start | bytes 393224 | tf_op jit(solution)/shard_map/ppermute | solution.py:28
  16.2 7.0 %collective-permute-start.5 = (bf16[512,1024]{1,0:T(8,128)(2,1)S(1)}, bf16[512,1024]{1,0:T(8,128)(2,1)S(1)}, u32[]{:S(2)}, u32[]{:S(2)}) collective-permute-start(bf16[512,1024]{1,0:T(8,128)(2,1)S(1)} %upstream_terms.1.refs_1_), channel_id=1, source_target_pairs={{0,1},{1,0},{2,3},{3,2},{4,5},{5,4},{6,7},{7,6},{8,9},{9,8},{10,11... | collective-permute-start | bytes 3145736 | tf_op jit(solution)/shard_map/ppermute | solution.py:28
  17.8 4.2 %collective-permute-start.7 = (bf16[128,2048]{1,0:T(8,128)(2,1)S(1)}, bf16[128,2048]{1,0:T(8,128)(2,1)S(1)}, u32[]{:S(2)}, u32[]{:S(2)}) collective-permute-start(bf16[128,2048]{1,0:T(8,128)(2,1)S(1)} %copy-done.2), channel_id=1, source_target_pairs={{0,1},{1,0},{2,3},{3,2},{4,5},{5,4},{6,7},{7,6},{8,9},{9,8},{10,11... | collective-permute-start | bytes 1572872 | tf_op jit(solution)/shard_map/ppermute | solution.py:28
  18.2 7.9 %collective-permute-start.10 = (bf16[128,1024]{1,0:T(8,128)(2,1)S(1)}, bf16[128,1024]{1,0:T(8,128)(2,1)S(1)}, u32[]{:S(2)}, u32[]{:S(2)}) collective-permute-start(bf16[128,1024]{1,0:T(8,128)(2,1)S(1)} %collective-permute-done.3.refs_5_), channel_id=1, source_target_pairs={{0,2},{2,0},{4,6},{6,4},{1,3},{3,1},{5,7},{7,5},{8,10},{10,8},{12,... | collective-permute-start | bytes 786440 | tf_op jit(solution)/shard_map/ppermute | solution.py:28
  18.5 8.9 %collective-permute-start.12 = (bf16[1024,128]{1,0:T(8,128)(2,1)S(1)}, bf16[1024,128]{1,0:T(8,128)(2,1)S(1)}, u32[]{:S(2)}, u32[]{:S(2)}) collective-permute-start(bf16[1024,128]{1,0:T(8,128)(2,1)S(1)} %copy-done), channel_id=1, source_target_pairs={{0,8},{8,0},{16,24},{24,16},{1,9},{9,1},{17,25},{25,17},{2,10},{10... | collective-permute-start | bytes 786440 | tf_op jit(solution)/shard_map/ppermute | solution.py:28
  20.7 8.7 %collective-permute-start.13 = (bf16[1024,128]{1,0:T(8,128)(2,1)S(1)}, bf16[1024,128]{1,0:T(8,128)(2,1)S(1)}, u32[]{:S(2)}, u32[]{:S(2)}) collective-permute-start(bf16[1024,128]{1,0:T(8,128)(2,1)S(1)} %copy-done), channel_id=1, source_target_pairs={{0,16},{8,24},{16,0},{24,8},{1,17},{9,25},{17,1},{25,9},{2,18},{10... | collective-permute-start | bytes 786440 | tf_op jit(solution)/shard_map/ppermute | solution.py:28
  22.0 9.7 %collective-permute-start.14 = (bf16[1024,128]{1,0:T(8,128)(2,1)S(1)}, bf16[1024,128]{1,0:T(8,128)(2,1)S(1)}, u32[]{:S(2)}, u32[]{:S(2)}) collective-permute-start(bf16[1024,128]{1,0:T(8,128)(2,1)S(1)} %copy-done.1), channel_id=1, source_target_pairs={{0,8},{8,0},{16,24},{24,16},{1,9},{9,1},{17,25},{25,17},{2,10},{10... | collective-permute-start | bytes 786440 | tf_op jit(solution)/shard_map/ppermute | solution.py:28
  23.2 10.7 %collective-permute-start.15 = (bf16[1024,128]{1,0:T(8,128)(2,1)S(1)}, bf16[1024,128]{1,0:T(8,128)(2,1)S(1)}, u32[]{:S(2)}, u32[]{:S(2)}) collective-permute-start(bf16[1024,128]{1,0:T(8,128)(2,1)S(1)} %copy-done.1), channel_id=1, source_target_pairs={{0,16},{8,24},{16,0},{24,8},{1,17},{9,25},{17,1},{25,9},{2,18},{10... | collective-permute-start | bytes 786440 | tf_op jit(solution)/shard_map/ppermute | solution.py:28
  26.1 10.5 %collective-permute-start.8 = (bf16[512,128]{1,0:T(8,128)(2,1)S(1)}, bf16[512,128]{1,0:T(8,128)(2,1)S(1)}, u32[]{:S(2)}, u32[]{:S(2)}) collective-permute-start(bf16[512,128]{1,0:T(8,128)(2,1)S(1)} %get-tuple-element.72), channel_id=1, source_target_pairs={{0,2},{2,0},{4,6},{6,4},{1,3},{3,1},{5,7},{7,5},{8,10},{10,8},{12,... | collective-permute-start | bytes 393224 | tf_op jit(solution)/shard_map/ppermute | solution.py:28
  27.3 9.8 %collective-permute-start.9 = (bf16[512,128]{1,0:T(8,128)(2,1)S(1)}, bf16[512,128]{1,0:T(8,128)(2,1)S(1)}, u32[]{:S(2)}, u32[]{:S(2)}) collective-permute-start(bf16[512,128]{1,0:T(8,128)(2,1)S(1)} %get-tuple-element.73), channel_id=1, source_target_pairs={{0,4},{2,6},{4,0},{6,2},{1,5},{3,7},{5,1},{7,3},{8,12},{10,14},{12... | collective-permute-start | bytes 393224 | tf_op jit(solution)/shard_map/ppermute | solution.py:28
  29.4 11.9 %collective-permute-start.11 = (bf16[512,128]{1,0:T(8,128)(2,1)S(1)}, bf16[512,128]{1,0:T(8,128)(2,1)S(1)}, u32[]{:S(2)}, u32[]{:S(2)}) collective-permute-start(bf16[512,128]{1,0:T(8,128)(2,1)S(1)} %hidden_last.1), channel_id=1, source_target_pairs={{0,6},{2,4},{4,2},{6,0},{1,7},{3,5},{5,3},{7,1},{8,14},{10,12},{12... | collective-permute-start | bytes 393224 | tf_op jit(solution)/shard_map/ppermute | solution.py:28
  31.6 20.1 %collective-permute-start.19 = (bf16[1024,128]{1,0:T(8,128)(2,1)S(1)}, bf16[1024,128]{1,0:T(8,128)(2,1)S(1)}, u32[]{:S(2)}, u32[]{:S(2)}) collective-permute-start(bf16[1024,128]{1,0:T(8,128)(2,1)S(1)} %collective-permute-done.12.refs_2_.refs_6_.refs_8_), channel_id=1, source_target_pairs={{0,16},{8,24},{16,0},{24,8},{1,17},{9,25},{17,1},{25,9},{2,18},{10... | collective-permute-start | bytes 786440 | tf_op jit(solution)/shard_map/ppermute | solution.py:28
  33.9 17.9 %collective-permute-start.20 = (bf16[1024,128]{1,0:T(8,128)(2,1)S(1)}, bf16[1024,128]{1,0:T(8,128)(2,1)S(1)}, u32[]{:S(2)}, u32[]{:S(2)}) collective-permute-start(bf16[1024,128]{1,0:T(8,128)(2,1)S(1)} %collective-permute-done.15.refs_6_.refs_11_.refs_13_), channel_id=1, source_target_pairs={{0,8},{8,0},{16,24},{24,16},{1,9},{9,1},{17,25},{25,17},{2,10},{10... | collective-permute-start | bytes 786440 | tf_op jit(solution)/shard_map/ppermute | solution.py:28
  41.9 4.2 %collective-permute-start.16 = (bf16[128,640]{1,0:T(8,128)(2,1)S(1)}, bf16[128,640]{1,0:T(8,128)(2,1)S(1)}, u32[]{:S(2)}, u32[]{:S(2)}) collective-permute-start(bf16[128,640]{1,0:T(8,128)(2,1)S(1)} %get-tuple-element.89), channel_id=1, source_target_pairs={{0,8},{8,0},{16,24},{24,16},{1,9},{9,1},{17,25},{25,17},{2,10},{10... | collective-permute-start | bytes 491528 | tf_op jit(solution)/shard_map/ppermute | solution.py:28
  43.2 4.5 %collective-permute-start.17 = (bf16[128,640]{1,0:T(8,128)(2,1)S(1)}, bf16[128,640]{1,0:T(8,128)(2,1)S(1)}, u32[]{:S(2)}, u32[]{:S(2)}) collective-permute-start(bf16[128,640]{1,0:T(8,128)(2,1)S(1)} %get-tuple-element.90), channel_id=1, source_target_pairs={{0,16},{8,24},{16,0},{24,8},{1,17},{9,25},{17,1},{25,9},{2,18},{10... | collective-permute-start | bytes 491528 | tf_op jit(solution)/shard_map/ppermute | solution.py:28
  44.4 7.1 %collective-permute-start.18 = (bf16[128,640]{1,0:T(8,128)(2,1)S(1)}, bf16[128,640]{1,0:T(8,128)(2,1)S(1)}, u32[]{:S(2)}, u32[]{:S(2)}) collective-permute-start(bf16[128,640]{1,0:T(8,128)(2,1)S(1)} %get-tuple-element.91), channel_id=1, source_target_pairs={{0,24},{8,16},{16,8},{24,0},{1,25},{9,17},{17,9},{25,1},{2,26},{10... | collective-permute-start | bytes 491528 | tf_op jit(solution)/shard_map/ppermute | solution.py:28
  51.5 5.6 %collective-permute-start.22 = (bf16[256,512]{1,0:T(8,128)(2,1)S(1)}, bf16[256,512]{1,0:T(8,128)(2,1)S(1)}, u32[]{:S(2)}, u32[]{:S(2)}) collective-permute-start(bf16[256,512]{1,0:T(8,128)(2,1)S(1)} %get-tuple-element.109), channel_id=1, source_target_pairs={{0,8},{8,0},{16,24},{24,16},{1,9},{9,1},{17,25},{25,17},{2,10},{10... | collective-permute-start | bytes 786440 | tf_op jit(solution)/shard_map/ppermute | solution.py:28
  53.1 4.5 %collective-permute-start.21 = (bf16[4,128,512]{2,1,0:T(8,128)(2,1)S(1)}, bf16[4,128,512]{2,1,0:T(8,128)(2,1)S(1)}, u32[]{:S(2)}, u32[]{:S(2)}) collective-permute-start(bf16[4,128,512]{2,1,0:T(8,128)(2,1)S(1)} %get-tuple-element.107), channel_id=1, source_target_pairs={{0,1},{1,0},{2,3},{3,2},{4,5},{5,4},{6,7},{7,6},{8,9},{9,8},{10,11... | collective-permute-start | bytes 1572872 | tf_op jit(solution)/shard_map/ppermute | solution.py:28
  57.8 9.1 %collective-permute-start.25 = (bf16[128,512]{1,0:T(8,128)(2,1)S(1)}, bf16[128,512]{1,0:T(8,128)(2,1)S(1)}, u32[]{:S(2)}, u32[]{:S(2)}) collective-permute-start(bf16[128,512]{1,0:T(8,128)(2,1)S(1)} %get-tuple-element.121), channel_id=1, source_target_pairs={{0,6},{2,4},{4,2},{6,0},{1,7},{3,5},{5,3},{7,1},{8,14},{10,12},{12... | collective-permute-start | bytes 393224 | tf_op jit(solution)/shard_map/ppermute | solution.py:28
  58.8 11.1 %collective-permute-start.24 = (bf16[128,512]{1,0:T(8,128)(2,1)S(1)}, bf16[128,512]{1,0:T(8,128)(2,1)S(1)}, u32[]{:S(2)}, u32[]{:S(2)}) collective-permute-start(bf16[128,512]{1,0:T(8,128)(2,1)S(1)} %get-tuple-element.122), channel_id=1, source_target_pairs={{0,4},{2,6},{4,0},{6,2},{1,5},{3,7},{5,1},{7,3},{8,12},{10,14},{12... | collective-permute-start | bytes 393224 | tf_op jit(solution)/shard_map/ppermute | solution.py:28
  58.9 11.1 %collective-permute-start.23 = (bf16[128,512]{1,0:T(8,128)(2,1)S(1)}, bf16[128,512]{1,0:T(8,128)(2,1)S(1)}, u32[]{:S(2)}, u32[]{:S(2)}) collective-permute-start(bf16[128,512]{1,0:T(8,128)(2,1)S(1)} %get-tuple-element.120), channel_id=1, source_target_pairs={{0,2},{2,0},{4,6},{6,4},{1,3},{3,1},{5,7},{7,5},{8,10},{10,8},{12,... | collective-permute-start | bytes 393224 | tf_op jit(solution)/shard_map/ppermute | solution.py:28
  60.6 9.4 %collective-permute-start.26 = (bf16[256,512]{1,0:T(8,128)(2,1)S(1)}, bf16[256,512]{1,0:T(8,128)(2,1)S(1)}, u32[]{:S(2)}, u32[]{:S(2)}) collective-permute-start(bf16[256,512]{1,0:T(8,128)(2,1)S(1)} %pad_maximum_fusion.1), channel_id=1, source_target_pairs={{0,16},{8,24},{16,0},{24,8},{1,17},{9,25},{17,1},{25,9},{2,18},{10... | collective-permute-start | bytes 786440 | tf_op jit(solution)/shard_map/ppermute | solution.py:28
  70.0 8.9 %collective-permute-start.30 = (bf16[512,512]{1,0:T(8,128)(2,1)S(1)}, bf16[512,512]{1,0:T(8,128)(2,1)S(1)}, u32[]{:S(2)}, u32[]{:S(2)}) collective-permute-start(bf16[512,512]{1,0:T(8,128)(2,1)S(1)} %pad_maximum_fusion.refs_5_), channel_id=1, source_target_pairs={{0,1},{1,0},{2,3},{3,2},{4,5},{5,4},{6,7},{7,6},{8,9},{9,8},{10,11... | collective-permute-start | bytes 1572872 | tf_op jit(solution)/shard_map/ppermute | solution.py:28
  70.9 7.1 %collective-permute-start.27 = (bf16[128,512]{1,0:T(8,128)(2,1)S(1)}, bf16[128,512]{1,0:T(8,128)(2,1)S(1)}, u32[]{:S(2)}, u32[]{:S(2)}) collective-permute-start(bf16[128,512]{1,0:T(8,128)(2,1)S(1)} %fusion.2.refs_1_), channel_id=1, source_target_pairs={{0,2},{2,0},{4,6},{6,4},{1,3},{3,1},{5,7},{7,5},{8,10},{10,8},{12,... | collective-permute-start | bytes 393224 | tf_op jit(solution)/shard_map/ppermute | solution.py:28
  72.8 9.6 %collective-permute-start.28 = (bf16[128,512]{1,0:T(8,128)(2,1)S(1)}, bf16[128,512]{1,0:T(8,128)(2,1)S(1)}, u32[]{:S(2)}, u32[]{:S(2)}) collective-permute-start(bf16[128,512]{1,0:T(8,128)(2,1)S(1)} %fusion.2.refs_1_), channel_id=1, source_target_pairs={{0,4},{2,6},{4,0},{6,2},{1,5},{3,7},{5,1},{7,3},{8,12},{10,14},{12... | collective-permute-start | bytes 393224 | tf_op jit(solution)/shard_map/ppermute | solution.py:28
  74.0 12.4 %collective-permute-start.29 = (bf16[128,512]{1,0:T(8,128)(2,1)S(1)}, bf16[128,512]{1,0:T(8,128)(2,1)S(1)}, u32[]{:S(2)}, u32[]{:S(2)}) collective-permute-start(bf16[128,512]{1,0:T(8,128)(2,1)S(1)} %fusion.2.refs_1_), channel_id=1, source_target_pairs={{0,6},{2,4},{4,2},{6,0},{1,7},{3,5},{5,3},{7,1},{8,14},{10,12},{12... | collective-permute-start | bytes 393224 | tf_op jit(solution)/shard_map/ppermute | solution.py:28
  74.3 12.9 %collective-permute-start.31 = (bf16[128,512]{1,0:T(8,128)(2,1)S(1)}, bf16[128,512]{1,0:T(8,128)(2,1)S(1)}, u32[]{:S(2)}, u32[]{:S(2)}) collective-permute-start(bf16[128,512]{1,0:T(8,128)(2,1)S(1)} %fusion.2.refs_1_), channel_id=1, source_target_pairs={{0,1},{1,0},{2,3},{3,2},{4,5},{5,4},{6,7},{7,6},{8,9},{9,8},{10,11... | collective-permute-start | bytes 393224 | tf_op jit(solution)/shard_map/ppermute | solution.py:28
  78.0 9.3 %collective-permute-start.32 = (bf16[128,512]{1,0:T(8,128)(2,1)S(1)}, bf16[128,512]{1,0:T(8,128)(2,1)S(1)}, u32[]{:S(2)}, u32[]{:S(2)}) collective-permute-start(bf16[128,512]{1,0:T(8,128)(2,1)S(1)} %collective-permute-done.27.refs_2_), channel_id=1, source_target_pairs={{0,1},{1,0},{2,3},{3,2},{4,5},{5,4},{6,7},{7,6},{8,9},{9,8},{10,11... | collective-permute-start | bytes 393224 | tf_op jit(solution)/shard_map/ppermute | solution.py:28
  (9 other events, 35.5 us)

commit v8 on v7

--- a/solution.py
+++ b/solution.py
@@ -168,6 +168,10 @@
     for k, out in enumerate(outs):
         tok, half = out.shape
         out[...] = upstream[k * tok : (k + 1) * tok, aligned(where[2] * half, half)]
+
+
+def last_kernel(where, upstream, down, out):
+    out[...] = dot_nt(upstream[...], down[...]).astype(out.dtype)
 
 
 def owner_kernel(n_dp, n_pipe, where, *refs):
@@ -352,17 +356,18 @@
         "hidden_terms",
         [shaped((n_dp * tok, units), F32)]
         + [shaped((n_dp * tok, units), BF16)] * (n_pipe - 2)
-        + [shaped((tok, half), BF16)] * n_dp,
+        + [shaped((tok, half), BF16)] * n_dp
+        + [shaped((n_dp * tok, cols), BF16)],
         [where, mine, other, *downs[:-1]],
-        [pltpu.VMEM((n_dp * tok, cols), BF16), pltpu.VMEM((group - units, cols), BF16)],
+        [pltpu.VMEM((group - units, cols), BF16)],
         flops=2 * n_dp * tok * cols * group,
     )
+    *outs, upstream = outs
     (last_out,) = call(
-        lambda *refs: hidden_kernel(1, n_ten, *refs),
+        last_kernel,
         "hidden_last",
         [shaped((n_dp * tok, units), BF16)],
-        [where, mine, other, downs[-1]],
-        [pltpu.VMEM((n_dp * tok, cols), BF16), pltpu.VMEM((units, cols), BF16)],
+        [where, upstream, downs[-1]],
         flops=2 * n_dp * tok * cols * units,
     )
     outs = [*outs[: n_pipe - 1], last_out, *outs[n_pipe - 1 :]]

time: 90.3 us -> 90.3 us (level)
  no operation moved by 1% of the time
where the time goes in v8:
time: 90.3 us; the launch traced here: 90.2 us
  waiting for transfers between devices  40.6 us (45%)
  starting transfers between devices  33 us (37%)
  Pallas kernels  11.7 us (13%)
  local copies, waits for them, and re-layouts  3.56 us (4%)
    ppermute x35, waiting for transfers between devices, send(): return lax.ppermute(value, axis, [(src, src ^ step) for src in range(size)])  40.6 us
    ppermute x35, starting transfers between devices, send(): return lax.ppermute(value, axis, [(src, src ^ step) for src in range(size)])  33 us
    pallas_call x10, Pallas kernels, call(): pl.pallas_call(body, name=name, out_shape=out, in_specs=specs, out_specs=...  11.7 us
    unnamed x14, local copies, waits for them, and re-layouts  2.39 us
  transfers between devices with their start and end apart: 35, of which 20 were waited for; matrix products, arithmetic and copies ran while one was open for 4% of the time, Pallas kernels for 10%

profile of v8, /device:TPU:9, one launch (start us, length us, event | category | flops | bytes accessed | tf_op | source)
XLA Modules:
  0.0 90.2 jit_solution(5677559004261869908)
XLA Ops:
  0.6 2.4 %collective-permute-start.3 = (bf16[128,1024]{1,0:T(8,128)(2,1)}, bf16[128,1024]{1,0:T(8,128)(2,1)S(1)}, u32[]{:S(2)}, u32[]{:S(2)}) collective-permute-start(bf16[128,1024]{1,0:T(8,128)(2,1)} %refs_3_.1), channel_id=1, source_target_pairs={{0,4},{2,6},{4,0},{6,2},{1,5},{3,7},{5,1},{7,3},{8,12},{10,14},{12... | collective-permute-start | bytes 786440 | tf_op jit(solution)/shard_map/ppermute | solution.py:28
  4.1 1.3 %collective-permute-start = (bf16[128,512]{1,0:T(8,128)(2,1)S(1)}, bf16[128,512]{1,0:T(8,128)(2,1)S(1)}, u32[]{:S(2)}, u32[]{:S(2)}) collective-permute-start(bf16[128,512]{1,0:T(8,128)(2,1)S(1)} %bitcast.27), channel_id=1, source_target_pairs={{0,8},{8,0},{16,24},{24,16},{1,9},{9,1},{17,25},{25,17},{2,10},{10... | collective-permute-start | bytes 393224 | tf_op jit(solution)/shard_map/ppermute | solution.py:28
  5.4 1.2 %collective-permute-start.1 = (bf16[128,512]{1,0:T(8,128)(2,1)S(1)}, bf16[128,512]{1,0:T(8,128)(2,1)S(1)}, u32[]{:S(2)}, u32[]{:S(2)}) collective-permute-start(bf16[128,512]{1,0:T(8,128)(2,1)S(1)} %bitcast.28), channel_id=1, source_target_pairs={{0,16},{8,24},{16,0},{24,8},{1,17},{9,25},{17,1},{25,9},{2,18},{10... | collective-permute-start | bytes 393224 | tf_op jit(solution)/shard_map/ppermute | solution.py:28
  6.8 1.4 %copy.12 = bf16[128,8,2,256]{3,1,2,0:T(8,128)(2,1)S(1)} copy(bf16[128,8,2,256]{3,2,1,0:T(2,128)(2,1)} %bitcast.32) | data formatting | bytes 2097152
  9.5 2.6 %collective-permute-done.2.refs_4_ = bf16[128,512]{1,0:T(8,128)(2,1)S(1)} collective-permute-done((bf16[128,512]{1,0:T(8,128)(2,1)S(1)}, bf16[128,512]{1,0:T(8,128)(2,1)S(1)}, u32[]{:S(2)}, u32[]{:S(2)}) %collective-permute-start.2) | collective-permute-done | bytes 131104 | tf_op jit(solution)/shard_map/ppermute | solution.py:28
  12.1 2.8 %collective-permute-done.3.refs_5_ = bf16[128,1024]{1,0:T(8,128)(2,1)S(1)} collective-permute-done((bf16[128,1024]{1,0:T(8,128)(2,1)}, bf16[128,1024]{1,0:T(8,128)(2,1)S(1)}, u32[]{:S(2)}, u32[]{:S(2)}) %collective-permute-start.3) | collective-permute-done | bytes 262176 | tf_op jit(solution)/shard_map/ppermute | solution.py:28
  14.9 1.3 %upstream_terms.1.refs_1_ = bf16[512,1024]{1,0:T(8,128)(2,1)S(1)} custom-call(s32[3]{0:T(128)S(1)} %pad_add_fusion.refs_0_.where, bf16[128,512]{1,0:T(8,128)(2,1)S(1)} %bitcast.30, bf16[128,512]{1,0:T(8,128)(2,1)S(1)} %collective-permute-done.refs_2_, bf16[128,512]{1,0:T(8,128)(2,1)S(1)} %collective-permute-done.1.refs_3_, ...), custom_call_target="tpu_custom_call" | custom-call | flops 536870912 | bytes 2621452 | tf_op jit(solution)/shard_map/upstream_terms/pallas_call | solution.py:134
  16.2 1.5 %collective-permute-start.5 = (bf16[512,1024]{1,0:T(8,128)(2,1)S(1)}, bf16[512,1024]{1,0:T(8,128)(2,1)S(1)}, u32[]{:S(2)}, u32[]{:S(2)}) collective-permute-start(bf16[512,1024]{1,0:T(8,128)(2,1)S(1)} %upstream_terms.1.refs_1_), channel_id=1, source_target_pairs={{0,1},{1,0},{2,3},{3,2},{4,5},{5,4},{6,7},{7,6},{8,9},{9,8},{10,11... | collective-permute-start | bytes 3145736 | tf_op jit(solution)/shard_map/ppermute | solution.py:28
  18.5 1.3 %collective-permute-start.12 = (bf16[1024,128]{1,0:T(8,128)(2,1)S(1)}, bf16[1024,128]{1,0:T(8,128)(2,1)S(1)}, u32[]{:S(2)}, u32[]{:S(2)}) collective-permute-start(bf16[1024,128]{1,0:T(8,128)(2,1)S(1)} %copy-done), channel_id=1, source_target_pairs={{0,8},{8,0},{16,24},{24,16},{1,9},{9,1},{17,25},{25,17},{2,10},{10... | collective-permute-start | bytes 786440 | tf_op jit(solution)/shard_map/ppermute | solution.py:28
  20.7 1.2 %collective-permute-start.13 = (bf16[1024,128]{1,0:T(8,128)(2,1)S(1)}, bf16[1024,128]{1,0:T(8,128)(2,1)S(1)}, u32[]{:S(2)}, u32[]{:S(2)}) collective-permute-start(bf16[1024,128]{1,0:T(8,128)(2,1)S(1)} %copy-done), channel_id=1, source_target_pairs={{0,16},{8,24},{16,0},{24,8},{1,17},{9,25},{17,1},{25,9},{2,18},{10... | collective-permute-start | bytes 786440 | tf_op jit(solution)/shard_map/ppermute | solution.py:28
  22.0 1.2 %collective-permute-start.14 = (bf16[1024,128]{1,0:T(8,128)(2,1)S(1)}, bf16[1024,128]{1,0:T(8,128)(2,1)S(1)}, u32[]{:S(2)}, u32[]{:S(2)}) collective-permute-start(bf16[1024,128]{1,0:T(8,128)(2,1)S(1)} %copy-done.1), channel_id=1, source_target_pairs={{0,8},{8,0},{16,24},{24,16},{1,9},{9,1},{17,25},{25,17},{2,10},{10... | collective-permute-start | bytes 786440 | tf_op jit(solution)/shard_map/ppermute | solution.py:28
  23.9 1.3 %hidden_terms.1 = (f32[512,128]{1,0:T(8,128)S(1)}, bf16[512,128]{1,0:T(8,128)(2,1)S(1)}, bf16[512,128]{1,0:T(8,128)(2,1)S(1)}, bf16[128,512]{1,0:T(8,128)(2,1)S(...) custom-call(s32[3]{0:T(128)S(1)} %pad_add_fusion.refs_0_.where, ...), custom_call_target="tpu_custom_call" | custom-call | flops 536870912 | bytes 4980748 | tf_op jit(solution)/shard_map/hidden_terms/pallas_call | solution.py:134
  27.3 2.0 %collective-permute-start.9 = (bf16[512,128]{1,0:T(8,128)(2,1)S(1)}, bf16[512,128]{1,0:T(8,128)(2,1)S(1)}, u32[]{:S(2)}, u32[]{:S(2)}) collective-permute-start(bf16[512,128]{1,0:T(8,128)(2,1)S(1)} %get-tuple-element.74), channel_id=1, source_target_pairs={{0,4},{2,6},{4,0},{6,2},{1,5},{3,7},{5,1},{7,3},{8,12},{10,14},{12... | collective-permute-start | bytes 393224 | tf_op jit(solution)/shard_map/ppermute | solution.py:28
  29.8 1.8 %collective-permute-done.14.refs_5_.refs_10_.refs_12_ = bf16[1024,128]{1,0:T(8,128)(2,1)S(1)} collective-permute-done((bf16[1024,128]{1,0:T(8,128)(2,1)S(1)}, bf16[1024,128]{1,0:T(8,128)(2,1)S(1)}, u32[]{:S(2)}, u32[]{:S(2)}) %collective-permute-start.14) | collective-permute-done | bytes 262176 | tf_op jit(solution)/shard_map/ppermute | solution.py:28
  31.6 1.3 %collective-permute-start.19 = (bf16[1024,128]{1,0:T(8,128)(2,1)S(1)}, bf16[1024,128]{1,0:T(8,128)(2,1)S(1)}, u32[]{:S(2)}, u32[]{:S(2)}) collective-permute-start(bf16[1024,128]{1,0:T(8,128)(2,1)S(1)} %collective-permute-done.12.refs_2_.refs_6_.refs_8_), channel_id=1, source_target_pairs={{0,16},{8,24},{16,0},{24,8},{1,17},{9,25},{17,1},{25,9},{2,18},{10... | collective-permute-start | bytes 786440 | tf_op jit(solution)/shard_map/ppermute | solution.py:28
  33.9 1.2 %collective-permute-start.20 = (bf16[1024,128]{1,0:T(8,128)(2,1)S(1)}, bf16[1024,128]{1,0:T(8,128)(2,1)S(1)}, u32[]{:S(2)}, u32[]{:S(2)}) collective-permute-start(bf16[1024,128]{1,0:T(8,128)(2,1)S(1)} %collective-permute-done.15.refs_6_.refs_11_.refs_13_), channel_id=1, source_target_pairs={{0,8},{8,0},{16,24},{24,16},{1,9},{9,1},{17,25},{25,17},{2,10},{10... | collective-permute-start | bytes 786440 | tf_op jit(solution)/shard_map/ppermute | solution.py:28
  35.1 1.5 %mlp_forward.1 = (bf16[128,4096]{1,0:T(8,128)(2,1)S(1)}, f32[128,128]{1,0:T(8,128)S(1)}, f32[128,256]{1,0:T(8,128)S(1)}, bf16[128,1024]{1,0:T(8,128)(2,1)S(1)}) custom-call(s32[3]{0:T(128)S(1)} %pad_add_fusion.refs_0_.where, bf16[1024,128]{1,0:T(8,128)(2,1)S(1)} %copy-done, bf16[1024,128]{1,0:T(8,128)(2,1)S(1)} %collective-permute-done.12.refs_2_.refs_6_.refs_8_, ...), custom_call_target="tpu_custom_call" | custom-call | flops 268435456 | bytes 4136972 | tf_op jit(solution)/shard_map/mlp_forward/pallas_call | solution.py:134
  37.1 4.2 %collective-permute-done.11.refs_4_ = bf16[512,128]{1,0:T(8,128)(2,1)S(1)} collective-permute-done((bf16[512,128]{1,0:T(8,128)(2,1)S(1)}, bf16[512,128]{1,0:T(8,128)(2,1)S(1)}, u32[]{:S(2)}, u32[]{:S(2)}) %collective-permute-start.11) | collective-permute-done | bytes 131104 | tf_op jit(solution)/shard_map/ppermute | solution.py:28
  41.9 1.3 %collective-permute-start.16 = (bf16[128,640]{1,0:T(8,128)(2,1)S(1)}, bf16[128,640]{1,0:T(8,128)(2,1)S(1)}, u32[]{:S(2)}, u32[]{:S(2)}) collective-permute-start(bf16[128,640]{1,0:T(8,128)(2,1)S(1)} %get-tuple-element.91), channel_id=1, source_target_pairs={{0,8},{8,0},{16,24},{24,16},{1,9},{9,1},{17,25},{25,17},{2,10},{10... | collective-permute-start | bytes 491528 | tf_op jit(solution)/shard_map/ppermute | solution.py:28
  43.2 1.2 %collective-permute-start.17 = (bf16[128,640]{1,0:T(8,128)(2,1)S(1)}, bf16[128,640]{1,0:T(8,128)(2,1)S(1)}, u32[]{:S(2)}, u32[]{:S(2)}) collective-permute-start(bf16[128,640]{1,0:T(8,128)(2,1)S(1)} %get-tuple-element.92), channel_id=1, source_target_pairs={{0,16},{8,24},{16,0},{24,8},{1,17},{9,25},{17,1},{25,9},{2,18},{10... | collective-permute-start | bytes 491528 | tf_op jit(solution)/shard_map/ppermute | solution.py:28
  46.1 1.5 %collective-permute-done.17.refs_3_.refs_4_ = bf16[128,640]{1,0:T(8,128)(2,1)S(1)} collective-permute-done((bf16[128,640]{1,0:T(8,128)(2,1)S(1)}, bf16[128,640]{1,0:T(8,128)(2,1)S(1)}, u32[]{:S(2)}, u32[]{:S(2)}) %collective-permute-start.17) | collective-permute-done | bytes 163872 | tf_op jit(solution)/shard_map/ppermute | solution.py:28
  47.6 3.8 %collective-permute-done.18.refs_4_.refs_5_ = bf16[128,640]{1,0:T(8,128)(2,1)S(1)} collective-permute-done((bf16[128,640]{1,0:T(8,128)(2,1)S(1)}, bf16[128,640]{1,0:T(8,128)(2,1)S(1)}, u32[]{:S(2)}, u32[]{:S(2)}) %collective-permute-start.18) | collective-permute-done | bytes 163872 | tf_op jit(solution)/shard_map/ppermute | solution.py:28
  51.7 1.4 %mlp_backward.1 = (bf16[4,128,512]{2,1,0:T(8,128)(2,1)S(1)}, bf16[128,256]{1,0:T(8,128)(2,1)S(1)}, f32[128,128]{1,0:T(8,128)S(1)}) custom-call(s32[3]{0:T(128)S(1)} %pad_add_fusion.refs_0_.where, f32[128,128]{1,0:T(8,128)S(1)} %get-tuple-element.98.refs_1_, bf16[128,640]{1,0:T(8,128)(2,1)S(1)} %collective-permute-done.16.refs_2_.refs_3_, ...), custom_call_target="tpu_custom_call" | custom-call | flops 134217728 | bytes 4825100 | tf_op jit(solution)/shard_map/mlp_backward/pallas_call | solution.py:134
  53.1 2.9 %collective-permute-start.21 = (bf16[4,128,512]{2,1,0:T(8,128)(2,1)S(1)}, bf16[4,128,512]{2,1,0:T(8,128)(2,1)S(1)}, u32[]{:S(2)}, u32[]{:S(2)}) collective-permute-start(bf16[4,128,512]{2,1,0:T(8,128)(2,1)S(1)} %get-tuple-element.109), channel_id=1, source_target_pairs={{0,1},{1,0},{2,3},{3,2},{4,5},{5,4},{6,7},{7,6},{8,9},{9,8},{10,11... | collective-permute-start | bytes 1572872 | tf_op jit(solution)/shard_map/ppermute | solution.py:28
  58.8 1.7 %collective-permute-start.23 = (bf16[128,512]{1,0:T(8,128)(2,1)S(1)}, bf16[128,512]{1,0:T(8,128)(2,1)S(1)}, u32[]{:S(2)}, u32[]{:S(2)}) collective-permute-start(bf16[128,512]{1,0:T(8,128)(2,1)S(1)} %get-tuple-element.122), channel_id=1, source_target_pairs={{0,2},{2,0},{4,6},{6,4},{1,3},{3,1},{5,7},{7,5},{8,10},{10,8},{12,... | collective-permute-start | bytes 393224 | tf_op jit(solution)/shard_map/ppermute | solution.py:28
  61.1 5.9 %collective-permute-done.25 = bf16[128,512]{1,0:T(8,128)(2,1)S(1)} collective-permute-done((bf16[128,512]{1,0:T(8,128)(2,1)S(1)}, bf16[128,512]{1,0:T(8,128)(2,1)S(1)}, u32[]{:S(2)}, u32[]{:S(2)}) %collective-permute-start.25) | collective-permute-done | bytes 131104 | tf_op jit(solution)/shard_map/ppermute | solution.py:28
  67.0 3.0 %collective-permute-done.24 = bf16[128,512]{1,0:T(8,128)(2,1)S(1)} collective-permute-done((bf16[128,512]{1,0:T(8,128)(2,1)S(1)}, bf16[128,512]{1,0:T(8,128)(2,1)S(1)}, u32[]{:S(2)}, u32[]{:S(2)}) %collective-permute-start.24) | collective-permute-done | bytes 131104 | tf_op jit(solution)/shard_map/ppermute | solution.py:28
  70.9 2.0 %collective-permute-start.27 = (bf16[128,512]{1,0:T(8,128)(2,1)S(1)}, bf16[128,512]{1,0:T(8,128)(2,1)S(1)}, u32[]{:S(2)}, u32[]{:S(2)}) collective-permute-start(bf16[128,512]{1,0:T(8,128)(2,1)S(1)} %fusion.2.refs_1_), channel_id=1, source_target_pairs={{0,2},{2,0},{4,6},{6,4},{1,3},{3,1},{5,7},{7,5},{8,10},{10,8},{12,... | collective-permute-start | bytes 393224 | tf_op jit(solution)/shard_map/ppermute | solution.py:28
  74.9 3.1 %collective-permute-done.27.refs_2_ = bf16[128,512]{1,0:T(8,128)(2,1)S(1)} collective-permute-done((bf16[128,512]{1,0:T(8,128)(2,1)S(1)}, bf16[128,512]{1,0:T(8,128)(2,1)S(1)}, u32[]{:S(2)}, u32[]{:S(2)}) %collective-permute-start.27) | collective-permute-done | bytes 131104 | tf_op jit(solution)/shard_map/ppermute | solution.py:28
  79.0 1.3 %kv_grad.1 = bf16[1024,512]{1,0:T(8,128)(2,1)S(1)} custom-call(s32[3]{0:T(128)S(1)} %pad_add_fusion.refs_0_.where, bf16[128,512]{1,0:T(8,128)(2,1)S(1)} %bitcast.31, bf16[128,512]{1,0:T(8,128)(2,1)S(1)} %collective-permute-done.refs_2_, bf16[128,512]{1,0:T(8,128)(2,1)S(1)} %collective-permute-done.1.refs_3_, ...), custom_call_target="tpu_custom_call" | custom-call | flops 536870912 | bytes 2621452 | tf_op jit(solution)/shard_map/kv_grad/pallas_call | solution.py:134
  82.4 3.9 %collective-permute-done.29.refs_4_ = bf16[128,512]{1,0:T(8,128)(2,1)S(1)} collective-permute-done((bf16[128,512]{1,0:T(8,128)(2,1)S(1)}, bf16[128,512]{1,0:T(8,128)(2,1)S(1)}, u32[]{:S(2)}, u32[]{:S(2)}) %collective-permute-start.29) | collective-permute-done | bytes 131104 | tf_op jit(solution)/shard_map/ppermute | solution.py:28
  88.6 1.6 %input_grad.1 = bf16[128,4096]{1,0:T(8,128)(2,1)} custom-call(s32[3]{0:T(128)S(1)} %pad_add_fusion.refs_0_.where, bf16[128,512]{1,0:T(8,128)(2,1)S(1)} %fusion.2.refs_1_, bf16[128,512]{1,0:T(8,128)(2,1)S(1)} %collective-permute-done.27.refs_2_, bf16[128,512]{1,0:T(8,128)(2,1)S(1)} %collective-permute-done.28.refs_3_, ...), custom_call_target="tpu_custom_call" | custom-call | bytes 2097164 | tf_op jit(solution)/shard_map/input_grad/pallas_call | solution.py:134
  (72 shorter events, 23.1 us)
Async XLA Ops:
  0.6 14.2 %collective-permute-start.3 = (bf16[128,1024]{1,0:T(8,128)(2,1)}, bf16[128,1024]{1,0:T(8,128)(2,1)S(1)}, u32[]{:S(2)}, u32[]{:S(2)}) collective-permute-start(bf16[128,1024]{1,0:T(8,128)(2,1)} %refs_3_.1), channel_id=1, source_target_pairs={{0,4},{2,6},{4,0},{6,2},{1,5},{3,7},{5,1},{7,3},{8,12},{10,14},{12... | collective-permute-start | bytes 786440 | tf_op jit(solution)/shard_map/ppermute | solution.py:28
  3.0 11.8 %collective-permute-start.4 = (bf16[128,1024]{1,0:T(8,128)(2,1)}, bf16[128,1024]{1,0:T(8,128)(2,1)S(1)}, u32[]{:S(2)}, u32[]{:S(2)}) collective-permute-start(bf16[128,1024]{1,0:T(8,128)(2,1)} %refs_3_.1), channel_id=1, source_target_pairs={{0,2},{2,0},{4,6},{6,4},{1,3},{3,1},{5,7},{7,5},{8,10},{10,8},{12,... | collective-permute-start | bytes 786440 | tf_op jit(solution)/shard_map/ppermute | solution.py:28
  4.1 4.3 %collective-permute-start = (bf16[128,512]{1,0:T(8,128)(2,1)S(1)}, bf16[128,512]{1,0:T(8,128)(2,1)S(1)}, u32[]{:S(2)}, u32[]{:S(2)}) collective-permute-start(bf16[128,512]{1,0:T(8,128)(2,1)S(1)} %bitcast.27), channel_id=1, source_target_pairs={{0,8},{8,0},{16,24},{24,16},{1,9},{9,1},{17,25},{25,17},{2,10},{10... | collective-permute-start | bytes 393224 | tf_op jit(solution)/shard_map/ppermute | solution.py:28
  5.4 4.1 %collective-permute-start.1 = (bf16[128,512]{1,0:T(8,128)(2,1)S(1)}, bf16[128,512]{1,0:T(8,128)(2,1)S(1)}, u32[]{:S(2)}, u32[]{:S(2)}) collective-permute-start(bf16[128,512]{1,0:T(8,128)(2,1)S(1)} %bitcast.28), channel_id=1, source_target_pairs={{0,16},{8,24},{16,0},{24,8},{1,17},{9,25},{17,1},{25,9},{2,18},{10... | collective-permute-start | bytes 393224 | tf_op jit(solution)/shard_map/ppermute | solution.py:28
  6.6 5.5 %collective-permute-start.2 = (bf16[128,512]{1,0:T(8,128)(2,1)S(1)}, bf16[128,512]{1,0:T(8,128)(2,1)S(1)}, u32[]{:S(2)}, u32[]{:S(2)}) collective-permute-start(bf16[128,512]{1,0:T(8,128)(2,1)S(1)} %bitcast.29), channel_id=1, source_target_pairs={{0,24},{8,16},{16,8},{24,0},{1,25},{9,17},{17,9},{25,1},{2,26},{10... | collective-permute-start | bytes 393224 | tf_op jit(solution)/shard_map/ppermute | solution.py:28
  16.2 7.0 %collective-permute-start.5 = (bf16[512,1024]{1,0:T(8,128)(2,1)S(1)}, bf16[512,1024]{1,0:T(8,128)(2,1)S(1)}, u32[]{:S(2)}, u32[]{:S(2)}) collective-permute-start(bf16[512,1024]{1,0:T(8,128)(2,1)S(1)} %upstream_terms.1.refs_1_), channel_id=1, source_target_pairs={{0,1},{1,0},{2,3},{3,2},{4,5},{5,4},{6,7},{7,6},{8,9},{9,8},{10,11... | collective-permute-start | bytes 3145736 | tf_op jit(solution)/shard_map/ppermute | solution.py:28
  17.8 4.2 %collective-permute-start.7 = (bf16[128,2048]{1,0:T(8,128)(2,1)S(1)}, bf16[128,2048]{1,0:T(8,128)(2,1)S(1)}, u32[]{:S(2)}, u32[]{:S(2)}) collective-permute-start(bf16[128,2048]{1,0:T(8,128)(2,1)S(1)} %copy-done.2), channel_id=1, source_target_pairs={{0,1},{1,0},{2,3},{3,2},{4,5},{5,4},{6,7},{7,6},{8,9},{9,8},{10,11... | collective-permute-start | bytes 1572872 | tf_op jit(solution)/shard_map/ppermute | solution.py:28
  18.2 7.9 %collective-permute-start.10 = (bf16[128,1024]{1,0:T(8,128)(2,1)S(1)}, bf16[128,1024]{1,0:T(8,128)(2,1)S(1)}, u32[]{:S(2)}, u32[]{:S(2)}) collective-permute-start(bf16[128,1024]{1,0:T(8,128)(2,1)S(1)} %collective-permute-done.3.refs_5_), channel_id=1, source_target_pairs={{0,2},{2,0},{4,6},{6,4},{1,3},{3,1},{5,7},{7,5},{8,10},{10,8},{12,... | collective-permute-start | bytes 786440 | tf_op jit(solution)/shard_map/ppermute | solution.py:28
  18.5 8.8 %collective-permute-start.12 = (bf16[1024,128]{1,0:T(8,128)(2,1)S(1)}, bf16[1024,128]{1,0:T(8,128)(2,1)S(1)}, u32[]{:S(2)}, u32[]{:S(2)}) collective-permute-start(bf16[1024,128]{1,0:T(8,128)(2,1)S(1)} %copy-done), channel_id=1, source_target_pairs={{0,8},{8,0},{16,24},{24,16},{1,9},{9,1},{17,25},{25,17},{2,10},{10... | collective-permute-start | bytes 786440 | tf_op jit(solution)/shard_map/ppermute | solution.py:28
  20.7 8.7 %collective-permute-start.13 = (bf16[1024,128]{1,0:T(8,128)(2,1)S(1)}, bf16[1024,128]{1,0:T(8,128)(2,1)S(1)}, u32[]{:S(2)}, u32[]{:S(2)}) collective-permute-start(bf16[1024,128]{1,0:T(8,128)(2,1)S(1)} %copy-done), channel_id=1, source_target_pairs={{0,16},{8,24},{16,0},{24,8},{1,17},{9,25},{17,1},{25,9},{2,18},{10... | collective-permute-start | bytes 786440 | tf_op jit(solution)/shard_map/ppermute | solution.py:28
  22.0 9.7 %collective-permute-start.14 = (bf16[1024,128]{1,0:T(8,128)(2,1)S(1)}, bf16[1024,128]{1,0:T(8,128)(2,1)S(1)}, u32[]{:S(2)}, u32[]{:S(2)}) collective-permute-start(bf16[1024,128]{1,0:T(8,128)(2,1)S(1)} %copy-done.1), channel_id=1, source_target_pairs={{0,8},{8,0},{16,24},{24,16},{1,9},{9,1},{17,25},{25,17},{2,10},{10... | collective-permute-start | bytes 786440 | tf_op jit(solution)/shard_map/ppermute | solution.py:28
  23.2 10.7 %collective-permute-start.15 = (bf16[1024,128]{1,0:T(8,128)(2,1)S(1)}, bf16[1024,128]{1,0:T(8,128)(2,1)S(1)}, u32[]{:S(2)}, u32[]{:S(2)}) collective-permute-start(bf16[1024,128]{1,0:T(8,128)(2,1)S(1)} %copy-done.1), channel_id=1, source_target_pairs={{0,16},{8,24},{16,0},{24,8},{1,17},{9,25},{17,1},{25,9},{2,18},{10... | collective-permute-start | bytes 786440 | tf_op jit(solution)/shard_map/ppermute | solution.py:28
  26.1 10.5 %collective-permute-start.8 = (bf16[512,128]{1,0:T(8,128)(2,1)S(1)}, bf16[512,128]{1,0:T(8,128)(2,1)S(1)}, u32[]{:S(2)}, u32[]{:S(2)}) collective-permute-start(bf16[512,128]{1,0:T(8,128)(2,1)S(1)} %get-tuple-element.73), channel_id=1, source_target_pairs={{0,2},{2,0},{4,6},{6,4},{1,3},{3,1},{5,7},{7,5},{8,10},{10,8},{12,... | collective-permute-start | bytes 393224 | tf_op jit(solution)/shard_map/ppermute | solution.py:28
  27.3 9.8 %collective-permute-start.9 = (bf16[512,128]{1,0:T(8,128)(2,1)S(1)}, bf16[512,128]{1,0:T(8,128)(2,1)S(1)}, u32[]{:S(2)}, u32[]{:S(2)}) collective-permute-start(bf16[512,128]{1,0:T(8,128)(2,1)S(1)} %get-tuple-element.74), channel_id=1, source_target_pairs={{0,4},{2,6},{4,0},{6,2},{1,5},{3,7},{5,1},{7,3},{8,12},{10,14},{12... | collective-permute-start | bytes 393224 | tf_op jit(solution)/shard_map/ppermute | solution.py:28
  29.4 11.9 %collective-permute-start.11 = (bf16[512,128]{1,0:T(8,128)(2,1)S(1)}, bf16[512,128]{1,0:T(8,128)(2,1)S(1)}, u32[]{:S(2)}, u32[]{:S(2)}) collective-permute-start(bf16[512,128]{1,0:T(8,128)(2,1)S(1)} %hidden_last.1), channel_id=1, source_target_pairs={{0,6},{2,4},{4,2},{6,0},{1,7},{3,5},{5,3},{7,1},{8,14},{10,12},{12... | collective-permute-start | bytes 393224 | tf_op jit(solution)/shard_map/ppermute | solution.py:28
  31.6 20.0 %collective-permute-start.19 = (bf16[1024,128]{1,0:T(8,128)(2,1)S(1)}, bf16[1024,128]{1,0:T(8,128)(2,1)S(1)}, u32[]{:S(2)}, u32[]{:S(2)}) collective-permute-start(bf16[1024,128]{1,0:T(8,128)(2,1)S(1)} %collective-permute-done.12.refs_2_.refs_6_.refs_8_), channel_id=1, source_target_pairs={{0,16},{8,24},{16,0},{24,8},{1,17},{9,25},{17,1},{25,9},{2,18},{10... | collective-permute-start | bytes 786440 | tf_op jit(solution)/shard_map/ppermute | solution.py:28
  33.9 17.8 %collective-permute-start.20 = (bf16[1024,128]{1,0:T(8,128)(2,1)S(1)}, bf16[1024,128]{1,0:T(8,128)(2,1)S(1)}, u32[]{:S(2)}, u32[]{:S(2)}) collective-permute-start(bf16[1024,128]{1,0:T(8,128)(2,1)S(1)} %collective-permute-done.15.refs_6_.refs_11_.refs_13_), channel_id=1, source_target_pairs={{0,8},{8,0},{16,24},{24,16},{1,9},{9,1},{17,25},{25,17},{2,10},{10... | collective-permute-start | bytes 786440 | tf_op jit(solution)/shard_map/ppermute | solution.py:28
  41.9 4.2 %collective-permute-start.16 = (bf16[128,640]{1,0:T(8,128)(2,1)S(1)}, bf16[128,640]{1,0:T(8,128)(2,1)S(1)}, u32[]{:S(2)}, u32[]{:S(2)}) collective-permute-start(bf16[128,640]{1,0:T(8,128)(2,1)S(1)} %get-tuple-element.91), channel_id=1, source_target_pairs={{0,8},{8,0},{16,24},{24,16},{1,9},{9,1},{17,25},{25,17},{2,10},{10... | collective-permute-start | bytes 491528 | tf_op jit(solution)/shard_map/ppermute | solution.py:28
  43.2 4.5 %collective-permute-start.17 = (bf16[128,640]{1,0:T(8,128)(2,1)S(1)}, bf16[128,640]{1,0:T(8,128)(2,1)S(1)}, u32[]{:S(2)}, u32[]{:S(2)}) collective-permute-start(bf16[128,640]{1,0:T(8,128)(2,1)S(1)} %get-tuple-element.92), channel_id=1, source_target_pairs={{0,16},{8,24},{16,0},{24,8},{1,17},{9,25},{17,1},{25,9},{2,18},{10... | collective-permute-start | bytes 491528 | tf_op jit(solution)/shard_map/ppermute | solution.py:28
  44.4 7.0 %collective-permute-start.18 = (bf16[128,640]{1,0:T(8,128)(2,1)S(1)}, bf16[128,640]{1,0:T(8,128)(2,1)S(1)}, u32[]{:S(2)}, u32[]{:S(2)}) collective-permute-start(bf16[128,640]{1,0:T(8,128)(2,1)S(1)} %get-tuple-element.93), channel_id=1, source_target_pairs={{0,24},{8,16},{16,8},{24,0},{1,25},{9,17},{17,9},{25,1},{2,26},{10... | collective-permute-start | bytes 491528 | tf_op jit(solution)/shard_map/ppermute | solution.py:28
  51.5 5.6 %collective-permute-start.22 = (bf16[256,512]{1,0:T(8,128)(2,1)S(1)}, bf16[256,512]{1,0:T(8,128)(2,1)S(1)}, u32[]{:S(2)}, u32[]{:S(2)}) collective-permute-start(bf16[256,512]{1,0:T(8,128)(2,1)S(1)} %get-tuple-element.111), channel_id=1, source_target_pairs={{0,8},{8,0},{16,24},{24,16},{1,9},{9,1},{17,25},{25,17},{2,10},{10... | collective-permute-start | bytes 786440 | tf_op jit(solution)/shard_map/ppermute | solution.py:28
  53.1 4.5 %collective-permute-start.21 = (bf16[4,128,512]{2,1,0:T(8,128)(2,1)S(1)}, bf16[4,128,512]{2,1,0:T(8,128)(2,1)S(1)}, u32[]{:S(2)}, u32[]{:S(2)}) collective-permute-start(bf16[4,128,512]{2,1,0:T(8,128)(2,1)S(1)} %get-tuple-element.109), channel_id=1, source_target_pairs={{0,1},{1,0},{2,3},{3,2},{4,5},{5,4},{6,7},{7,6},{8,9},{9,8},{10,11... | collective-permute-start | bytes 1572872 | tf_op jit(solution)/shard_map/ppermute | solution.py:28
  57.8 9.2 %collective-permute-start.25 = (bf16[128,512]{1,0:T(8,128)(2,1)S(1)}, bf16[128,512]{1,0:T(8,128)(2,1)S(1)}, u32[]{:S(2)}, u32[]{:S(2)}) collective-permute-start(bf16[128,512]{1,0:T(8,128)(2,1)S(1)} %get-tuple-element.123), channel_id=1, source_target_pairs={{0,6},{2,4},{4,2},{6,0},{1,7},{3,5},{5,3},{7,1},{8,14},{10,12},{12... | collective-permute-start | bytes 393224 | tf_op jit(solution)/shard_map/ppermute | solution.py:28
  58.8 11.1 %collective-permute-start.24 = (bf16[128,512]{1,0:T(8,128)(2,1)S(1)}, bf16[128,512]{1,0:T(8,128)(2,1)S(1)}, u32[]{:S(2)}, u32[]{:S(2)}) collective-permute-start(bf16[128,512]{1,0:T(8,128)(2,1)S(1)} %get-tuple-element.124), channel_id=1, source_target_pairs={{0,4},{2,6},{4,0},{6,2},{1,5},{3,7},{5,1},{7,3},{8,12},{10,14},{12... | collective-permute-start | bytes 393224 | tf_op jit(solution)/shard_map/ppermute | solution.py:28
  58.8 11.1 %collective-permute-start.23 = (bf16[128,512]{1,0:T(8,128)(2,1)S(1)}, bf16[128,512]{1,0:T(8,128)(2,1)S(1)}, u32[]{:S(2)}, u32[]{:S(2)}) collective-permute-start(bf16[128,512]{1,0:T(8,128)(2,1)S(1)} %get-tuple-element.122), channel_id=1, source_target_pairs={{0,2},{2,0},{4,6},{6,4},{1,3},{3,1},{5,7},{7,5},{8,10},{10,8},{12,... | collective-permute-start | bytes 393224 | tf_op jit(solution)/shard_map/ppermute | solution.py:28
  60.5 9.5 %collective-permute-start.26 = (bf16[256,512]{1,0:T(8,128)(2,1)S(1)}, bf16[256,512]{1,0:T(8,128)(2,1)S(1)}, u32[]{:S(2)}, u32[]{:S(2)}) collective-permute-start(bf16[256,512]{1,0:T(8,128)(2,1)S(1)} %pad_maximum_fusion.1), channel_id=1, source_target_pairs={{0,16},{8,24},{16,0},{24,8},{1,17},{9,25},{17,1},{25,9},{2,18},{10... | collective-permute-start | bytes 786440 | tf_op jit(solution)/shard_map/ppermute | solution.py:28
  70.1 8.9 %collective-permute-start.30 = (bf16[512,512]{1,0:T(8,128)(2,1)S(1)}, bf16[512,512]{1,0:T(8,128)(2,1)S(1)}, u32[]{:S(2)}, u32[]{:S(2)}) collective-permute-start(bf16[512,512]{1,0:T(8,128)(2,1)S(1)} %pad_maximum_fusion.refs_5_), channel_id=1, source_target_pairs={{0,1},{1,0},{2,3},{3,2},{4,5},{5,4},{6,7},{7,6},{8,9},{9,8},{10,11... | collective-permute-start | bytes 1572872 | tf_op jit(solution)/shard_map/ppermute | solution.py:28
  70.9 7.1 %collective-permute-start.27 = (bf16[128,512]{1,0:T(8,128)(2,1)S(1)}, bf16[128,512]{1,0:T(8,128)(2,1)S(1)}, u32[]{:S(2)}, u32[]{:S(2)}) collective-permute-start(bf16[128,512]{1,0:T(8,128)(2,1)S(1)} %fusion.2.refs_1_), channel_id=1, source_target_pairs={{0,2},{2,0},{4,6},{6,4},{1,3},{3,1},{5,7},{7,5},{8,10},{10,8},{12,... | collective-permute-start | bytes 393224 | tf_op jit(solution)/shard_map/ppermute | solution.py:28
  72.9 9.6 %collective-permute-start.28 = (bf16[128,512]{1,0:T(8,128)(2,1)S(1)}, bf16[128,512]{1,0:T(8,128)(2,1)S(1)}, u32[]{:S(2)}, u32[]{:S(2)}) collective-permute-start(bf16[128,512]{1,0:T(8,128)(2,1)S(1)} %fusion.2.refs_1_), channel_id=1, source_target_pairs={{0,4},{2,6},{4,0},{6,2},{1,5},{3,7},{5,1},{7,3},{8,12},{10,14},{12... | collective-permute-start | bytes 393224 | tf_op jit(solution)/shard_map/ppermute | solution.py:28
  74.0 12.4 %collective-permute-start.29 = (bf16[128,512]{1,0:T(8,128)(2,1)S(1)}, bf16[128,512]{1,0:T(8,128)(2,1)S(1)}, u32[]{:S(2)}, u32[]{:S(2)}) collective-permute-start(bf16[128,512]{1,0:T(8,128)(2,1)S(1)} %fusion.2.refs_1_), channel_id=1, source_target_pairs={{0,6},{2,4},{4,2},{6,0},{1,7},{3,5},{5,3},{7,1},{8,14},{10,12},{12... | collective-permute-start | bytes 393224 | tf_op jit(solution)/shard_map/ppermute | solution.py:28
  74.3 12.9 %collective-permute-start.31 = (bf16[128,512]{1,0:T(8,128)(2,1)S(1)}, bf16[128,512]{1,0:T(8,128)(2,1)S(1)}, u32[]{:S(2)}, u32[]{:S(2)}) collective-permute-start(bf16[128,512]{1,0:T(8,128)(2,1)S(1)} %fusion.2.refs_1_), channel_id=1, source_target_pairs={{0,1},{1,0},{2,3},{3,2},{4,5},{5,4},{6,7},{7,6},{8,9},{9,8},{10,11... | collective-permute-start | bytes 393224 | tf_op jit(solution)/shard_map/ppermute | solution.py:28
  78.0 9.2 %collective-permute-start.32 = (bf16[128,512]{1,0:T(8,128)(2,1)S(1)}, bf16[128,512]{1,0:T(8,128)(2,1)S(1)}, u32[]{:S(2)}, u32[]{:S(2)}) collective-permute-start(bf16[128,512]{1,0:T(8,128)(2,1)S(1)} %collective-permute-done.27.refs_2_), channel_id=1, source_target_pairs={{0,1},{1,0},{2,3},{3,2},{4,5},{5,4},{6,7},{7,6},{8,9},{9,8},{10,11... | collective-permute-start | bytes 393224 | tf_op jit(solution)/shard_map/ppermute | solution.py:28
  (9 other events, 35.2 us)

commit v9 on v7

--- a/solution.py
+++ b/solution.py
@@ -328,8 +328,9 @@
     x_other = send(mlp_input, TENSOR, 1)
     far, near = send(down_weight, PIPE, 2), send(down_weight, PIPE, 1)
     grads, gate, up = lax.optimization_barrier((grads, gate_weight, up_weight))
-    gates = [gate, send(gate, DP, 1), send(gate, DP, 2)]
-    ups = [up, send(up, DP, 1), send(up, DP, 2)]
+    far, first_gate, first_up = lax.optimization_barrier((far, gate_weight, up_weight))
+    gates = [gate, send(first_gate, DP, 1), send(gate, DP, 2)]
+    ups = [up, send(up, DP, 1), send(first_up, DP, 2)]
     grads, far, near = lax.optimization_barrier((grads, far, near))
     downs = [down_weight, near, far, send(far, PIPE, 1)]
 

time: 90.3 us -> 90.4 us (level)
  transfers between devices with their start and end apart: 35 -> 35, of which waited for: 20 -> 18; matrix products, arithmetic and copies ran while one was open for 4% -> 4% of each run, Pallas kernels for 10% -> 10%
where the time goes in v9:
time: 90.4 us; the launch traced here: 90.2 us
  waiting for transfers between devices  40.7 us (45%)
  starting transfers between devices  33 us (37%)
  Pallas kernels  11.7 us (13%)
  local copies, waits for them, and re-layouts  3.56 us (4%)
    ppermute x35, waiting for transfers between devices, send(): return lax.ppermute(value, axis, [(src, src ^ step) for src in range(size)])  40.7 us
    ppermute x35, starting transfers between devices, send(): return lax.ppermute(value, axis, [(src, src ^ step) for src in range(size)])  33 us
    pallas_call x10, Pallas kernels, call(): pl.pallas_call(body, name=name, out_shape=out, in_specs=specs, out_specs=...  11.7 us
    unnamed x14, local copies, waits for them, and re-layouts  2.39 us
  transfers between devices with their start and end apart: 35, of which 18 were waited for; matrix products, arithmetic and copies ran while one was open for 4% of the time, Pallas kernels for 10%

profile of v9, /device:TPU:9, one launch (start us, length us, event | category | flops | bytes accessed | tf_op | source)
XLA Modules:
  0.0 90.2 jit_solution(15520053868785144372)
XLA Ops:
  0.6 2.4 %collective-permute-start.3 = (bf16[128,1024]{1,0:T(8,128)(2,1)}, bf16[128,1024]{1,0:T(8,128)(2,1)S(1)}, u32[]{:S(2)}, u32[]{:S(2)}) collective-permute-start(bf16[128,1024]{1,0:T(8,128)(2,1)} %refs_3_.1), channel_id=1, source_target_pairs={{0,4},{2,6},{4,0},{6,2},{1,5},{3,7},{5,1},{7,3},{8,12},{10,14},{12... | collective-permute-start | bytes 786440 | tf_op jit(solution)/shard_map/ppermute | solution.py:28
  4.1 1.3 %collective-permute-start = (bf16[128,512]{1,0:T(8,128)(2,1)S(1)}, bf16[128,512]{1,0:T(8,128)(2,1)S(1)}, u32[]{:S(2)}, u32[]{:S(2)}) collective-permute-start(bf16[128,512]{1,0:T(8,128)(2,1)S(1)} %bitcast.27), channel_id=1, source_target_pairs={{0,8},{8,0},{16,24},{24,16},{1,9},{9,1},{17,25},{25,17},{2,10},{10... | collective-permute-start | bytes 393224 | tf_op jit(solution)/shard_map/ppermute | solution.py:28
  5.4 1.2 %collective-permute-start.1 = (bf16[128,512]{1,0:T(8,128)(2,1)S(1)}, bf16[128,512]{1,0:T(8,128)(2,1)S(1)}, u32[]{:S(2)}, u32[]{:S(2)}) collective-permute-start(bf16[128,512]{1,0:T(8,128)(2,1)S(1)} %bitcast.28), channel_id=1, source_target_pairs={{0,16},{8,24},{16,0},{24,8},{1,17},{9,25},{17,1},{25,9},{2,18},{10... | collective-permute-start | bytes 393224 | tf_op jit(solution)/shard_map/ppermute | solution.py:28
  6.8 1.4 %copy.12 = bf16[128,8,2,256]{3,1,2,0:T(8,128)(2,1)S(1)} copy(bf16[128,8,2,256]{3,2,1,0:T(2,128)(2,1)} %bitcast.32) | data formatting | bytes 2097152
  9.5 2.6 %collective-permute-done.2.refs_4_ = bf16[128,512]{1,0:T(8,128)(2,1)S(1)} collective-permute-done((bf16[128,512]{1,0:T(8,128)(2,1)S(1)}, bf16[128,512]{1,0:T(8,128)(2,1)S(1)}, u32[]{:S(2)}, u32[]{:S(2)}) %collective-permute-start.2) | collective-permute-done | bytes 131104 | tf_op jit(solution)/shard_map/ppermute | solution.py:28
  12.1 2.8 %collective-permute-done.3.refs_5_ = bf16[128,1024]{1,0:T(8,128)(2,1)S(1)} collective-permute-done((bf16[128,1024]{1,0:T(8,128)(2,1)}, bf16[128,1024]{1,0:T(8,128)(2,1)S(1)}, u32[]{:S(2)}, u32[]{:S(2)}) %collective-permute-start.3) | collective-permute-done | bytes 262176 | tf_op jit(solution)/shard_map/ppermute | solution.py:28
  14.9 1.3 %upstream_terms.1.refs_1_ = bf16[512,1024]{1,0:T(8,128)(2,1)S(1)} custom-call(s32[3]{0:T(128)S(1)} %pad_add_fusion.refs_0_, bf16[128,512]{1,0:T(8,128)(2,1)S(1)} %bitcast.30, bf16[128,512]{1,0:T(8,128)(2,1)S(1)} %collective-permute-done.refs_2_, bf16[128,512]{1,0:T(8,128)(2,1)S(1)} %collective-permute-done.1.refs_3_, ...), custom_call_target="tpu_custom_call" | custom-call | flops 536870912 | bytes 2621452 | tf_op jit(solution)/shard_map/upstream_terms/pallas_call | solution.py:134
  16.2 1.5 %collective-permute-start.5 = (bf16[512,1024]{1,0:T(8,128)(2,1)S(1)}, bf16[512,1024]{1,0:T(8,128)(2,1)S(1)}, u32[]{:S(2)}, u32[]{:S(2)}) collective-permute-start(bf16[512,1024]{1,0:T(8,128)(2,1)S(1)} %upstream_terms.1.refs_1_), channel_id=1, source_target_pairs={{0,1},{1,0},{2,3},{3,2},{4,5},{5,4},{6,7},{7,6},{8,9},{9,8},{10,11... | collective-permute-start | bytes 3145736 | tf_op jit(solution)/shard_map/ppermute | solution.py:28
  18.5 1.3 %collective-permute-start.13 = (bf16[1024,128]{1,0:T(8,128)(2,1)S(1)}, bf16[1024,128]{1,0:T(8,128)(2,1)S(1)}, u32[]{:S(2)}, u32[]{:S(2)}) collective-permute-start(bf16[1024,128]{1,0:T(8,128)(2,1)S(1)} %copy-done), channel_id=1, source_target_pairs={{0,16},{8,24},{16,0},{24,8},{1,17},{9,25},{17,1},{25,9},{2,18},{10... | collective-permute-start | bytes 786440 | tf_op jit(solution)/shard_map/ppermute | solution.py:28
  22.7 1.2 %collective-permute-start.15 = (bf16[1024,128]{1,0:T(8,128)(2,1)S(1)}, bf16[1024,128]{1,0:T(8,128)(2,1)S(1)}, u32[]{:S(2)}, u32[]{:S(2)}) collective-permute-start(bf16[1024,128]{1,0:T(8,128)(2,1)S(1)} %copy-done.1), channel_id=1, source_target_pairs={{0,16},{8,24},{16,0},{24,8},{1,17},{9,25},{17,1},{25,9},{2,18},{10... | collective-permute-start | bytes 786440 | tf_op jit(solution)/shard_map/ppermute | solution.py:28
  23.9 1.3 %hidden_terms.1 = (f32[512,128]{1,0:T(8,128)S(1)}, bf16[512,128]{1,0:T(8,128)(2,1)S(1)}, bf16[512,128]{1,0:T(8,128)(2,1)S(1)}, bf16[128,512]{1,0:T(8,128)(2,1)S(...) custom-call(s32[3]{0:T(128)S(1)} %pad_add_fusion.refs_0_, ...), custom_call_target="tpu_custom_call" | custom-call | flops 536870912 | bytes 3932172 | tf_op jit(solution)/shard_map/hidden_terms/pallas_call | solution.py:134
  27.3 2.1 %collective-permute-start.9 = (bf16[512,128]{1,0:T(8,128)(2,1)S(1)}, bf16[512,128]{1,0:T(8,128)(2,1)S(1)}, u32[]{:S(2)}, u32[]{:S(2)}) collective-permute-start(bf16[512,128]{1,0:T(8,128)(2,1)S(1)} %get-tuple-element.77), channel_id=1, source_target_pairs={{0,4},{2,6},{4,0},{6,2},{1,5},{3,7},{5,1},{7,3},{8,12},{10,14},{12... | collective-permute-start | bytes 393224 | tf_op jit(solution)/shard_map/ppermute | solution.py:28
  29.8 4.0 %collective-permute-done.12.refs_2_.refs_6_.refs_8_ = bf16[1024,128]{1,0:T(8,128)(2,1)S(1)} collective-permute-done((bf16[1024,128]{1,0:T(8,128)(2,1)S(1)}, bf16[1024,128]{1,0:T(8,128)(2,1)S(1)}, u32[]{:S(2)}, u32[]{:S(2)}) %collective-permute-start.12) | collective-permute-done | bytes 262176 | tf_op jit(solution)/shard_map/ppermute | solution.py:28
  33.9 1.2 %collective-permute-start.19 = (bf16[1024,128]{1,0:T(8,128)(2,1)S(1)}, bf16[1024,128]{1,0:T(8,128)(2,1)S(1)}, u32[]{:S(2)}, u32[]{:S(2)}) collective-permute-start(bf16[1024,128]{1,0:T(8,128)(2,1)S(1)} %collective-permute-done.12.refs_2_.refs_6_.refs_8_), channel_id=1, source_target_pairs={{0,16},{8,24},{16,0},{24,8},{1,17},{9,25},{17,1},{25,9},{2,18},{10... | collective-permute-start | bytes 786440 | tf_op jit(solution)/shard_map/ppermute | solution.py:28
  36.3 1.5 %mlp_forward.1 = (bf16[128,4096]{1,0:T(8,128)(2,1)S(1)}, f32[128,128]{1,0:T(8,128)S(1)}, f32[128,256]{1,0:T(8,128)S(1)}, bf16[128,1024]{1,0:T(8,128)(2,1)S(1)}) custom-call(s32[3]{0:T(128)S(1)} %pad_add_fusion.refs_0_, bf16[1024,128]{1,0:T(8,128)(2,1)S(1)} %copy-done, bf16[1024,128]{1,0:T(8,128)(2,1)S(1)} %collective-permute-done.12.refs_2_.refs_6_.refs_8_, ...), custom_call_target="tpu_custom_call" | custom-call | flops 268435456 | bytes 4136972 | tf_op jit(solution)/shard_map/mlp_forward/pallas_call | solution.py:134
  37.8 3.5 %collective-permute-done.11.refs_4_ = bf16[512,128]{1,0:T(8,128)(2,1)S(1)} collective-permute-done((bf16[512,128]{1,0:T(8,128)(2,1)S(1)}, bf16[512,128]{1,0:T(8,128)(2,1)S(1)}, u32[]{:S(2)}, u32[]{:S(2)}) %collective-permute-start.11) | collective-permute-done | bytes 131104 | tf_op jit(solution)/shard_map/ppermute | solution.py:28
  41.9 1.3 %collective-permute-start.16 = (bf16[128,640]{1,0:T(8,128)(2,1)S(1)}, bf16[128,640]{1,0:T(8,128)(2,1)S(1)}, u32[]{:S(2)}, u32[]{:S(2)}) collective-permute-start(bf16[128,640]{1,0:T(8,128)(2,1)S(1)} %get-tuple-element.95), channel_id=1, source_target_pairs={{0,8},{8,0},{16,24},{24,16},{1,9},{9,1},{17,25},{25,17},{2,10},{10... | collective-permute-start | bytes 491528 | tf_op jit(solution)/shard_map/ppermute | solution.py:28
  43.2 1.2 %collective-permute-start.17 = (bf16[128,640]{1,0:T(8,128)(2,1)S(1)}, bf16[128,640]{1,0:T(8,128)(2,1)S(1)}, u32[]{:S(2)}, u32[]{:S(2)}) collective-permute-start(bf16[128,640]{1,0:T(8,128)(2,1)S(1)} %get-tuple-element.96), channel_id=1, source_target_pairs={{0,16},{8,24},{16,0},{24,8},{1,17},{9,25},{17,1},{25,9},{2,18},{10... | collective-permute-start | bytes 491528 | tf_op jit(solution)/shard_map/ppermute | solution.py:28
  46.2 1.5 %collective-permute-done.17.refs_3_.refs_4_ = bf16[128,640]{1,0:T(8,128)(2,1)S(1)} collective-permute-done((bf16[128,640]{1,0:T(8,128)(2,1)S(1)}, bf16[128,640]{1,0:T(8,128)(2,1)S(1)}, u32[]{:S(2)}, u32[]{:S(2)}) %collective-permute-start.17) | collective-permute-done | bytes 163872 | tf_op jit(solution)/shard_map/ppermute | solution.py:28
  47.7 3.8 %collective-permute-done.18.refs_4_.refs_5_ = bf16[128,640]{1,0:T(8,128)(2,1)S(1)} collective-permute-done((bf16[128,640]{1,0:T(8,128)(2,1)S(1)}, bf16[128,640]{1,0:T(8,128)(2,1)S(1)}, u32[]{:S(2)}, u32[]{:S(2)}) %collective-permute-start.18) | collective-permute-done | bytes 163872 | tf_op jit(solution)/shard_map/ppermute | solution.py:28
  51.7 1.4 %mlp_backward.1 = (bf16[4,128,512]{2,1,0:T(8,128)(2,1)S(1)}, bf16[128,256]{1,0:T(8,128)(2,1)S(1)}, f32[128,128]{1,0:T(8,128)S(1)}) custom-call(s32[3]{0:T(128)S(1)} %pad_add_fusion.refs_0_, f32[128,128]{1,0:T(8,128)S(1)} %get-tuple-element.102.refs_1_, bf16[128,640]{1,0:T(8,128)(2,1)S(1)} %collective-permute-done.16.refs_2_.refs_3_, ...), custom_call_target="tpu_custom_call" | custom-call | flops 134217728 | bytes 4825100 | tf_op jit(solution)/shard_map/mlp_backward/pallas_call | solution.py:134
  53.1 2.9 %collective-permute-start.21 = (bf16[4,128,512]{2,1,0:T(8,128)(2,1)S(1)}, bf16[4,128,512]{2,1,0:T(8,128)(2,1)S(1)}, u32[]{:S(2)}, u32[]{:S(2)}) collective-permute-start(bf16[4,128,512]{2,1,0:T(8,128)(2,1)S(1)} %get-tuple-element.113), channel_id=1, source_target_pairs={{0,1},{1,0},{2,3},{3,2},{4,5},{5,4},{6,7},{7,6},{8,9},{9,8},{10,11... | collective-permute-start | bytes 1572872 | tf_op jit(solution)/shard_map/ppermute | solution.py:28
  58.9 1.7 %collective-permute-start.23 = (bf16[128,512]{1,0:T(8,128)(2,1)S(1)}, bf16[128,512]{1,0:T(8,128)(2,1)S(1)}, u32[]{:S(2)}, u32[]{:S(2)}) collective-permute-start(bf16[128,512]{1,0:T(8,128)(2,1)S(1)} %get-tuple-element.126), channel_id=1, source_target_pairs={{0,2},{2,0},{4,6},{6,4},{1,3},{3,1},{5,7},{7,5},{8,10},{10,8},{12,... | collective-permute-start | bytes 393224 | tf_op jit(solution)/shard_map/ppermute | solution.py:28
  61.1 6.0 %collective-permute-done.25 = bf16[128,512]{1,0:T(8,128)(2,1)S(1)} collective-permute-done((bf16[128,512]{1,0:T(8,128)(2,1)S(1)}, bf16[128,512]{1,0:T(8,128)(2,1)S(1)}, u32[]{:S(2)}, u32[]{:S(2)}) %collective-permute-start.25) | collective-permute-done | bytes 131104 | tf_op jit(solution)/shard_map/ppermute | solution.py:28
  67.0 3.0 %collective-permute-done.24 = bf16[128,512]{1,0:T(8,128)(2,1)S(1)} collective-permute-done((bf16[128,512]{1,0:T(8,128)(2,1)S(1)}, bf16[128,512]{1,0:T(8,128)(2,1)S(1)}, u32[]{:S(2)}, u32[]{:S(2)}) %collective-permute-start.24) | collective-permute-done | bytes 131104 | tf_op jit(solution)/shard_map/ppermute | solution.py:28
  70.9 1.7 %collective-permute-start.27 = (bf16[128,512]{1,0:T(8,128)(2,1)S(1)}, bf16[128,512]{1,0:T(8,128)(2,1)S(1)}, u32[]{:S(2)}, u32[]{:S(2)}) collective-permute-start(bf16[128,512]{1,0:T(8,128)(2,1)S(1)} %fusion.2.refs_1_), channel_id=1, source_target_pairs={{0,2},{2,0},{4,6},{6,4},{1,3},{3,1},{5,7},{7,5},{8,10},{10,8},{12,... | collective-permute-start | bytes 393224 | tf_op jit(solution)/shard_map/ppermute | solution.py:28
  72.6 1.4 %collective-permute-start.28 = (bf16[128,512]{1,0:T(8,128)(2,1)S(1)}, bf16[128,512]{1,0:T(8,128)(2,1)S(1)}, u32[]{:S(2)}, u32[]{:S(2)}) collective-permute-start(bf16[128,512]{1,0:T(8,128)(2,1)S(1)} %fusion.2.refs_1_), channel_id=1, source_target_pairs={{0,4},{2,6},{4,0},{6,2},{1,5},{3,7},{5,1},{7,3},{8,12},{10,14},{12... | collective-permute-start | bytes 393224 | tf_op jit(solution)/shard_map/ppermute | solution.py:28
  74.9 2.9 %collective-permute-done.27.refs_2_ = bf16[128,512]{1,0:T(8,128)(2,1)S(1)} collective-permute-done((bf16[128,512]{1,0:T(8,128)(2,1)S(1)}, bf16[128,512]{1,0:T(8,128)(2,1)S(1)}, u32[]{:S(2)}, u32[]{:S(2)}) %collective-permute-start.27) | collective-permute-done | bytes 131104 | tf_op jit(solution)/shard_map/ppermute | solution.py:28
  78.8 1.3 %kv_grad.1 = bf16[1024,512]{1,0:T(8,128)(2,1)S(1)} custom-call(s32[3]{0:T(128)S(1)} %pad_add_fusion.refs_0_, bf16[128,512]{1,0:T(8,128)(2,1)S(1)} %bitcast.31, bf16[128,512]{1,0:T(8,128)(2,1)S(1)} %collective-permute-done.refs_2_, bf16[128,512]{1,0:T(8,128)(2,1)S(1)} %collective-permute-done.1.refs_3_, bf16[128,512]{1,0:T(8,128)(2,1)S(1)} %collective-permute-done.2.refs_4_, ...), custom_call_target="tpu_custom_call" | custom-call | flops 536870912 | bytes 2621452 | tf_op jit(solution)/shard_map/kv_grad/pallas_call | solution.py:134
  81.2 1.2 %collective-permute-done.28.refs_3_ = bf16[128,512]{1,0:T(8,128)(2,1)S(1)} collective-permute-done((bf16[128,512]{1,0:T(8,128)(2,1)S(1)}, bf16[128,512]{1,0:T(8,128)(2,1)S(1)}, u32[]{:S(2)}, u32[]{:S(2)}) %collective-permute-start.28) | collective-permute-done | bytes 131104 | tf_op jit(solution)/shard_map/ppermute | solution.py:28
  82.4 3.9 %collective-permute-done.29.refs_4_ = bf16[128,512]{1,0:T(8,128)(2,1)S(1)} collective-permute-done((bf16[128,512]{1,0:T(8,128)(2,1)S(1)}, bf16[128,512]{1,0:T(8,128)(2,1)S(1)}, u32[]{:S(2)}, u32[]{:S(2)}) %collective-permute-start.29) | collective-permute-done | bytes 131104 | tf_op jit(solution)/shard_map/ppermute | solution.py:28
  88.6 1.6 %input_grad.1 = bf16[128,4096]{1,0:T(8,128)(2,1)} custom-call(s32[3]{0:T(128)S(1)} %pad_add_fusion.refs_0_, bf16[128,512]{1,0:T(8,128)(2,1)S(1)} %fusion.2.refs_1_, bf16[128,512]{1,0:T(8,128)(2,1)S(1)} %collective-permute-done.27.refs_2_, bf16[128,512]{1,0:T(8,128)(2,1)S(1)} %collective-permute-done.28.refs_3_, ...), custom_call_target="tpu_custom_call" | custom-call | bytes 2097164 | tf_op jit(solution)/shard_map/input_grad/pallas_call | solution.py:134
  (72 shorter events, 22.0 us)
Async XLA Ops:
  0.6 14.2 %collective-permute-start.3 = (bf16[128,1024]{1,0:T(8,128)(2,1)}, bf16[128,1024]{1,0:T(8,128)(2,1)S(1)}, u32[]{:S(2)}, u32[]{:S(2)}) collective-permute-start(bf16[128,1024]{1,0:T(8,128)(2,1)} %refs_3_.1), channel_id=1, source_target_pairs={{0,4},{2,6},{4,0},{6,2},{1,5},{3,7},{5,1},{7,3},{8,12},{10,14},{12... | collective-permute-start | bytes 786440 | tf_op jit(solution)/shard_map/ppermute | solution.py:28
  3.0 11.8 %collective-permute-start.4 = (bf16[128,1024]{1,0:T(8,128)(2,1)}, bf16[128,1024]{1,0:T(8,128)(2,1)S(1)}, u32[]{:S(2)}, u32[]{:S(2)}) collective-permute-start(bf16[128,1024]{1,0:T(8,128)(2,1)} %refs_3_.1), channel_id=1, source_target_pairs={{0,2},{2,0},{4,6},{6,4},{1,3},{3,1},{5,7},{7,5},{8,10},{10,8},{12,... | collective-permute-start | bytes 786440 | tf_op jit(solution)/shard_map/ppermute | solution.py:28
  4.1 4.3 %collective-permute-start = (bf16[128,512]{1,0:T(8,128)(2,1)S(1)}, bf16[128,512]{1,0:T(8,128)(2,1)S(1)}, u32[]{:S(2)}, u32[]{:S(2)}) collective-permute-start(bf16[128,512]{1,0:T(8,128)(2,1)S(1)} %bitcast.27), channel_id=1, source_target_pairs={{0,8},{8,0},{16,24},{24,16},{1,9},{9,1},{17,25},{25,17},{2,10},{10... | collective-permute-start | bytes 393224 | tf_op jit(solution)/shard_map/ppermute | solution.py:28
  5.4 4.1 %collective-permute-start.1 = (bf16[128,512]{1,0:T(8,128)(2,1)S(1)}, bf16[128,512]{1,0:T(8,128)(2,1)S(1)}, u32[]{:S(2)}, u32[]{:S(2)}) collective-permute-start(bf16[128,512]{1,0:T(8,128)(2,1)S(1)} %bitcast.28), channel_id=1, source_target_pairs={{0,16},{8,24},{16,0},{24,8},{1,17},{9,25},{17,1},{25,9},{2,18},{10... | collective-permute-start | bytes 393224 | tf_op jit(solution)/shard_map/ppermute | solution.py:28
  6.6 5.5 %collective-permute-start.2 = (bf16[128,512]{1,0:T(8,128)(2,1)S(1)}, bf16[128,512]{1,0:T(8,128)(2,1)S(1)}, u32[]{:S(2)}, u32[]{:S(2)}) collective-permute-start(bf16[128,512]{1,0:T(8,128)(2,1)S(1)} %bitcast.29), channel_id=1, source_target_pairs={{0,24},{8,16},{16,8},{24,0},{1,25},{9,17},{17,9},{25,1},{2,26},{10... | collective-permute-start | bytes 393224 | tf_op jit(solution)/shard_map/ppermute | solution.py:28
  16.2 6.5 %collective-permute-start.5 = (bf16[512,1024]{1,0:T(8,128)(2,1)S(1)}, bf16[512,1024]{1,0:T(8,128)(2,1)S(1)}, u32[]{:S(2)}, u32[]{:S(2)}) collective-permute-start(bf16[512,1024]{1,0:T(8,128)(2,1)S(1)} %upstream_terms.1.refs_1_), channel_id=1, source_target_pairs={{0,1},{1,0},{2,3},{3,2},{4,5},{5,4},{6,7},{7,6},{8,9},{9,8},{10,11... | collective-permute-start | bytes 3145736 | tf_op jit(solution)/shard_map/ppermute | solution.py:28
  17.8 4.2 %collective-permute-start.7 = (bf16[128,2048]{1,0:T(8,128)(2,1)S(1)}, bf16[128,2048]{1,0:T(8,128)(2,1)S(1)}, u32[]{:S(2)}, u32[]{:S(2)}) collective-permute-start(bf16[128,2048]{1,0:T(8,128)(2,1)S(1)} %copy-done.2), channel_id=1, source_target_pairs={{0,1},{1,0},{2,3},{3,2},{4,5},{5,4},{6,7},{7,6},{8,9},{9,8},{10,11... | collective-permute-start | bytes 1572872 | tf_op jit(solution)/shard_map/ppermute | solution.py:28
  18.2 7.9 %collective-permute-start.10 = (bf16[128,1024]{1,0:T(8,128)(2,1)S(1)}, bf16[128,1024]{1,0:T(8,128)(2,1)S(1)}, u32[]{:S(2)}, u32[]{:S(2)}) collective-permute-start(bf16[128,1024]{1,0:T(8,128)(2,1)S(1)} %collective-permute-done.3.refs_5_), channel_id=1, source_target_pairs={{0,2},{2,0},{4,6},{6,4},{1,3},{3,1},{5,7},{7,5},{8,10},{10,8},{12,... | collective-permute-start | bytes 786440 | tf_op jit(solution)/shard_map/ppermute | solution.py:28
  18.5 8.9 %collective-permute-start.13 = (bf16[1024,128]{1,0:T(8,128)(2,1)S(1)}, bf16[1024,128]{1,0:T(8,128)(2,1)S(1)}, u32[]{:S(2)}, u32[]{:S(2)}) collective-permute-start(bf16[1024,128]{1,0:T(8,128)(2,1)S(1)} %copy-done), channel_id=1, source_target_pairs={{0,16},{8,24},{16,0},{24,8},{1,17},{9,25},{17,1},{25,9},{2,18},{10... | collective-permute-start | bytes 786440 | tf_op jit(solution)/shard_map/ppermute | solution.py:28
  20.7 8.7 %collective-permute-start.14 = (bf16[1024,128]{1,0:T(8,128)(2,1)S(1)}, bf16[1024,128]{1,0:T(8,128)(2,1)S(1)}, u32[]{:S(2)}, u32[]{:S(2)}) collective-permute-start(bf16[1024,128]{1,0:T(8,128)(2,1)S(1)} %copy-done.1), channel_id=1, source_target_pairs={{0,8},{8,0},{16,24},{24,16},{1,9},{9,1},{17,25},{25,17},{2,10},{10... | collective-permute-start | bytes 786440 | tf_op jit(solution)/shard_map/ppermute | solution.py:28
  21.9 11.9 %collective-permute-start.12 = (bf16[1024,128]{1,0:T(8,128)(2,1)S(1)}, bf16[1024,128]{1,0:T(8,128)(2,1)S(1)}, u32[]{:S(2)}, u32[]{:S(2)}) collective-permute-start(bf16[1024,128]{1,0:T(8,128)(2,1)S(1)} %copy-done), channel_id=1, source_target_pairs={{0,8},{8,0},{16,24},{24,16},{1,9},{9,1},{17,25},{25,17},{2,10},{10... | collective-permute-start | bytes 786440 | tf_op jit(solution)/shard_map/ppermute | solution.py:28
  22.7 12.4 %collective-permute-start.15 = (bf16[1024,128]{1,0:T(8,128)(2,1)S(1)}, bf16[1024,128]{1,0:T(8,128)(2,1)S(1)}, u32[]{:S(2)}, u32[]{:S(2)}) collective-permute-start(bf16[1024,128]{1,0:T(8,128)(2,1)S(1)} %copy-done.1), channel_id=1, source_target_pairs={{0,16},{8,24},{16,0},{24,8},{1,17},{9,25},{17,1},{25,9},{2,18},{10... | collective-permute-start | bytes 786440 | tf_op jit(solution)/shard_map/ppermute | solution.py:28
  26.1 11.8 %collective-permute-start.8 = (bf16[512,128]{1,0:T(8,128)(2,1)S(1)}, bf16[512,128]{1,0:T(8,128)(2,1)S(1)}, u32[]{:S(2)}, u32[]{:S(2)}) collective-permute-start(bf16[512,128]{1,0:T(8,128)(2,1)S(1)} %get-tuple-element.76), channel_id=1, source_target_pairs={{0,2},{2,0},{4,6},{6,4},{1,3},{3,1},{5,7},{7,5},{8,10},{10,8},{12,... | collective-permute-start | bytes 393224 | tf_op jit(solution)/shard_map/ppermute | solution.py:28
  27.3 10.5 %collective-permute-start.9 = (bf16[512,128]{1,0:T(8,128)(2,1)S(1)}, bf16[512,128]{1,0:T(8,128)(2,1)S(1)}, u32[]{:S(2)}, u32[]{:S(2)}) collective-permute-start(bf16[512,128]{1,0:T(8,128)(2,1)S(1)} %get-tuple-element.77), channel_id=1, source_target_pairs={{0,4},{2,6},{4,0},{6,2},{1,5},{3,7},{5,1},{7,3},{8,12},{10,14},{12... | collective-permute-start | bytes 393224 | tf_op jit(solution)/shard_map/ppermute | solution.py:28
  29.4 11.9 %collective-permute-start.11 = (bf16[512,128]{1,0:T(8,128)(2,1)S(1)}, bf16[512,128]{1,0:T(8,128)(2,1)S(1)}, u32[]{:S(2)}, u32[]{:S(2)}) collective-permute-start(bf16[512,128]{1,0:T(8,128)(2,1)S(1)} %hidden_last.1), channel_id=1, source_target_pairs={{0,6},{2,4},{4,2},{6,0},{1,7},{3,5},{5,3},{7,1},{8,14},{10,12},{12... | collective-permute-start | bytes 393224 | tf_op jit(solution)/shard_map/ppermute | solution.py:28
  33.9 17.8 %collective-permute-start.19 = (bf16[1024,128]{1,0:T(8,128)(2,1)S(1)}, bf16[1024,128]{1,0:T(8,128)(2,1)S(1)}, u32[]{:S(2)}, u32[]{:S(2)}) collective-permute-start(bf16[1024,128]{1,0:T(8,128)(2,1)S(1)} %collective-permute-done.12.refs_2_.refs_6_.refs_8_), channel_id=1, source_target_pairs={{0,16},{8,24},{16,0},{24,8},{1,17},{9,25},{17,1},{25,9},{2,18},{10... | collective-permute-start | bytes 786440 | tf_op jit(solution)/shard_map/ppermute | solution.py:28
  35.1 16.6 %collective-permute-start.20 = (bf16[1024,128]{1,0:T(8,128)(2,1)S(1)}, bf16[1024,128]{1,0:T(8,128)(2,1)S(1)}, u32[]{:S(2)}, u32[]{:S(2)}) collective-permute-start(bf16[1024,128]{1,0:T(8,128)(2,1)S(1)} %collective-permute-done.15.refs_6_.refs_11_.refs_13_), channel_id=1, source_target_pairs={{0,8},{8,0},{16,24},{24,16},{1,9},{9,1},{17,25},{25,17},{2,10},{10... | collective-permute-start | bytes 786440 | tf_op jit(solution)/shard_map/ppermute | solution.py:28
  41.9 4.2 %collective-permute-start.16 = (bf16[128,640]{1,0:T(8,128)(2,1)S(1)}, bf16[128,640]{1,0:T(8,128)(2,1)S(1)}, u32[]{:S(2)}, u32[]{:S(2)}) collective-permute-start(bf16[128,640]{1,0:T(8,128)(2,1)S(1)} %get-tuple-element.95), channel_id=1, source_target_pairs={{0,8},{8,0},{16,24},{24,16},{1,9},{9,1},{17,25},{25,17},{2,10},{10... | collective-permute-start | bytes 491528 | tf_op jit(solution)/shard_map/ppermute | solution.py:28
  43.2 4.5 %collective-permute-start.17 = (bf16[128,640]{1,0:T(8,128)(2,1)S(1)}, bf16[128,640]{1,0:T(8,128)(2,1)S(1)}, u32[]{:S(2)}, u32[]{:S(2)}) collective-permute-start(bf16[128,640]{1,0:T(8,128)(2,1)S(1)} %get-tuple-element.96), channel_id=1, source_target_pairs={{0,16},{8,24},{16,0},{24,8},{1,17},{9,25},{17,1},{25,9},{2,18},{10... | collective-permute-start | bytes 491528 | tf_op jit(solution)/shard_map/ppermute | solution.py:28
  44.4 7.1 %collective-permute-start.18 = (bf16[128,640]{1,0:T(8,128)(2,1)S(1)}, bf16[128,640]{1,0:T(8,128)(2,1)S(1)}, u32[]{:S(2)}, u32[]{:S(2)}) collective-permute-start(bf16[128,640]{1,0:T(8,128)(2,1)S(1)} %get-tuple-element.97), channel_id=1, source_target_pairs={{0,24},{8,16},{16,8},{24,0},{1,25},{9,17},{17,9},{25,1},{2,26},{10... | collective-permute-start | bytes 491528 | tf_op jit(solution)/shard_map/ppermute | solution.py:28
  51.5 5.6 %collective-permute-start.22 = (bf16[256,512]{1,0:T(8,128)(2,1)S(1)}, bf16[256,512]{1,0:T(8,128)(2,1)S(1)}, u32[]{:S(2)}, u32[]{:S(2)}) collective-permute-start(bf16[256,512]{1,0:T(8,128)(2,1)S(1)} %get-tuple-element.115), channel_id=1, source_target_pairs={{0,8},{8,0},{16,24},{24,16},{1,9},{9,1},{17,25},{25,17},{2,10},{10... | collective-permute-start | bytes 786440 | tf_op jit(solution)/shard_map/ppermute | solution.py:28
  53.1 4.5 %collective-permute-start.21 = (bf16[4,128,512]{2,1,0:T(8,128)(2,1)S(1)}, bf16[4,128,512]{2,1,0:T(8,128)(2,1)S(1)}, u32[]{:S(2)}, u32[]{:S(2)}) collective-permute-start(bf16[4,128,512]{2,1,0:T(8,128)(2,1)S(1)} %get-tuple-element.113), channel_id=1, source_target_pairs={{0,1},{1,0},{2,3},{3,2},{4,5},{5,4},{6,7},{7,6},{8,9},{9,8},{10,11... | collective-permute-start | bytes 1572872 | tf_op jit(solution)/shard_map/ppermute | solution.py:28
  57.8 9.2 %collective-permute-start.25 = (bf16[128,512]{1,0:T(8,128)(2,1)S(1)}, bf16[128,512]{1,0:T(8,128)(2,1)S(1)}, u32[]{:S(2)}, u32[]{:S(2)}) collective-permute-start(bf16[128,512]{1,0:T(8,128)(2,1)S(1)} %get-tuple-element.127), channel_id=1, source_target_pairs={{0,6},{2,4},{4,2},{6,0},{1,7},{3,5},{5,3},{7,1},{8,14},{10,12},{12... | collective-permute-start | bytes 393224 | tf_op jit(solution)/shard_map/ppermute | solution.py:28
  58.8 11.1 %collective-permute-start.24 = (bf16[128,512]{1,0:T(8,128)(2,1)S(1)}, bf16[128,512]{1,0:T(8,128)(2,1)S(1)}, u32[]{:S(2)}, u32[]{:S(2)}) collective-permute-start(bf16[128,512]{1,0:T(8,128)(2,1)S(1)} %get-tuple-element.128), channel_id=1, source_target_pairs={{0,4},{2,6},{4,0},{6,2},{1,5},{3,7},{5,1},{7,3},{8,12},{10,14},{12... | collective-permute-start | bytes 393224 | tf_op jit(solution)/shard_map/ppermute | solution.py:28
  58.9 11.1 %collective-permute-start.23 = (bf16[128,512]{1,0:T(8,128)(2,1)S(1)}, bf16[128,512]{1,0:T(8,128)(2,1)S(1)}, u32[]{:S(2)}, u32[]{:S(2)}) collective-permute-start(bf16[128,512]{1,0:T(8,128)(2,1)S(1)} %get-tuple-element.126), channel_id=1, source_target_pairs={{0,2},{2,0},{4,6},{6,4},{1,3},{3,1},{5,7},{7,5},{8,10},{10,8},{12,... | collective-permute-start | bytes 393224 | tf_op jit(solution)/shard_map/ppermute | solution.py:28
  60.6 9.5 %collective-permute-start.26 = (bf16[256,512]{1,0:T(8,128)(2,1)S(1)}, bf16[256,512]{1,0:T(8,128)(2,1)S(1)}, u32[]{:S(2)}, u32[]{:S(2)}) collective-permute-start(bf16[256,512]{1,0:T(8,128)(2,1)S(1)} %pad_maximum_fusion.1), channel_id=1, source_target_pairs={{0,16},{8,24},{16,0},{24,8},{1,17},{9,25},{17,1},{25,9},{2,18},{10... | collective-permute-start | bytes 786440 | tf_op jit(solution)/shard_map/ppermute | solution.py:28
  70.1 8.7 %collective-permute-start.30 = (bf16[512,512]{1,0:T(8,128)(2,1)S(1)}, bf16[512,512]{1,0:T(8,128)(2,1)S(1)}, u32[]{:S(2)}, u32[]{:S(2)}) collective-permute-start(bf16[512,512]{1,0:T(8,128)(2,1)S(1)} %pad_maximum_fusion.refs_5_), channel_id=1, source_target_pairs={{0,1},{1,0},{2,3},{3,2},{4,5},{5,4},{6,7},{7,6},{8,9},{9,8},{10,11... | collective-permute-start | bytes 1572872 | tf_op jit(solution)/shard_map/ppermute | solution.py:28
  70.9 6.9 %collective-permute-start.27 = (bf16[128,512]{1,0:T(8,128)(2,1)S(1)}, bf16[128,512]{1,0:T(8,128)(2,1)S(1)}, u32[]{:S(2)}, u32[]{:S(2)}) collective-permute-start(bf16[128,512]{1,0:T(8,128)(2,1)S(1)} %fusion.2.refs_1_), channel_id=1, source_target_pairs={{0,2},{2,0},{4,6},{6,4},{1,3},{3,1},{5,7},{7,5},{8,10},{10,8},{12,... | collective-permute-start | bytes 393224 | tf_op jit(solution)/shard_map/ppermute | solution.py:28
  72.6 9.8 %collective-permute-start.28 = (bf16[128,512]{1,0:T(8,128)(2,1)S(1)}, bf16[128,512]{1,0:T(8,128)(2,1)S(1)}, u32[]{:S(2)}, u32[]{:S(2)}) collective-permute-start(bf16[128,512]{1,0:T(8,128)(2,1)S(1)} %fusion.2.refs_1_), channel_id=1, source_target_pairs={{0,4},{2,6},{4,0},{6,2},{1,5},{3,7},{5,1},{7,3},{8,12},{10,14},{12... | collective-permute-start | bytes 393224 | tf_op jit(solution)/shard_map/ppermute | solution.py:28
  74.0 12.4 %collective-permute-start.29 = (bf16[128,512]{1,0:T(8,128)(2,1)S(1)}, bf16[128,512]{1,0:T(8,128)(2,1)S(1)}, u32[]{:S(2)}, u32[]{:S(2)}) collective-permute-start(bf16[128,512]{1,0:T(8,128)(2,1)S(1)} %fusion.2.refs_1_), channel_id=1, source_target_pairs={{0,6},{2,4},{4,2},{6,0},{1,7},{3,5},{5,3},{7,1},{8,14},{10,12},{12... | collective-permute-start | bytes 393224 | tf_op jit(solution)/shard_map/ppermute | solution.py:28
  74.3 12.9 %collective-permute-start.31 = (bf16[128,512]{1,0:T(8,128)(2,1)S(1)}, bf16[128,512]{1,0:T(8,128)(2,1)S(1)}, u32[]{:S(2)}, u32[]{:S(2)}) collective-permute-start(bf16[128,512]{1,0:T(8,128)(2,1)S(1)} %fusion.2.refs_1_), channel_id=1, source_target_pairs={{0,1},{1,0},{2,3},{3,2},{4,5},{5,4},{6,7},{7,6},{8,9},{9,8},{10,11... | collective-permute-start | bytes 393224 | tf_op jit(solution)/shard_map/ppermute | solution.py:28
  77.8 9.4 %collective-permute-start.32 = (bf16[128,512]{1,0:T(8,128)(2,1)S(1)}, bf16[128,512]{1,0:T(8,128)(2,1)S(1)}, u32[]{:S(2)}, u32[]{:S(2)}) collective-permute-start(bf16[128,512]{1,0:T(8,128)(2,1)S(1)} %collective-permute-done.27.refs_2_), channel_id=1, source_target_pairs={{0,1},{1,0},{2,3},{3,2},{4,5},{5,4},{6,7},{7,6},{8,9},{9,8},{10,11... | collective-permute-start | bytes 393224 | tf_op jit(solution)/shard_map/ppermute | solution.py:28
  (9 other events, 34.2 us)
